TPU v7x, 512 devices: a whole 4x4x16 slice. The times are simulated.
512 devices in a mesh: row: 16 (over y, x), col: 32 (over z, core).
Axes of the slice: x: 4, y: 4, z: 16, core: 2. Of those that a mesh axis runs over, the one named last changes fastest.
Arguments:
- right_sides: float32 [4, 16, 64, 64, 128], P(None, 'row', 'col'), may hold values from -6 to 6
- inverse_blocks: float32 [4, 16, 64, 128, 128], P(None, 'row', 'col')
- coupling_blocks: float32 [3, 16, 512, 128, 128], P(None, 'row', 'col'), may hold values from -0.25 to 0.25
- slot_counts: int32 [4, 16, 32], P(None, 'row', 'col'), may hold values from 1 to 2, as said below
- edge_sources: int32 [3, 16, 512], P(None, 'row', 'col'), may hold values from -1 to 191, as said below
- edge_targets: int32 [3, 16, 512], P(None, 'row', 'col'), may hold values from -1 to 31, as said below
Outputs:
- solution: float32 [4, 16, 64, 64, 128], P(None, 'row', 'col')
Inputs may be any that keep to these rules, and one draw needn't show every extreme that they name: `slot_counts`: at every level some device holds 2 live slots. `edge_sources`: for the 16 slots of one device at level l + 1 (l the first index): used slots come first and hold m * 32 * 2 + p, a live slot (m, this device row, p) with m <= l; unused slots hold -1; at every level some device uses all 16. `edge_targets`: -1 exactly where edge_sources is -1; else r * 2 + s, where slot (l + 1, r, c * 2 + s) is live and c is this device's column.
All inputs are finite; a program needn't handle non-finite values.
Results may differ from a plain program's by a relative error of at most 0.0001.
Values sent between devices are 32-bit elements; how exact they have to be, the bound alone decides.
No kernel may reach another device: no remote copies, remote signals or barrier semaphores. Data moves between devices by JAX's collectives and lax.ppermute only.
A program may use at most 64 MiB of HBM per device.

v0:
```python
import jax
import jax.numpy as jnp
from jax import lax
from jax.sharding import PartitionSpec as P


def edge_terms(history, sources, targets, blocks, usable, target_total):
    clipped = jnp.clip(sources, 0, history.shape[0] - 1)
    picked = jnp.take(history, clipped, axis=0) * usable.astype(jnp.float32)[:, None, None]
    terms = jnp.einsum("erb,ebd->erd", picked, blocks, precision=lax.Precision.HIGHEST)
    onehot = (
        (targets[None, :] == jnp.arange(target_total, dtype=jnp.int32)[:, None]) & usable[None, :]
    ).astype(jnp.float32)
    return jnp.einsum("te,erd->trd", onehot, terms, precision=lax.Precision.HIGHEST)


def on_device(
    right_sides, inverse_blocks, coupling_blocks, slot_counts, edge_sources, edge_targets
):
    level_total = right_sides.shape[0]
    slot_total = right_sides.shape[2]
    target_total = lax.axis_size("row") * slot_total
    row_span = lax.axis_size("col") * slot_total
    history = jnp.zeros((level_total * row_span,) + right_sides.shape[3:], jnp.float32)
    results = []
    for level_index in range(level_total):
        if level_index == 0:
            update = jnp.zeros((slot_total,) + right_sides.shape[3:], jnp.float32)
        else:
            sources = edge_sources[level_index - 1, 0]
            targets = edge_targets[level_index - 1, 0]
            blocks = coupling_blocks[level_index - 1, 0]
            buffer = edge_terms(history, sources, targets, blocks, sources >= 0, target_total)
            update = lax.psum_scatter(buffer, "row", scatter_dimension=0, tiled=True)
        alive_mask = jnp.arange(slot_total, dtype=jnp.int32) < slot_counts[level_index, 0, 0]
        solved = jnp.einsum(
            "srb,sbd->srd",
            right_sides[level_index, 0] - update,
            inverse_blocks[level_index, 0],
            precision=lax.Precision.HIGHEST,
        )
        solved = jnp.where(alive_mask[:, None, None], solved, jnp.float32(0.0))
        results.append(solved)
        if level_index + 1 < level_total:
            gathered = lax.all_gather(solved, "col", axis=0, tiled=True)
            history = lax.dynamic_update_slice_in_dim(history, gathered, level_index * row_span, 0)
    return jnp.stack(results)[:, None]


def solution(mesh):
    return jax.shard_map(
        on_device,
        mesh=mesh,
        in_specs=(
            P(None, "row", "col", None, None),
            P(None, "row", "col", None, None),
            P(None, "row", "col", None, None),
            P(None, "row", "col"),
            P(None, "row", "col"),
            P(None, "row", "col"),
        ),
        out_specs=P(None, "row", "col", None, None),
        check_vma=False,
    )
```

profile of v0, /device:TPU:1, one launch (start us, length us, event | category | flops | bytes accessed | tf_op | source)
XLA Modules:
  0.0 538.2 jit_solution(970591676571964878)
XLA Ops:
  6.5 1.5 fusion.59
  8.0 0.7 iota_compare_fusion.6
  8.7 1.8 convolution_select_fusion.3
  10.5 0.7 compare_and_fusion
  11.3 0.7 slice_bitcast_fusion
  12.0 0.7 compare_bitcast_fusion
  12.7 75.5 %all-gather.4.cloned.1.call-done = f32[64,64,128]{2,1,0:T(8,128)} async-done(((f32[2,64,128]{2,1,0:T(8,128)}), f32[64,64,128]{2,1,0:T(8,128)}) %all-gather.4.cloned.1.call-update) | async-done | bytes 2097168 | tf_op jit(solution)/shard_map/all_gather | solution.py:45
  88.2 6.0 %dynamic_update_slice.9 = f32[256,64,128]{2,1,0:T(8,128)} pad(f32[64,64,128]{2,1,0:T(8,128)} %all-gather.4.cloned.1.call-done, f32[]{:T(128)} %constant.0.clone.1), padding=0_192x0_0x0_0 | pad | bytes 10485764 | tf_op jit(solution)/shard_map/dynamic_update_slice | solution.py:46
  94.2 4.8 gather_fusion
  99.0 2.2 fusion.5
  101.2 0.8 fusion.14
  102.0 1.7 copy.10
  104.3 82.6 %reduce-scatter.4.cloned.1.call-done = f32[2,64,128]{2,1,0:T(8,128)} async-done(((f32[32,64,128]{2,1,0:T(8,128)}), f32[2,64,128]{2,1,0:T(8,128)}) %reduce-scatter.4.cloned.1.call-update) | async-done | bytes 65552 | tf_op jit(solution)/shard_map/reduce_scatter | solution.py:34
  186.9 1.8 convolution_select_fusion.2
  188.8 73.8 %all-gather.6.cloned.1.call-done = f32[64,64,128]{2,1,0:T(8,128)} async-done(((f32[2,64,128]{2,1,0:T(8,128)}), f32[64,64,128]{2,1,0:T(8,128)}) %all-gather.6.cloned.1.call-update) | async-done | bytes 2097168 | tf_op jit(solution)/shard_map/all_gather | solution.py:45
  262.5 3.2 constant_dynamic-update-slice_fusion.1
  265.7 4.8 gather_fusion.1
  270.5 2.2 fusion.3
  272.7 0.8 fusion.12
  273.5 1.7 copy.12
  275.8 82.5 %reduce-scatter.6.cloned.1.call-done = f32[2,64,128]{2,1,0:T(8,128)} async-done(((f32[32,64,128]{2,1,0:T(8,128)}), f32[2,64,128]{2,1,0:T(8,128)}) %reduce-scatter.6.cloned.1.call-update) | async-done | bytes 65552 | tf_op jit(solution)/shard_map/reduce_scatter | solution.py:34
  358.3 1.8 convolution_select_fusion.1
  360.2 73.4 %all-gather.8.cloned.1.call-done = f32[64,64,128]{2,1,0:T(8,128)} async-done(((f32[2,64,128]{2,1,0:T(8,128)}), f32[64,64,128]{2,1,0:T(8,128)}) %all-gather.8.cloned.1.call-update) | async-done | bytes 2097168 | tf_op jit(solution)/shard_map/all_gather | solution.py:45
  433.6 3.2 constant_dynamic-update-slice_fusion
  436.8 4.8 gather_fusion.2
  441.6 2.2 fusion.1
  443.8 0.8 fusion.10
  444.6 1.6 copy.14
  446.2 0.7 iota_compare_fusion.3
  446.9 82.5 %reduce-scatter.8.cloned.1.call-done = f32[2,64,128]{2,1,0:T(8,128)} async-done(((f32[32,64,128]{2,1,0:T(8,128)}), f32[2,64,128]{2,1,0:T(8,128)}) %reduce-scatter.8.cloned.1.call-update) | async-done | bytes 65552 | tf_op jit(solution)/shard_map/reduce_scatter | solution.py:34
  529.4 1.2 fusion
  530.7 0.7 maximum_bitcast_fusion
  (27 shorter events, 1.5 us)
Async XLA Ops:
  6.5 81.6 %all-gather.4.cloned.1.call-start = ((), (), s32[]{:S(2)}) async-start(), calls=%async_computation.3 | async-start | bytes 2162688 | tf_op jit(solution)/shard_map/all_gather | solution.py:45
  10.5 176.4 %reduce-scatter.4.cloned.1.call-start = ((), (), s32[]{:S(2)}) async-start(), calls=%async_computation.4 | async-start | bytes 1114112 | tf_op jit(solution)/shard_map/reduce_scatter | solution.py:34
  12.7 86.3 %copy-start = (f32[3,1,16,128,128]{4,3,2,1,0:T(8,128)S(1)}, f32[3,1,16,128,128]{4,3,2,1,0:T(8,128)}, u32[]{:S(2)}) copy-start(f32[3,1,16,128,128]{4,3,2,1,0:T(8,128)} %param.10) | copy-start | bytes 9437188
  99.0 87.9 %copy-start.4 = (f32[4,1,2,64,128]{4,3,2,1,0:T(8,128)S(1)}, f32[4,1,2,64,128]{4,3,2,1,0:T(8,128)}, u32[]{:S(2)}) copy-start(f32[4,1,2,64,128]{4,3,2,1,0:T(8,128)} %param.8) | copy-start | bytes 786436
  103.7 158.8 %all-gather.6.cloned.1.call-start = ((), (), s32[]{:S(2)}) async-start(), calls=%async_computation.5 | async-start | bytes 2162688 | tf_op jit(solution)/shard_map/all_gather | solution.py:45
  188.7 169.6 %reduce-scatter.6.cloned.1.call-start = ((), (), s32[]{:S(2)}) async-start(), calls=%async_computation.6 | async-start | bytes 1114112 | tf_op jit(solution)/shard_map/reduce_scatter | solution.py:34
  275.2 158.4 %all-gather.8.cloned.1.call-start = ((), (), s32[]{:S(2)}) async-start(), calls=%async_computation.7 | async-start | bytes 2162688 | tf_op jit(solution)/shard_map/all_gather | solution.py:45
  360.1 169.3 %reduce-scatter.8.cloned.1.call-start = ((), (), s32[]{:S(2)}) async-start(), calls=%async_computation.8 | async-start | bytes 1114112 | tf_op jit(solution)/shard_map/reduce_scatter | solution.py:34
  441.6 89.1 %copy-start.1 = (f32[2,64,128]{2,1,0:T(8,128)S(1)}, f32[2,64,128]{2,1,0:T(8,128)}, u32[]{:S(2)}) copy-start(f32[2,64,128]{2,1,0:T(8,128)} %convolution_select_fusion.2) | copy-start | bytes 196612
  441.6 89.1 %copy-start.2 = (f32[2,64,128]{2,1,0:T(8,128)S(1)}, f32[2,64,128]{2,1,0:T(8,128)}, u32[]{:S(2)}) copy-start(f32[2,64,128]{2,1,0:T(8,128)} %convolution_select_fusion.1) | copy-start | bytes 196612
  441.6 89.1 %copy-start.3 = (f32[2,64,128]{2,1,0:T(8,128)S(1)}, f32[2,64,128]{2,1,0:T(8,128)}, u32[]{:S(2)}) copy-start(f32[2,64,128]{2,1,0:T(8,128)} %convolution_select_fusion.3) | copy-start | bytes 196612
Sparse Core Ops, SparseCore 0:
  10.6 77.5 all-gather.3
  103.8 83.0 reduce-scatter.3
  189.2 73.2 all-gather.5
  275.3 82.9 reduce-scatter.5
  360.3 73.2 all-gather.7
  446.3 83.0 reduce-scatter.7
where the time goes:
time: 539 us; the launch traced here: 538 us
  waiting for transfers between devices  470 us (87%)
  local copies, waits for them, and re-layouts  33.9 us (6%)
  matrix products  15.6 us (3%)
  between operations  13.6 us (3%)
    reduce_scatter x3, waiting for transfers between devices, on_device(): update = lax.psum_scatter(buffer, 'row', scatter_dimension=0, tiled=True)  248 us
    all_gather x3, waiting for transfers between devices, on_device(): gathered = lax.all_gather(solved, 'col', axis=0, tiled=True)  223 us
    gather x3, local copies, waits for them, and re-layouts, edge_terms(): jnp.take(history, clipped, axis=0)  14.4 us
    dynamic_update_slice x3, local copies, waits for them, and re-layouts, on_device(): lax.dynamic_update_slice_in_dim(history, gathered, level_index * row_span...  12.4 us
  transfers between devices with their start and end apart: 6, of which 6 were waited for; matrix products, arithmetic and copies ran while one was open for 1% of the time, Pallas kernels for 0%

commit v1 on v0

v1 whole, which is shorter than its diff:
```python
import functools

import jax
import jax.numpy as jnp
from jax import lax
from jax.experimental import pallas as pl
from jax.experimental.pallas import tpu as pltpu
from jax.sharding import PartitionSpec as P

HIGHEST = lax.Precision.HIGHEST
ANY = pl.BlockSpec(memory_space=pl.ANY)
VMEM = pl.BlockSpec(memory_space=pltpu.VMEM)
SMEM = pl.BlockSpec(memory_space=pltpu.SMEM)
LIMIT = 32 * 1024 * 1024
GROUP = 4


def dot(a, b):
    return lax.dot_general(
        a, b, (((1,), (0,)), ((), ())), precision=HIGHEST, preferred_element_type=jnp.float32
    )


def solve_kernel(level, peers, *refs):
    if peers:
        received, counts, right, inverse, solved, copies = refs
    else:
        counts, right, inverse, solved, copies = refs
    for s in range(right.shape[0]):
        value = right[s]
        if peers:
            update = received[s]
            for peer in range(1, peers):
                update = update + received[peer * right.shape[0] + s]
            value = value - update
        value = dot(value, inverse[s])
        value = jnp.where(s < counts[level], value, jnp.zeros_like(value))
        solved[s] = value
        if copies is not None:
            for copy in range(copies.shape[0]):
                copies[copy, s] = value


def last_kernel(level, peers, received, counts, right, inverse, solved):
    solve_kernel(level, peers, received, counts, right, inverse, solved, None)


def solve(level, received, counts, right, inverse):
    block = jax.ShapeDtypeStruct(right.shape, jnp.float32)
    args = (counts, right, inverse)
    specs = [SMEM, VMEM, VMEM]
    peers = 0
    if received is not None:
        peers = received.shape[0] // right.shape[0]
        args, specs = (received,) + args, [VMEM] + specs
    params = pltpu.CompilerParams(vmem_limit_bytes=LIMIT)
    if level == 3:
        return pl.pallas_call(
            functools.partial(last_kernel, level, peers),
            out_shape=block, in_specs=specs, out_specs=VMEM, compiler_params=params,
        )(*args), None
    return pl.pallas_call(
        functools.partial(solve_kernel, level, peers),
        out_shape=(block, jax.ShapeDtypeStruct((GROUP,) + right.shape, jnp.float32)),
        in_specs=specs, out_specs=(VMEM, VMEM), compiler_params=params,
    )(*args)


def edge_kernel(level, edges, parts, *refs):
    part, place, target, coupling = refs[:4]
    history = refs[4 : 4 + parts]
    out, picked, blocks, picked_sem, block_sem = refs[4 + parts :]
    for e in range(edges):
        pltpu.make_async_copy(coupling.at[level - 1, 0, e], blocks.at[e], block_sem.at[e]).start()
    for e in range(edges):
        for index in range(parts):
            @pl.when(part[level - 1, e] == index)
            def _():
                pltpu.make_async_copy(
                    history[index].at[place[level - 1, e]], picked.at[e], picked_sem.at[e]
                ).start()
    out[...] = jnp.zeros_like(out)
    for e in range(edges):
        pltpu.make_async_copy(history[0].at[0], picked.at[e], picked_sem.at[e]).wait()
        pltpu.make_async_copy(coupling.at[level - 1, 0, e], blocks.at[e], block_sem.at[e]).wait()
        goal = target[level - 1, e]
        live = (goal >= 0).astype(jnp.float32)
        goal = jnp.maximum(goal, 0)
        out[goal] = out[goal] + dot(picked[e] * live, blocks[e])


def edge_terms(level, part, place, target, coupling, history, target_total):
    edges = coupling.shape[2]
    rows, order = history[0].shape[1:]
    return pl.pallas_call(
        functools.partial(edge_kernel, level, edges, len(history)),
        out_shape=jax.ShapeDtypeStruct((target_total, rows, order), jnp.float32),
        in_specs=[SMEM, SMEM, SMEM, ANY] + [ANY] * len(history),
        out_specs=VMEM,
        scratch_shapes=[
            pltpu.VMEM((edges, rows, order), jnp.float32),
            pltpu.VMEM((edges, order, order), jnp.float32),
            pltpu.SemaphoreType.DMA((edges,)),
            pltpu.SemaphoreType.DMA((edges,)),
        ],
        compiler_params=pltpu.CompilerParams(vmem_limit_bytes=LIMIT),
    )(part, place, target, coupling, *history)


def gather_col(copies, cols):
    chips = cols // 2
    far = [
        [2 * (GROUP * hi + lo) + core for hi in range(chips // GROUP)]
        for lo in range(GROUP)
        for core in range(2)
    ]

    def shift(x, k):
        return lax.ppermute(x, "col", [(i, (i + 2 * k) % cols) for i in range(cols)])

    mine = lax.all_to_all(copies, "col", 0, 0, tiled=True, axis_index_groups=far)
    half = mine.shape[0] // 2
    below, above = shift(mine, 1), shift(mine, -1)
    low, high = shift(mine[:half], 2), shift(mine[half:], -2)
    same = jnp.concatenate([mine, below, low, high, above])
    return same.reshape((-1,) + same.shape[2:])


def on_device(
    right_sides, inverse_blocks, coupling_blocks, slot_counts, edge_sources, edge_targets
):
    level_total = right_sides.shape[0]
    slots = right_sides.shape[2]
    rows, cols = lax.axis_size("row"), lax.axis_size("col")
    column = lax.axis_index("col")
    core, low_chip = column % 2, (column // 2) % GROUP
    sources = jnp.maximum(edge_sources[:, 0], 0)
    source_level, source_slot = sources // (cols * slots), sources % slots
    source_col = (sources // slots) % cols
    source_chip = source_col // 2
    distance = (low_chip - source_chip) % GROUP
    part = source_level * 2 + (source_col % 2 != core).astype(jnp.int32)
    place = (distance * (cols // 2 // GROUP) + source_chip // GROUP) * slots + source_slot
    targets = edge_targets[:, 0]
    counts = slot_counts[:, 0, 0]
    history, results, received = [], [], None
    for level in range(level_total):
        if level:
            terms = edge_terms(
                level, part, place, targets, coupling_blocks, history, rows * slots
            )
            received = lax.all_to_all(terms, "row", 0, 0, tiled=True)
        solved, copies = solve(
            level, received, counts, right_sides[level, 0], inverse_blocks[level, 0]
        )
        results.append(solved)
        if level + 1 < level_total:
            same = gather_col(copies, cols)
            other = lax.ppermute(same, "col", [(i, i ^ 1) for i in range(cols)])
            history += [same, other]
    return jnp.stack(results)[:, None]


def solution(mesh):
    return jax.shard_map(
        on_device,
        mesh=mesh,
        in_specs=(
            P(None, "row", "col", None, None),
            P(None, "row", "col", None, None),
            P(None, "row", "col", None, None),
            P(None, "row", "col"),
            P(None, "row", "col"),
            P(None, "row", "col"),
        ),
        out_specs=P(None, "row", "col", None, None),
        check_vma=False,
    )
```

time: 539 us -> 250 us (0.46)
  waiting for transfers between devices: 470 us -> 18.9 us
  blocking collectives: 0 us -> 129 us
  starting transfers between devices: 0.21 us -> 69.6 us
  local copies, waits for them, and re-layouts: 33.9 us -> 7.29 us
  Pallas kernels: 0 us -> 23.3 us
  matrix products: 15.6 us -> 0 us
  between operations: 13.6 us -> 0.45 us
    reduce_scatter x3 -> x0, waiting for transfers between devices: 248 us -> none  [on_device(): update = lax.psum_scatter(buffer, 'row', scatter_dimension=0, tiled=True)]
    all_gather x3 -> x0, waiting for transfers between devices: 223 us -> none  [on_device(): gathered = lax.all_gather(solved, 'col', axis=0, tiled=True)]
    all_to_all x0 -> x6, blocking collectives: none -> 129 us  [the longest x3 65.6 us: gather_col(): lax.all_to_all(copies, 'col', 0, 0, tiled=True, axis_index_groups=far)]
    ppermute x0 -> x15, starting transfers between devices: none -> 69.6 us  [the longest x12 55.5 us: shift(): lax.ppermute(x, 'col', [(i, (i + 2 * k) % cols) for i in range(cols)])]
    pallas_call x0 -> x7, Pallas kernels: none -> 23.3 us  [the longest x3 20 us: edge_terms(): pl.pallas_call(functools.partial(edge_kernel, level, edges, len(history))...]
    ppermute x0 -> x15, waiting for transfers between devices: none -> 18.9 us  [the longest x12 11.9 us: shift(): lax.ppermute(x, 'col', [(i, (i + 2 * k) % cols) for i in range(cols)])]
    dot_general x10 -> x0, matrix products: 15.6 us -> none  [the longest x4 6.63 us: on_device(): jnp.einsum('srb,sbd->srd', right_sides[level_index, 0] - update, inverse_...]
    gather x3 -> x0, local copies, waits for them, and re-layouts: 14.4 us -> none  [edge_terms(): jnp.take(history, clipped, axis=0)]
  transfers between devices with their start and end apart: 6 -> 15, of which waited for: 6 -> 7; matrix products, arithmetic and copies ran while one was open for 1% -> 1% of each run, Pallas kernels for 0% -> 0%
where the time goes in v1:
time: 250 us; the launch traced here: 249 us
  blocking collectives  129 us (52%)
  starting transfers between devices  69.6 us (28%)
  Pallas kernels  23.3 us (9%)
  waiting for transfers between devices  18.9 us (8%)
  local copies, waits for them, and re-layouts  7.29 us (3%)
    all_to_all x3, blocking collectives, gather_col(): lax.all_to_all(copies, 'col', 0, 0, tiled=True, axis_index_groups=far)  65.6 us
    all_to_all x3, blocking collectives, on_device(): received = lax.all_to_all(terms, 'row', 0, 0, tiled=True)  63.2 us
    ppermute x12, starting transfers between devices, shift(): lax.ppermute(x, 'col', [(i, (i + 2 * k) % cols) for i in range(cols)])  55.5 us
    pallas_call x3, Pallas kernels, edge_terms(): pl.pallas_call(functools.partial(edge_kernel, level, edges, len(history))...  20 us
    ppermute x3, starting transfers between devices, on_device(): other = lax.ppermute(same, 'col', [(i, i ^ 1) for i in range(cols)])  14.1 us
    ppermute x12, waiting for transfers between devices, shift(): lax.ppermute(x, 'col', [(i, (i + 2 * k) % cols) for i in range(cols)])  11.9 us
    ppermute x3, waiting for transfers between devices, on_device(): other = lax.ppermute(same, 'col', [(i, i ^ 1) for i in range(cols)])  6.99 us
  transfers between devices with their start and end apart: 15, of which 7 were waited for; matrix products, arithmetic and copies ran while one was open for 1% of the time, Pallas kernels for 0%

profile of v1, /device:TPU:1, one launch (start us, length us, event | category | flops | bytes accessed | tf_op | source)
XLA Modules:
  0.0 249.1 jit_solution(9666563800276509538)
XLA Ops:
  0.0 1.8 slice_bitcast_fusion.4
  4.4 29.6 %all_to_all.30 = f32[4,2,64,128]{3,2,1,0:T(8,128)S(1)} all-to-all(f32[4,2,64,128]{3,2,1,0:T(8,128)S(1)} %get-tuple-element.12), channel_id=1, replica_groups={{0,8,16,24},{1,9,17,25},{2,10,18,26},{3,11,19,27},{4,12,20,28},{5,13,21..., dimensions={0} | all-to-all | bytes 524288 | tf_op jit(solution)/shard_map/all_to_all | solution.py:121
  34.0 8.8 %collective-permute-start = (f32[4,2,64,128]{3,2,1,0:T(8,128)S(1)}, f32[4,2,64,128]{3,2,1,0:T(8,128)S(1)}, u32[]{:S(2)}, u32[]{:S(2)}) collective-permute-start(f32[4,2,64,128]{3,2,1,0:T(8,128)S(1)} %all_to_all.30), channel_id=1, source_target_pairs={{0,2},{1,3},{2,4},{3,5},{4,6},{5,7},{6,8},{7,9},{8,10},{9,11},{10,... | collective-permute-start | bytes 786440 | tf_op jit(solution)/shard_map/ppermute | solution.py:119
  42.8 2.3 collective-permute-start.2
  45.2 3.8 %collective-permute-start.1 = (f32[2,2,64,128]{3,2,1,0:T(8,128)S(1)}, f32[2,2,64,128]{3,2,1,0:T(8,128)S(1)}, u32[]{:S(2)}, u32[]{:S(2)}) collective-permute-start(f32[2,2,64,128]{3,2,1,0:T(8,128)S(1)} %get-tuple-element.30), channel_id=1, source_target_pairs={{0,4},{1,5},{2,6},{3,7},{4,8},{5,9},{6,10},{7,11},{8,12},{9,13},{1... | collective-permute-start | bytes 393224 | tf_op jit(solution)/shard_map/ppermute | solution.py:119
  49.0 3.1 %collective-permute-start.3 = (f32[4,2,64,128]{3,2,1,0:T(8,128)S(1)}, f32[4,2,64,128]{3,2,1,0:T(8,128)S(1)}, u32[]{:S(2)}, u32[]{:S(2)}) collective-permute-start(f32[4,2,64,128]{3,2,1,0:T(8,128)S(1)} %all_to_all.30), channel_id=1, source_target_pairs={{0,30},{1,31},{2,0},{3,1},{4,2},{5,3},{6,4},{7,5},{8,6},{9,7},{10,... | collective-permute-start | bytes 786440 | tf_op jit(solution)/shard_map/ppermute | solution.py:119
  53.6 2.5 %collective-permute-done.1 = f32[2,2,64,128]{3,2,1,0:T(8,128)S(1)} collective-permute-done((f32[2,2,64,128]{3,2,1,0:T(8,128)S(1)}, f32[2,2,64,128]{3,2,1,0:T(8,128)S(1)}, u32[]{:S(2)}, u32[]{:S(2)}) %collective-permute-start.1) | collective-permute-done | bytes 131104 | tf_op jit(solution)/shard_map/ppermute | solution.py:119
  58.2 4.5 %collective-permute-start.4 = (f32[32,64,128]{2,1,0:T(8,128)}, f32[32,64,128]{2,1,0:T(8,128)}, u32[]{:S(2)}, u32[]{:S(2)}) collective-permute-start(f32[32,64,128]{2,1,0:T(8,128)} %bitcast.4.refs_4_), channel_id=1, source_target_pairs={{0,1},{1,0},{2,3},{3,2},{4,5},{5,4},{6,7},{7,6},{8,9},{9,8},{10,11... | collective-permute-start | bytes 3145736 | tf_op jit(solution)/shard_map/ppermute | solution.py:159
  62.8 2.5 collective-permute-done.4.refs_5_
  65.2 6.7 %shard_map.65 = f32[32,64,128]{2,1,0:T(8,128)S(1)} custom-call(s32[3,16]{1,0:T(4,128)S(1)} %get-tuple-element.32.refs_0_, s32[3,16]{1,0:T(4,128)S(1)} %get-tuple-element.31.refs_1_, s32[3,16]{1,0:T(4,128)S(1)} %bitcast.81, f32[3,1,16,128,128]{4,3,2,1,0:T(8,128)S(1)} %copy-done, f32[32,64,128]{2,1,0:T(8,128)} %bitcast.4.refs_4_, ...), custom_call_target="tpu_custom_call" | custom-call | tf_op jit(solution)/shard_map/pallas_call | solution.py:95
  71.9 22.9 %all_to_all.31.refs_0_ = f32[32,64,128]{2,1,0:T(8,128)S(1)} all-to-all(f32[32,64,128]{2,1,0:T(8,128)S(1)} %shard_map.65), channel_id=1, replica_groups=mesh['row'=16,'col'=32] {'row'}, dimensions={0} | all-to-all | bytes 2097152 | tf_op jit(solution)/shard_map/all_to_all | solution.py:152
  95.7 18.3 %all_to_all.32 = f32[4,2,64,128]{3,2,1,0:T(8,128)S(1)} all-to-all(f32[4,2,64,128]{3,2,1,0:T(8,128)S(1)} %get-tuple-element.14), channel_id=1, replica_groups={{0,8,16,24},{1,9,17,25},{2,10,18,26},{3,11,19,27},{4,12,20,28},{5,13,21..., dimensions={0} | all-to-all | bytes 524288 | tf_op jit(solution)/shard_map/all_to_all | solution.py:121
  114.0 2.3 collective-permute-start.5
  116.3 9.2 %collective-permute-start.7 = (f32[2,2,64,128]{3,2,1,0:T(8,128)S(1)}, f32[2,2,64,128]{3,2,1,0:T(8,128)S(1)}, u32[]{:S(2)}, u32[]{:S(2)}) collective-permute-start(f32[2,2,64,128]{3,2,1,0:T(8,128)S(1)} %get-tuple-element.27), channel_id=1, source_target_pairs={{0,28},{1,29},{2,30},{3,31},{4,0},{5,1},{6,2},{7,3},{8,4},{9,5},{1... | collective-permute-start | bytes 393224 | tf_op jit(solution)/shard_map/ppermute | solution.py:119
  125.6 1.9 collective-permute-start.6
  127.5 4.3 %collective-permute-start.8 = (f32[4,2,64,128]{3,2,1,0:T(8,128)S(1)}, f32[4,2,64,128]{3,2,1,0:T(8,128)S(1)}, u32[]{:S(2)}, u32[]{:S(2)}) collective-permute-start(f32[4,2,64,128]{3,2,1,0:T(8,128)S(1)} %all_to_all.32), channel_id=1, source_target_pairs={{0,30},{1,31},{2,0},{3,1},{4,2},{5,3},{6,4},{7,5},{8,6},{9,7},{10,... | collective-permute-start | bytes 786440 | tf_op jit(solution)/shard_map/ppermute | solution.py:119
  131.9 4.4 %collective-permute-done.6 = f32[2,2,64,128]{3,2,1,0:T(8,128)S(1)} collective-permute-done((f32[2,2,64,128]{3,2,1,0:T(8,128)S(1)}, f32[2,2,64,128]{3,2,1,0:T(8,128)S(1)}, u32[]{:S(2)}, u32[]{:S(2)}) %collective-permute-start.6) | collective-permute-done | bytes 131104 | tf_op jit(solution)/shard_map/ppermute | solution.py:119
  136.3 5.5 %collective-permute-start.9 = (f32[32,64,128]{2,1,0:T(8,128)S(1)}, f32[32,64,128]{2,1,0:T(8,128)S(1)}, u32[]{:S(2)}, u32[]{:S(2)}) collective-permute-start(f32[32,64,128]{2,1,0:T(8,128)S(1)} %bitcast.72), channel_id=1, source_target_pairs={{0,1},{1,0},{2,3},{3,2},{4,5},{5,4},{6,7},{7,6},{8,9},{9,8},{10,11... | collective-permute-start | bytes 3145736 | tf_op jit(solution)/shard_map/ppermute | solution.py:159
  141.8 2.3 collective-permute-done.9.refs_7_
  144.1 6.7 %shard_map.67 = f32[32,64,128]{2,1,0:T(8,128)S(1)} custom-call(s32[3,16]{1,0:T(4,128)S(1)} %get-tuple-element.32.refs_0_, s32[3,16]{1,0:T(4,128)S(1)} %get-tuple-element.31.refs_1_, s32[3,16]{1,0:T(4,128)S(1)} %bitcast.82, f32[3,1,16,128,128]{4,3,2,1,0:T(8,128)S(1)} %copy-done, f32[32,64,128]{2,1,0:T(8,128)} %bitcast.4.refs_4_, ...), custom_call_target="tpu_custom_call" | custom-call | tf_op jit(solution)/shard_map/pallas_call | solution.py:95
  150.8 20.3 %all_to_all.33.refs_0_ = f32[32,64,128]{2,1,0:T(8,128)S(1)} all-to-all(f32[32,64,128]{2,1,0:T(8,128)S(1)} %shard_map.67), channel_id=1, replica_groups=mesh['row'=16,'col'=32] {'row'}, dimensions={0} | all-to-all | bytes 2097152 | tf_op jit(solution)/shard_map/all_to_all | solution.py:152
  171.9 17.6 %all_to_all.34 = f32[4,2,64,128]{3,2,1,0:T(8,128)S(1)} all-to-all(f32[4,2,64,128]{3,2,1,0:T(8,128)S(1)} %get-tuple-element.16), channel_id=1, replica_groups={{0,8,16,24},{1,9,17,25},{2,10,18,26},{3,11,19,27},{4,12,20,28},{5,13,21..., dimensions={0} | all-to-all | bytes 524288 | tf_op jit(solution)/shard_map/all_to_all | solution.py:121
  189.6 2.6 %collective-permute-start.10 = (f32[4,2,64,128]{3,2,1,0:T(8,128)S(1)}, f32[4,2,64,128]{3,2,1,0:T(8,128)S(1)}, u32[]{:S(2)}, u32[]{:S(2)}) collective-permute-start(f32[4,2,64,128]{3,2,1,0:T(8,128)S(1)} %all_to_all.34), channel_id=1, source_target_pairs={{0,2},{1,3},{2,4},{3,5},{4,6},{5,7},{6,8},{7,9},{8,10},{9,11},{10,... | collective-permute-start | bytes 786440 | tf_op jit(solution)/shard_map/ppermute | solution.py:119
  192.2 9.5 %collective-permute-start.12 = (f32[2,2,64,128]{3,2,1,0:T(8,128)S(1)}, f32[2,2,64,128]{3,2,1,0:T(8,128)S(1)}, u32[]{:S(2)}, u32[]{:S(2)}) collective-permute-start(f32[2,2,64,128]{3,2,1,0:T(8,128)S(1)} %get-tuple-element.25), channel_id=1, source_target_pairs={{0,28},{1,29},{2,30},{3,31},{4,0},{5,1},{6,2},{7,3},{8,4},{9,5},{1... | collective-permute-start | bytes 393224 | tf_op jit(solution)/shard_map/ppermute | solution.py:119
  201.7 3.0 %collective-permute-start.11 = (f32[2,2,64,128]{3,2,1,0:T(8,128)S(1)}, f32[2,2,64,128]{3,2,1,0:T(8,128)S(1)}, u32[]{:S(2)}, u32[]{:S(2)}) collective-permute-start(f32[2,2,64,128]{3,2,1,0:T(8,128)S(1)} %get-tuple-element.26), channel_id=1, source_target_pairs={{0,4},{1,5},{2,6},{3,7},{4,8},{5,9},{6,10},{7,11},{8,12},{9,13},{1... | collective-permute-start | bytes 393224 | tf_op jit(solution)/shard_map/ppermute | solution.py:119
  204.7 4.6 %collective-permute-start.13 = (f32[4,2,64,128]{3,2,1,0:T(8,128)S(1)}, f32[4,2,64,128]{3,2,1,0:T(8,128)S(1)}, u32[]{:S(2)}, u32[]{:S(2)}) collective-permute-start(f32[4,2,64,128]{3,2,1,0:T(8,128)S(1)} %all_to_all.34), channel_id=1, source_target_pairs={{0,30},{1,31},{2,0},{3,1},{4,2},{5,3},{6,4},{7,5},{8,6},{9,7},{10,... | collective-permute-start | bytes 786440 | tf_op jit(solution)/shard_map/ppermute | solution.py:119
  209.4 2.6 %collective-permute-done.11 = f32[2,2,64,128]{3,2,1,0:T(8,128)S(1)} collective-permute-done((f32[2,2,64,128]{3,2,1,0:T(8,128)S(1)}, f32[2,2,64,128]{3,2,1,0:T(8,128)S(1)}, u32[]{:S(2)}, u32[]{:S(2)}) %collective-permute-start.11) | collective-permute-done | bytes 131104 | tf_op jit(solution)/shard_map/ppermute | solution.py:119
  212.0 2.4 collective-permute-done.13
  214.4 4.1 %collective-permute-start.14 = (f32[32,64,128]{2,1,0:T(8,128)S(1)}, f32[32,64,128]{2,1,0:T(8,128)S(1)}, u32[]{:S(2)}, u32[]{:S(2)}) collective-permute-start(f32[32,64,128]{2,1,0:T(8,128)S(1)} %bitcast.75), channel_id=1, source_target_pairs={{0,1},{1,0},{2,3},{3,2},{4,5},{5,4},{6,7},{7,6},{8,9},{9,8},{10,11... | collective-permute-start | bytes 3145736 | tf_op jit(solution)/shard_map/ppermute | solution.py:159
  218.6 2.3 collective-permute-done.14.refs_9_
  220.8 6.7 %shard_map.69 = f32[32,64,128]{2,1,0:T(8,128)S(1)} custom-call(s32[3,16]{1,0:T(4,128)S(1)} %get-tuple-element.32.refs_0_, s32[3,16]{1,0:T(4,128)S(1)} %get-tuple-element.31.refs_1_, s32[3,16]{1,0:T(4,128)S(1)} %bitcast.83, f32[3,1,16,128,128]{4,3,2,1,0:T(8,128)S(1)} %copy-done, f32[32,64,128]{2,1,0:T(8,128)} %bitcast.4.refs_4_, ...), custom_call_target="tpu_custom_call" | custom-call | tf_op jit(solution)/shard_map/pallas_call | solution.py:95
  227.5 20.0 %all_to_all.35.received = f32[32,64,128]{2,1,0:T(8,128)S(1)} all-to-all(f32[32,64,128]{2,1,0:T(8,128)S(1)} %shard_map.69), channel_id=1, replica_groups=mesh['row'=16,'col'=32] {'row'}, dimensions={0} | all-to-all | bytes 2097152 | tf_op jit(solution)/shard_map/all_to_all | solution.py:152
  (56 shorter events, 9.6 us)
Async XLA Ops:
  0.0 65.2 %copy-start = (f32[3,1,16,128,128]{4,3,2,1,0:T(8,128)S(1)}, f32[3,1,16,128,128]{4,3,2,1,0:T(8,128)}, u32[]{:S(2)}) copy-start(f32[3,1,16,128,128]{4,3,2,1,0:T(8,128)} %refs_3_.5) | copy-start | bytes 9437188
  2.9 0.7 copy-start.6
  3.6 59.1 %copy-start.9 = (s32[3,1,16]{2,1,0:T(1,128)S(1)}, s32[3,1,16]{2,1,0:T(1,128)}, u32[]{:S(2)}) copy-start(s32[3,1,16]{2,1,0:T(1,128)} %param.11) | copy-start | bytes 580
  3.6 59.1 %copy-start.8 = (s32[3,1,16]{2,1,0:T(1,128)S(1)}, s32[3,1,16]{2,1,0:T(1,128)}, u32[]{:S(2)}) copy-start(s32[3,1,16]{2,1,0:T(1,128)} %param.10) | copy-start | bytes 580
  4.4 29.6 %copy-start.4 = (f32[2,64,128]{2,1,0:T(8,128)}, f32[2,64,128]{2,1,0:T(8,128)S(1)}, u32[]{:S(2)}) copy-start(f32[2,64,128]{2,1,0:T(8,128)S(1)} %get-tuple-element.11) | copy-start | bytes 196612
  34.0 18.9 %collective-permute-start = (f32[4,2,64,128]{3,2,1,0:T(8,128)S(1)}, f32[4,2,64,128]{3,2,1,0:T(8,128)S(1)}, u32[]{:S(2)}, u32[]{:S(2)}) collective-permute-start(f32[4,2,64,128]{3,2,1,0:T(8,128)S(1)} %all_to_all.30), channel_id=1, source_target_pairs={{0,2},{1,3},{2,4},{3,5},{4,6},{5,7},{6,8},{7,9},{8,10},{9,11},{10,... | collective-permute-start | bytes 786440 | tf_op jit(solution)/shard_map/ppermute | solution.py:119
  42.8 14.0 %collective-permute-start.2 = (f32[2,2,64,128]{3,2,1,0:T(8,128)S(1)}, f32[2,2,64,128]{3,2,1,0:T(8,128)S(1)}, u32[]{:S(2)}, u32[]{:S(2)}) collective-permute-start(f32[2,2,64,128]{3,2,1,0:T(8,128)S(1)} %get-tuple-element.29), channel_id=1, source_target_pairs={{0,28},{1,29},{2,30},{3,31},{4,0},{5,1},{6,2},{7,3},{8,4},{9,5},{1... | collective-permute-start | bytes 393224 | tf_op jit(solution)/shard_map/ppermute | solution.py:119
  45.2 11.0 %collective-permute-start.1 = (f32[2,2,64,128]{3,2,1,0:T(8,128)S(1)}, f32[2,2,64,128]{3,2,1,0:T(8,128)S(1)}, u32[]{:S(2)}, u32[]{:S(2)}) collective-permute-start(f32[2,2,64,128]{3,2,1,0:T(8,128)S(1)} %get-tuple-element.30), channel_id=1, source_target_pairs={{0,4},{1,5},{2,6},{3,7},{4,8},{5,9},{6,10},{7,11},{8,12},{9,13},{1... | collective-permute-start | bytes 393224 | tf_op jit(solution)/shard_map/ppermute | solution.py:119
  49.0 8.4 %collective-permute-start.3 = (f32[4,2,64,128]{3,2,1,0:T(8,128)S(1)}, f32[4,2,64,128]{3,2,1,0:T(8,128)S(1)}, u32[]{:S(2)}, u32[]{:S(2)}) collective-permute-start(f32[4,2,64,128]{3,2,1,0:T(8,128)S(1)} %all_to_all.30), channel_id=1, source_target_pairs={{0,30},{1,31},{2,0},{3,1},{4,2},{5,3},{6,4},{7,5},{8,6},{9,7},{10,... | collective-permute-start | bytes 786440 | tf_op jit(solution)/shard_map/ppermute | solution.py:119
  58.2 7.1 %collective-permute-start.4 = (f32[32,64,128]{2,1,0:T(8,128)}, f32[32,64,128]{2,1,0:T(8,128)}, u32[]{:S(2)}, u32[]{:S(2)}) collective-permute-start(f32[32,64,128]{2,1,0:T(8,128)} %bitcast.4.refs_4_), channel_id=1, source_target_pairs={{0,1},{1,0},{2,3},{3,2},{4,5},{5,4},{6,7},{7,6},{8,9},{9,8},{10,11... | collective-permute-start | bytes 3145736 | tf_op jit(solution)/shard_map/ppermute | solution.py:159
  65.2 29.6 %copy-start.3 = (f32[2,64,128]{2,1,0:T(8,128)S(1)}, f32[2,64,128]{2,1,0:T(8,128)}, u32[]{:S(2)}) copy-start(f32[2,64,128]{2,1,0:T(8,128)} %get-tuple-element.22.refs_2_) | copy-start | bytes 196612
  65.2 29.6 %copy-start.7 = (s32[4,1,1]{0,2,1:T(1,128)S(1)}, s32[4,1,1]{0,2,1:T(1,128)}, u32[]{:S(2)}) copy-start(s32[4,1,1]{0,2,1:T(1,128)} %param.9) | copy-start | bytes 52
  114.0 17.8 %collective-permute-start.5 = (f32[4,2,64,128]{3,2,1,0:T(8,128)S(1)}, f32[4,2,64,128]{3,2,1,0:T(8,128)S(1)}, u32[]{:S(2)}, u32[]{:S(2)}) collective-permute-start(f32[4,2,64,128]{3,2,1,0:T(8,128)S(1)} %all_to_all.32), channel_id=1, source_target_pairs={{0,2},{1,3},{2,4},{3,5},{4,6},{5,7},{6,8},{7,9},{8,10},{9,11},{10,... | collective-permute-start | bytes 786440 | tf_op jit(solution)/shard_map/ppermute | solution.py:119
  116.3 20.0 %collective-permute-start.7 = (f32[2,2,64,128]{3,2,1,0:T(8,128)S(1)}, f32[2,2,64,128]{3,2,1,0:T(8,128)S(1)}, u32[]{:S(2)}, u32[]{:S(2)}) collective-permute-start(f32[2,2,64,128]{3,2,1,0:T(8,128)S(1)} %get-tuple-element.27), channel_id=1, source_target_pairs={{0,28},{1,29},{2,30},{3,31},{4,0},{5,1},{6,2},{7,3},{8,4},{9,5},{1... | collective-permute-start | bytes 393224 | tf_op jit(solution)/shard_map/ppermute | solution.py:119
  125.6 10.7 %collective-permute-start.6 = (f32[2,2,64,128]{3,2,1,0:T(8,128)S(1)}, f32[2,2,64,128]{3,2,1,0:T(8,128)S(1)}, u32[]{:S(2)}, u32[]{:S(2)}) collective-permute-start(f32[2,2,64,128]{3,2,1,0:T(8,128)S(1)} %get-tuple-element.28), channel_id=1, source_target_pairs={{0,4},{1,5},{2,6},{3,7},{4,8},{5,9},{6,10},{7,11},{8,12},{9,13},{1... | collective-permute-start | bytes 393224 | tf_op jit(solution)/shard_map/ppermute | solution.py:119
  127.5 8.8 %collective-permute-start.8 = (f32[4,2,64,128]{3,2,1,0:T(8,128)S(1)}, f32[4,2,64,128]{3,2,1,0:T(8,128)S(1)}, u32[]{:S(2)}, u32[]{:S(2)}) collective-permute-start(f32[4,2,64,128]{3,2,1,0:T(8,128)S(1)} %all_to_all.32), channel_id=1, source_target_pairs={{0,30},{1,31},{2,0},{3,1},{4,2},{5,3},{6,4},{7,5},{8,6},{9,7},{10,... | collective-permute-start | bytes 786440 | tf_op jit(solution)/shard_map/ppermute | solution.py:119
  136.3 34.7 %copy-start.2 = (f32[2,64,128]{2,1,0:T(8,128)S(1)}, f32[2,64,128]{2,1,0:T(8,128)}, u32[]{:S(2)}) copy-start(f32[2,64,128]{2,1,0:T(8,128)} %get-tuple-element.24.refs_2_) | copy-start | bytes 196612
  136.3 7.7 %collective-permute-start.9 = (f32[32,64,128]{2,1,0:T(8,128)S(1)}, f32[32,64,128]{2,1,0:T(8,128)S(1)}, u32[]{:S(2)}, u32[]{:S(2)}) collective-permute-start(f32[32,64,128]{2,1,0:T(8,128)S(1)} %bitcast.72), channel_id=1, source_target_pairs={{0,1},{1,0},{2,3},{3,2},{4,5},{5,4},{6,7},{7,6},{8,9},{9,8},{10,11... | collective-permute-start | bytes 3145736 | tf_op jit(solution)/shard_map/ppermute | solution.py:159
  189.6 19.8 %collective-permute-start.10 = (f32[4,2,64,128]{3,2,1,0:T(8,128)S(1)}, f32[4,2,64,128]{3,2,1,0:T(8,128)S(1)}, u32[]{:S(2)}, u32[]{:S(2)}) collective-permute-start(f32[4,2,64,128]{3,2,1,0:T(8,128)S(1)} %all_to_all.34), channel_id=1, source_target_pairs={{0,2},{1,3},{2,4},{3,5},{4,6},{5,7},{6,8},{7,9},{8,10},{9,11},{10,... | collective-permute-start | bytes 786440 | tf_op jit(solution)/shard_map/ppermute | solution.py:119
  192.2 19.7 %collective-permute-start.12 = (f32[2,2,64,128]{3,2,1,0:T(8,128)S(1)}, f32[2,2,64,128]{3,2,1,0:T(8,128)S(1)}, u32[]{:S(2)}, u32[]{:S(2)}) collective-permute-start(f32[2,2,64,128]{3,2,1,0:T(8,128)S(1)} %get-tuple-element.25), channel_id=1, source_target_pairs={{0,28},{1,29},{2,30},{3,31},{4,0},{5,1},{6,2},{7,3},{8,4},{9,5},{1... | collective-permute-start | bytes 393224 | tf_op jit(solution)/shard_map/ppermute | solution.py:119
  201.7 10.2 %collective-permute-start.11 = (f32[2,2,64,128]{3,2,1,0:T(8,128)S(1)}, f32[2,2,64,128]{3,2,1,0:T(8,128)S(1)}, u32[]{:S(2)}, u32[]{:S(2)}) collective-permute-start(f32[2,2,64,128]{3,2,1,0:T(8,128)S(1)} %get-tuple-element.26), channel_id=1, source_target_pairs={{0,4},{1,5},{2,6},{3,7},{4,8},{5,9},{6,10},{7,11},{8,12},{9,13},{1... | collective-permute-start | bytes 393224 | tf_op jit(solution)/shard_map/ppermute | solution.py:119
  204.7 9.7 %collective-permute-start.13 = (f32[4,2,64,128]{3,2,1,0:T(8,128)S(1)}, f32[4,2,64,128]{3,2,1,0:T(8,128)S(1)}, u32[]{:S(2)}, u32[]{:S(2)}) collective-permute-start(f32[4,2,64,128]{3,2,1,0:T(8,128)S(1)} %all_to_all.34), channel_id=1, source_target_pairs={{0,30},{1,31},{2,0},{3,1},{4,2},{5,3},{6,4},{7,5},{8,6},{9,7},{10,... | collective-permute-start | bytes 786440 | tf_op jit(solution)/shard_map/ppermute | solution.py:119
  214.4 33.1 %copy-start.1 = (f32[2,64,128]{2,1,0:T(8,128)S(1)}, f32[2,64,128]{2,1,0:T(8,128)}, u32[]{:S(2)}) copy-start(f32[2,64,128]{2,1,0:T(8,128)} %get-tuple-element.21.right) | copy-start | bytes 196612
  214.4 6.4 %collective-permute-start.14 = (f32[32,64,128]{2,1,0:T(8,128)S(1)}, f32[32,64,128]{2,1,0:T(8,128)S(1)}, u32[]{:S(2)}, u32[]{:S(2)}) collective-permute-start(f32[32,64,128]{2,1,0:T(8,128)S(1)} %bitcast.75), channel_id=1, source_target_pairs={{0,1},{1,0},{2,3},{3,2},{4,5},{5,4},{6,7},{7,6},{8,9},{9,8},{10,11... | collective-permute-start | bytes 3145736 | tf_op jit(solution)/shard_map/ppermute | solution.py:159
  227.5 20.8 %copy-start.5 = (f32[2,64,128]{2,1,0:T(8,128)S(1)}, f32[2,64,128]{2,1,0:T(8,128)}, u32[]{:S(2)}) copy-start(f32[2,64,128]{2,1,0:T(8,128)} %copy-done.4) | copy-start | bytes 196612

commit v2 on v1

v2 whole, which is shorter than its diff:
```python
import functools

import jax
import jax.numpy as jnp
from jax import lax
from jax.experimental import pallas as pl
from jax.experimental.pallas import tpu as pltpu
from jax.sharding import PartitionSpec as P

HIGHEST = lax.Precision.HIGHEST
ANY = pl.BlockSpec(memory_space=pl.ANY)
VMEM = pl.BlockSpec(memory_space=pltpu.VMEM)
SMEM = pl.BlockSpec(memory_space=pltpu.SMEM)
PARAMS = pltpu.CompilerParams(vmem_limit_bytes=32 * 1024 * 1024)
CORES = 2
STRIDE = 2


def dot(a, b):
    return lax.dot_general(
        a, b, (((1,), (0,)), ((), ())), precision=HIGHEST, preferred_element_type=jnp.float32
    )


def solve_kernel(level, peers, last, *refs):
    received = None
    if peers:
        received, refs = refs[0], refs[1:]
    counts, right_all, inverse_all = refs[:3]
    earlier = refs[3 : 3 + level] if last else ()
    outs = refs[3 + len(earlier) : -3]
    right, inverse, sem = refs[-3:]
    loads = [
        pltpu.make_async_copy(right_all.at[level, 0], right, sem.at[0]),
        pltpu.make_async_copy(inverse_all.at[level, 0], inverse, sem.at[1]),
    ]
    for load in loads:
        load.start()
    slots = right.shape[0]
    updates = []
    if peers:
        for s in range(slots):
            update = received[s]
            for peer in range(1, peers):
                update = update + received[peer * slots + s]
            updates.append(update)
    if last:
        for index, block in enumerate(earlier):
            outs[0][index, 0] = block[...]
    for load in loads:
        load.wait()
    for s in range(slots):
        value = right[s]
        if peers:
            value = value - updates[s]
        value = dot(value, inverse[s])
        value = jnp.where(s < counts[level, 0, 0], value, jnp.zeros_like(value))
        if last:
            outs[0][level, 0, s] = value
        else:
            outs[0][s] = value
            for copy in range(outs[1].shape[0]):
                outs[1][copy, s] = value


def solve(level, received, counts, right, inverse, earlier, fan):
    slots, rows, order = right.shape[2:]
    last = level + 1 == right.shape[0]
    args, specs, peers = (counts, right, inverse), [SMEM, ANY, ANY], 0
    if received is not None:
        peers = received.shape[0] // slots
        args, specs = (received,) + args, [VMEM] + specs
    if last:
        args, specs = args + tuple(earlier), specs + [VMEM] * len(earlier)
        shapes, outs = jax.ShapeDtypeStruct(right.shape, jnp.float32), VMEM
    else:
        shapes = (
            jax.ShapeDtypeStruct((slots, rows, order), jnp.float32),
            jax.ShapeDtypeStruct((fan, slots, rows, order), jnp.float32),
        )
        outs = (VMEM, VMEM)
    return pl.pallas_call(
        functools.partial(solve_kernel, level, peers, last),
        out_shape=shapes, in_specs=specs, out_specs=outs,
        scratch_shapes=[
            pltpu.VMEM((slots, rows, order), jnp.float32),
            pltpu.VMEM((slots, order, order), jnp.float32),
            pltpu.SemaphoreType.DMA((2,)),
        ],
        compiler_params=PARAMS,
    )(*args)


def edge_kernel(level, edges, cols, slots, column, source, target, coupling, *refs):
    parts = level * CORES
    history = refs[:parts]
    out, picked, blocks, products, picked_sem, block_sem = refs[parts:]
    block_copy = pltpu.make_async_copy(coupling.at[level - 1, 0], blocks, block_sem)
    block_copy.start()
    core, chip = column[0] % CORES, column[0] // CORES
    chips = cols // CORES
    for e in range(edges):
        p = jnp.maximum(source[level - 1, 0, e], 0)
        where = (p // slots) % cols
        there = where // CORES
        part = (p // (slots * cols)) * CORES + ((where % CORES) != core).astype(jnp.int32)
        group = (there % STRIDE - chip % STRIDE) % STRIDE
        place = (group * (chips // STRIDE) + there // STRIDE) * slots + p % slots
        for index in range(parts):
            @pl.when(part == index)
            def _():
                pltpu.make_async_copy(
                    history[index].at[place], picked.at[e], picked_sem.at[e]
                ).start()
    out[...] = jnp.zeros_like(out)
    for e in range(edges):
        pltpu.make_async_copy(history[0].at[0], picked.at[e], picked_sem.at[e]).wait()
    block_copy.wait()
    for e in range(edges):
        products[e] = dot(picked[e], blocks[e])
    for e in range(edges):
        goal = target[level - 1, 0, e]
        live = (goal >= 0).astype(jnp.float32)
        goal = jnp.maximum(goal, 0)
        out[goal] = out[goal] + products[e] * live


def edge_terms(level, column, source, target, coupling, history, target_total, cols, slots):
    edges = coupling.shape[2]
    rows, order = history[0].shape[1:]
    return pl.pallas_call(
        functools.partial(edge_kernel, level, edges, cols, slots),
        out_shape=jax.ShapeDtypeStruct((target_total, rows, order), jnp.float32),
        in_specs=[SMEM, SMEM, SMEM, ANY] + [ANY] * len(history),
        out_specs=VMEM,
        scratch_shapes=[
            pltpu.VMEM((edges, rows, order), jnp.float32),
            pltpu.VMEM((edges, order, order), jnp.float32),
            pltpu.VMEM((edges, rows, order), jnp.float32),
            pltpu.SemaphoreType.DMA((edges,)),
            pltpu.SemaphoreType.DMA,
        ],
        compiler_params=PARAMS,
    )(column, source, target, coupling, *history)


def gather_col(copies, cols):
    chips = cols // CORES
    far = [
        [CORES * (STRIDE * hi + lo) + core for hi in range(chips // STRIDE)]
        for lo in range(STRIDE)
        for core in range(CORES)
    ]

    def shift(x, k):
        return lax.ppermute(x, "col", [(i, (i + CORES * k) % cols) for i in range(cols)])

    mine = lax.all_to_all(copies, "col", 0, 0, tiled=True, axis_index_groups=far)
    half = mine.shape[0] // 2
    same = jnp.concatenate([mine, shift(mine[:half], 1), shift(mine[half:], -1)])
    return same.reshape((-1,) + same.shape[2:])


def on_device(
    right_sides, inverse_blocks, coupling_blocks, slot_counts, edge_sources, edge_targets
):
    level_total = right_sides.shape[0]
    slots = right_sides.shape[2]
    rows, cols = lax.axis_size("row"), lax.axis_size("col")
    column = lax.axis_index("col").reshape(1).astype(jnp.int32)
    history, results, received = [], [], None
    for level in range(level_total):
        if level:
            terms = edge_terms(
                level, column, edge_sources, edge_targets, coupling_blocks, history,
                rows * slots, cols, slots,
            )
            received = lax.all_to_all(terms, "row", 0, 0, tiled=True)
        solved = solve(
            level, received, slot_counts, right_sides, inverse_blocks, results,
            cols // CORES // STRIDE,
        )
        if level + 1 == level_total:
            return solved
        results.append(solved[0])
        same = gather_col(solved[1], cols)
        other = lax.ppermute(same, "col", [(i, i ^ 1) for i in range(cols)])
        history += [same, other]


def solution(mesh):
    return jax.shard_map(
        on_device,
        mesh=mesh,
        in_specs=(
            P(None, "row", "col", None, None),
            P(None, "row", "col", None, None),
            P(None, "row", "col", None, None),
            P(None, "row", "col"),
            P(None, "row", "col"),
            P(None, "row", "col"),
        ),
        out_specs=P(None, "row", "col", None, None),
        check_vma=False,
    )
```

time: 250 us -> 254 us (1.016)
  blocking collectives: 129 us -> 155 us
  starting transfers between devices: 69.6 us -> 54.6 us
  Pallas kernels: 23.3 us -> 15.1 us
  waiting for transfers between devices: 18.9 us -> 23.6 us
  local copies, waits for them, and re-layouts: 7.29 us -> 3.07 us
    all_to_all x3, blocking collectives: 65.6 us -> 92.6 us  [gather_col(): lax.all_to_all(copies, 'col', 0, 0, tiled=True, axis_index_groups=far)]
    ppermute x12 -> x6, starting transfers between devices: 55.5 us -> 37.5 us  [shift(): lax.ppermute(x, 'col', [(i, (i + CORES * k) % cols) for i in range(cols)])]
    pallas_call x7, Pallas kernels: 23.3 us -> 15.1 us  [the longest x3 9.79 us: edge_terms(): pl.pallas_call(functools.partial(edge_kernel, level, edges, cols, slots),...]
    ppermute x12 -> x6, waiting for transfers between devices: 11.9 us -> 16.5 us  [shift(): lax.ppermute(x, 'col', [(i, (i + CORES * k) % cols) for i in range(cols)])]
    ppermute x3, starting transfers between devices: 14.1 us -> 17 us  [on_device(): other = lax.ppermute(same, 'col', [(i, i ^ 1) for i in range(cols)])]
    squeeze x2 -> x0, local copies, waits for them, and re-layouts: 2.89 us -> none  [the longest x1 1.77 us: on_device(): right_sides[level, 0]]
  transfers between devices with their start and end apart: 15 -> 9, of which waited for: 7 -> 8; matrix products, arithmetic and copies ran while one was open for 1% -> 0% of each run, Pallas kernels for 0% -> 0%
where the time goes in v2:
time: 254 us; the launch traced here: 253 us
  blocking collectives  155 us (61%)
  starting transfers between devices  54.6 us (21%)
  waiting for transfers between devices  23.6 us (9%)
  Pallas kernels  15.1 us (6%)
  local copies, waits for them, and re-layouts  3.07 us (1%)
    all_to_all x3, blocking collectives, gather_col(): lax.all_to_all(copies, 'col', 0, 0, tiled=True, axis_index_groups=far)  92.6 us
    all_to_all x3, blocking collectives, on_device(): received = lax.all_to_all(terms, 'row', 0, 0, tiled=True)  62.3 us
    ppermute x6, starting transfers between devices, shift(): lax.ppermute(x, 'col', [(i, (i + CORES * k) % cols) for i in range(cols)])  37.5 us
    ppermute x3, starting transfers between devices, on_device(): other = lax.ppermute(same, 'col', [(i, i ^ 1) for i in range(cols)])  17 us
    ppermute x6, waiting for transfers between devices, shift(): lax.ppermute(x, 'col', [(i, (i + CORES * k) % cols) for i in range(cols)])  16.5 us
    pallas_call x3, Pallas kernels, edge_terms(): pl.pallas_call(functools.partial(edge_kernel, level, edges, cols, slots),...  9.79 us
    ppermute x3, waiting for transfers between devices, on_device(): other = lax.ppermute(same, 'col', [(i, i ^ 1) for i in range(cols)])  7.13 us
    pallas_call x4, Pallas kernels, solve(): pl.pallas_call(functools.partial(solve_kernel, level, peers, last), out_s...  5.29 us
  transfers between devices with their start and end apart: 9, of which 8 were waited for; matrix products, arithmetic and copies ran while one was open for 0% of the time, Pallas kernels for 0%

profile of v2, /device:TPU:1, one launch (start us, length us, event | category | flops | bytes accessed | tf_op | source)
XLA Modules:
  0.0 252.7 jit_solution(9954557372091010940)
XLA Ops:
  0.9 1.1 copy-done.1
  2.0 0.9 copy-done.3
  3.0 1.1 shard_map.64
  4.1 40.7 %all_to_all.30 = f32[8,2,64,128]{3,2,1,0:T(8,128)S(1)} all-to-all(f32[8,2,64,128]{3,2,1,0:T(8,128)S(1)} %get-tuple-element.11), channel_id=1, replica_groups={{0,4,8,12,16,20,24,28},{1,5,9,13,17,21,25,29},{2,6,10,14,18,22,26,30},{..., dimensions={0} | all-to-all | bytes 1048576 | tf_op jit(solution)/shard_map/all_to_all | solution.py:158
  44.8 3.5 %collective-permute-start = (f32[4,2,64,128]{3,2,1,0:T(8,128)S(1)}, f32[4,2,64,128]{3,2,1,0:T(8,128)S(1)}, u32[]{:S(2)}, u32[]{:S(2)}) collective-permute-start(f32[4,2,64,128]{3,2,1,0:T(8,128)S(1)} %get-tuple-element.21), channel_id=1, source_target_pairs={{0,2},{1,3},{2,4},{3,5},{4,6},{5,7},{6,8},{7,9},{8,10},{9,11},{10,... | collective-permute-start | bytes 786440 | tf_op jit(solution)/shard_map/ppermute | solution.py:156
  48.3 5.9 %collective-permute-start.1 = (f32[4,2,64,128]{3,2,1,0:T(8,128)S(1)}, f32[4,2,64,128]{3,2,1,0:T(8,128)S(1)}, u32[]{:S(2)}, u32[]{:S(2)}) collective-permute-start(f32[4,2,64,128]{3,2,1,0:T(8,128)S(1)} %get-tuple-element.22), channel_id=1, source_target_pairs={{0,30},{1,31},{2,0},{3,1},{4,2},{5,3},{6,4},{7,5},{8,6},{9,7},{10,... | collective-permute-start | bytes 786440 | tf_op jit(solution)/shard_map/ppermute | solution.py:156
  54.2 1.8 collective-permute-done
  56.1 5.6 %collective-permute-done.1 = f32[4,2,64,128]{3,2,1,0:T(8,128)S(1)} collective-permute-done((f32[4,2,64,128]{3,2,1,0:T(8,128)S(1)}, f32[4,2,64,128]{3,2,1,0:T(8,128)S(1)}, u32[]{:S(2)}, u32[]{:S(2)}) %collective-permute-start.1) | collective-permute-done | bytes 262176 | tf_op jit(solution)/shard_map/ppermute | solution.py:156
  61.7 1.1 pad_maximum_fusion
  62.8 4.3 %collective-permute-start.2 = (f32[32,64,128]{2,1,0:T(8,128)}, f32[32,64,128]{2,1,0:T(8,128)}, u32[]{:S(2)}, u32[]{:S(2)}) collective-permute-start(f32[32,64,128]{2,1,0:T(8,128)} %bitcast.1.refs_0_), channel_id=1, source_target_pairs={{0,1},{1,0},{2,3},{3,2},{4,5},{5,4},{6,7},{7,6},{8,9},{9,8},{10,11... | collective-permute-start | bytes 3145736 | tf_op jit(solution)/shard_map/ppermute | solution.py:187
  67.1 2.6 %collective-permute-done.2.refs_1_ = f32[32,64,128]{2,1,0:T(8,128)} collective-permute-done((f32[32,64,128]{2,1,0:T(8,128)}, f32[32,64,128]{2,1,0:T(8,128)}, u32[]{:S(2)}, u32[]{:S(2)}) %collective-permute-start.2) | collective-permute-done | bytes 1048608 | tf_op jit(solution)/shard_map/ppermute | solution.py:187
  69.7 3.1 %shard_map.65 = f32[32,64,128]{2,1,0:T(8,128)S(1)} custom-call(s32[1]{0:T(128)} %bitcast.column, s32[3,1,16]{2,1,0:T(1,128)S(1)} %copy-done.5, s32[3,1,16]{2,1,0:T(1,128)S(1)} %copy-done.6, f32[3,1,16,128,128]{4,3,2,1,0:T(8,128)S(1)} %copy-done, f32[32,64,128]{2,1,0:T(8,128)} %bitcast.1.refs_0_, f32[32,64,128]{2,1,0:T(8,128)} %collective-permute-done.2.refs_1_), custom_call_target="tpu_custom_call" | custom-call | tf_op jit(solution)/shard_map/pallas_call | solution.py:131
  72.8 22.9 %all_to_all.31.refs_0_ = f32[32,64,128]{2,1,0:T(8,128)S(1)} all-to-all(f32[32,64,128]{2,1,0:T(8,128)S(1)} %shard_map.65), channel_id=1, replica_groups=mesh['row'=16,'col'=32] {'row'}, dimensions={0} | all-to-all | bytes 2097152 | tf_op jit(solution)/shard_map/all_to_all | solution.py:178
  95.7 1.2 shard_map.66
  96.9 25.5 %all_to_all.32 = f32[8,2,64,128]{3,2,1,0:T(8,128)S(1)} all-to-all(f32[8,2,64,128]{3,2,1,0:T(8,128)S(1)} %get-tuple-element.12), channel_id=1, replica_groups={{0,4,8,12,16,20,24,28},{1,5,9,13,17,21,25,29},{2,6,10,14,18,22,26,30},{..., dimensions={0} | all-to-all | bytes 1048576 | tf_op jit(solution)/shard_map/all_to_all | solution.py:158
  122.5 10.0 %collective-permute-start.3 = (f32[4,2,64,128]{3,2,1,0:T(8,128)S(1)}, f32[4,2,64,128]{3,2,1,0:T(8,128)S(1)}, u32[]{:S(2)}, u32[]{:S(2)}) collective-permute-start(f32[4,2,64,128]{3,2,1,0:T(8,128)S(1)} %get-tuple-element.19), channel_id=1, source_target_pairs={{0,2},{1,3},{2,4},{3,5},{4,6},{5,7},{6,8},{7,9},{8,10},{9,11},{10,... | collective-permute-start | bytes 786440 | tf_op jit(solution)/shard_map/ppermute | solution.py:156
  132.5 4.2 %collective-permute-start.4 = (f32[4,2,64,128]{3,2,1,0:T(8,128)S(1)}, f32[4,2,64,128]{3,2,1,0:T(8,128)S(1)}, u32[]{:S(2)}, u32[]{:S(2)}) collective-permute-start(f32[4,2,64,128]{3,2,1,0:T(8,128)S(1)} %get-tuple-element.20), channel_id=1, source_target_pairs={{0,30},{1,31},{2,0},{3,1},{4,2},{5,3},{6,4},{7,5},{8,6},{9,7},{10,... | collective-permute-start | bytes 786440 | tf_op jit(solution)/shard_map/ppermute | solution.py:156
  136.7 4.1 %collective-permute-done.3 = f32[4,2,64,128]{3,2,1,0:T(8,128)S(1)} collective-permute-done((f32[4,2,64,128]{3,2,1,0:T(8,128)S(1)}, f32[4,2,64,128]{3,2,1,0:T(8,128)S(1)}, u32[]{:S(2)}, u32[]{:S(2)}) %collective-permute-start.3) | collective-permute-done | bytes 262176 | tf_op jit(solution)/shard_map/ppermute | solution.py:156
  140.9 6.7 %collective-permute-start.5 = (f32[32,64,128]{2,1,0:T(8,128)S(1)}, f32[32,64,128]{2,1,0:T(8,128)S(1)}, u32[]{:S(2)}, u32[]{:S(2)}) collective-permute-start(f32[32,64,128]{2,1,0:T(8,128)S(1)} %bitcast.4), channel_id=1, source_target_pairs={{0,1},{1,0},{2,3},{3,2},{4,5},{5,4},{6,7},{7,6},{8,9},{9,8},{10,11... | collective-permute-start | bytes 3145736 | tf_op jit(solution)/shard_map/ppermute | solution.py:187
  147.6 2.3 collective-permute-done.5.refs_3_
  149.8 3.3 %shard_map.67 = f32[32,64,128]{2,1,0:T(8,128)S(1)} custom-call(s32[1]{0:T(128)} %bitcast.column, s32[3,1,16]{2,1,0:T(1,128)S(1)} %copy-done.5, s32[3,1,16]{2,1,0:T(1,128)S(1)} %copy-done.6, f32[3,1,16,128,128]{4,3,2,1,0:T(8,128)S(1)} %copy-done, f32[32,64,128]{2,1,0:T(8,128)} %bitcast.1.refs_0_, f32[32,64,128]{2,1,0:T(8,128)} %collective-permute-done.2.refs_1_, ...), custom_call_target="tpu_custom_call" | custom-call | tf_op jit(solution)/shard_map/pallas_call | solution.py:131
  153.1 19.5 %all_to_all.33.refs_0_ = f32[32,64,128]{2,1,0:T(8,128)S(1)} all-to-all(f32[32,64,128]{2,1,0:T(8,128)S(1)} %shard_map.67), channel_id=1, replica_groups=mesh['row'=16,'col'=32] {'row'}, dimensions={0} | all-to-all | bytes 2097152 | tf_op jit(solution)/shard_map/all_to_all | solution.py:178
  172.6 1.2 shard_map.68
  173.8 26.4 %all_to_all.34 = f32[8,2,64,128]{3,2,1,0:T(8,128)S(1)} all-to-all(f32[8,2,64,128]{3,2,1,0:T(8,128)S(1)} %get-tuple-element.13), channel_id=1, replica_groups={{0,4,8,12,16,20,24,28},{1,5,9,13,17,21,25,29},{2,6,10,14,18,22,26,30},{..., dimensions={0} | all-to-all | bytes 1048576 | tf_op jit(solution)/shard_map/all_to_all | solution.py:158
  200.2 11.5 %collective-permute-start.6 = (f32[4,2,64,128]{3,2,1,0:T(8,128)S(1)}, f32[4,2,64,128]{3,2,1,0:T(8,128)S(1)}, u32[]{:S(2)}, u32[]{:S(2)}) collective-permute-start(f32[4,2,64,128]{3,2,1,0:T(8,128)S(1)} %get-tuple-element.17), channel_id=1, source_target_pairs={{0,2},{1,3},{2,4},{3,5},{4,6},{5,7},{6,8},{7,9},{8,10},{9,11},{10,... | collective-permute-start | bytes 786440 | tf_op jit(solution)/shard_map/ppermute | solution.py:156
  211.7 2.4 collective-permute-start.7
  214.1 4.1 %collective-permute-done.6 = f32[4,2,64,128]{3,2,1,0:T(8,128)S(1)} collective-permute-done((f32[4,2,64,128]{3,2,1,0:T(8,128)S(1)}, f32[4,2,64,128]{3,2,1,0:T(8,128)S(1)}, u32[]{:S(2)}, u32[]{:S(2)}) %collective-permute-start.6) | collective-permute-done | bytes 262176 | tf_op jit(solution)/shard_map/ppermute | solution.py:156
  219.1 6.0 %collective-permute-start.8 = (f32[32,64,128]{2,1,0:T(8,128)S(1)}, f32[32,64,128]{2,1,0:T(8,128)S(1)}, u32[]{:S(2)}, u32[]{:S(2)}) collective-permute-start(f32[32,64,128]{2,1,0:T(8,128)S(1)} %bitcast.7), channel_id=1, source_target_pairs={{0,1},{1,0},{2,3},{3,2},{4,5},{5,4},{6,7},{7,6},{8,9},{9,8},{10,11... | collective-permute-start | bytes 3145736 | tf_op jit(solution)/shard_map/ppermute | solution.py:187
  225.1 2.3 collective-permute-done.8.refs_5_
  227.4 3.5 %shard_map.69 = f32[32,64,128]{2,1,0:T(8,128)S(1)} custom-call(s32[1]{0:T(128)} %bitcast.column, s32[3,1,16]{2,1,0:T(1,128)S(1)} %copy-done.5, s32[3,1,16]{2,1,0:T(1,128)S(1)} %copy-done.6, f32[3,1,16,128,128]{4,3,2,1,0:T(8,128)S(1)} %copy-done, f32[32,64,128]{2,1,0:T(8,128)} %bitcast.1.refs_0_, f32[32,64,128]{2,1,0:T(8,128)} %collective-permute-done.2.refs_1_, ...), custom_call_target="tpu_custom_call" | custom-call | tf_op jit(solution)/shard_map/pallas_call | solution.py:131
  230.9 20.0 %all_to_all.35.refs_0_ = f32[32,64,128]{2,1,0:T(8,128)S(1)} all-to-all(f32[32,64,128]{2,1,0:T(8,128)S(1)} %shard_map.69), channel_id=1, replica_groups=mesh['row'=16,'col'=32] {'row'}, dimensions={0} | all-to-all | bytes 2097152 | tf_op jit(solution)/shard_map/all_to_all | solution.py:178
  250.8 1.8 shard_map.70
  (20 shorter events, 2.0 us)
Async XLA Ops:
  0.0 69.7 %copy-start = (f32[3,1,16,128,128]{4,3,2,1,0:T(8,128)S(1)}, f32[3,1,16,128,128]{4,3,2,1,0:T(8,128)}, u32[]{:S(2)}) copy-start(f32[3,1,16,128,128]{4,3,2,1,0:T(8,128)} %coupling.5) | copy-start | bytes 9437188
  0.9 1.1 copy-start.1
  2.0 0.9 copy-start.3
  3.0 66.8 %copy-start.5 = (s32[3,1,16]{2,1,0:T(1,128)S(1)}, s32[3,1,16]{2,1,0:T(1,128)}, u32[]{:S(2)}) copy-start(s32[3,1,16]{2,1,0:T(1,128)} %source.5) | copy-start | bytes 580
  3.0 66.8 %copy-start.6 = (s32[3,1,16]{2,1,0:T(1,128)S(1)}, s32[3,1,16]{2,1,0:T(1,128)}, u32[]{:S(2)}) copy-start(s32[3,1,16]{2,1,0:T(1,128)} %target.5) | copy-start | bytes 580
  44.8 11.2 %collective-permute-start = (f32[4,2,64,128]{3,2,1,0:T(8,128)S(1)}, f32[4,2,64,128]{3,2,1,0:T(8,128)S(1)}, u32[]{:S(2)}, u32[]{:S(2)}) collective-permute-start(f32[4,2,64,128]{3,2,1,0:T(8,128)S(1)} %get-tuple-element.21), channel_id=1, source_target_pairs={{0,2},{1,3},{2,4},{3,5},{4,6},{5,7},{6,8},{7,9},{8,10},{9,11},{10,... | collective-permute-start | bytes 786440 | tf_op jit(solution)/shard_map/ppermute | solution.py:156
  48.3 13.4 %collective-permute-start.1 = (f32[4,2,64,128]{3,2,1,0:T(8,128)S(1)}, f32[4,2,64,128]{3,2,1,0:T(8,128)S(1)}, u32[]{:S(2)}, u32[]{:S(2)}) collective-permute-start(f32[4,2,64,128]{3,2,1,0:T(8,128)S(1)} %get-tuple-element.22), channel_id=1, source_target_pairs={{0,30},{1,31},{2,0},{3,1},{4,2},{5,3},{6,4},{7,5},{8,6},{9,7},{10,... | collective-permute-start | bytes 786440 | tf_op jit(solution)/shard_map/ppermute | solution.py:156
  62.8 6.9 %collective-permute-start.2 = (f32[32,64,128]{2,1,0:T(8,128)}, f32[32,64,128]{2,1,0:T(8,128)}, u32[]{:S(2)}, u32[]{:S(2)}) collective-permute-start(f32[32,64,128]{2,1,0:T(8,128)} %bitcast.1.refs_0_), channel_id=1, source_target_pairs={{0,1},{1,0},{2,3},{3,2},{4,5},{5,4},{6,7},{7,6},{8,9},{9,8},{10,11... | collective-permute-start | bytes 3145736 | tf_op jit(solution)/shard_map/ppermute | solution.py:187
  69.7 26.0 %copy-start.2 = (f32[4,1,2,128,128]{4,3,2,1,0:T(8,128)S(1)}, f32[4,1,2,128,128]{4,3,2,1,0:T(8,128)}, u32[]{:S(2)}) copy-start(f32[4,1,2,128,128]{4,3,2,1,0:T(8,128)} %refs_3_.5) | copy-start | bytes 1572868
  69.7 26.0 %copy-start.4 = (f32[4,1,2,64,128]{4,3,2,1,0:T(8,128)S(1)}, f32[4,1,2,64,128]{4,3,2,1,0:T(8,128)}, u32[]{:S(2)}) copy-start(f32[4,1,2,64,128]{4,3,2,1,0:T(8,128)} %refs_2_.7) | copy-start | bytes 786436
  122.5 18.3 %collective-permute-start.3 = (f32[4,2,64,128]{3,2,1,0:T(8,128)S(1)}, f32[4,2,64,128]{3,2,1,0:T(8,128)S(1)}, u32[]{:S(2)}, u32[]{:S(2)}) collective-permute-start(f32[4,2,64,128]{3,2,1,0:T(8,128)S(1)} %get-tuple-element.19), channel_id=1, source_target_pairs={{0,2},{1,3},{2,4},{3,5},{4,6},{5,7},{6,8},{7,9},{8,10},{9,11},{10,... | collective-permute-start | bytes 786440 | tf_op jit(solution)/shard_map/ppermute | solution.py:156
  132.5 8.3 %collective-permute-start.4 = (f32[4,2,64,128]{3,2,1,0:T(8,128)S(1)}, f32[4,2,64,128]{3,2,1,0:T(8,128)S(1)}, u32[]{:S(2)}, u32[]{:S(2)}) collective-permute-start(f32[4,2,64,128]{3,2,1,0:T(8,128)S(1)} %get-tuple-element.20), channel_id=1, source_target_pairs={{0,30},{1,31},{2,0},{3,1},{4,2},{5,3},{6,4},{7,5},{8,6},{9,7},{10,... | collective-permute-start | bytes 786440 | tf_op jit(solution)/shard_map/ppermute | solution.py:156
  140.9 9.0 %collective-permute-start.5 = (f32[32,64,128]{2,1,0:T(8,128)S(1)}, f32[32,64,128]{2,1,0:T(8,128)S(1)}, u32[]{:S(2)}, u32[]{:S(2)}) collective-permute-start(f32[32,64,128]{2,1,0:T(8,128)S(1)} %bitcast.4), channel_id=1, source_target_pairs={{0,1},{1,0},{2,3},{3,2},{4,5},{5,4},{6,7},{7,6},{8,9},{9,8},{10,11... | collective-permute-start | bytes 3145736 | tf_op jit(solution)/shard_map/ppermute | solution.py:187
  200.2 18.1 %collective-permute-start.6 = (f32[4,2,64,128]{3,2,1,0:T(8,128)S(1)}, f32[4,2,64,128]{3,2,1,0:T(8,128)S(1)}, u32[]{:S(2)}, u32[]{:S(2)}) collective-permute-start(f32[4,2,64,128]{3,2,1,0:T(8,128)S(1)} %get-tuple-element.17), channel_id=1, source_target_pairs={{0,2},{1,3},{2,4},{3,5},{4,6},{5,7},{6,8},{7,9},{8,10},{9,11},{10,... | collective-permute-start | bytes 786440 | tf_op jit(solution)/shard_map/ppermute | solution.py:156
  211.7 7.3 %collective-permute-start.7 = (f32[4,2,64,128]{3,2,1,0:T(8,128)S(1)}, f32[4,2,64,128]{3,2,1,0:T(8,128)S(1)}, u32[]{:S(2)}, u32[]{:S(2)}) collective-permute-start(f32[4,2,64,128]{3,2,1,0:T(8,128)S(1)} %get-tuple-element.18), channel_id=1, source_target_pairs={{0,30},{1,31},{2,0},{3,1},{4,2},{5,3},{6,4},{7,5},{8,6},{9,7},{10,... | collective-permute-start | bytes 786440 | tf_op jit(solution)/shard_map/ppermute | solution.py:156
  219.1 8.3 %collective-permute-start.8 = (f32[32,64,128]{2,1,0:T(8,128)S(1)}, f32[32,64,128]{2,1,0:T(8,128)S(1)}, u32[]{:S(2)}, u32[]{:S(2)}) collective-permute-start(f32[32,64,128]{2,1,0:T(8,128)S(1)} %bitcast.7), channel_id=1, source_target_pairs={{0,1},{1,0},{2,3},{3,2},{4,5},{5,4},{6,7},{7,6},{8,9},{9,8},{10,11... | collective-permute-start | bytes 3145736 | tf_op jit(solution)/shard_map/ppermute | solution.py:187

commit v3 on v2

--- a/solution.py
+++ b/solution.py
@@ -9,11 +9,12 @@
 
 HIGHEST = lax.Precision.HIGHEST
 ANY = pl.BlockSpec(memory_space=pl.ANY)
+HBM = pl.BlockSpec(memory_space=pltpu.HBM)
 VMEM = pl.BlockSpec(memory_space=pltpu.VMEM)
 SMEM = pl.BlockSpec(memory_space=pltpu.SMEM)
 PARAMS = pltpu.CompilerParams(vmem_limit_bytes=32 * 1024 * 1024)
 CORES = 2
-STRIDE = 2
+STRIDE = 4
 
 
 def dot(a, b):
@@ -54,19 +55,17 @@
         if peers:
             value = value - updates[s]
         value = dot(value, inverse[s])
-        value = jnp.where(s < counts[level, 0, 0], value, jnp.zeros_like(value))
+        value = jnp.where(s < counts[0, 0, level], value, jnp.zeros_like(value))
         if last:
             outs[0][level, 0, s] = value
         else:
             outs[0][s] = value
-            for copy in range(outs[1].shape[0]):
-                outs[1][copy, s] = value
-
-
-def solve(level, received, counts, right, inverse, earlier, fan):
+
+
+def solve(level, received, counts, right, inverse, earlier):
     slots, rows, order = right.shape[2:]
     last = level + 1 == right.shape[0]
-    args, specs, peers = (counts, right, inverse), [SMEM, ANY, ANY], 0
+    args, specs, peers = (counts, right, inverse), [SMEM, HBM, HBM], 0
     if received is not None:
         peers = received.shape[0] // slots
         args, specs = (received,) + args, [VMEM] + specs
@@ -74,11 +73,7 @@
         args, specs = args + tuple(earlier), specs + [VMEM] * len(earlier)
         shapes, outs = jax.ShapeDtypeStruct(right.shape, jnp.float32), VMEM
     else:
-        shapes = (
-            jax.ShapeDtypeStruct((slots, rows, order), jnp.float32),
-            jax.ShapeDtypeStruct((fan, slots, rows, order), jnp.float32),
-        )
-        outs = (VMEM, VMEM)
+        shapes, outs = jax.ShapeDtypeStruct((slots, rows, order), jnp.float32), VMEM
     return pl.pallas_call(
         functools.partial(solve_kernel, level, peers, last),
         out_shape=shapes, in_specs=specs, out_specs=outs,
@@ -104,7 +99,7 @@
         where = (p // slots) % cols
         there = where // CORES
         part = (p // (slots * cols)) * CORES + ((where % CORES) != core).astype(jnp.int32)
-        group = (there % STRIDE - chip % STRIDE) % STRIDE
+        group = (chip + STRIDE - there % STRIDE) % STRIDE
         place = (group * (chips // STRIDE) + there // STRIDE) * slots + p % slots
         for index in range(parts):
             @pl.when(part == index)
@@ -144,7 +139,7 @@
     )(column, source, target, coupling, *history)
 
 
-def gather_col(copies, cols):
+def gather_col(solved, cols):
     chips = cols // CORES
     far = [
         [CORES * (STRIDE * hi + lo) + core for hi in range(chips // STRIDE)]
@@ -155,9 +150,11 @@
     def shift(x, k):
         return lax.ppermute(x, "col", [(i, (i + CORES * k) % cols) for i in range(cols)])
 
-    mine = lax.all_to_all(copies, "col", 0, 0, tiled=True, axis_index_groups=far)
+    mine = lax.all_gather(solved, "col", axis=0, tiled=False, axis_index_groups=far)
     half = mine.shape[0] // 2
-    same = jnp.concatenate([mine, shift(mine[:half], 1), shift(mine[half:], -1)])
+    below, above = shift(mine, 1), shift(mine, -1)
+    low, high = shift(mine[:half], 2), shift(mine[half:], -2)
+    same = jnp.concatenate([mine, below, low, high, above])
     return same.reshape((-1,) + same.shape[2:])
 
 
@@ -168,6 +165,7 @@
     slots = right_sides.shape[2]
     rows, cols = lax.axis_size("row"), lax.axis_size("col")
     column = lax.axis_index("col").reshape(1).astype(jnp.int32)
+    counts = jnp.transpose(slot_counts, (1, 2, 0))
     history, results, received = [], [], None
     for level in range(level_total):
         if level:
@@ -177,13 +175,12 @@
             )
             received = lax.all_to_all(terms, "row", 0, 0, tiled=True)
         solved = solve(
-            level, received, slot_counts, right_sides, inverse_blocks, results,
-            cols // CORES // STRIDE,
+            level, received, counts, right_sides, inverse_blocks, results,
         )
         if level + 1 == level_total:
             return solved
-        results.append(solved[0])
-        same = gather_col(solved[1], cols)
+        results.append(solved)
+        same = gather_col(solved, cols)
         other = lax.ppermute(same, "col", [(i, i ^ 1) for i in range(cols)])
         history += [same, other]
 

time: 254 us -> 225 us (0.89)
  blocking collectives: 155 us -> 119 us
  starting transfers between devices: 54.6 us -> 66.9 us
  waiting for transfers between devices: 23.6 us -> 15.3 us
  local copies, waits for them, and re-layouts: 3.07 us -> 6.53 us
    all_to_all x3 -> x0, blocking collectives: 92.6 us -> none  [gather_col(): lax.all_to_all(copies, 'col', 0, 0, tiled=True, axis_index_groups=far)]
    all_gather x0 -> x3, blocking collectives: none -> 58.2 us  [gather_col(): lax.all_gather(solved, 'col', axis=0, tiled=False, axis_index_groups=far)]
    ppermute x3, starting transfers between devices: 17 us -> 25.6 us  [on_device(): other = lax.ppermute(same, 'col', [(i, i ^ 1) for i in range(cols)])]
    ppermute x6 -> x12, waiting for transfers between devices: 16.5 us -> 8.2 us  [shift(): lax.ppermute(x, 'col', [(i, (i + CORES * k) % cols) for i in range(cols)])]
    ppermute x6 -> x12, starting transfers between devices: 37.5 us -> 41.3 us  [shift(): lax.ppermute(x, 'col', [(i, (i + CORES * k) % cols) for i in range(cols)])]
    unnamed x15 -> x30, local copies, waits for them, and re-layouts: 2.97 us -> 5.7 us
  transfers between devices with their start and end apart: 9 -> 15, of which waited for: 8 -> 8; matrix products, arithmetic and copies ran while one was open for 0% -> 1% of each run, Pallas kernels for 0% -> 0%
where the time goes in v3:
time: 225 us; the launch traced here: 224 us
  blocking collectives  119 us (53%)
  starting transfers between devices  66.9 us (30%)
  Pallas kernels  15.4 us (7%)
  waiting for transfers between devices  15.3 us (7%)
  local copies, waits for them, and re-layouts  6.53 us (3%)
    all_to_all x3, blocking collectives, on_device(): received = lax.all_to_all(terms, 'row', 0, 0, tiled=True)  61.2 us
    all_gather x3, blocking collectives, gather_col(): lax.all_gather(solved, 'col', axis=0, tiled=False, axis_index_groups=far)  58.2 us
    ppermute x12, starting transfers between devices, shift(): lax.ppermute(x, 'col', [(i, (i + CORES * k) % cols) for i in range(cols)])  41.3 us
    ppermute x3, starting transfers between devices, on_device(): other = lax.ppermute(same, 'col', [(i, i ^ 1) for i in range(cols)])  25.6 us
    pallas_call x3, Pallas kernels, edge_terms(): pl.pallas_call(functools.partial(edge_kernel, level, edges, cols, slots),...  10.3 us
    ppermute x12, waiting for transfers between devices, shift(): lax.ppermute(x, 'col', [(i, (i + CORES * k) % cols) for i in range(cols)])  8.2 us
    ppermute x3, waiting for transfers between devices, on_device(): other = lax.ppermute(same, 'col', [(i, i ^ 1) for i in range(cols)])  7.13 us
    unnamed x30, local copies, waits for them, and re-layouts  5.7 us
  transfers between devices with their start and end apart: 15, of which 8 were waited for; matrix products, arithmetic and copies ran while one was open for 1% of the time, Pallas kernels for 0%

profile of v3, /device:TPU:1, one launch (start us, length us, event | category | flops | bytes accessed | tf_op | source)
XLA Modules:
  0.0 223.8 jit_solution(14729705746486064384)
XLA Ops:
  3.9 25.3 %all-gather = f32[8,64,128]{2,1,0:T(8,128)S(1)} all-gather(f32[2,64,128]{2,1,0:T(8,128)S(1)} %shard_map.64.refs_4_), channel_id=2, replica_groups={{0,8,16,24},{1,9,17,25},{2,10,18,26},{3,11,19,27},{4,12,20,28},{5,13,21..., dimensions={0}, use_global_device_ids=true | all-gather | bytes 327680 | tf_op jit(solution)/shard_map/all_gather | solution.py:153
  29.2 3.2 %collective-permute-start.3 = (f32[4,2,64,128]{3,2,1,0:T(8,128)S(1)}, f32[4,2,64,128]{3,2,1,0:T(8,128)S(1)}, u32[]{:S(2)}, u32[]{:S(2)}) collective-permute-start(f32[4,2,64,128]{3,2,1,0:T(8,128)S(1)} %bitcast.23), channel_id=1, source_target_pairs={{0,30},{1,31},{2,0},{3,1},{4,2},{5,3},{6,4},{7,5},{8,6},{9,7},{10,... | collective-permute-start | bytes 786440 | tf_op jit(solution)/shard_map/ppermute | solution.py:151
  32.4 2.1 collective-permute-start
  34.5 3.0 %collective-permute-start.1 = (f32[2,2,64,128]{3,2,1,0:T(8,128)S(1)}, f32[2,2,64,128]{3,2,1,0:T(8,128)S(1)}, u32[]{:S(2)}, u32[]{:S(2)}) collective-permute-start(f32[2,2,64,128]{3,2,1,0:T(8,128)S(1)} %bitcast.35), channel_id=1, source_target_pairs={{0,4},{1,5},{2,6},{3,7},{4,8},{5,9},{6,10},{7,11},{8,12},{9,13},{1... | collective-permute-start | bytes 393224 | tf_op jit(solution)/shard_map/ppermute | solution.py:151
  37.5 4.4 %collective-permute-start.2 = (f32[2,2,64,128]{3,2,1,0:T(8,128)S(1)}, f32[2,2,64,128]{3,2,1,0:T(8,128)S(1)}, u32[]{:S(2)}, u32[]{:S(2)}) collective-permute-start(f32[2,2,64,128]{3,2,1,0:T(8,128)S(1)} %bitcast.32), channel_id=1, source_target_pairs={{0,28},{1,29},{2,30},{3,31},{4,0},{5,1},{6,2},{7,3},{8,4},{9,5},{1... | collective-permute-start | bytes 393224 | tf_op jit(solution)/shard_map/ppermute | solution.py:151
  43.4 1.5 collective-permute-done.1
  46.9 6.4 %collective-permute-start.4 = (f32[32,64,128]{2,1,0:T(8,128)}, f32[32,64,128]{2,1,0:T(8,128)}, u32[]{:S(2)}, u32[]{:S(2)}) collective-permute-start(f32[32,64,128]{2,1,0:T(8,128)} %bitcast.5.refs_0_), channel_id=1, source_target_pairs={{0,1},{1,0},{2,3},{3,2},{4,5},{5,4},{6,7},{7,6},{8,9},{9,8},{10,11... | collective-permute-start | bytes 3145736 | tf_op jit(solution)/shard_map/ppermute | solution.py:184
  53.3 2.6 %collective-permute-done.4.refs_1_ = f32[32,64,128]{2,1,0:T(8,128)} collective-permute-done((f32[32,64,128]{2,1,0:T(8,128)}, f32[32,64,128]{2,1,0:T(8,128)}, u32[]{:S(2)}, u32[]{:S(2)}) %collective-permute-start.4) | collective-permute-done | bytes 1048608 | tf_op jit(solution)/shard_map/ppermute | solution.py:184
  56.0 3.2 %shard_map.65 = f32[32,64,128]{2,1,0:T(8,128)S(1)} custom-call(s32[1]{0:T(128)} %bitcast.column, s32[3,1,16]{2,1,0:T(1,128)S(1)} %copy-done.5, s32[3,1,16]{2,1,0:T(1,128)S(1)} %copy-done.6, f32[3,1,16,128,128]{4,3,2,1,0:T(8,128)S(1)} %copy-done, f32[32,64,128]{2,1,0:T(8,128)} %bitcast.5.refs_0_, f32[32,64,128]{2,1,0:T(8,128)} %collective-permute-done.4.refs_1_), custom_call_target="tpu_custom_call" | custom-call | tf_op jit(solution)/shard_map/pallas_call | solution.py:126
  59.2 22.8 %all_to_all.15.refs_0_ = f32[32,64,128]{2,1,0:T(8,128)S(1)} all-to-all(f32[32,64,128]{2,1,0:T(8,128)S(1)} %shard_map.65), channel_id=1, replica_groups=mesh['row'=16,'col'=32] {'row'}, dimensions={0} | all-to-all | bytes 2097152 | tf_op jit(solution)/shard_map/all_to_all | solution.py:176
  83.1 16.5 %all-gather.1 = f32[8,64,128]{2,1,0:T(8,128)S(1)} all-gather(f32[2,64,128]{2,1,0:T(8,128)S(1)} %shard_map.66.refs_5_), channel_id=3, replica_groups={{0,8,16,24},{1,9,17,25},{2,10,18,26},{3,11,19,27},{4,12,20,28},{5,13,21..., dimensions={0}, use_global_device_ids=true | all-gather | bytes 327680 | tf_op jit(solution)/shard_map/all_gather | solution.py:153
  99.6 5.3 %collective-permute-start.8 = (f32[4,2,64,128]{3,2,1,0:T(8,128)S(1)}, f32[4,2,64,128]{3,2,1,0:T(8,128)S(1)}, u32[]{:S(2)}, u32[]{:S(2)}) collective-permute-start(f32[4,2,64,128]{3,2,1,0:T(8,128)S(1)} %bitcast.26), channel_id=1, source_target_pairs={{0,30},{1,31},{2,0},{3,1},{4,2},{5,3},{6,4},{7,5},{8,6},{9,7},{10,... | collective-permute-start | bytes 786440 | tf_op jit(solution)/shard_map/ppermute | solution.py:151
  104.9 1.9 collective-permute-start.5
  106.9 3.7 %collective-permute-start.6 = (f32[2,2,64,128]{3,2,1,0:T(8,128)S(1)}, f32[2,2,64,128]{3,2,1,0:T(8,128)S(1)}, u32[]{:S(2)}, u32[]{:S(2)}) collective-permute-start(f32[2,2,64,128]{3,2,1,0:T(8,128)S(1)} %bitcast.36), channel_id=1, source_target_pairs={{0,4},{1,5},{2,6},{3,7},{4,8},{5,9},{6,10},{7,11},{8,12},{9,13},{1... | collective-permute-start | bytes 393224 | tf_op jit(solution)/shard_map/ppermute | solution.py:151
  110.6 3.7 %collective-permute-start.7 = (f32[2,2,64,128]{3,2,1,0:T(8,128)S(1)}, f32[2,2,64,128]{3,2,1,0:T(8,128)S(1)}, u32[]{:S(2)}, u32[]{:S(2)}) collective-permute-start(f32[2,2,64,128]{3,2,1,0:T(8,128)S(1)} %bitcast.33), channel_id=1, source_target_pairs={{0,28},{1,29},{2,30},{3,31},{4,0},{5,1},{6,2},{7,3},{8,4},{9,5},{1... | collective-permute-start | bytes 393224 | tf_op jit(solution)/shard_map/ppermute | solution.py:151
  114.3 1.4 collective-permute-done.6
  115.8 2.8 %collective-permute-done.7 = f32[2,2,64,128]{3,2,1,0:T(8,128)S(1)} collective-permute-done((f32[2,2,64,128]{3,2,1,0:T(8,128)S(1)}, f32[2,2,64,128]{3,2,1,0:T(8,128)S(1)}, u32[]{:S(2)}, u32[]{:S(2)}) %collective-permute-start.7) | collective-permute-done | bytes 131104 | tf_op jit(solution)/shard_map/ppermute | solution.py:151
  118.6 9.4 %collective-permute-start.9 = (f32[32,64,128]{2,1,0:T(8,128)S(1)}, f32[32,64,128]{2,1,0:T(8,128)S(1)}, u32[]{:S(2)}, u32[]{:S(2)}) collective-permute-start(f32[32,64,128]{2,1,0:T(8,128)S(1)} %bitcast.14), channel_id=1, source_target_pairs={{0,1},{1,0},{2,3},{3,2},{4,5},{5,4},{6,7},{7,6},{8,9},{9,8},{10,11... | collective-permute-start | bytes 3145736 | tf_op jit(solution)/shard_map/ppermute | solution.py:184
  128.1 2.3 %collective-permute-done.9.refs_3_ = f32[32,64,128]{2,1,0:T(8,128)S(1)} collective-permute-done((f32[32,64,128]{2,1,0:T(8,128)S(1)}, f32[32,64,128]{2,1,0:T(8,128)S(1)}, u32[]{:S(2)}, u32[]{:S(2)}) %collective-permute-start.9) | collective-permute-done | bytes 1048608 | tf_op jit(solution)/shard_map/ppermute | solution.py:184
  130.3 3.5 %shard_map.67 = f32[32,64,128]{2,1,0:T(8,128)S(1)} custom-call(s32[1]{0:T(128)} %bitcast.column, s32[3,1,16]{2,1,0:T(1,128)S(1)} %copy-done.5, s32[3,1,16]{2,1,0:T(1,128)S(1)} %copy-done.6, f32[3,1,16,128,128]{4,3,2,1,0:T(8,128)S(1)} %copy-done, f32[32,64,128]{2,1,0:T(8,128)} %bitcast.5.refs_0_, f32[32,64,128]{2,1,0:T(8,128)} %collective-permute-done.4.refs_1_, ...), custom_call_target="tpu_custom_call" | custom-call | tf_op jit(solution)/shard_map/pallas_call | solution.py:126
  133.8 19.1 %all_to_all.16.refs_0_ = f32[32,64,128]{2,1,0:T(8,128)S(1)} all-to-all(f32[32,64,128]{2,1,0:T(8,128)S(1)} %shard_map.67), channel_id=1, replica_groups=mesh['row'=16,'col'=32] {'row'}, dimensions={0} | all-to-all | bytes 2097152 | tf_op jit(solution)/shard_map/all_to_all | solution.py:176
  154.0 16.4 %all-gather.2 = f32[8,64,128]{2,1,0:T(8,128)S(1)} all-gather(f32[2,64,128]{2,1,0:T(8,128)S(1)} %shard_map.68.refs_6_), channel_id=4, replica_groups={{0,8,16,24},{1,9,17,25},{2,10,18,26},{3,11,19,27},{4,12,20,28},{5,13,21..., dimensions={0}, use_global_device_ids=true | all-gather | bytes 327680 | tf_op jit(solution)/shard_map/all_gather | solution.py:153
  170.4 4.7 %collective-permute-start.13 = (f32[4,2,64,128]{3,2,1,0:T(8,128)S(1)}, f32[4,2,64,128]{3,2,1,0:T(8,128)S(1)}, u32[]{:S(2)}, u32[]{:S(2)}) collective-permute-start(f32[4,2,64,128]{3,2,1,0:T(8,128)S(1)} %bitcast.29), channel_id=1, source_target_pairs={{0,30},{1,31},{2,0},{3,1},{4,2},{5,3},{6,4},{7,5},{8,6},{9,7},{10,... | collective-permute-start | bytes 786440 | tf_op jit(solution)/shard_map/ppermute | solution.py:151
  175.1 1.9 collective-permute-start.10
  177.0 3.1 %collective-permute-start.11 = (f32[2,2,64,128]{3,2,1,0:T(8,128)S(1)}, f32[2,2,64,128]{3,2,1,0:T(8,128)S(1)}, u32[]{:S(2)}, u32[]{:S(2)}) collective-permute-start(f32[2,2,64,128]{3,2,1,0:T(8,128)S(1)} %bitcast.37), channel_id=1, source_target_pairs={{0,4},{1,5},{2,6},{3,7},{4,8},{5,9},{6,10},{7,11},{8,12},{9,13},{1... | collective-permute-start | bytes 393224 | tf_op jit(solution)/shard_map/ppermute | solution.py:151
  180.2 4.2 %collective-permute-start.12 = (f32[2,2,64,128]{3,2,1,0:T(8,128)S(1)}, f32[2,2,64,128]{3,2,1,0:T(8,128)S(1)}, u32[]{:S(2)}, u32[]{:S(2)}) collective-permute-start(f32[2,2,64,128]{3,2,1,0:T(8,128)S(1)} %bitcast.34), channel_id=1, source_target_pairs={{0,28},{1,29},{2,30},{3,31},{4,0},{5,1},{6,2},{7,3},{8,4},{9,5},{1... | collective-permute-start | bytes 393224 | tf_op jit(solution)/shard_map/ppermute | solution.py:151
  185.0 2.0 collective-permute-done.12
  187.0 9.8 %collective-permute-start.14 = (f32[32,64,128]{2,1,0:T(8,128)S(1)}, f32[32,64,128]{2,1,0:T(8,128)S(1)}, u32[]{:S(2)}, u32[]{:S(2)}) collective-permute-start(f32[32,64,128]{2,1,0:T(8,128)S(1)} %bitcast.17), channel_id=1, source_target_pairs={{0,1},{1,0},{2,3},{3,2},{4,5},{5,4},{6,7},{7,6},{8,9},{9,8},{10,11... | collective-permute-start | bytes 3145736 | tf_op jit(solution)/shard_map/ppermute | solution.py:184
  196.8 2.3 %collective-permute-done.14.refs_5_ = f32[32,64,128]{2,1,0:T(8,128)S(1)} collective-permute-done((f32[32,64,128]{2,1,0:T(8,128)S(1)}, f32[32,64,128]{2,1,0:T(8,128)S(1)}, u32[]{:S(2)}, u32[]{:S(2)}) %collective-permute-start.14) | collective-permute-done | bytes 1048608 | tf_op jit(solution)/shard_map/ppermute | solution.py:184
  199.0 3.7 %shard_map.69 = f32[32,64,128]{2,1,0:T(8,128)S(1)} custom-call(s32[1]{0:T(128)} %bitcast.column, s32[3,1,16]{2,1,0:T(1,128)S(1)} %copy-done.5, s32[3,1,16]{2,1,0:T(1,128)S(1)} %copy-done.6, f32[3,1,16,128,128]{4,3,2,1,0:T(8,128)S(1)} %copy-done, f32[32,64,128]{2,1,0:T(8,128)} %bitcast.5.refs_0_, f32[32,64,128]{2,1,0:T(8,128)} %collective-permute-done.4.refs_1_, ...), custom_call_target="tpu_custom_call" | custom-call | tf_op jit(solution)/shard_map/pallas_call | solution.py:126
  202.7 19.3 %all_to_all.17.refs_0_ = f32[32,64,128]{2,1,0:T(8,128)S(1)} all-to-all(f32[32,64,128]{2,1,0:T(8,128)S(1)} %shard_map.69), channel_id=1, replica_groups=mesh['row'=16,'col'=32] {'row'}, dimensions={0} | all-to-all | bytes 2097152 | tf_op jit(solution)/shard_map/all_to_all | solution.py:176
  222.0 1.8 shard_map.70
  (47 shorter events, 10.3 us)
Async XLA Ops:
  0.0 56.0 %copy-start = (f32[3,1,16,128,128]{4,3,2,1,0:T(8,128)S(1)}, f32[3,1,16,128,128]{4,3,2,1,0:T(8,128)}, u32[]{:S(2)}) copy-start(f32[3,1,16,128,128]{4,3,2,1,0:T(8,128)} %coupling.5) | copy-start | bytes 9437188
  0.0 1.2 copy-start.1
  1.2 0.9 copy-start.3
  2.1 0.7 copy-start.7
  2.8 53.2 %copy-start.5 = (s32[3,1,16]{2,1,0:T(1,128)S(1)}, s32[3,1,16]{2,1,0:T(1,128)}, u32[]{:S(2)}) copy-start(s32[3,1,16]{2,1,0:T(1,128)} %source.5) | copy-start | bytes 580
  2.8 53.2 %copy-start.6 = (s32[3,1,16]{2,1,0:T(1,128)S(1)}, s32[3,1,16]{2,1,0:T(1,128)}, u32[]{:S(2)}) copy-start(s32[3,1,16]{2,1,0:T(1,128)} %target.5) | copy-start | bytes 580
  29.2 17.0 %collective-permute-start.3 = (f32[4,2,64,128]{3,2,1,0:T(8,128)S(1)}, f32[4,2,64,128]{3,2,1,0:T(8,128)S(1)}, u32[]{:S(2)}, u32[]{:S(2)}) collective-permute-start(f32[4,2,64,128]{3,2,1,0:T(8,128)S(1)} %bitcast.23), channel_id=1, source_target_pairs={{0,30},{1,31},{2,0},{3,1},{4,2},{5,3},{6,4},{7,5},{8,6},{9,7},{10,... | collective-permute-start | bytes 786440 | tf_op jit(solution)/shard_map/ppermute | solution.py:151
  32.4 10.2 %collective-permute-start = (f32[4,2,64,128]{3,2,1,0:T(8,128)S(1)}, f32[4,2,64,128]{3,2,1,0:T(8,128)S(1)}, u32[]{:S(2)}, u32[]{:S(2)}) collective-permute-start(f32[4,2,64,128]{3,2,1,0:T(8,128)S(1)} %bitcast.24), channel_id=1, source_target_pairs={{0,2},{1,3},{2,4},{3,5},{4,6},{5,7},{6,8},{7,9},{8,10},{9,11},{10,... | collective-permute-start | bytes 786440 | tf_op jit(solution)/shard_map/ppermute | solution.py:151
  34.5 10.4 %collective-permute-start.1 = (f32[2,2,64,128]{3,2,1,0:T(8,128)S(1)}, f32[2,2,64,128]{3,2,1,0:T(8,128)S(1)}, u32[]{:S(2)}, u32[]{:S(2)}) collective-permute-start(f32[2,2,64,128]{3,2,1,0:T(8,128)S(1)} %bitcast.35), channel_id=1, source_target_pairs={{0,4},{1,5},{2,6},{3,7},{4,8},{5,9},{6,10},{7,11},{8,12},{9,13},{1... | collective-permute-start | bytes 393224 | tf_op jit(solution)/shard_map/ppermute | solution.py:151
  37.5 8.0 %collective-permute-start.2 = (f32[2,2,64,128]{3,2,1,0:T(8,128)S(1)}, f32[2,2,64,128]{3,2,1,0:T(8,128)S(1)}, u32[]{:S(2)}, u32[]{:S(2)}) collective-permute-start(f32[2,2,64,128]{3,2,1,0:T(8,128)S(1)} %bitcast.32), channel_id=1, source_target_pairs={{0,28},{1,29},{2,30},{3,31},{4,0},{5,1},{6,2},{7,3},{8,4},{9,5},{1... | collective-permute-start | bytes 393224 | tf_op jit(solution)/shard_map/ppermute | solution.py:151
  46.9 9.0 %collective-permute-start.4 = (f32[32,64,128]{2,1,0:T(8,128)}, f32[32,64,128]{2,1,0:T(8,128)}, u32[]{:S(2)}, u32[]{:S(2)}) collective-permute-start(f32[32,64,128]{2,1,0:T(8,128)} %bitcast.5.refs_0_), channel_id=1, source_target_pairs={{0,1},{1,0},{2,3},{3,2},{4,5},{5,4},{6,7},{7,6},{8,9},{9,8},{10,11... | collective-permute-start | bytes 3145736 | tf_op jit(solution)/shard_map/ppermute | solution.py:184
  56.0 26.0 %copy-start.2 = (f32[4,1,2,128,128]{4,3,2,1,0:T(8,128)S(1)}, f32[4,1,2,128,128]{4,3,2,1,0:T(8,128)}, u32[]{:S(2)}) copy-start(f32[4,1,2,128,128]{4,3,2,1,0:T(8,128)} %refs_3_.5) | copy-start | bytes 1572868
  56.0 26.0 %copy-start.4 = (f32[4,1,2,64,128]{4,3,2,1,0:T(8,128)S(1)}, f32[4,1,2,64,128]{4,3,2,1,0:T(8,128)}, u32[]{:S(2)}) copy-start(f32[4,1,2,64,128]{4,3,2,1,0:T(8,128)} %refs_2_.7) | copy-start | bytes 786436
  56.0 26.0 %copy-start.8 = (s32[4,1,1]{0,2,1:T(1,128)S(1)}, s32[4,1,1]{0,2,1:T(1,128)}, u32[]{:S(2)}) copy-start(s32[4,1,1]{0,2,1:T(1,128)} %param.9) | copy-start | bytes 52
  99.6 19.0 %collective-permute-start.8 = (f32[4,2,64,128]{3,2,1,0:T(8,128)S(1)}, f32[4,2,64,128]{3,2,1,0:T(8,128)S(1)}, u32[]{:S(2)}, u32[]{:S(2)}) collective-permute-start(f32[4,2,64,128]{3,2,1,0:T(8,128)S(1)} %bitcast.26), channel_id=1, source_target_pairs={{0,30},{1,31},{2,0},{3,1},{4,2},{5,3},{6,4},{7,5},{8,6},{9,7},{10,... | collective-permute-start | bytes 786440 | tf_op jit(solution)/shard_map/ppermute | solution.py:151
  104.9 9.4 %collective-permute-start.5 = (f32[4,2,64,128]{3,2,1,0:T(8,128)S(1)}, f32[4,2,64,128]{3,2,1,0:T(8,128)S(1)}, u32[]{:S(2)}, u32[]{:S(2)}) collective-permute-start(f32[4,2,64,128]{3,2,1,0:T(8,128)S(1)} %bitcast.27), channel_id=1, source_target_pairs={{0,2},{1,3},{2,4},{3,5},{4,6},{5,7},{6,8},{7,9},{8,10},{9,11},{10,... | collective-permute-start | bytes 786440 | tf_op jit(solution)/shard_map/ppermute | solution.py:151
  106.9 8.9 %collective-permute-start.6 = (f32[2,2,64,128]{3,2,1,0:T(8,128)S(1)}, f32[2,2,64,128]{3,2,1,0:T(8,128)S(1)}, u32[]{:S(2)}, u32[]{:S(2)}) collective-permute-start(f32[2,2,64,128]{3,2,1,0:T(8,128)S(1)} %bitcast.36), channel_id=1, source_target_pairs={{0,4},{1,5},{2,6},{3,7},{4,8},{5,9},{6,10},{7,11},{8,12},{9,13},{1... | collective-permute-start | bytes 393224 | tf_op jit(solution)/shard_map/ppermute | solution.py:151
  110.6 7.9 %collective-permute-start.7 = (f32[2,2,64,128]{3,2,1,0:T(8,128)S(1)}, f32[2,2,64,128]{3,2,1,0:T(8,128)S(1)}, u32[]{:S(2)}, u32[]{:S(2)}) collective-permute-start(f32[2,2,64,128]{3,2,1,0:T(8,128)S(1)} %bitcast.33), channel_id=1, source_target_pairs={{0,28},{1,29},{2,30},{3,31},{4,0},{5,1},{6,2},{7,3},{8,4},{9,5},{1... | collective-permute-start | bytes 393224 | tf_op jit(solution)/shard_map/ppermute | solution.py:151
  118.6 11.7 %collective-permute-start.9 = (f32[32,64,128]{2,1,0:T(8,128)S(1)}, f32[32,64,128]{2,1,0:T(8,128)S(1)}, u32[]{:S(2)}, u32[]{:S(2)}) collective-permute-start(f32[32,64,128]{2,1,0:T(8,128)S(1)} %bitcast.14), channel_id=1, source_target_pairs={{0,1},{1,0},{2,3},{3,2},{4,5},{5,4},{6,7},{7,6},{8,9},{9,8},{10,11... | collective-permute-start | bytes 3145736 | tf_op jit(solution)/shard_map/ppermute | solution.py:184
  170.4 16.6 %collective-permute-start.13 = (f32[4,2,64,128]{3,2,1,0:T(8,128)S(1)}, f32[4,2,64,128]{3,2,1,0:T(8,128)S(1)}, u32[]{:S(2)}, u32[]{:S(2)}) collective-permute-start(f32[4,2,64,128]{3,2,1,0:T(8,128)S(1)} %bitcast.29), channel_id=1, source_target_pairs={{0,30},{1,31},{2,0},{3,1},{4,2},{5,3},{6,4},{7,5},{8,6},{9,7},{10,... | collective-permute-start | bytes 786440 | tf_op jit(solution)/shard_map/ppermute | solution.py:151
  175.1 9.4 %collective-permute-start.10 = (f32[4,2,64,128]{3,2,1,0:T(8,128)S(1)}, f32[4,2,64,128]{3,2,1,0:T(8,128)S(1)}, u32[]{:S(2)}, u32[]{:S(2)}) collective-permute-start(f32[4,2,64,128]{3,2,1,0:T(8,128)S(1)} %bitcast.30), channel_id=1, source_target_pairs={{0,2},{1,3},{2,4},{3,5},{4,6},{5,7},{6,8},{7,9},{8,10},{9,11},{10,... | collective-permute-start | bytes 786440 | tf_op jit(solution)/shard_map/ppermute | solution.py:151
  177.0 7.9 %collective-permute-start.11 = (f32[2,2,64,128]{3,2,1,0:T(8,128)S(1)}, f32[2,2,64,128]{3,2,1,0:T(8,128)S(1)}, u32[]{:S(2)}, u32[]{:S(2)}) collective-permute-start(f32[2,2,64,128]{3,2,1,0:T(8,128)S(1)} %bitcast.37), channel_id=1, source_target_pairs={{0,4},{1,5},{2,6},{3,7},{4,8},{5,9},{6,10},{7,11},{8,12},{9,13},{1... | collective-permute-start | bytes 393224 | tf_op jit(solution)/shard_map/ppermute | solution.py:151
  180.2 6.8 %collective-permute-start.12 = (f32[2,2,64,128]{3,2,1,0:T(8,128)S(1)}, f32[2,2,64,128]{3,2,1,0:T(8,128)S(1)}, u32[]{:S(2)}, u32[]{:S(2)}) collective-permute-start(f32[2,2,64,128]{3,2,1,0:T(8,128)S(1)} %bitcast.34), channel_id=1, source_target_pairs={{0,28},{1,29},{2,30},{3,31},{4,0},{5,1},{6,2},{7,3},{8,4},{9,5},{1... | collective-permute-start | bytes 393224 | tf_op jit(solution)/shard_map/ppermute | solution.py:151
  187.0 12.1 %collective-permute-start.14 = (f32[32,64,128]{2,1,0:T(8,128)S(1)}, f32[32,64,128]{2,1,0:T(8,128)S(1)}, u32[]{:S(2)}, u32[]{:S(2)}) collective-permute-start(f32[32,64,128]{2,1,0:T(8,128)S(1)} %bitcast.17), channel_id=1, source_target_pairs={{0,1},{1,0},{2,3},{3,2},{4,5},{5,4},{6,7},{7,6},{8,9},{9,8},{10,11... | collective-permute-start | bytes 3145736 | tf_op jit(solution)/shard_map/ppermute | solution.py:184

commit v4 on v3

v4 whole, which is shorter than its diff:
```python
import functools

import jax
import jax.numpy as jnp
from jax import lax
from jax.experimental import pallas as pl
from jax.experimental.pallas import tpu as pltpu
from jax.sharding import PartitionSpec as P

HIGHEST = lax.Precision.HIGHEST
ANY = pl.BlockSpec(memory_space=pl.ANY)
VMEM = pl.BlockSpec(memory_space=pltpu.VMEM)
SMEM = pl.BlockSpec(memory_space=pltpu.SMEM)
PARAMS = pltpu.CompilerParams(vmem_limit_bytes=32 * 1024 * 1024)
CORES = 2
STRIDE = 4


def dot(a, b):
    return lax.dot_general(
        a, b, (((1,), (0,)), ((), ())), precision=HIGHEST, preferred_element_type=jnp.float32
    )


def half_kernel(level, peers, levels, *refs):
    received = None
    if peers:
        received, refs = refs[0], refs[1:]
    core = refs[0][0] % CORES
    infos, rights, inverses = refs[1:3], refs[3:5], refs[5:7]
    out, right, inverse, sem = refs[7:]
    slots, half = right.shape[1:3]
    first = pl.multiple_of(core * half, half)
    loads = []
    for c in range(CORES):
        loads.append(pltpu.make_async_copy(
            rights[c].at[level, 0, :, pl.ds(first, half)], right.at[c], sem.at[2 * c]))
        loads.append(pltpu.make_async_copy(
            inverses[c].at[level, 0], inverse.at[c], sem.at[2 * c + 1]))
    for load in loads:
        load.start()
    updates = []
    if peers:
        for s in range(CORES * slots):
            update = received[s]
            for peer in range(1, peers):
                update = update + received[peer * CORES * slots + s]
            updates.append(update)
    for load in loads:
        load.wait()
    for c in range(CORES):
        for s in range(slots):
            value = right[c, s]
            if peers:
                value = value - updates[c * slots + s]
            value = dot(value, inverse[c, s])
            live = s < infos[c][2 * (levels - 1) + level, 0]
            out[c * slots + s] = jnp.where(live, value, jnp.zeros_like(value))


def half_solve(level, received, column, infos, rights, inverses):
    levels, _, slots, rows, order = rights[0].shape
    half = rows // CORES
    args, specs, peers = (), [], 0
    if received is not None:
        peers = received.shape[0] // (CORES * slots)
        args, specs = (received,), [VMEM]
    return pl.pallas_call(
        functools.partial(half_kernel, level, peers, levels),
        out_shape=jax.ShapeDtypeStruct((CORES * slots, half, order), jnp.float32),
        in_specs=specs + [SMEM] * 3 + [ANY] * 4,
        out_specs=VMEM,
        scratch_shapes=[
            pltpu.VMEM((CORES, slots, half, order), jnp.float32),
            pltpu.VMEM((CORES, slots, order, order), jnp.float32),
            pltpu.SemaphoreType.DMA((2 * CORES,)),
        ],
        compiler_params=PARAMS,
    )(*args, column, *infos, *rights, *inverses)


def last_kernel(level, peers, *refs):
    received, column, info, right_all, inverse_all = refs[:5]
    mine, theirs = refs[5 : 5 + level], refs[5 + level]
    out, right, inverse, sem = refs[6 + level :]
    slots, rows = right.shape[:2]
    half = rows // CORES
    core = column[0] % CORES
    loads = [
        pltpu.make_async_copy(right_all.at[level, 0], right, sem.at[0]),
        pltpu.make_async_copy(inverse_all.at[level, 0], inverse, sem.at[1]),
    ]
    for load in loads:
        load.start()
    near = pl.multiple_of(core * half, half)
    away = pl.multiple_of((1 - core) * half, half)
    for index in range(level):
        for s in range(slots):
            out[index, 0, s, pl.ds(near, half), :] = mine[index][s]
            out[index, 0, s, pl.ds(away, half), :] = theirs[index, s]
    updates = []
    for s in range(slots):
        pieces = []
        for c in range(CORES):
            update = received[c * slots + s]
            for peer in range(1, peers):
                update = update + received[(peer * CORES + c) * slots + s]
            pieces.append(update)
        updates.append(jnp.concatenate(pieces, axis=0))
    for load in loads:
        load.wait()
    for s in range(slots):
        value = dot(right[s] - updates[s], inverse[s])
        live = s < info[2 * level + level, 0]
        out[level, 0, s] = jnp.where(live, value, jnp.zeros_like(value))


def last_solve(received, column, info, right, inverse, mine, theirs):
    levels, _, slots, rows, order = right.shape
    return pl.pallas_call(
        functools.partial(last_kernel, levels - 1, received.shape[0] // (CORES * slots)),
        out_shape=jax.ShapeDtypeStruct(right.shape, jnp.float32),
        in_specs=[VMEM, SMEM, SMEM, ANY, ANY] + [VMEM] * (len(mine) + 1),
        out_specs=VMEM,
        scratch_shapes=[
            pltpu.VMEM((slots, rows, order), jnp.float32),
            pltpu.VMEM((slots, order, order), jnp.float32),
            pltpu.SemaphoreType.DMA((2,)),
        ],
        compiler_params=PARAMS,
    )(received, column, info, right, inverse, *mine, theirs)


def edge_kernel(level, last, edges, cols, slots, column, *refs):
    infos, couplings, history = refs[:2], refs[2:4], refs[4 : 4 + level]
    out, picked, blocks, products, picked_sem, block_sem = refs[4 + level :]
    block_copies = [
        pltpu.make_async_copy(couplings[c].at[level - 1, 0], blocks.at[c], block_sem.at[c])
        for c in range(CORES)
    ]
    for copy in block_copies:
        copy.start()
    core, chip = column[0] % CORES, column[0] // CORES
    levels_after = infos[0].shape[0]
    target_row = (levels_after - 1) // 3
    chips = cols // CORES
    for c in range(CORES):
        for e in range(edges):
            p = jnp.maximum(infos[c][level - 1, e], 0)
            where = (p // slots) % cols
            there = where // CORES
            other = ((where % CORES) != core).astype(jnp.int32)
            group = (chip + STRIDE - there % STRIDE) % STRIDE
            place = ((group * (chips // STRIDE) + there // STRIDE) * CORES + other) * slots
            place = place + p % slots
            for index in range(level):
                @pl.when(p // (slots * cols) == index)
                def _():
                    pltpu.make_async_copy(
                        history[index].at[place], picked.at[c, e], picked_sem.at[c, e]
                    ).start()
    out[...] = jnp.zeros_like(out)
    for c in range(CORES):
        for e in range(edges):
            pltpu.make_async_copy(
                history[0].at[0], picked.at[c, e], picked_sem.at[c, e]
            ).wait()
        block_copies[c].wait()
    for c in range(CORES):
        for e in range(edges):
            products[c, e] = dot(picked[c, e], blocks[c, e])
    for c in range(CORES):
        slot_of = jnp.where(core == c, 0, 1) if last else c
        for e in range(edges):
            goal = infos[c][target_row + level - 1, e]
            live = (goal >= 0).astype(jnp.float32)
            goal = jnp.maximum(goal, 0)
            goal = ((goal // slots) * CORES + slot_of) * slots + goal % slots
            out[goal] = out[goal] + products[c, e] * live


def edge_terms(level, last, column, infos, couplings, history, row_total, cols, slots):
    edges = couplings[0].shape[2]
    rows, order = history[0].shape[1:]
    return pl.pallas_call(
        functools.partial(edge_kernel, level, last, edges, cols, slots),
        out_shape=jax.ShapeDtypeStruct((row_total * CORES * slots, rows, order), jnp.float32),
        in_specs=[SMEM] * 3 + [ANY] * (2 + len(history)),
        out_specs=VMEM,
        scratch_shapes=[
            pltpu.VMEM((CORES, edges, rows, order), jnp.float32),
            pltpu.VMEM((CORES, edges, order, order), jnp.float32),
            pltpu.VMEM((CORES, edges, rows, order), jnp.float32),
            pltpu.SemaphoreType.DMA((CORES, edges)),
            pltpu.SemaphoreType.DMA((CORES,)),
        ],
        compiler_params=PARAMS,
    )(column, *infos, *couplings, *history)


def swap(x, cols):
    return lax.ppermute(x, "col", [(i, i ^ 1) for i in range(cols)])


def gather_far(solved, cols):
    far = [
        [CORES * (STRIDE * hi + lo) + core for hi in range(cols // CORES // STRIDE)]
        for lo in range(STRIDE)
        for core in range(CORES)
    ]
    return lax.all_gather(solved, "col", axis=0, tiled=False, axis_index_groups=far)


def gather_near(mine, cols):
    def shift(x, k):
        return lax.ppermute(x, "col", [(i, (i + CORES * k) % cols) for i in range(cols)])

    half = mine.shape[0] // 2
    below, above = shift(mine, 1), shift(mine, -1)
    low, high = shift(mine[:half], 2), shift(mine[half:], -2)
    same = jnp.concatenate([mine, below, low, high, above])
    return same.reshape((-1,) + same.shape[2:])


def on_device(
    right_sides, inverse_blocks, coupling_blocks, slot_counts, edge_sources, edge_targets
):
    level_total, _, slots = right_sides.shape[:3]
    edges = edge_sources.shape[2]
    rows, cols = lax.axis_size("row"), lax.axis_size("col")
    column = lax.axis_index("col").reshape(1).astype(jnp.int32)
    info = jnp.concatenate([
        edge_sources[:, 0],
        edge_targets[:, 0],
        jnp.broadcast_to(slot_counts[:, 0], (level_total, edges)),
    ])
    rights = (right_sides, swap(right_sides, cols))
    inverses = (inverse_blocks, swap(inverse_blocks, cols))
    infos = (info, swap(info, cols))
    history, results, received = [], [], None
    for level in range(level_total - 1):
        if level:
            terms = edge_terms(
                level, False, column, infos, couplings, history, rows, cols, slots
            )
            received = lax.all_to_all(terms, "row", 0, 0, tiled=True)
        solved = half_solve(level, received, column, infos, rights, inverses)
        results.append(solved)
        mine = gather_far(solved, cols)
        if level == 0:
            coupling, mine = lax.optimization_barrier((coupling_blocks, mine))
            couplings = (coupling_blocks, swap(coupling, cols))
        history.append(gather_near(mine, cols))
    terms = edge_terms(
        level_total - 1, True, column, infos, couplings, history, rows, cols, slots
    )
    theirs = swap(jnp.stack([block[slots:] for block in results]), cols)
    chip_groups = [
        [row * cols + CORES * chip + core for row in range(rows) for core in range(CORES)]
        for chip in range(cols // CORES)
    ]
    received = lax.all_to_all(
        terms, ("row", "col"), 0, 0, tiled=True, axis_index_groups=chip_groups
    )
    return last_solve(
        received, column, info, right_sides, inverse_blocks, results, theirs
    )


def solution(mesh):
    return jax.shard_map(
        on_device,
        mesh=mesh,
        in_specs=(
            P(None, "row", "col", None, None),
            P(None, "row", "col", None, None),
            P(None, "row", "col", None, None),
            P(None, "row", "col"),
            P(None, "row", "col"),
            P(None, "row", "col"),
        ),
        out_specs=P(None, "row", "col", None, None),
        check_vma=False,
    )
```

time: 225 us -> 232 us (1.031)
  blocking collectives: 119 us -> 88.4 us
  waiting for transfers between devices: 15.3 us -> 35 us
  starting transfers between devices: 66.9 us -> 75.4 us
  Pallas kernels: 15.4 us -> 23.9 us
    all_to_all x3 -> x2, blocking collectives: 61.2 us -> 37.1 us  [on_device(): received = lax.all_to_all(terms, 'row', 0, 0, tiled=True)]
    all_to_all x0 -> x1, starting transfers between devices: none -> 15.8 us  [on_device(): lax.all_to_all(terms, ('row', 'col'), 0, 0, tiled=True, axis_index_groups...]
    all_to_all x0 -> x1, waiting for transfers between devices: none -> 13.3 us  [on_device(): lax.all_to_all(terms, ('row', 'col'), 0, 0, tiled=True, axis_index_groups...]
    ppermute x12, waiting for transfers between devices: 8.2 us -> 20 us  [shift(): lax.ppermute(x, 'col', [(i, (i + CORES * k) % cols) for i in range(cols)])]
    pallas_call x7, Pallas kernels: 15.4 us -> 23.9 us  [the longest x3 15.1 us: edge_terms(): pl.pallas_call(functools.partial(edge_kernel, level, last, edges, cols, s...]
    all_gather x3, blocking collectives: 58.2 us -> 51.3 us  [gather_far(): lax.all_gather(solved, 'col', axis=0, tiled=False, axis_index_groups=far)]
    ppermute x3 -> x5, waiting for transfers between devices: 7.13 us -> 1.74 us  [swap(): return lax.ppermute(x, 'col', [(i, i ^ 1) for i in range(cols)])]
    ppermute x3 -> x5, starting transfers between devices: 25.6 us -> 21.1 us  [swap(): return lax.ppermute(x, 'col', [(i, i ^ 1) for i in range(cols)])]
  transfers between devices with their start and end apart: 15 -> 18, of which waited for: 8 -> 7; matrix products, arithmetic and copies ran while one was open for 1% -> 1% of each run, Pallas kernels for 0% -> 0%
where the time goes in v4:
time: 232 us; the launch traced here: 231 us
  blocking collectives  88.4 us (38%)
  starting transfers between devices  75.4 us (33%)
  waiting for transfers between devices  35 us (15%)
  Pallas kernels  23.9 us (10%)
  local copies, waits for them, and re-layouts  7.37 us (3%)
    all_gather x3, blocking collectives, gather_far(): lax.all_gather(solved, 'col', axis=0, tiled=False, axis_index_groups=far)  51.3 us
    ppermute x12, starting transfers between devices, shift(): lax.ppermute(x, 'col', [(i, (i + CORES * k) % cols) for i in range(cols)])  38.4 us
    all_to_all x2, blocking collectives, on_device(): received = lax.all_to_all(terms, 'row', 0, 0, tiled=True)  37.1 us
    ppermute x5, starting transfers between devices, swap(): return lax.ppermute(x, 'col', [(i, i ^ 1) for i in range(cols)])  21.1 us
    ppermute x12, waiting for transfers between devices, shift(): lax.ppermute(x, 'col', [(i, (i + CORES * k) % cols) for i in range(cols)])  20 us
    all_to_all x1, starting transfers between devices, on_device(): lax.all_to_all(terms, ('row', 'col'), 0, 0, tiled=True, axis_index_groups...  15.8 us
    pallas_call x3, Pallas kernels, edge_terms(): pl.pallas_call(functools.partial(edge_kernel, level, last, edges, cols, s...  15.1 us
    all_to_all x1, waiting for transfers between devices, on_device(): lax.all_to_all(terms, ('row', 'col'), 0, 0, tiled=True, axis_index_groups...  13.3 us
  transfers between devices with their start and end apart: 18, of which 7 were waited for; matrix products, arithmetic and copies ran while one was open for 1% of the time, Pallas kernels for 0%

profile of v4, /device:TPU:1, one launch (start us, length us, event | category | flops | bytes accessed | tf_op | source)
XLA Modules:
  0.0 230.7 jit_solution(11561510459157129655)
XLA Ops:
  0.0 9.0 %collective-permute-start.2 = (f32[4,1,2,128,128]{4,3,2,1,0:T(8,128)}, f32[4,1,2,128,128]{4,3,2,1,0:T(8,128)}, u32[]{:S(2)}, u32[]{:S(2)}) collective-permute-start(f32[4,1,2,128,128]{4,3,2,1,0:T(8,128)} %refs_4_.5), channel_id=1, source_target_pairs={{0,1},{1,0},{2,3},{3,2},{4,5},{5,4},{6,7},{7,6},{8,9},{9,8},{10,11... | collective-permute-start | bytes 1572872 | tf_op jit(solution)/shard_map/ppermute | solution.py:202
  9.1 1.9 collective-permute-start.1
  12.5 2.4 %collective-permute-start = (s32[10,16]{1,0:T(8,128)S(1)}, s32[10,16]{1,0:T(8,128)S(1)}, u32[]{:S(2)}, u32[]{:S(2)}) collective-permute-start(s32[10,16]{1,0:T(8,128)S(1)} %add_add_fusion.refs_1_.refs_0_.refs_2_), channel_id=1, source_target_pairs={{0,1},{1,0},{2,3},{3,2},{4,5},{5,4},{6,7},{7,6},{8,9},{9,8},{10,11... | collective-permute-start | bytes 1928 | tf_op jit(solution)/shard_map/ppermute | solution.py:202
  17.7 2.3 shard_map.64.refs_5_
  20.0 19.2 %all-gather = f32[16,32,128]{2,1,0:T(8,128)S(1)} all-gather(f32[4,32,128]{2,1,0:T(8,128)S(1)} %shard_map.64.refs_5_), channel_id=2, replica_groups={{0,8,16,24},{1,9,17,25},{2,10,18,26},{3,11,19,27},{4,12,20,28},{5,13,21..., dimensions={0}, use_global_device_ids=true | all-gather | bytes 327680 | tf_op jit(solution)/shard_map/all_gather | solution.py:211
  39.2 5.5 %collective-permute-start.3 = (f32[3,1,16,128,128]{4,3,2,1,0:T(8,128)}, f32[3,1,16,128,128]{4,3,2,1,0:T(8,128)S(1)}, u32[]{:S(2)}, u32[]{:S(2)}) collective-permute-start(f32[3,1,16,128,128]{4,3,2,1,0:T(8,128)} %refs_2_.5), channel_id=1, source_target_pairs={{0,1},{1,0},{2,3},{3,2},{4,5},{5,4},{6,7},{7,6},{8,9},{9,8},{10,11... | collective-permute-start | bytes 9437192 | tf_op jit(solution)/shard_map/ppermute | solution.py:202
  44.7 2.9 %collective-permute-start.4 = (f32[4,4,32,128]{3,2,1,0:T(8,128)S(1)}, f32[4,4,32,128]{3,2,1,0:T(8,128)S(1)}, u32[]{:S(2)}, u32[]{:S(2)}) collective-permute-start(f32[4,4,32,128]{3,2,1,0:T(8,128)S(1)} %bitcast.28), channel_id=1, source_target_pairs={{0,2},{1,3},{2,4},{3,5},{4,6},{5,7},{6,8},{7,9},{8,10},{9,11},{10,... | collective-permute-start | bytes 786440 | tf_op jit(solution)/shard_map/ppermute | solution.py:216
  47.6 2.8 %collective-permute-start.5 = (f32[2,4,32,128]{3,2,1,0:T(8,128)S(1)}, f32[2,4,32,128]{3,2,1,0:T(8,128)S(1)}, u32[]{:S(2)}, u32[]{:S(2)}) collective-permute-start(f32[2,4,32,128]{3,2,1,0:T(8,128)S(1)} %get-tuple-element.14), channel_id=1, source_target_pairs={{0,4},{1,5},{2,6},{3,7},{4,8},{5,9},{6,10},{7,11},{8,12},{9,13},{1... | collective-permute-start | bytes 393224 | tf_op jit(solution)/shard_map/ppermute | solution.py:216
  50.5 4.1 %collective-permute-start.7 = (f32[4,4,32,128]{3,2,1,0:T(8,128)S(1)}, f32[4,4,32,128]{3,2,1,0:T(8,128)S(1)}, u32[]{:S(2)}, u32[]{:S(2)}) collective-permute-start(f32[4,4,32,128]{3,2,1,0:T(8,128)S(1)} %bitcast.31), channel_id=1, source_target_pairs={{0,30},{1,31},{2,0},{3,1},{4,2},{5,3},{6,4},{7,5},{8,6},{9,7},{10,... | collective-permute-start | bytes 786440 | tf_op jit(solution)/shard_map/ppermute | solution.py:216
  54.6 2.9 %collective-permute-start.6 = (f32[2,4,32,128]{3,2,1,0:T(8,128)S(1)}, f32[2,4,32,128]{3,2,1,0:T(8,128)S(1)}, u32[]{:S(2)}, u32[]{:S(2)}) collective-permute-start(f32[2,4,32,128]{3,2,1,0:T(8,128)S(1)} %get-tuple-element.13), channel_id=1, source_target_pairs={{0,28},{1,29},{2,30},{3,31},{4,0},{5,1},{6,2},{7,3},{8,4},{9,5},{1... | collective-permute-start | bytes 393224 | tf_op jit(solution)/shard_map/ppermute | solution.py:216
  57.5 3.9 %collective-permute-done.5 = f32[2,4,32,128]{3,2,1,0:T(8,128)S(1)} collective-permute-done((f32[2,4,32,128]{3,2,1,0:T(8,128)S(1)}, f32[2,4,32,128]{3,2,1,0:T(8,128)S(1)}, u32[]{:S(2)}, u32[]{:S(2)}) %collective-permute-start.5) | collective-permute-done | bytes 131104 | tf_op jit(solution)/shard_map/ppermute | solution.py:216
  61.4 5.0 %collective-permute-done.6 = f32[2,4,32,128]{3,2,1,0:T(8,128)S(1)} collective-permute-done((f32[2,4,32,128]{3,2,1,0:T(8,128)S(1)}, f32[2,4,32,128]{3,2,1,0:T(8,128)S(1)}, u32[]{:S(2)}, u32[]{:S(2)}) %collective-permute-start.6) | collective-permute-done | bytes 131104 | tf_op jit(solution)/shard_map/ppermute | solution.py:216
  66.5 4.8 %shard_map.65 = f32[64,32,128]{2,1,0:T(8,128)S(1)} custom-call(s32[1]{0:T(128)} %bitcast.refs_0_.column.refs_1_, s32[10,16]{1,0:T(8,128)S(1)} %add_add_fusion.refs_1_.refs_0_.refs_2_, s32[10,16]{1,0:T(8,128)S(1)} %collective-permute-done.refs_2_.refs_1_.refs_3_, f32[3,1,16,128,128]{4,3,2,1,0:T(8,128)S(1)} %copy-done, ...), custom_call_target="tpu_custom_call" | custom-call | tf_op jit(solution)/shard_map/pallas_call | solution.py:185
  71.3 22.2 %all_to_all.15.refs_0_ = f32[64,32,128]{2,1,0:T(8,128)S(1)} all-to-all(f32[64,32,128]{2,1,0:T(8,128)S(1)} %shard_map.65), channel_id=1, replica_groups=mesh['row'=16,'col'=32] {'row'}, dimensions={0} | all-to-all | bytes 2097152 | tf_op jit(solution)/shard_map/all_to_all | solution.py:246
  93.6 2.3 shard_map.66.refs_6_
  95.9 16.0 %all-gather.1 = f32[16,32,128]{2,1,0:T(8,128)S(1)} all-gather(f32[4,32,128]{2,1,0:T(8,128)S(1)} %shard_map.66.refs_6_), channel_id=3, replica_groups={{0,8,16,24},{1,9,17,25},{2,10,18,26},{3,11,19,27},{4,12,20,28},{5,13,21..., dimensions={0}, use_global_device_ids=true | all-gather | bytes 327680 | tf_op jit(solution)/shard_map/all_gather | solution.py:211
  113.8 4.4 %collective-permute-start.9 = (f32[2,4,32,128]{3,2,1,0:T(8,128)S(1)}, f32[2,4,32,128]{3,2,1,0:T(8,128)S(1)}, u32[]{:S(2)}, u32[]{:S(2)}) collective-permute-start(f32[2,4,32,128]{3,2,1,0:T(8,128)S(1)} %bitcast.40), channel_id=1, source_target_pairs={{0,4},{1,5},{2,6},{3,7},{4,8},{5,9},{6,10},{7,11},{8,12},{9,13},{1... | collective-permute-start | bytes 393224 | tf_op jit(solution)/shard_map/ppermute | solution.py:216
  118.2 4.6 %collective-permute-start.11 = (f32[4,4,32,128]{3,2,1,0:T(8,128)S(1)}, f32[4,4,32,128]{3,2,1,0:T(8,128)S(1)}, u32[]{:S(2)}, u32[]{:S(2)}) collective-permute-start(f32[4,4,32,128]{3,2,1,0:T(8,128)S(1)} %bitcast.34), channel_id=1, source_target_pairs={{0,30},{1,31},{2,0},{3,1},{4,2},{5,3},{6,4},{7,5},{8,6},{9,7},{10,... | collective-permute-start | bytes 786440 | tf_op jit(solution)/shard_map/ppermute | solution.py:216
  122.8 1.9 collective-permute-start.10
  124.8 6.3 %collective-permute-done.10 = f32[2,4,32,128]{3,2,1,0:T(8,128)S(1)} collective-permute-done((f32[2,4,32,128]{3,2,1,0:T(8,128)S(1)}, f32[2,4,32,128]{3,2,1,0:T(8,128)S(1)}, u32[]{:S(2)}, u32[]{:S(2)}) %collective-permute-start.10) | collective-permute-done | bytes 131104 | tf_op jit(solution)/shard_map/ppermute | solution.py:216
  131.2 5.0 %shard_map.67 = f32[64,32,128]{2,1,0:T(8,128)S(1)} custom-call(s32[1]{0:T(128)} %bitcast.refs_0_.column.refs_1_, s32[10,16]{1,0:T(8,128)S(1)} %add_add_fusion.refs_1_.refs_0_.refs_2_, s32[10,16]{1,0:T(8,128)S(1)} %collective-permute-done.refs_2_.refs_1_.refs_3_, f32[3,1,16,128,128]{4,3,2,1,0:T(8,128)S(1)} %copy-done, ...), custom_call_target="tpu_custom_call" | custom-call | tf_op jit(solution)/shard_map/pallas_call | solution.py:185
  136.2 14.9 %all_to_all.16.refs_0_ = f32[64,32,128]{2,1,0:T(8,128)S(1)} all-to-all(f32[64,32,128]{2,1,0:T(8,128)S(1)} %shard_map.67), channel_id=1, replica_groups=mesh['row'=16,'col'=32] {'row'}, dimensions={0} | all-to-all | bytes 2097152 | tf_op jit(solution)/shard_map/all_to_all | solution.py:246
  151.0 2.3 shard_map.68.refs_7_
  153.3 16.1 %all-gather.2 = f32[16,32,128]{2,1,0:T(8,128)S(1)} all-gather(f32[4,32,128]{2,1,0:T(8,128)S(1)} %shard_map.68.refs_7_), channel_id=4, replica_groups={{0,8,16,24},{1,9,17,25},{2,10,18,26},{3,11,19,27},{4,12,20,28},{5,13,21..., dimensions={0}, use_global_device_ids=true | all-gather | bytes 327680 | tf_op jit(solution)/shard_map/all_gather | solution.py:211
  171.4 4.5 %collective-permute-start.13 = (f32[2,4,32,128]{3,2,1,0:T(8,128)S(1)}, f32[2,4,32,128]{3,2,1,0:T(8,128)S(1)}, u32[]{:S(2)}, u32[]{:S(2)}) collective-permute-start(f32[2,4,32,128]{3,2,1,0:T(8,128)S(1)} %bitcast.41), channel_id=1, source_target_pairs={{0,4},{1,5},{2,6},{3,7},{4,8},{5,9},{6,10},{7,11},{8,12},{9,13},{1... | collective-permute-start | bytes 393224 | tf_op jit(solution)/shard_map/ppermute | solution.py:216
  176.0 4.6 %collective-permute-start.15 = (f32[4,4,32,128]{3,2,1,0:T(8,128)S(1)}, f32[4,4,32,128]{3,2,1,0:T(8,128)S(1)}, u32[]{:S(2)}, u32[]{:S(2)}) collective-permute-start(f32[4,4,32,128]{3,2,1,0:T(8,128)S(1)} %bitcast.37), channel_id=1, source_target_pairs={{0,30},{1,31},{2,0},{3,1},{4,2},{5,3},{6,4},{7,5},{8,6},{9,7},{10,... | collective-permute-start | bytes 786440 | tf_op jit(solution)/shard_map/ppermute | solution.py:216
  182.5 4.7 %collective-permute-done.14 = f32[2,4,32,128]{3,2,1,0:T(8,128)S(1)} collective-permute-done((f32[2,4,32,128]{3,2,1,0:T(8,128)S(1)}, f32[2,4,32,128]{3,2,1,0:T(8,128)S(1)}, u32[]{:S(2)}, u32[]{:S(2)}) %collective-permute-start.14) | collective-permute-done | bytes 131104 | tf_op jit(solution)/shard_map/ppermute | solution.py:216
  187.4 5.3 %shard_map.69 = f32[64,32,128]{2,1,0:T(8,128)S(1)} custom-call(s32[1]{0:T(128)} %bitcast.refs_0_.column.refs_1_, s32[10,16]{1,0:T(8,128)S(1)} %add_add_fusion.refs_1_.refs_0_.refs_2_, s32[10,16]{1,0:T(8,128)S(1)} %collective-permute-done.refs_2_.refs_1_.refs_3_, f32[3,1,16,128,128]{4,3,2,1,0:T(8,128)S(1)} %copy-done, ...), custom_call_target="tpu_custom_call" | custom-call | tf_op jit(solution)/shard_map/pallas_call | solution.py:185
  193.6 15.8 %all-to-all-start.2 = ((f32[64,32,128]{2,1,0:T(8,128)}), f32[64,32,128]{2,1,0:T(8,128)S(1)}, u32[]{:S(2)}, u32[]{:S(2)}) async-start(f32[64,32,128]{2,1,0:T(8,128)} %copy-done.5), calls=%async_computation.2 | async-start | bytes 2097152 | tf_op jit(solution)/shard_map/all_to_all | solution.py:262
  210.3 2.3 collective-permute-start.16
  213.5 13.3 %all-to-all-done.2.refs_0_ = f32[64,32,128]{2,1,0:T(8,128)S(1)} async-done(((f32[64,32,128]{2,1,0:T(8,128)}), f32[64,32,128]{2,1,0:T(8,128)S(1)}, u32[]{:S(2)}, u32[]{:S(2)}) %all-to-all-start.2) | async-done | bytes 1048608 | tf_op jit(solution)/shard_map/all_to_all | solution.py:262
  228.6 1.9 shard_map.70
  (57 shorter events, 15.0 us)
Async XLA Ops:
  0.0 66.5 %copy-start = (f32[3,1,16,128,128]{4,3,2,1,0:T(8,128)S(1)}, f32[3,1,16,128,128]{4,3,2,1,0:T(8,128)}, u32[]{:S(2)}) copy-start(f32[3,1,16,128,128]{4,3,2,1,0:T(8,128)} %refs_2_.5) | copy-start | bytes 9437188
  0.0 15.7 %collective-permute-start.2 = (f32[4,1,2,128,128]{4,3,2,1,0:T(8,128)}, f32[4,1,2,128,128]{4,3,2,1,0:T(8,128)}, u32[]{:S(2)}, u32[]{:S(2)}) collective-permute-start(f32[4,1,2,128,128]{4,3,2,1,0:T(8,128)} %refs_4_.5), channel_id=1, source_target_pairs={{0,1},{1,0},{2,3},{3,2},{4,5},{5,4},{6,7},{7,6},{8,9},{9,8},{10,11... | collective-permute-start | bytes 1572872 | tf_op jit(solution)/shard_map/ppermute | solution.py:202
  9.1 6.6 %collective-permute-start.1 = (f32[4,1,2,64,128]{4,3,2,1,0:T(8,128)}, f32[4,1,2,64,128]{4,3,2,1,0:T(8,128)S(1)}, u32[]{:S(2)}, u32[]{:S(2)}) collective-permute-start(f32[4,1,2,64,128]{4,3,2,1,0:T(8,128)} %refs_3_.3), channel_id=1, source_target_pairs={{0,1},{1,0},{2,3},{3,2},{4,5},{5,4},{6,7},{7,6},{8,9},{9,8},{10,11... | collective-permute-start | bytes 786440 | tf_op jit(solution)/shard_map/ppermute | solution.py:202
  12.5 3.2 %collective-permute-start = (s32[10,16]{1,0:T(8,128)S(1)}, s32[10,16]{1,0:T(8,128)S(1)}, u32[]{:S(2)}, u32[]{:S(2)}) collective-permute-start(s32[10,16]{1,0:T(8,128)S(1)} %add_add_fusion.refs_1_.refs_0_.refs_2_), channel_id=1, source_target_pairs={{0,1},{1,0},{2,3},{3,2},{4,5},{5,4},{6,7},{7,6},{8,9},{9,8},{10,11... | collective-permute-start | bytes 1928 | tf_op jit(solution)/shard_map/ppermute | solution.py:202
  15.7 1.0 copy-start.1
  16.7 0.9 copy-start.3
  39.2 27.3 %collective-permute-start.3 = (f32[3,1,16,128,128]{4,3,2,1,0:T(8,128)}, f32[3,1,16,128,128]{4,3,2,1,0:T(8,128)S(1)}, u32[]{:S(2)}, u32[]{:S(2)}) collective-permute-start(f32[3,1,16,128,128]{4,3,2,1,0:T(8,128)} %refs_2_.5), channel_id=1, source_target_pairs={{0,1},{1,0},{2,3},{3,2},{4,5},{5,4},{6,7},{7,6},{8,9},{9,8},{10,11... | collective-permute-start | bytes 9437192 | tf_op jit(solution)/shard_map/ppermute | solution.py:202
  44.7 12.8 %collective-permute-start.4 = (f32[4,4,32,128]{3,2,1,0:T(8,128)S(1)}, f32[4,4,32,128]{3,2,1,0:T(8,128)S(1)}, u32[]{:S(2)}, u32[]{:S(2)}) collective-permute-start(f32[4,4,32,128]{3,2,1,0:T(8,128)S(1)} %bitcast.28), channel_id=1, source_target_pairs={{0,2},{1,3},{2,4},{3,5},{4,6},{5,7},{6,8},{7,9},{8,10},{9,11},{10,... | collective-permute-start | bytes 786440 | tf_op jit(solution)/shard_map/ppermute | solution.py:216
  47.6 13.8 %collective-permute-start.5 = (f32[2,4,32,128]{3,2,1,0:T(8,128)S(1)}, f32[2,4,32,128]{3,2,1,0:T(8,128)S(1)}, u32[]{:S(2)}, u32[]{:S(2)}) collective-permute-start(f32[2,4,32,128]{3,2,1,0:T(8,128)S(1)} %get-tuple-element.14), channel_id=1, source_target_pairs={{0,4},{1,5},{2,6},{3,7},{4,8},{5,9},{6,10},{7,11},{8,12},{9,13},{1... | collective-permute-start | bytes 393224 | tf_op jit(solution)/shard_map/ppermute | solution.py:216
  50.5 16.0 %collective-permute-start.7 = (f32[4,4,32,128]{3,2,1,0:T(8,128)S(1)}, f32[4,4,32,128]{3,2,1,0:T(8,128)S(1)}, u32[]{:S(2)}, u32[]{:S(2)}) collective-permute-start(f32[4,4,32,128]{3,2,1,0:T(8,128)S(1)} %bitcast.31), channel_id=1, source_target_pairs={{0,30},{1,31},{2,0},{3,1},{4,2},{5,3},{6,4},{7,5},{8,6},{9,7},{10,... | collective-permute-start | bytes 786440 | tf_op jit(solution)/shard_map/ppermute | solution.py:216
  54.6 11.9 %collective-permute-start.6 = (f32[2,4,32,128]{3,2,1,0:T(8,128)S(1)}, f32[2,4,32,128]{3,2,1,0:T(8,128)S(1)}, u32[]{:S(2)}, u32[]{:S(2)}) collective-permute-start(f32[2,4,32,128]{3,2,1,0:T(8,128)S(1)} %get-tuple-element.13), channel_id=1, source_target_pairs={{0,28},{1,29},{2,30},{3,31},{4,0},{5,1},{6,2},{7,3},{8,4},{9,5},{1... | collective-permute-start | bytes 393224 | tf_op jit(solution)/shard_map/ppermute | solution.py:216
  111.8 12.9 %collective-permute-start.8 = (f32[4,4,32,128]{3,2,1,0:T(8,128)S(1)}, f32[4,4,32,128]{3,2,1,0:T(8,128)S(1)}, u32[]{:S(2)}, u32[]{:S(2)}) collective-permute-start(f32[4,4,32,128]{3,2,1,0:T(8,128)S(1)} %bitcast.32), channel_id=1, source_target_pairs={{0,2},{1,3},{2,4},{3,5},{4,6},{5,7},{6,8},{7,9},{8,10},{9,11},{10,... | collective-permute-start | bytes 786440 | tf_op jit(solution)/shard_map/ppermute | solution.py:216
  113.8 11.0 %collective-permute-start.9 = (f32[2,4,32,128]{3,2,1,0:T(8,128)S(1)}, f32[2,4,32,128]{3,2,1,0:T(8,128)S(1)}, u32[]{:S(2)}, u32[]{:S(2)}) collective-permute-start(f32[2,4,32,128]{3,2,1,0:T(8,128)S(1)} %bitcast.40), channel_id=1, source_target_pairs={{0,4},{1,5},{2,6},{3,7},{4,8},{5,9},{6,10},{7,11},{8,12},{9,13},{1... | collective-permute-start | bytes 393224 | tf_op jit(solution)/shard_map/ppermute | solution.py:216
  118.2 12.9 %collective-permute-start.11 = (f32[4,4,32,128]{3,2,1,0:T(8,128)S(1)}, f32[4,4,32,128]{3,2,1,0:T(8,128)S(1)}, u32[]{:S(2)}, u32[]{:S(2)}) collective-permute-start(f32[4,4,32,128]{3,2,1,0:T(8,128)S(1)} %bitcast.34), channel_id=1, source_target_pairs={{0,30},{1,31},{2,0},{3,1},{4,2},{5,3},{6,4},{7,5},{8,6},{9,7},{10,... | collective-permute-start | bytes 786440 | tf_op jit(solution)/shard_map/ppermute | solution.py:216
  122.8 8.3 %collective-permute-start.10 = (f32[2,4,32,128]{3,2,1,0:T(8,128)S(1)}, f32[2,4,32,128]{3,2,1,0:T(8,128)S(1)}, u32[]{:S(2)}, u32[]{:S(2)}) collective-permute-start(f32[2,4,32,128]{3,2,1,0:T(8,128)S(1)} %bitcast.38), channel_id=1, source_target_pairs={{0,28},{1,29},{2,30},{3,31},{4,0},{5,1},{6,2},{7,3},{8,4},{9,5},{1... | collective-permute-start | bytes 393224 | tf_op jit(solution)/shard_map/ppermute | solution.py:216
  153.3 18.1 %copy-start.6 = (f32[4,32,128]{2,1,0:T(8,128)}, f32[4,32,128]{2,1,0:T(8,128)S(1)}, u32[]{:S(2)}) copy-start(f32[4,32,128]{2,1,0:T(8,128)S(1)} %shard_map.68.refs_7_) | copy-start | bytes 196612
  169.4 13.0 %collective-permute-start.12 = (f32[4,4,32,128]{3,2,1,0:T(8,128)S(1)}, f32[4,4,32,128]{3,2,1,0:T(8,128)S(1)}, u32[]{:S(2)}, u32[]{:S(2)}) collective-permute-start(f32[4,4,32,128]{3,2,1,0:T(8,128)S(1)} %bitcast.35), channel_id=1, source_target_pairs={{0,2},{1,3},{2,4},{3,5},{4,6},{5,7},{6,8},{7,9},{8,10},{9,11},{10,... | collective-permute-start | bytes 786440 | tf_op jit(solution)/shard_map/ppermute | solution.py:216
  171.4 11.1 %collective-permute-start.13 = (f32[2,4,32,128]{3,2,1,0:T(8,128)S(1)}, f32[2,4,32,128]{3,2,1,0:T(8,128)S(1)}, u32[]{:S(2)}, u32[]{:S(2)}) collective-permute-start(f32[2,4,32,128]{3,2,1,0:T(8,128)S(1)} %bitcast.41), channel_id=1, source_target_pairs={{0,4},{1,5},{2,6},{3,7},{4,8},{5,9},{6,10},{7,11},{8,12},{9,13},{1... | collective-permute-start | bytes 393224 | tf_op jit(solution)/shard_map/ppermute | solution.py:216
  176.0 11.3 %collective-permute-start.15 = (f32[4,4,32,128]{3,2,1,0:T(8,128)S(1)}, f32[4,4,32,128]{3,2,1,0:T(8,128)S(1)}, u32[]{:S(2)}, u32[]{:S(2)}) collective-permute-start(f32[4,4,32,128]{3,2,1,0:T(8,128)S(1)} %bitcast.37), channel_id=1, source_target_pairs={{0,30},{1,31},{2,0},{3,1},{4,2},{5,3},{6,4},{7,5},{8,6},{9,7},{10,... | collective-permute-start | bytes 786440 | tf_op jit(solution)/shard_map/ppermute | solution.py:216
  180.5 6.7 %collective-permute-start.14 = (f32[2,4,32,128]{3,2,1,0:T(8,128)S(1)}, f32[2,4,32,128]{3,2,1,0:T(8,128)S(1)}, u32[]{:S(2)}, u32[]{:S(2)}) collective-permute-start(f32[2,4,32,128]{3,2,1,0:T(8,128)S(1)} %bitcast.39), channel_id=1, source_target_pairs={{0,28},{1,29},{2,30},{3,31},{4,0},{5,1},{6,2},{7,3},{8,4},{9,5},{1... | collective-permute-start | bytes 393224 | tf_op jit(solution)/shard_map/ppermute | solution.py:216
  187.3 39.4 %copy-start.4 = (f32[4,1,2,64,128]{4,3,2,1,0:T(8,128)S(1)}, f32[4,1,2,64,128]{4,3,2,1,0:T(8,128)}, u32[]{:S(2)}) copy-start(f32[4,1,2,64,128]{4,3,2,1,0:T(8,128)} %refs_3_.3) | copy-start | bytes 786436
  192.7 1.0 copy-start.5
  193.6 33.1 %all-to-all-start.2 = ((f32[64,32,128]{2,1,0:T(8,128)}), f32[64,32,128]{2,1,0:T(8,128)S(1)}, u32[]{:S(2)}, u32[]{:S(2)}) async-start(f32[64,32,128]{2,1,0:T(8,128)} %copy-done.5), calls=%async_computation.2 | async-start | bytes 2097152 | tf_op jit(solution)/shard_map/all_to_all | solution.py:262
  210.3 3.2 %collective-permute-start.16 = (f32[3,2,32,128]{3,2,1,0:T(8,128)S(1)}, f32[3,2,32,128]{3,2,1,0:T(8,128)S(1)}, u32[]{:S(2)}, u32[]{:S(2)}) collective-permute-start(f32[3,2,32,128]{3,2,1,0:T(8,128)S(1)} %pad_maximum_fusion), channel_id=1, source_target_pairs={{0,1},{1,0},{2,3},{3,2},{4,5},{5,4},{6,7},{7,6},{8,9},{9,8},{10,11... | collective-permute-start | bytes 294920 | tf_op jit(solution)/shard_map/ppermute | solution.py:202
  226.8 1.0 copy-start.2
  227.8 0.8 copy-start.7

commit v5 on v0

v5 whole, which is shorter than its diff:
```python
import functools

import jax
import jax.numpy as jnp
from jax import lax
from jax.experimental import pallas as pl
from jax.experimental.pallas import tpu as pltpu
from jax.sharding import PartitionSpec as P

HIGHEST = lax.Precision.HIGHEST
ANY = pl.BlockSpec(memory_space=pl.ANY)
VMEM = pl.BlockSpec(memory_space=pltpu.VMEM)
SMEM = pl.BlockSpec(memory_space=pltpu.SMEM)
PARAMS = pltpu.CompilerParams(vmem_limit_bytes=32 * 1024 * 1024)
CORES = 2
STRIDE = 4


def dot(a, b):
    return lax.dot_general(
        a, b, (((1,), (0,)), ((), ())), precision=HIGHEST, preferred_element_type=jnp.float32
    )


def first_kernel(counts, right_all, inverse_all, out, right, inverse, sem):
    loads = [
        pltpu.make_async_copy(right_all.at[0, 0], right, sem.at[0]),
        pltpu.make_async_copy(inverse_all.at[0, 0], inverse, sem.at[1]),
    ]
    for load in loads:
        load.start()
    for load in loads:
        load.wait()
    for s in range(right.shape[0]):
        value = dot(right[s], inverse[s])
        out[s] = jnp.where(s < counts[0, 0, 0], value, jnp.zeros_like(value))


def first_solve(counts, right, inverse):
    slots, rows, order = right.shape[2:]
    return pl.pallas_call(
        first_kernel,
        out_shape=jax.ShapeDtypeStruct((slots, rows, order), jnp.float32),
        in_specs=[SMEM, ANY, ANY],
        out_specs=VMEM,
        scratch_shapes=[
            pltpu.VMEM((slots, rows, order), jnp.float32),
            pltpu.VMEM((slots, order, order), jnp.float32),
            pltpu.SemaphoreType.DMA((2,)),
        ],
        compiler_params=pltpu.CompilerParams(vmem_limit_bytes=60 * 1024 * 1024),
    )(counts, right, inverse)


def solve_kernel(level, last, received, counts, right, inverse, *refs):
    earlier, out = refs[:-1], refs[-1]
    slots = right.shape[2]
    peers = received.shape[0] // (CORES * slots)
    for index, block in enumerate(earlier):
        out[index, 0] = block[...]
    for s in range(slots):
        pieces = []
        for c in range(CORES):
            update = received[c * slots + s]
            for peer in range(1, peers):
                update = update + received[(peer * CORES + c) * slots + s]
            pieces.append(update)
        update = jnp.concatenate(pieces, axis=0)
        value = dot(right[level, 0, s] - update, inverse[level, 0, s])
        value = jnp.where(s < counts[0, 0, level], value, jnp.zeros_like(value))
        if last:
            out[level, 0, s] = value
        else:
            out[s] = value


def solve(level, received, counts, right, inverse, results):
    last = level + 1 == right.shape[0]
    earlier = results if last else []
    shape = right.shape if last else right.shape[2:]
    return pl.pallas_call(
        functools.partial(solve_kernel, level, last),
        out_shape=jax.ShapeDtypeStruct(shape, jnp.float32),
        in_specs=[VMEM, SMEM, VMEM, VMEM] + [VMEM] * len(earlier),
        out_specs=VMEM,
        compiler_params=PARAMS,
    )(received, counts, right, inverse, *earlier)


def edge_kernel(level, edges, cols, slots, column, *refs):
    infos, couplings, history = refs[:2], refs[2:4], refs[4 : 4 + level]
    out, products = refs[4 + level :]
    core, chip = column[0] % CORES, column[0] // CORES
    chips = cols // CORES
    target_row = infos[0].shape[0] // 2
    for c in range(CORES):
        for e in range(edges):
            p = jnp.maximum(infos[c][level - 1, e], 0)
            where = (p // slots) % cols
            there = where // CORES
            other = ((where % CORES) != core).astype(jnp.int32)
            group = (chip + STRIDE - there % STRIDE) % STRIDE
            place = ((group * (chips // STRIDE) + there // STRIDE) * CORES + other) * slots
            place = place + p % slots
            source_level = p // (slots * cols)
            block = history[0][place]
            for index in range(1, level):
                block = jnp.where(source_level == index, history[index][place], block)
            products[c, e] = dot(block, couplings[c][level - 1, 0, e])
    out[...] = jnp.zeros_like(out)
    for c in range(CORES):
        owner = jnp.where(core == c, 0, 1)
        for e in range(edges):
            goal = infos[c][target_row + level - 1, e]
            live = (goal >= 0).astype(jnp.float32)
            goal = jnp.maximum(goal, 0)
            goal = ((goal // slots) * CORES + owner) * slots + goal % slots
            out[goal] = out[goal] + products[c, e] * live


def edge_terms(level, column, infos, couplings, history, row_total, cols, slots):
    edges = couplings[0].shape[2]
    rows, order = history[0].shape[1:]
    return pl.pallas_call(
        functools.partial(edge_kernel, level, edges, cols, slots),
        out_shape=jax.ShapeDtypeStruct((row_total * CORES * slots, rows, order), jnp.float32),
        in_specs=[SMEM] * 3 + [VMEM] * (2 + len(history)),
        out_specs=VMEM,
        scratch_shapes=[pltpu.VMEM((CORES, edges, rows, order), jnp.float32)],
        compiler_params=PARAMS,
    )(column, *infos, *couplings, *history)


def swap(x, cols):
    return lax.ppermute(x, "col", [(i, i ^ 1) for i in range(cols)])


def gather_far(solved, cols):
    far = [
        [CORES * (STRIDE * hi + lo) + core for hi in range(cols // CORES // STRIDE)]
        for lo in range(STRIDE)
        for core in range(CORES)
    ]
    return lax.all_gather(solved, "col", axis=0, tiled=False, axis_index_groups=far)


def gather_near(mine, cols):
    def shift(x, k):
        return lax.ppermute(x, "col", [(i, (i + CORES * k) % cols) for i in range(cols)])

    half = mine.shape[0] // 2
    below, above = shift(mine, 1), shift(mine, -1)
    low, high = shift(mine[:half], 2), shift(mine[half:], -2)
    same = jnp.concatenate([mine, below, low, high, above])
    return same.reshape((-1,) + same.shape[2:])


def split_rows(solved, core, cols):
    pairs = [[CORES * chip + core for core in range(CORES)] for chip in range(cols // CORES)]
    both = lax.all_gather(solved, "col", axis=0, tiled=False, axis_index_groups=pairs)
    half = both.shape[2] // CORES
    both = lax.dynamic_slice_in_dim(both, core * half, half, axis=2)
    both = jnp.where(core == 0, both, jnp.flip(both, axis=0))
    return both.reshape((-1,) + both.shape[2:])


def on_device(
    right_sides, inverse_blocks, coupling_blocks, slot_counts, edge_sources, edge_targets
):
    level_total, _, slots = right_sides.shape[:3]
    rows, cols = lax.axis_size("row"), lax.axis_size("col")
    column = lax.axis_index("col").astype(jnp.int32)
    counts = jnp.transpose(slot_counts, (1, 2, 0))
    chip_groups = [
        [row * cols + CORES * chip + core for row in range(rows) for core in range(CORES)]
        for chip in range(cols // CORES)
    ]
    solved = first_solve(counts, right_sides, inverse_blocks)
    history, results = [], []
    for level in range(1, level_total):
        results.append(solved)
        mine = gather_far(split_rows(solved, column % CORES, cols), cols)
        if level == 1:
            coupling, sources, targets, mine = lax.optimization_barrier(
                (coupling_blocks, edge_sources[:, 0], edge_targets[:, 0], mine)
            )
            info = jnp.concatenate([sources, targets])
            infos = (info, swap(info, cols))
            couplings = (coupling_blocks, swap(coupling, cols))
        history.append(gather_near(mine, cols))
        terms = edge_terms(
            level, column.reshape(1), infos, couplings, history, rows, cols, slots
        )
        received = lax.all_to_all(
            terms, ("row", "col"), 0, 0, tiled=True, axis_index_groups=chip_groups
        )
        solved = solve(level, received, counts, right_sides, inverse_blocks, results)
    return solved


def solution(mesh):
    return jax.shard_map(
        on_device,
        mesh=mesh,
        in_specs=(
            P(None, "row", "col", None, None),
            P(None, "row", "col", None, None),
            P(None, "row", "col", None, None),
            P(None, "row", "col"),
            P(None, "row", "col"),
            P(None, "row", "col"),
        ),
        out_specs=P(None, "row", "col", None, None),
        check_vma=False,
    )
```

time: 539 us -> 223 us (0.41)
  waiting for transfers between devices: 470 us -> 18 us
  blocking collectives: 0 us -> 136 us
  starting transfers between devices: 0.21 us -> 53.4 us
  local copies, waits for them, and re-layouts: 33.9 us -> 1.04 us
  matrix products: 15.6 us -> 0 us
  Pallas kernels: 0 us -> 13.4 us
  between operations: 13.6 us -> 0.39 us
    reduce_scatter x3 -> x0, waiting for transfers between devices: 248 us -> none  [on_device(): update = lax.psum_scatter(buffer, 'row', scatter_dimension=0, tiled=True)]
    all_gather x3 -> x0, waiting for transfers between devices: 223 us -> none  [on_device(): gathered = lax.all_gather(solved, 'col', axis=0, tiled=True)]
    all_to_all x0 -> x3, blocking collectives: none -> 72 us  [on_device(): lax.all_to_all(terms, ('row', 'col'), 0, 0, tiled=True, axis_index_groups...]
    all_gather x0 -> x6, blocking collectives: none -> 63.9 us  [the longest x3 51.4 us: gather_far(): lax.all_gather(solved, 'col', axis=0, tiled=False, axis_index_groups=far)]
    ppermute x0 -> x14, starting transfers between devices: none -> 53.4 us  [the longest x12 44.7 us: shift(): lax.ppermute(x, 'col', [(i, (i + CORES * k) % cols) for i in range(cols)])]
    ppermute x0 -> x14, waiting for transfers between devices: none -> 18 us  [the longest x12 18 us: shift(): lax.ppermute(x, 'col', [(i, (i + CORES * k) % cols) for i in range(cols)])]
    dot_general x10 -> x0, matrix products: 15.6 us -> none  [the longest x4 6.63 us: on_device(): jnp.einsum('srb,sbd->srd', right_sides[level_index, 0] - update, inverse_...]
    gather x3 -> x0, local copies, waits for them, and re-layouts: 14.4 us -> none  [edge_terms(): jnp.take(history, clipped, axis=0)]
  transfers between devices with their start and end apart: 6 -> 14, of which waited for: 6 -> 4; matrix products, arithmetic and copies ran while one was open for 1% -> 0% of each run, Pallas kernels for 0% -> 0%
where the time goes in v5:
time: 223 us; the launch traced here: 222 us
  blocking collectives  136 us (61%)
  starting transfers between devices  53.4 us (24%)
  waiting for transfers between devices  18 us (8%)
  Pallas kernels  13.4 us (6%)
    all_to_all x3, blocking collectives, on_device(): lax.all_to_all(terms, ('row', 'col'), 0, 0, tiled=True, axis_index_groups...  72 us
    all_gather x3, blocking collectives, gather_far(): lax.all_gather(solved, 'col', axis=0, tiled=False, axis_index_groups=far)  51.4 us
    ppermute x12, starting transfers between devices, shift(): lax.ppermute(x, 'col', [(i, (i + CORES * k) % cols) for i in range(cols)])  44.7 us
    ppermute x12, waiting for transfers between devices, shift(): lax.ppermute(x, 'col', [(i, (i + CORES * k) % cols) for i in range(cols)])  18 us
    all_gather x3, blocking collectives, split_rows(): lax.all_gather(solved, 'col', axis=0, tiled=False, axis_index_groups=pairs)  12.5 us
    ppermute x2, starting transfers between devices, swap(): return lax.ppermute(x, 'col', [(i, i ^ 1) for i in range(cols)])  8.66 us
    pallas_call x3, Pallas kernels, edge_terms(): pl.pallas_call(functools.partial(edge_kernel, level, edges, cols, slots),...  7.5 us
  transfers between devices with their start and end apart: 14, of which 4 were waited for; matrix products, arithmetic and copies ran while one was open for 0% of the time, Pallas kernels for 0%

profile of v5, /device:TPU:1, one launch (start us, length us, event | category | flops | bytes accessed | tf_op | source)
XLA Modules:
  0.0 222.2 jit_solution(5335351122688189343)
XLA Ops:
  0.0 2.8 %shard_map.64.refs_0_ = f32[2,64,128]{2,1,0:T(8,128)} custom-call(s32[1,1,4]{2,1,0:T(1,128)} %bitcast.21, f32[4,1,2,64,128]{4,3,2,1,0:T(8,128)} %right.5, f32[4,1,2,128,128]{4,3,2,1,0:T(8,128)} %inverse.5), custom_call_target="tpu_custom_call" | custom-call | tf_op jit(solution)/shard_map/pallas_call | solution.py:41
  2.8 8.6 %all-gather = f32[4,64,128]{2,1,0:T(8,128)S(1)} all-gather(f32[2,64,128]{2,1,0:T(8,128)} %shard_map.64.refs_0_), channel_id=2, replica_groups={{0,1},{2,3},{4,5},{6,7},{8,9},{10,11},{12,13},{14,15},{16,17},{18,19},{..., dimensions={0}, use_global_device_ids=true | all-gather | bytes 196608 | tf_op jit(solution)/shard_map/all_gather | solution.py:160
  11.4 19.1 %all_gather.29 = f32[4,4,32,128]{3,2,1,0:T(8,128)S(1)} all-gather(f32[1,4,32,128]{3,2,1,0:T(8,128)S(1)} %bitcast.29), channel_id=1, replica_groups={{0,8,16,24},{1,9,17,25},{2,10,18,26},{3,11,19,27},{4,12,20,28},{5,13,21..., dimensions={0}, use_global_device_ids=true | all-gather | bytes 327680 | tf_op jit(solution)/shard_map/all_gather | solution.py:144
  31.2 5.6 %collective-permute-start.1 = (f32[3,1,16,128,128]{4,3,2,1,0:T(8,128)}, f32[3,1,16,128,128]{4,3,2,1,0:T(8,128)S(1)}, u32[]{:S(2)}, u32[]{:S(2)}) collective-permute-start(f32[3,1,16,128,128]{4,3,2,1,0:T(8,128)} %refs_2_.5), channel_id=1, source_target_pairs={{0,1},{1,0},{2,3},{3,2},{4,5},{5,4},{6,7},{7,6},{8,9},{9,8},{10,11... | collective-permute-start | bytes 9437192 | tf_op jit(solution)/shard_map/ppermute | solution.py:135
  36.9 2.9 %collective-permute-start.2 = (f32[4,4,32,128]{3,2,1,0:T(8,128)S(1)}, f32[4,4,32,128]{3,2,1,0:T(8,128)S(1)}, u32[]{:S(2)}, u32[]{:S(2)}) collective-permute-start(f32[4,4,32,128]{3,2,1,0:T(8,128)S(1)} %all_gather.29), channel_id=1, source_target_pairs={{0,2},{1,3},{2,4},{3,5},{4,6},{5,7},{6,8},{7,9},{8,10},{9,11},{10,... | collective-permute-start | bytes 786440 | tf_op jit(solution)/shard_map/ppermute | solution.py:149
  39.7 3.6 %collective-permute-start.5 = (f32[4,4,32,128]{3,2,1,0:T(8,128)S(1)}, f32[4,4,32,128]{3,2,1,0:T(8,128)S(1)}, u32[]{:S(2)}, u32[]{:S(2)}) collective-permute-start(f32[4,4,32,128]{3,2,1,0:T(8,128)S(1)} %all_gather.29), channel_id=1, source_target_pairs={{0,30},{1,31},{2,0},{3,1},{4,2},{5,3},{6,4},{7,5},{8,6},{9,7},{10,... | collective-permute-start | bytes 786440 | tf_op jit(solution)/shard_map/ppermute | solution.py:149
  43.4 2.1 collective-permute-start.3
  45.5 5.3 %collective-permute-start.4 = (f32[2,4,32,128]{3,2,1,0:T(8,128)S(1)}, f32[2,4,32,128]{3,2,1,0:T(8,128)S(1)}, u32[]{:S(2)}, u32[]{:S(2)}) collective-permute-start(f32[2,4,32,128]{3,2,1,0:T(8,128)S(1)} %get-tuple-element.17), channel_id=1, source_target_pairs={{0,28},{1,29},{2,30},{3,31},{4,0},{5,1},{6,2},{7,3},{8,4},{9,5},{1... | collective-permute-start | bytes 393224 | tf_op jit(solution)/shard_map/ppermute | solution.py:149
  50.9 3.0 %collective-permute-start = (s32[6,16]{1,0:T(8,128)S(1)}, s32[6,16]{1,0:T(8,128)S(1)}, u32[]{:S(2)}, u32[]{:S(2)}) collective-permute-start(s32[6,16]{1,0:T(8,128)S(1)} %pad_add_fusion.refs_0_), channel_id=1, source_target_pairs={{0,1},{1,0},{2,3},{3,2},{4,5},{5,4},{6,7},{7,6},{8,9},{9,8},{10,11... | collective-permute-start | bytes 1160 | tf_op jit(solution)/shard_map/ppermute | solution.py:135
  54.4 2.4 %collective-permute-done.4 = f32[2,4,32,128]{3,2,1,0:T(8,128)S(1)} collective-permute-done((f32[2,4,32,128]{3,2,1,0:T(8,128)S(1)}, f32[2,4,32,128]{3,2,1,0:T(8,128)S(1)}, u32[]{:S(2)}, u32[]{:S(2)}) %collective-permute-start.4) | collective-permute-done | bytes 131104 | tf_op jit(solution)/shard_map/ppermute | solution.py:149
  56.9 2.5 %shard_map.65 = f32[64,32,128]{2,1,0:T(8,128)S(1)} custom-call(s32[1]{0:T(128)} %bitcast.column, s32[6,16]{1,0:T(8,128)S(1)} %pad_add_fusion.refs_0_, s32[6,16]{1,0:T(8,128)S(1)} %collective-permute-done.refs_1_, f32[3,1,16,128,128]{4,3,2,1,0:T(8,128)S(1)} %copy-done, f32[3,1,16,128,128]{4,3,2,1,0:T(8,128)S(1)} %collective-permute-done.1.refs_3_, ...), custom_call_target="tpu_custom_call" | custom-call | tf_op jit(solution)/shard_map/pallas_call | solution.py:124
  59.4 24.6 %all_to_all.15.received = f32[64,32,128]{2,1,0:T(8,128)S(1)} all-to-all(f32[64,32,128]{2,1,0:T(8,128)S(1)} %shard_map.65), channel_id=1, replica_groups={{0,1,32,33,64,65,96,97,128,129,160,161,192,193,224,225,256,257,288,289,..., dimensions={0} | all-to-all | bytes 2097152 | tf_op jit(solution)/shard_map/all_to_all | solution.py:194
  84.0 0.8 shard_map.66.refs_1_
  84.8 1.9 all-gather.1
  86.8 15.9 %all_gather.32 = f32[4,4,32,128]{3,2,1,0:T(8,128)S(1)} all-gather(f32[1,4,32,128]{3,2,1,0:T(8,128)S(1)} %bitcast.30), channel_id=1, replica_groups={{0,8,16,24},{1,9,17,25},{2,10,18,26},{3,11,19,27},{4,12,20,28},{5,13,21..., dimensions={0}, use_global_device_ids=true | all-gather | bytes 327680 | tf_op jit(solution)/shard_map/all_gather | solution.py:144
  102.7 1.9 collective-permute-start.6
  104.7 5.1 %collective-permute-start.7 = (f32[2,4,32,128]{3,2,1,0:T(8,128)S(1)}, f32[2,4,32,128]{3,2,1,0:T(8,128)S(1)}, u32[]{:S(2)}, u32[]{:S(2)}) collective-permute-start(f32[2,4,32,128]{3,2,1,0:T(8,128)S(1)} %get-tuple-element.16), channel_id=1, source_target_pairs={{0,4},{1,5},{2,6},{3,7},{4,8},{5,9},{6,10},{7,11},{8,12},{9,13},{1... | collective-permute-start | bytes 393224 | tf_op jit(solution)/shard_map/ppermute | solution.py:149
  109.8 4.6 %collective-permute-start.9 = (f32[4,4,32,128]{3,2,1,0:T(8,128)S(1)}, f32[4,4,32,128]{3,2,1,0:T(8,128)S(1)}, u32[]{:S(2)}, u32[]{:S(2)}) collective-permute-start(f32[4,4,32,128]{3,2,1,0:T(8,128)S(1)} %all_gather.32), channel_id=1, source_target_pairs={{0,30},{1,31},{2,0},{3,1},{4,2},{5,3},{6,4},{7,5},{8,6},{9,7},{10,... | collective-permute-start | bytes 786440 | tf_op jit(solution)/shard_map/ppermute | solution.py:149
  114.4 2.7 %collective-permute-start.8 = (f32[2,4,32,128]{3,2,1,0:T(8,128)S(1)}, f32[2,4,32,128]{3,2,1,0:T(8,128)S(1)}, u32[]{:S(2)}, u32[]{:S(2)}) collective-permute-start(f32[2,4,32,128]{3,2,1,0:T(8,128)S(1)} %get-tuple-element.15), channel_id=1, source_target_pairs={{0,28},{1,29},{2,30},{3,31},{4,0},{5,1},{6,2},{7,3},{8,4},{9,5},{1... | collective-permute-start | bytes 393224 | tf_op jit(solution)/shard_map/ppermute | solution.py:149
  117.2 6.6 %collective-permute-done.8 = f32[2,4,32,128]{3,2,1,0:T(8,128)S(1)} collective-permute-done((f32[2,4,32,128]{3,2,1,0:T(8,128)S(1)}, f32[2,4,32,128]{3,2,1,0:T(8,128)S(1)}, u32[]{:S(2)}, u32[]{:S(2)}) %collective-permute-start.8) | collective-permute-done | bytes 131104 | tf_op jit(solution)/shard_map/ppermute | solution.py:149
  123.9 2.5 %shard_map.67 = f32[64,32,128]{2,1,0:T(8,128)S(1)} custom-call(s32[1]{0:T(128)} %bitcast.column, s32[6,16]{1,0:T(8,128)S(1)} %pad_add_fusion.refs_0_, s32[6,16]{1,0:T(8,128)S(1)} %collective-permute-done.refs_1_, f32[3,1,16,128,128]{4,3,2,1,0:T(8,128)S(1)} %copy-done, f32[3,1,16,128,128]{4,3,2,1,0:T(8,128)S(1)} %collective-permute-done.1.refs_3_, ...), custom_call_target="tpu_custom_call" | custom-call | tf_op jit(solution)/shard_map/pallas_call | solution.py:124
  126.4 25.5 %all_to_all.16.received = f32[64,32,128]{2,1,0:T(8,128)S(1)} all-to-all(f32[64,32,128]{2,1,0:T(8,128)S(1)} %shard_map.67), channel_id=1, replica_groups={{0,1,32,33,64,65,96,97,128,129,160,161,192,193,224,225,256,257,288,289,..., dimensions={0} | all-to-all | bytes 2097152 | tf_op jit(solution)/shard_map/all_to_all | solution.py:194
  152.7 1.9 all-gather.2
  154.7 16.3 %all_gather.35 = f32[4,4,32,128]{3,2,1,0:T(8,128)S(1)} all-gather(f32[1,4,32,128]{3,2,1,0:T(8,128)S(1)} %bitcast.28), channel_id=1, replica_groups={{0,8,16,24},{1,9,17,25},{2,10,18,26},{3,11,19,27},{4,12,20,28},{5,13,21..., dimensions={0}, use_global_device_ids=true | all-gather | bytes 327680 | tf_op jit(solution)/shard_map/all_gather | solution.py:144
  171.0 2.1 collective-permute-start.10
  173.1 7.9 %collective-permute-start.11 = (f32[2,4,32,128]{3,2,1,0:T(8,128)S(1)}, f32[2,4,32,128]{3,2,1,0:T(8,128)S(1)}, u32[]{:S(2)}, u32[]{:S(2)}) collective-permute-start(f32[2,4,32,128]{3,2,1,0:T(8,128)S(1)} %get-tuple-element.14), channel_id=1, source_target_pairs={{0,4},{1,5},{2,6},{3,7},{4,8},{5,9},{6,10},{7,11},{8,12},{9,13},{1... | collective-permute-start | bytes 393224 | tf_op jit(solution)/shard_map/ppermute | solution.py:149
  181.0 4.6 %collective-permute-start.13 = (f32[4,4,32,128]{3,2,1,0:T(8,128)S(1)}, f32[4,4,32,128]{3,2,1,0:T(8,128)S(1)}, u32[]{:S(2)}, u32[]{:S(2)}) collective-permute-start(f32[4,4,32,128]{3,2,1,0:T(8,128)S(1)} %all_gather.35), channel_id=1, source_target_pairs={{0,30},{1,31},{2,0},{3,1},{4,2},{5,3},{6,4},{7,5},{8,6},{9,7},{10,... | collective-permute-start | bytes 786440 | tf_op jit(solution)/shard_map/ppermute | solution.py:149
  185.6 1.9 collective-permute-start.12
  187.6 8.5 %collective-permute-done.12 = f32[2,4,32,128]{3,2,1,0:T(8,128)S(1)} collective-permute-done((f32[2,4,32,128]{3,2,1,0:T(8,128)S(1)}, f32[2,4,32,128]{3,2,1,0:T(8,128)S(1)}, u32[]{:S(2)}, u32[]{:S(2)}) %collective-permute-start.12) | collective-permute-done | bytes 131104 | tf_op jit(solution)/shard_map/ppermute | solution.py:149
  196.2 2.5 %shard_map.69 = f32[64,32,128]{2,1,0:T(8,128)S(1)} custom-call(s32[1]{0:T(128)} %bitcast.column, s32[6,16]{1,0:T(8,128)S(1)} %pad_add_fusion.refs_0_, s32[6,16]{1,0:T(8,128)S(1)} %collective-permute-done.refs_1_, f32[3,1,16,128,128]{4,3,2,1,0:T(8,128)S(1)} %copy-done, f32[3,1,16,128,128]{4,3,2,1,0:T(8,128)S(1)} %collective-permute-done.1.refs_3_, ...), custom_call_target="tpu_custom_call" | custom-call | tf_op jit(solution)/shard_map/pallas_call | solution.py:124
  198.7 21.9 %all_to_all.17.received = f32[64,32,128]{2,1,0:T(8,128)S(1)} all-to-all(f32[64,32,128]{2,1,0:T(8,128)S(1)} %shard_map.69), channel_id=1, replica_groups={{0,1,32,33,64,65,96,97,128,129,160,161,192,193,224,225,256,257,288,289,..., dimensions={0} | all-to-all | bytes 2097152 | tf_op jit(solution)/shard_map/all_to_all | solution.py:194
  220.6 1.5 shard_map.70
  (48 shorter events, 2.3 us)
Async XLA Ops:
  0.0 56.8 %copy-start = (f32[3,1,16,128,128]{4,3,2,1,0:T(8,128)S(1)}, f32[3,1,16,128,128]{4,3,2,1,0:T(8,128)}, u32[]{:S(2)}) copy-start(f32[3,1,16,128,128]{4,3,2,1,0:T(8,128)} %refs_2_.5) | copy-start | bytes 9437188
  31.2 25.6 %collective-permute-start.1 = (f32[3,1,16,128,128]{4,3,2,1,0:T(8,128)}, f32[3,1,16,128,128]{4,3,2,1,0:T(8,128)S(1)}, u32[]{:S(2)}, u32[]{:S(2)}) collective-permute-start(f32[3,1,16,128,128]{4,3,2,1,0:T(8,128)} %refs_2_.5), channel_id=1, source_target_pairs={{0,1},{1,0},{2,3},{3,2},{4,5},{5,4},{6,7},{7,6},{8,9},{9,8},{10,11... | collective-permute-start | bytes 9437192 | tf_op jit(solution)/shard_map/ppermute | solution.py:135
  36.9 14.0 %collective-permute-start.2 = (f32[4,4,32,128]{3,2,1,0:T(8,128)S(1)}, f32[4,4,32,128]{3,2,1,0:T(8,128)S(1)}, u32[]{:S(2)}, u32[]{:S(2)}) collective-permute-start(f32[4,4,32,128]{3,2,1,0:T(8,128)S(1)} %all_gather.29), channel_id=1, source_target_pairs={{0,2},{1,3},{2,4},{3,5},{4,6},{5,7},{6,8},{7,9},{8,10},{9,11},{10,... | collective-permute-start | bytes 786440 | tf_op jit(solution)/shard_map/ppermute | solution.py:149
  39.7 17.0 %collective-permute-start.5 = (f32[4,4,32,128]{3,2,1,0:T(8,128)S(1)}, f32[4,4,32,128]{3,2,1,0:T(8,128)S(1)}, u32[]{:S(2)}, u32[]{:S(2)}) collective-permute-start(f32[4,4,32,128]{3,2,1,0:T(8,128)S(1)} %all_gather.29), channel_id=1, source_target_pairs={{0,30},{1,31},{2,0},{3,1},{4,2},{5,3},{6,4},{7,5},{8,6},{9,7},{10,... | collective-permute-start | bytes 786440 | tf_op jit(solution)/shard_map/ppermute | solution.py:149
  43.4 10.9 %collective-permute-start.3 = (f32[2,4,32,128]{3,2,1,0:T(8,128)S(1)}, f32[2,4,32,128]{3,2,1,0:T(8,128)S(1)}, u32[]{:S(2)}, u32[]{:S(2)}) collective-permute-start(f32[2,4,32,128]{3,2,1,0:T(8,128)S(1)} %get-tuple-element.18), channel_id=1, source_target_pairs={{0,4},{1,5},{2,6},{3,7},{4,8},{5,9},{6,10},{7,11},{8,12},{9,13},{1... | collective-permute-start | bytes 393224 | tf_op jit(solution)/shard_map/ppermute | solution.py:149
  45.5 11.3 %collective-permute-start.4 = (f32[2,4,32,128]{3,2,1,0:T(8,128)S(1)}, f32[2,4,32,128]{3,2,1,0:T(8,128)S(1)}, u32[]{:S(2)}, u32[]{:S(2)}) collective-permute-start(f32[2,4,32,128]{3,2,1,0:T(8,128)S(1)} %get-tuple-element.17), channel_id=1, source_target_pairs={{0,28},{1,29},{2,30},{3,31},{4,0},{5,1},{6,2},{7,3},{8,4},{9,5},{1... | collective-permute-start | bytes 393224 | tf_op jit(solution)/shard_map/ppermute | solution.py:149
  50.9 6.0 %collective-permute-start = (s32[6,16]{1,0:T(8,128)S(1)}, s32[6,16]{1,0:T(8,128)S(1)}, u32[]{:S(2)}, u32[]{:S(2)}) collective-permute-start(s32[6,16]{1,0:T(8,128)S(1)} %pad_add_fusion.refs_0_), channel_id=1, source_target_pairs={{0,1},{1,0},{2,3},{3,2},{4,5},{5,4},{6,7},{7,6},{8,9},{9,8},{10,11... | collective-permute-start | bytes 1160 | tf_op jit(solution)/shard_map/ppermute | solution.py:135
  56.8 27.1 %copy-start.1 = (f32[4,1,2,128,128]{4,3,2,1,0:T(8,128)S(1)}, f32[4,1,2,128,128]{4,3,2,1,0:T(8,128)}, u32[]{:S(2)}) copy-start(f32[4,1,2,128,128]{4,3,2,1,0:T(8,128)} %inverse.5) | copy-start | bytes 1572868
  56.9 27.1 %copy-start.2 = (f32[4,1,2,64,128]{4,3,2,1,0:T(8,128)S(1)}, f32[4,1,2,64,128]{4,3,2,1,0:T(8,128)}, u32[]{:S(2)}) copy-start(f32[4,1,2,64,128]{4,3,2,1,0:T(8,128)} %right.5) | copy-start | bytes 786436
  56.9 27.1 %copy-start.4 = (s32[4,1,1]{0,2,1:T(1,128)S(1)}, s32[4,1,1]{0,2,1:T(1,128)}, u32[]{:S(2)}) copy-start(s32[4,1,1]{0,2,1:T(1,128)} %param.9) | copy-start | bytes 52
  102.7 14.4 %collective-permute-start.6 = (f32[4,4,32,128]{3,2,1,0:T(8,128)S(1)}, f32[4,4,32,128]{3,2,1,0:T(8,128)S(1)}, u32[]{:S(2)}, u32[]{:S(2)}) collective-permute-start(f32[4,4,32,128]{3,2,1,0:T(8,128)S(1)} %all_gather.32), channel_id=1, source_target_pairs={{0,2},{1,3},{2,4},{3,5},{4,6},{5,7},{6,8},{7,9},{8,10},{9,11},{10,... | collective-permute-start | bytes 786440 | tf_op jit(solution)/shard_map/ppermute | solution.py:149
  104.7 12.5 %collective-permute-start.7 = (f32[2,4,32,128]{3,2,1,0:T(8,128)S(1)}, f32[2,4,32,128]{3,2,1,0:T(8,128)S(1)}, u32[]{:S(2)}, u32[]{:S(2)}) collective-permute-start(f32[2,4,32,128]{3,2,1,0:T(8,128)S(1)} %get-tuple-element.16), channel_id=1, source_target_pairs={{0,4},{1,5},{2,6},{3,7},{4,8},{5,9},{6,10},{7,11},{8,12},{9,13},{1... | collective-permute-start | bytes 393224 | tf_op jit(solution)/shard_map/ppermute | solution.py:149
  109.8 14.0 %collective-permute-start.9 = (f32[4,4,32,128]{3,2,1,0:T(8,128)S(1)}, f32[4,4,32,128]{3,2,1,0:T(8,128)S(1)}, u32[]{:S(2)}, u32[]{:S(2)}) collective-permute-start(f32[4,4,32,128]{3,2,1,0:T(8,128)S(1)} %all_gather.32), channel_id=1, source_target_pairs={{0,30},{1,31},{2,0},{3,1},{4,2},{5,3},{6,4},{7,5},{8,6},{9,7},{10,... | collective-permute-start | bytes 786440 | tf_op jit(solution)/shard_map/ppermute | solution.py:149
  114.4 9.4 %collective-permute-start.8 = (f32[2,4,32,128]{3,2,1,0:T(8,128)S(1)}, f32[2,4,32,128]{3,2,1,0:T(8,128)S(1)}, u32[]{:S(2)}, u32[]{:S(2)}) collective-permute-start(f32[2,4,32,128]{3,2,1,0:T(8,128)S(1)} %get-tuple-element.15), channel_id=1, source_target_pairs={{0,28},{1,29},{2,30},{3,31},{4,0},{5,1},{6,2},{7,3},{8,4},{9,5},{1... | collective-permute-start | bytes 393224 | tf_op jit(solution)/shard_map/ppermute | solution.py:149
  171.0 16.5 %collective-permute-start.10 = (f32[4,4,32,128]{3,2,1,0:T(8,128)S(1)}, f32[4,4,32,128]{3,2,1,0:T(8,128)S(1)}, u32[]{:S(2)}, u32[]{:S(2)}) collective-permute-start(f32[4,4,32,128]{3,2,1,0:T(8,128)S(1)} %all_gather.35), channel_id=1, source_target_pairs={{0,2},{1,3},{2,4},{3,5},{4,6},{5,7},{6,8},{7,9},{8,10},{9,11},{10,... | collective-permute-start | bytes 786440 | tf_op jit(solution)/shard_map/ppermute | solution.py:149
  173.1 14.5 %collective-permute-start.11 = (f32[2,4,32,128]{3,2,1,0:T(8,128)S(1)}, f32[2,4,32,128]{3,2,1,0:T(8,128)S(1)}, u32[]{:S(2)}, u32[]{:S(2)}) collective-permute-start(f32[2,4,32,128]{3,2,1,0:T(8,128)S(1)} %get-tuple-element.14), channel_id=1, source_target_pairs={{0,4},{1,5},{2,6},{3,7},{4,8},{5,9},{6,10},{7,11},{8,12},{9,13},{1... | collective-permute-start | bytes 393224 | tf_op jit(solution)/shard_map/ppermute | solution.py:149
  181.0 15.1 %collective-permute-start.13 = (f32[4,4,32,128]{3,2,1,0:T(8,128)S(1)}, f32[4,4,32,128]{3,2,1,0:T(8,128)S(1)}, u32[]{:S(2)}, u32[]{:S(2)}) collective-permute-start(f32[4,4,32,128]{3,2,1,0:T(8,128)S(1)} %all_gather.35), channel_id=1, source_target_pairs={{0,30},{1,31},{2,0},{3,1},{4,2},{5,3},{6,4},{7,5},{8,6},{9,7},{10,... | collective-permute-start | bytes 786440 | tf_op jit(solution)/shard_map/ppermute | solution.py:149
  185.6 10.5 %collective-permute-start.12 = (f32[2,4,32,128]{3,2,1,0:T(8,128)S(1)}, f32[2,4,32,128]{3,2,1,0:T(8,128)S(1)}, u32[]{:S(2)}, u32[]{:S(2)}) collective-permute-start(f32[2,4,32,128]{3,2,1,0:T(8,128)S(1)} %get-tuple-element.13), channel_id=1, source_target_pairs={{0,28},{1,29},{2,30},{3,31},{4,0},{5,1},{6,2},{7,3},{8,4},{9,5},{1... | collective-permute-start | bytes 393224 | tf_op jit(solution)/shard_map/ppermute | solution.py:149
  196.2 24.4 %copy-start.3 = (f32[2,64,128]{2,1,0:T(8,128)S(1)}, f32[2,64,128]{2,1,0:T(8,128)}, u32[]{:S(2)}) copy-start(f32[2,64,128]{2,1,0:T(8,128)} %shard_map.64.refs_0_) | copy-start | bytes 196612

commit v6 on v5

--- a/solution.py
+++ b/solution.py
@@ -52,12 +52,56 @@
     )(counts, right, inverse)
 
 
-def solve_kernel(level, last, received, counts, right, inverse, *refs):
-    earlier, out = refs[:-1], refs[-1]
-    slots = right.shape[2]
+def half_kernel(level, received, column, info, other_info, right, inverse, packed, out):
+    levels, _, slots, rows = right.shape[:4]
+    half, order = rows // CORES, inverse.shape[3]
     peers = received.shape[0] // (CORES * slots)
-    for index, block in enumerate(earlier):
-        out[index, 0] = block[...]
+    first = pl.multiple_of((column[0] % CORES) * half, half)
+    kept = levels - 2
+    for c in range(CORES):
+        for s in range(slots):
+            index = c * slots + s
+            update = received[index]
+            for peer in range(1, peers):
+                update = update + received[peer * CORES * slots + index]
+            if c == 0:
+                value = right[level, 0, s, pl.ds(first, half), :]
+                weight = inverse[level, 0, s]
+                count = info[2 * (levels - 1) + level, 0]
+            else:
+                place = (level - 1) * slots + s
+                start = pl.multiple_of(place * rows + first, half)
+                value = packed[pl.ds(start, half), :]
+                weight = packed[pl.ds(kept * slots * rows + place * order, order), :]
+                count = other_info[2 * (levels - 1) + level, 0]
+            value = dot(value - update, weight)
+            out[index] = jnp.where(s < count, value, jnp.zeros_like(value))
+
+
+def half_solve(level, received, column, infos, right, inverse, packed):
+    slots, rows, order = right.shape[2:]
+    return pl.pallas_call(
+        functools.partial(half_kernel, level),
+        out_shape=jax.ShapeDtypeStruct((CORES * slots, rows // CORES, order), jnp.float32),
+        in_specs=[VMEM, SMEM, SMEM, SMEM, VMEM, VMEM, VMEM],
+        out_specs=VMEM,
+        compiler_params=PARAMS,
+    )(received, column, *infos, right, inverse, packed)
+
+
+def last_kernel(level, received, column, info, right, inverse, first, *refs):
+    mine, theirs, out = refs[: level - 1], refs[level - 1], refs[level]
+    slots, rows = right.shape[2:4]
+    half = rows // CORES
+    peers = received.shape[0] // (CORES * slots)
+    core = column[0] % CORES
+    near = pl.multiple_of(core * half, half)
+    away = pl.multiple_of((1 - core) * half, half)
+    out[0, 0] = first[...]
+    for index in range(1, level):
+        for s in range(slots):
+            out[index, 0, s, pl.ds(near, half), :] = mine[index - 1][s]
+            out[index, 0, s, pl.ds(away, half), :] = theirs[index - 1, s]
     for s in range(slots):
         pieces = []
         for c in range(CORES):
@@ -67,32 +111,26 @@
             pieces.append(update)
         update = jnp.concatenate(pieces, axis=0)
         value = dot(right[level, 0, s] - update, inverse[level, 0, s])
-        value = jnp.where(s < counts[0, 0, level], value, jnp.zeros_like(value))
-        if last:
-            out[level, 0, s] = value
-        else:
-            out[s] = value
-
-
-def solve(level, received, counts, right, inverse, results):
-    last = level + 1 == right.shape[0]
-    earlier = results if last else []
-    shape = right.shape if last else right.shape[2:]
-    return pl.pallas_call(
-        functools.partial(solve_kernel, level, last),
-        out_shape=jax.ShapeDtypeStruct(shape, jnp.float32),
-        in_specs=[VMEM, SMEM, VMEM, VMEM] + [VMEM] * len(earlier),
+        live = s < info[3 * level, 0]
+        out[level, 0, s] = jnp.where(live, value, jnp.zeros_like(value))
+
+
+def last_solve(received, column, info, right, inverse, first, mine, theirs):
+    return pl.pallas_call(
+        functools.partial(last_kernel, right.shape[0] - 1),
+        out_shape=jax.ShapeDtypeStruct(right.shape, jnp.float32),
+        in_specs=[VMEM, SMEM, SMEM] + [VMEM] * (4 + len(mine)),
         out_specs=VMEM,
         compiler_params=PARAMS,
-    )(received, counts, right, inverse, *earlier)
-
-
-def edge_kernel(level, edges, cols, slots, column, *refs):
+    )(received, column, info, right, inverse, first, *mine, theirs)
+
+
+def edge_kernel(level, last, edges, cols, slots, column, *refs):
     infos, couplings, history = refs[:2], refs[2:4], refs[4 : 4 + level]
     out, products = refs[4 + level :]
     core, chip = column[0] % CORES, column[0] // CORES
     chips = cols // CORES
-    target_row = infos[0].shape[0] // 2
+    target_row = (infos[0].shape[0] - 1) // 3
     for c in range(CORES):
         for e in range(edges):
             p = jnp.maximum(infos[c][level - 1, e], 0)
@@ -109,7 +147,7 @@
             products[c, e] = dot(block, couplings[c][level - 1, 0, e])
     out[...] = jnp.zeros_like(out)
     for c in range(CORES):
-        owner = jnp.where(core == c, 0, 1)
+        owner = jnp.where(core == c, 0, 1) if last else c
         for e in range(edges):
             goal = infos[c][target_row + level - 1, e]
             live = (goal >= 0).astype(jnp.float32)
@@ -118,11 +156,11 @@
             out[goal] = out[goal] + products[c, e] * live
 
 
-def edge_terms(level, column, infos, couplings, history, row_total, cols, slots):
+def edge_terms(level, last, column, infos, couplings, history, row_total, cols, slots):
     edges = couplings[0].shape[2]
     rows, order = history[0].shape[1:]
     return pl.pallas_call(
-        functools.partial(edge_kernel, level, edges, cols, slots),
+        functools.partial(edge_kernel, level, last, edges, cols, slots),
         out_shape=jax.ShapeDtypeStruct((row_total * CORES * slots, rows, order), jnp.float32),
         in_specs=[SMEM] * 3 + [VMEM] * (2 + len(history)),
         out_specs=VMEM,
@@ -175,27 +213,53 @@
         [row * cols + CORES * chip + core for row in range(rows) for core in range(CORES)]
         for chip in range(cols // CORES)
     ]
-    solved = first_solve(counts, right_sides, inverse_blocks)
-    history, results = [], []
+    edges = edge_sources.shape[2]
+    first = first_solve(counts, right_sides, inverse_blocks)
+    solved = split_rows(first, column % CORES, cols)
+    column = column.reshape(1)
+    history, halves = [], []
     for level in range(1, level_total):
-        results.append(solved)
-        mine = gather_far(split_rows(solved, column % CORES, cols), cols)
+        last = level + 1 == level_total
+        mine = gather_far(solved, cols)
         if level == 1:
-            coupling, sources, targets, mine = lax.optimization_barrier(
-                (coupling_blocks, edge_sources[:, 0], edge_targets[:, 0], mine)
+            coupling, right, inverse, sources, targets, live, mine = lax.optimization_barrier((
+                coupling_blocks, right_sides, inverse_blocks, edge_sources, edge_targets,
+                slot_counts, mine,
+            ))
+            couplings = (coupling_blocks, swap(coupling, cols))
+            info = jnp.concatenate([
+                sources[:, 0], targets[:, 0],
+                jnp.broadcast_to(live[:, 0], (level_total, edges)),
+            ])
+            order = right.shape[-1]
+            note = jnp.pad(
+                info.astype(jnp.float32), ((0, -info.shape[0] % 8), (0, order - edges))
             )
-            info = jnp.concatenate([sources, targets])
-            infos = (info, swap(info, cols))
-            couplings = (coupling_blocks, swap(coupling, cols))
+            packed = swap(jnp.concatenate([
+                right[1:-1].reshape(-1, order), inverse[1:-1].reshape(-1, order), note,
+            ]), cols)
+            other = packed[packed.shape[0] - note.shape[0] :].astype(jnp.int32)
+            infos = (info, other[: info.shape[0], :edges])
+        if last:
+            *blocks, mine = lax.optimization_barrier((*[h[slots:] for h in halves], mine))
+            theirs = swap(jnp.stack(blocks), cols)
         history.append(gather_near(mine, cols))
         terms = edge_terms(
-            level, column.reshape(1), infos, couplings, history, rows, cols, slots
+            level, last, column, infos, couplings, history, rows, cols, slots
         )
-        received = lax.all_to_all(
-            terms, ("row", "col"), 0, 0, tiled=True, axis_index_groups=chip_groups
+        if last:
+            terms, theirs = lax.optimization_barrier((terms, theirs))
+            received = lax.all_to_all(
+                terms, ("row", "col"), 0, 0, tiled=True, axis_index_groups=chip_groups
+            )
+            return last_solve(
+                received, column, info, right_sides, inverse_blocks, first, halves, theirs
+            )
+        received = lax.all_to_all(terms, "row", 0, 0, tiled=True)
+        solved = half_solve(
+            level, received, column, infos, right_sides, inverse_blocks, packed
         )
-        solved = solve(level, received, counts, right_sides, inverse_blocks, results)
-    return solved
+        halves.append(solved)
 
 
 def solution(mesh):

time: 223 us -> 220 us (0.987)
  blocking collectives: 136 us -> 104 us
  starting transfers between devices: 53.4 us -> 64.5 us
  waiting for transfers between devices: 18 us -> 27.6 us
  local copies, waits for them, and re-layouts: 1.04 us -> 6.73 us
    all_to_all x3 -> x1, blocking collectives: 72 us -> 21.1 us  [on_device(): lax.all_to_all(terms, ('row', 'col'), 0, 0, tiled=True, axis_index_groups...]
    all_to_all x0 -> x1, blocking collectives: none -> 22.9 us  [on_device(): received = lax.all_to_all(terms, 'row', 0, 0, tiled=True)]
    all_to_all x0 -> x1, waiting for transfers between devices: none -> 13.1 us  [on_device(): received = lax.all_to_all(terms, 'row', 0, 0, tiled=True)]
    ppermute x2 -> x3, starting transfers between devices: 8.66 us -> 20.9 us  [swap(): return lax.ppermute(x, 'col', [(i, i ^ 1) for i in range(cols)])]
    ppermute x12, starting transfers between devices: 44.7 us -> 39.2 us  [shift(): lax.ppermute(x, 'col', [(i, (i + CORES * k) % cols) for i in range(cols)])]
    ppermute x12, waiting for transfers between devices: 18 us -> 13.5 us  [shift(): lax.ppermute(x, 'col', [(i, (i + CORES * k) % cols) for i in range(cols)])]
    all_to_all x0 -> x1, starting transfers between devices: none -> 4.34 us  [on_device(): received = lax.all_to_all(terms, 'row', 0, 0, tiled=True)]
    unnamed x23 -> x41, local copies, waits for them, and re-layouts: 0.91 us -> 4.95 us
  transfers between devices with their start and end apart: 14 -> 16, of which waited for: 4 -> 5; matrix products, arithmetic and copies ran while one was open for 0% -> 1% of each run, Pallas kernels for 0% -> 1%
where the time goes in v6:
time: 220 us; the launch traced here: 219 us
  blocking collectives  104 us (47%)
  starting transfers between devices  64.5 us (29%)
  waiting for transfers between devices  27.6 us (13%)
  Pallas kernels  15.3 us (7%)
  local copies, waits for them, and re-layouts  6.73 us (3%)
    all_gather x3, blocking collectives, gather_far(): lax.all_gather(solved, 'col', axis=0, tiled=False, axis_index_groups=far)  51.6 us
    ppermute x12, starting transfers between devices, shift(): lax.ppermute(x, 'col', [(i, (i + CORES * k) % cols) for i in range(cols)])  39.2 us
    all_to_all x1, blocking collectives, on_device(): received = lax.all_to_all(terms, 'row', 0, 0, tiled=True)  22.9 us
    all_to_all x1, blocking collectives, on_device(): lax.all_to_all(terms, ('row', 'col'), 0, 0, tiled=True, axis_index_groups...  21.1 us
    ppermute x3, starting transfers between devices, swap(): return lax.ppermute(x, 'col', [(i, i ^ 1) for i in range(cols)])  20.9 us
    ppermute x12, waiting for transfers between devices, shift(): lax.ppermute(x, 'col', [(i, (i + CORES * k) % cols) for i in range(cols)])  13.5 us
    all_to_all x1, waiting for transfers between devices, on_device(): received = lax.all_to_all(terms, 'row', 0, 0, tiled=True)  13.1 us
    all_gather x1, blocking collectives, split_rows(): lax.all_gather(solved, 'col', axis=0, tiled=False, axis_index_groups=pairs)  8.64 us
  transfers between devices with their start and end apart: 16, of which 5 were waited for; matrix products, arithmetic and copies ran while one was open for 1% of the time, Pallas kernels for 1%

profile of v6, /device:TPU:1, one launch (start us, length us, event | category | flops | bytes accessed | tf_op | source)
XLA Modules:
  0.0 218.9 jit_solution(12766027330347224399)
XLA Ops:
  0.0 2.8 %shard_map.64.first = f32[2,64,128]{2,1,0:T(8,128)} custom-call(s32[1,1,4]{2,1,0:T(1,128)} %bitcast.41, f32[4,1,2,64,128]{4,3,2,1,0:T(8,128)} %right.5, f32[4,1,2,128,128]{4,3,2,1,0:T(8,128)} %inverse.5), custom_call_target="tpu_custom_call" | custom-call | tf_op jit(solution)/shard_map/pallas_call | solution.py:41
  2.8 8.6 %all-gather = f32[4,64,128]{2,1,0:T(8,128)S(1)} all-gather(f32[2,64,128]{2,1,0:T(8,128)} %shard_map.64.first), channel_id=2, replica_groups={{0,1},{2,3},{4,5},{6,7},{8,9},{10,11},{12,13},{14,15},{16,17},{18,19},{..., dimensions={0}, use_global_device_ids=true | all-gather | bytes 196608 | tf_op jit(solution)/shard_map/all_gather | solution.py:198
  11.5 19.1 %all_gather.23 = f32[4,4,32,128]{3,2,1,0:T(8,128)S(1)} all-gather(f32[1,4,32,128]{3,2,1,0:T(8,128)S(1)} %bitcast.36), channel_id=1, replica_groups={{0,8,16,24},{1,9,17,25},{2,10,18,26},{3,11,19,27},{4,12,20,28},{5,13,21..., dimensions={0}, use_global_device_ids=true | all-gather | bytes 327680 | tf_op jit(solution)/shard_map/all_gather | solution.py:182
  30.6 5.6 %collective-permute-start.1 = (f32[3,1,16,128,128]{4,3,2,1,0:T(8,128)}, f32[3,1,16,128,128]{4,3,2,1,0:T(8,128)S(1)}, u32[]{:S(2)}, u32[]{:S(2)}) collective-permute-start(f32[3,1,16,128,128]{4,3,2,1,0:T(8,128)} %refs_2_.5), channel_id=1, source_target_pairs={{0,1},{1,0},{2,3},{3,2},{4,5},{5,4},{6,7},{7,6},{8,9},{9,8},{10,11... | collective-permute-start | bytes 9437192 | tf_op jit(solution)/shard_map/ppermute | solution.py:173
  36.2 2.9 %collective-permute-start.2 = (f32[4,4,32,128]{3,2,1,0:T(8,128)S(1)}, f32[4,4,32,128]{3,2,1,0:T(8,128)S(1)}, u32[]{:S(2)}, u32[]{:S(2)}) collective-permute-start(f32[4,4,32,128]{3,2,1,0:T(8,128)S(1)} %all_gather.23), channel_id=1, source_target_pairs={{0,2},{1,3},{2,4},{3,5},{4,6},{5,7},{6,8},{7,9},{8,10},{9,11},{10,... | collective-permute-start | bytes 786440 | tf_op jit(solution)/shard_map/ppermute | solution.py:187
  39.1 3.6 %collective-permute-start.5 = (f32[4,4,32,128]{3,2,1,0:T(8,128)S(1)}, f32[4,4,32,128]{3,2,1,0:T(8,128)S(1)}, u32[]{:S(2)}, u32[]{:S(2)}) collective-permute-start(f32[4,4,32,128]{3,2,1,0:T(8,128)S(1)} %all_gather.23), channel_id=1, source_target_pairs={{0,30},{1,31},{2,0},{3,1},{4,2},{5,3},{6,4},{7,5},{8,6},{9,7},{10,... | collective-permute-start | bytes 786440 | tf_op jit(solution)/shard_map/ppermute | solution.py:187
  42.8 2.1 collective-permute-start.3
  44.9 5.3 %collective-permute-start.4 = (f32[2,4,32,128]{3,2,1,0:T(8,128)S(1)}, f32[2,4,32,128]{3,2,1,0:T(8,128)S(1)}, u32[]{:S(2)}, u32[]{:S(2)}) collective-permute-start(f32[2,4,32,128]{3,2,1,0:T(8,128)S(1)} %get-tuple-element.33), channel_id=1, source_target_pairs={{0,28},{1,29},{2,30},{3,31},{4,0},{5,1},{6,2},{7,3},{8,4},{9,5},{1... | collective-permute-start | bytes 393224 | tf_op jit(solution)/shard_map/ppermute | solution.py:187
  52.7 3.0 %collective-permute-start = (f32[784,128]{1,0:T(8,128)S(1)}, f32[784,128]{1,0:T(8,128)S(1)}, u32[]{:S(2)}, u32[]{:S(2)}) collective-permute-start(f32[784,128]{1,0:T(8,128)S(1)} %select_maximum_fusion), channel_id=1, source_target_pairs={{0,1},{1,0},{2,3},{3,2},{4,5},{5,4},{6,7},{7,6},{8,9},{9,8},{10,11... | collective-permute-start | bytes 1204232 | tf_op jit(solution)/shard_map/ppermute | solution.py:173
  57.1 2.6 %shard_map.65 = f32[64,32,128]{2,1,0:T(8,128)S(1)} custom-call(s32[1]{0:T(128)} %bitcast.column, s32[10,16]{1,0:T(8,128)S(1)} %get-tuple-element.36.refs_0_.info, s32[10,16]{1,0:T(8,128)S(1)} %slice_convert_fusion.refs_1_.other_info, f32[3,1,16,128,128]{4,3,2,1,0:T(8,128)S(1)} %copy-done, f32[3,1,16,128,128]{4,3,2,1,0:T(8,128)S(1)} %collective-permute-done.1.refs_3_, ...), custom_call_target="tpu_custom_call" | custom-call | tf_op jit(solution)/shard_map/pallas_call | solution.py:162
  59.8 22.9 %all_to_all.15.received = f32[64,32,128]{2,1,0:T(8,128)S(1)} all-to-all(f32[64,32,128]{2,1,0:T(8,128)S(1)} %shard_map.65), channel_id=1, replica_groups=mesh['row'=16,'col'=32] {'row'}, dimensions={0} | all-to-all | bytes 2097152 | tf_op jit(solution)/shard_map/all_to_all | solution.py:258
  82.7 1.2 shard_map.66.refs_0_
  83.8 16.0 %all-gather.1 = f32[16,32,128]{2,1,0:T(8,128)S(1)} all-gather(f32[4,32,128]{2,1,0:T(8,128)S(1)} %shard_map.66.refs_0_), channel_id=3, replica_groups={{0,8,16,24},{1,9,17,25},{2,10,18,26},{3,11,19,27},{4,12,20,28},{5,13,21..., dimensions={0}, use_global_device_ids=true | all-gather | bytes 327680 | tf_op jit(solution)/shard_map/all_gather | solution.py:182
  99.8 1.9 collective-permute-start.6
  101.7 4.5 %collective-permute-start.7 = (f32[2,4,32,128]{3,2,1,0:T(8,128)S(1)}, f32[2,4,32,128]{3,2,1,0:T(8,128)S(1)}, u32[]{:S(2)}, u32[]{:S(2)}) collective-permute-start(f32[2,4,32,128]{3,2,1,0:T(8,128)S(1)} %bitcast.40), channel_id=1, source_target_pairs={{0,4},{1,5},{2,6},{3,7},{4,8},{5,9},{6,10},{7,11},{8,12},{9,13},{1... | collective-permute-start | bytes 393224 | tf_op jit(solution)/shard_map/ppermute | solution.py:187
  106.3 4.6 %collective-permute-start.9 = (f32[4,4,32,128]{3,2,1,0:T(8,128)S(1)}, f32[4,4,32,128]{3,2,1,0:T(8,128)S(1)}, u32[]{:S(2)}, u32[]{:S(2)}) collective-permute-start(f32[4,4,32,128]{3,2,1,0:T(8,128)S(1)} %bitcast.33), channel_id=1, source_target_pairs={{0,30},{1,31},{2,0},{3,1},{4,2},{5,3},{6,4},{7,5},{8,6},{9,7},{10,... | collective-permute-start | bytes 786440 | tf_op jit(solution)/shard_map/ppermute | solution.py:187
  110.9 1.9 collective-permute-start.8
  112.9 6.8 %collective-permute-done.8 = f32[2,4,32,128]{3,2,1,0:T(8,128)S(1)} collective-permute-done((f32[2,4,32,128]{3,2,1,0:T(8,128)S(1)}, f32[2,4,32,128]{3,2,1,0:T(8,128)S(1)}, u32[]{:S(2)}, u32[]{:S(2)}) %collective-permute-start.8) | collective-permute-done | bytes 131104 | tf_op jit(solution)/shard_map/ppermute | solution.py:187
  119.7 2.6 %shard_map.67 = f32[64,32,128]{2,1,0:T(8,128)S(1)} custom-call(s32[1]{0:T(128)} %bitcast.column, s32[10,16]{1,0:T(8,128)S(1)} %get-tuple-element.36.refs_0_.info, s32[10,16]{1,0:T(8,128)S(1)} %slice_convert_fusion.refs_1_.other_info, f32[3,1,16,128,128]{4,3,2,1,0:T(8,128)S(1)} %copy-done, f32[3,1,16,128,128]{4,3,2,1,0:T(8,128)S(1)} %collective-permute-done.1.refs_3_, ...), custom_call_target="tpu_custom_call" | custom-call | tf_op jit(solution)/shard_map/pallas_call | solution.py:162
  124.3 4.3 %all-to-all-start.1 = ((f32[64,32,128]{2,1,0:T(8,128)}), f32[64,32,128]{2,1,0:T(8,128)}, u32[]{:S(2)}, u32[]{:S(2)}) async-start(f32[64,32,128]{2,1,0:T(8,128)} %copy-done.10), calls=%async_computation.1 | async-start | bytes 2097152 | tf_op jit(solution)/shard_map/all_to_all | solution.py:258
  128.7 13.1 %all-to-all-done.1.received = f32[64,32,128]{2,1,0:T(8,128)} async-done(((f32[64,32,128]{2,1,0:T(8,128)}), f32[64,32,128]{2,1,0:T(8,128)}, u32[]{:S(2)}, u32[]{:S(2)}) %all-to-all-start.1) | async-done | bytes 1048608 | tf_op jit(solution)/shard_map/all_to_all | solution.py:258
  143.9 1.7 shard_map.68.refs_1_
  145.6 16.5 %all-gather.2 = f32[16,32,128]{2,1,0:T(8,128)S(1)} all-gather(f32[4,32,128]{2,1,0:T(8,128)S(1)} %shard_map.68.refs_1_), channel_id=4, replica_groups={{0,8,16,24},{1,9,17,25},{2,10,18,26},{3,11,19,27},{4,12,20,28},{5,13,21..., dimensions={0}, use_global_device_ids=true | all-gather | bytes 327680 | tf_op jit(solution)/shard_map/all_gather | solution.py:182
  162.1 1.9 collective-permute-start.10
  164.1 4.6 %collective-permute-start.13 = (f32[4,4,32,128]{3,2,1,0:T(8,128)S(1)}, f32[4,4,32,128]{3,2,1,0:T(8,128)S(1)}, u32[]{:S(2)}, u32[]{:S(2)}) collective-permute-start(f32[4,4,32,128]{3,2,1,0:T(8,128)S(1)} %bitcast.29), channel_id=1, source_target_pairs={{0,30},{1,31},{2,0},{3,1},{4,2},{5,3},{6,4},{7,5},{8,6},{9,7},{10,... | collective-permute-start | bytes 786440 | tf_op jit(solution)/shard_map/ppermute | solution.py:187
  168.7 1.9 collective-permute-start.11
  170.6 12.3 %collective-permute-start.14 = (f32[2,2,32,128]{3,2,1,0:T(8,128)S(1)}, f32[2,2,32,128]{3,2,1,0:T(8,128)S(1)}, u32[]{:S(2)}, u32[]{:S(2)}) collective-permute-start(f32[2,2,32,128]{3,2,1,0:T(8,128)S(1)} %pad_maximum_fusion), channel_id=1, source_target_pairs={{0,1},{1,0},{2,3},{3,2},{4,5},{5,4},{6,7},{7,6},{8,9},{9,8},{10,11... | collective-permute-start | bytes 196616 | tf_op jit(solution)/shard_map/ppermute | solution.py:173
  182.9 4.0 %collective-permute-start.12 = (f32[2,4,32,128]{3,2,1,0:T(8,128)S(1)}, f32[2,4,32,128]{3,2,1,0:T(8,128)S(1)}, u32[]{:S(2)}, u32[]{:S(2)}) collective-permute-start(f32[2,4,32,128]{3,2,1,0:T(8,128)S(1)} %get-tuple-element.29), channel_id=1, source_target_pairs={{0,28},{1,29},{2,30},{3,31},{4,0},{5,1},{6,2},{7,3},{8,4},{9,5},{1... | collective-permute-start | bytes 393224 | tf_op jit(solution)/shard_map/ppermute | solution.py:187
  187.0 6.4 %collective-permute-done.12 = f32[2,4,32,128]{3,2,1,0:T(8,128)S(1)} collective-permute-done((f32[2,4,32,128]{3,2,1,0:T(8,128)S(1)}, f32[2,4,32,128]{3,2,1,0:T(8,128)S(1)}, u32[]{:S(2)}, u32[]{:S(2)}) %collective-permute-start.12) | collective-permute-done | bytes 131104 | tf_op jit(solution)/shard_map/ppermute | solution.py:187
  193.5 2.6 %shard_map.69 = f32[64,32,128]{2,1,0:T(8,128)S(1)} custom-call(s32[1]{0:T(128)} %bitcast.column, s32[10,16]{1,0:T(8,128)S(1)} %get-tuple-element.36.refs_0_.info, s32[10,16]{1,0:T(8,128)S(1)} %slice_convert_fusion.refs_1_.other_info, f32[3,1,16,128,128]{4,3,2,1,0:T(8,128)S(1)} %copy-done, f32[3,1,16,128,128]{4,3,2,1,0:T(8,128)S(1)} %copy-done.2, ...), custom_call_target="tpu_custom_call" | custom-call | tf_op jit(solution)/shard_map/pallas_call | solution.py:162
  196.2 21.1 %all_to_all.16.received = f32[64,32,128]{2,1,0:T(8,128)S(1)} all-to-all(f32[64,32,128]{2,1,0:T(8,128)S(1)} %shard_map.69), channel_id=1, replica_groups={{0,1,32,33,64,65,96,97,128,129,160,161,192,193,224,225,256,257,288,289,..., dimensions={0} | all-to-all | bytes 2097152 | tf_op jit(solution)/shard_map/all_to_all | solution.py:252
  217.3 1.7 shard_map.70
  (73 shorter events, 8.1 us)
Async XLA Ops:
  0.0 52.6 %slice-start = ((f32[4,1,2,128,128]{4,3,2,1,0:T(8,128)}), f32[2,1,2,128,128]{4,3,2,1,0:T(8,128)S(1)}, s32[]{:S(2)}) async-start(f32[4,1,2,128,128]{4,3,2,1,0:T(8,128)} %inverse.5), calls=%async_computation.3 | async-start | bytes 524288 | tf_op jit(solution)/shard_map/slice | solution.py:239
  0.0 57.1 %copy-start = (f32[3,1,16,128,128]{4,3,2,1,0:T(8,128)S(1)}, f32[3,1,16,128,128]{4,3,2,1,0:T(8,128)}, u32[]{:S(2)}) copy-start(f32[3,1,16,128,128]{4,3,2,1,0:T(8,128)} %refs_2_.5) | copy-start | bytes 9437188
  30.6 26.5 %collective-permute-start.1 = (f32[3,1,16,128,128]{4,3,2,1,0:T(8,128)}, f32[3,1,16,128,128]{4,3,2,1,0:T(8,128)S(1)}, u32[]{:S(2)}, u32[]{:S(2)}) collective-permute-start(f32[3,1,16,128,128]{4,3,2,1,0:T(8,128)} %refs_2_.5), channel_id=1, source_target_pairs={{0,1},{1,0},{2,3},{3,2},{4,5},{5,4},{6,7},{7,6},{8,9},{9,8},{10,11... | collective-permute-start | bytes 9437192 | tf_op jit(solution)/shard_map/ppermute | solution.py:173
  36.2 16.4 %collective-permute-start.2 = (f32[4,4,32,128]{3,2,1,0:T(8,128)S(1)}, f32[4,4,32,128]{3,2,1,0:T(8,128)S(1)}, u32[]{:S(2)}, u32[]{:S(2)}) collective-permute-start(f32[4,4,32,128]{3,2,1,0:T(8,128)S(1)} %all_gather.23), channel_id=1, source_target_pairs={{0,2},{1,3},{2,4},{3,5},{4,6},{5,7},{6,8},{7,9},{8,10},{9,11},{10,... | collective-permute-start | bytes 786440 | tf_op jit(solution)/shard_map/ppermute | solution.py:187
  39.1 17.0 %collective-permute-start.5 = (f32[4,4,32,128]{3,2,1,0:T(8,128)S(1)}, f32[4,4,32,128]{3,2,1,0:T(8,128)S(1)}, u32[]{:S(2)}, u32[]{:S(2)}) collective-permute-start(f32[4,4,32,128]{3,2,1,0:T(8,128)S(1)} %all_gather.23), channel_id=1, source_target_pairs={{0,30},{1,31},{2,0},{3,1},{4,2},{5,3},{6,4},{7,5},{8,6},{9,7},{10,... | collective-permute-start | bytes 786440 | tf_op jit(solution)/shard_map/ppermute | solution.py:187
  42.8 13.0 %collective-permute-start.3 = (f32[2,4,32,128]{3,2,1,0:T(8,128)S(1)}, f32[2,4,32,128]{3,2,1,0:T(8,128)S(1)}, u32[]{:S(2)}, u32[]{:S(2)}) collective-permute-start(f32[2,4,32,128]{3,2,1,0:T(8,128)S(1)} %get-tuple-element.34), channel_id=1, source_target_pairs={{0,4},{1,5},{2,6},{3,7},{4,8},{5,9},{6,10},{7,11},{8,12},{9,13},{1... | collective-permute-start | bytes 393224 | tf_op jit(solution)/shard_map/ppermute | solution.py:187
  44.9 11.3 %collective-permute-start.4 = (f32[2,4,32,128]{3,2,1,0:T(8,128)S(1)}, f32[2,4,32,128]{3,2,1,0:T(8,128)S(1)}, u32[]{:S(2)}, u32[]{:S(2)}) collective-permute-start(f32[2,4,32,128]{3,2,1,0:T(8,128)S(1)} %get-tuple-element.33), channel_id=1, source_target_pairs={{0,28},{1,29},{2,30},{3,31},{4,0},{5,1},{6,2},{7,3},{8,4},{9,5},{1... | collective-permute-start | bytes 393224 | tf_op jit(solution)/shard_map/ppermute | solution.py:187
  52.7 4.4 %collective-permute-start = (f32[784,128]{1,0:T(8,128)S(1)}, f32[784,128]{1,0:T(8,128)S(1)}, u32[]{:S(2)}, u32[]{:S(2)}) collective-permute-start(f32[784,128]{1,0:T(8,128)S(1)} %select_maximum_fusion), channel_id=1, source_target_pairs={{0,1},{1,0},{2,3},{3,2},{4,5},{5,4},{6,7},{7,6},{8,9},{9,8},{10,11... | collective-permute-start | bytes 1204232 | tf_op jit(solution)/shard_map/ppermute | solution.py:173
  56.2 63.5 %copy-start.3 = (f32[16,4,32,128]{3,2,1,0:T(8,128)}, f32[16,4,32,128]{3,2,1,0:T(8,128)S(1)}, u32[]{:S(2)}) copy-start(f32[16,4,32,128]{3,2,1,0:T(8,128)S(1)} %constant_dynamic-update-slice_fusion) | copy-start | bytes 3145732
  57.1 25.6 %copy-start.11 = (f32[784,128]{1,0:T(8,128)}, f32[784,128]{1,0:T(8,128)S(1)}, u32[]{:S(2)}) copy-start(f32[784,128]{1,0:T(8,128)S(1)} %collective-permute-done.packed) | copy-start | bytes 1204228
  57.1 62.6 %copy-start.1 = (f32[3,1,16,128,128]{4,3,2,1,0:T(8,128)}, f32[3,1,16,128,128]{4,3,2,1,0:T(8,128)S(1)}, u32[]{:S(2)}) copy-start(f32[3,1,16,128,128]{4,3,2,1,0:T(8,128)S(1)} %collective-permute-done.1.refs_3_) | copy-start | bytes 9437188
  57.1 25.5 %copy-start.5 = (f32[4,1,2,128,128]{4,3,2,1,0:T(8,128)S(1)}, f32[4,1,2,128,128]{4,3,2,1,0:T(8,128)}, u32[]{:S(2)}) copy-start(f32[4,1,2,128,128]{4,3,2,1,0:T(8,128)} %inverse.5) | copy-start | bytes 1572868
  57.1 25.5 %copy-start.7 = (f32[4,1,2,64,128]{4,3,2,1,0:T(8,128)S(1)}, f32[4,1,2,64,128]{4,3,2,1,0:T(8,128)}, u32[]{:S(2)}) copy-start(f32[4,1,2,64,128]{4,3,2,1,0:T(8,128)} %right.5) | copy-start | bytes 786436
  99.8 13.0 %collective-permute-start.6 = (f32[4,4,32,128]{3,2,1,0:T(8,128)S(1)}, f32[4,4,32,128]{3,2,1,0:T(8,128)S(1)}, u32[]{:S(2)}, u32[]{:S(2)}) collective-permute-start(f32[4,4,32,128]{3,2,1,0:T(8,128)S(1)} %bitcast.31), channel_id=1, source_target_pairs={{0,2},{1,3},{2,4},{3,5},{4,6},{5,7},{6,8},{7,9},{8,10},{9,11},{10,... | collective-permute-start | bytes 786440 | tf_op jit(solution)/shard_map/ppermute | solution.py:187
  101.7 11.1 %collective-permute-start.7 = (f32[2,4,32,128]{3,2,1,0:T(8,128)S(1)}, f32[2,4,32,128]{3,2,1,0:T(8,128)S(1)}, u32[]{:S(2)}, u32[]{:S(2)}) collective-permute-start(f32[2,4,32,128]{3,2,1,0:T(8,128)S(1)} %bitcast.40), channel_id=1, source_target_pairs={{0,4},{1,5},{2,6},{3,7},{4,8},{5,9},{6,10},{7,11},{8,12},{9,13},{1... | collective-permute-start | bytes 393224 | tf_op jit(solution)/shard_map/ppermute | solution.py:187
  106.3 13.4 %collective-permute-start.9 = (f32[4,4,32,128]{3,2,1,0:T(8,128)S(1)}, f32[4,4,32,128]{3,2,1,0:T(8,128)S(1)}, u32[]{:S(2)}, u32[]{:S(2)}) collective-permute-start(f32[4,4,32,128]{3,2,1,0:T(8,128)S(1)} %bitcast.33), channel_id=1, source_target_pairs={{0,30},{1,31},{2,0},{3,1},{4,2},{5,3},{6,4},{7,5},{8,6},{9,7},{10,... | collective-permute-start | bytes 786440 | tf_op jit(solution)/shard_map/ppermute | solution.py:187
  110.9 8.8 %collective-permute-start.8 = (f32[2,4,32,128]{3,2,1,0:T(8,128)S(1)}, f32[2,4,32,128]{3,2,1,0:T(8,128)S(1)}, u32[]{:S(2)}, u32[]{:S(2)}) collective-permute-start(f32[2,4,32,128]{3,2,1,0:T(8,128)S(1)} %bitcast.39), channel_id=1, source_target_pairs={{0,28},{1,29},{2,30},{3,31},{4,0},{5,1},{6,2},{7,3},{8,4},{9,5},{1... | collective-permute-start | bytes 393224 | tf_op jit(solution)/shard_map/ppermute | solution.py:187
  122.3 1.0 copy-start.8
  123.4 1.0 copy-start.10
  124.3 17.5 %all-to-all-start.1 = ((f32[64,32,128]{2,1,0:T(8,128)}), f32[64,32,128]{2,1,0:T(8,128)}, u32[]{:S(2)}, u32[]{:S(2)}) async-start(f32[64,32,128]{2,1,0:T(8,128)} %copy-done.10), calls=%async_computation.1 | async-start | bytes 2097152 | tf_op jit(solution)/shard_map/all_to_all | solution.py:258
  141.8 1.0 copy-start.6
  142.8 1.0 copy-start.12
  143.8 49.6 %copy-start.2 = (f32[3,1,16,128,128]{4,3,2,1,0:T(8,128)S(1)}, f32[3,1,16,128,128]{4,3,2,1,0:T(8,128)}, u32[]{:S(2)}) copy-start(f32[3,1,16,128,128]{4,3,2,1,0:T(8,128)} %copy-done.1) | copy-start | bytes 9437188
  143.8 49.6 %copy-start.4 = (f32[16,4,32,128]{3,2,1,0:T(8,128)S(1)}, f32[16,4,32,128]{3,2,1,0:T(8,128)}, u32[]{:S(2)}) copy-start(f32[16,4,32,128]{3,2,1,0:T(8,128)} %copy-done.3) | copy-start | bytes 3145732
  143.9 49.7 %copy-start.9 = (f32[16,4,32,128]{3,2,1,0:T(8,128)S(1)}, f32[16,4,32,128]{3,2,1,0:T(8,128)}, u32[]{:S(2)}) copy-start(f32[16,4,32,128]{3,2,1,0:T(8,128)} %copy-done.8) | copy-start | bytes 3145732
  162.1 24.8 %collective-permute-start.10 = (f32[4,4,32,128]{3,2,1,0:T(8,128)S(1)}, f32[4,4,32,128]{3,2,1,0:T(8,128)S(1)}, u32[]{:S(2)}, u32[]{:S(2)}) collective-permute-start(f32[4,4,32,128]{3,2,1,0:T(8,128)S(1)} %bitcast.27), channel_id=1, source_target_pairs={{0,2},{1,3},{2,4},{3,5},{4,6},{5,7},{6,8},{7,9},{8,10},{9,11},{10,... | collective-permute-start | bytes 786440 | tf_op jit(solution)/shard_map/ppermute | solution.py:187
  164.1 29.4 %collective-permute-start.13 = (f32[4,4,32,128]{3,2,1,0:T(8,128)S(1)}, f32[4,4,32,128]{3,2,1,0:T(8,128)S(1)}, u32[]{:S(2)}, u32[]{:S(2)}) collective-permute-start(f32[4,4,32,128]{3,2,1,0:T(8,128)S(1)} %bitcast.29), channel_id=1, source_target_pairs={{0,30},{1,31},{2,0},{3,1},{4,2},{5,3},{6,4},{7,5},{8,6},{9,7},{10,... | collective-permute-start | bytes 786440 | tf_op jit(solution)/shard_map/ppermute | solution.py:187
  168.7 18.3 %collective-permute-start.11 = (f32[2,4,32,128]{3,2,1,0:T(8,128)S(1)}, f32[2,4,32,128]{3,2,1,0:T(8,128)S(1)}, u32[]{:S(2)}, u32[]{:S(2)}) collective-permute-start(f32[2,4,32,128]{3,2,1,0:T(8,128)S(1)} %get-tuple-element.30), channel_id=1, source_target_pairs={{0,4},{1,5},{2,6},{3,7},{4,8},{5,9},{6,10},{7,11},{8,12},{9,13},{1... | collective-permute-start | bytes 393224 | tf_op jit(solution)/shard_map/ppermute | solution.py:187
  170.6 25.5 %collective-permute-start.14 = (f32[2,2,32,128]{3,2,1,0:T(8,128)S(1)}, f32[2,2,32,128]{3,2,1,0:T(8,128)S(1)}, u32[]{:S(2)}, u32[]{:S(2)}) collective-permute-start(f32[2,2,32,128]{3,2,1,0:T(8,128)S(1)} %pad_maximum_fusion), channel_id=1, source_target_pairs={{0,1},{1,0},{2,3},{3,2},{4,5},{5,4},{6,7},{7,6},{8,9},{9,8},{10,11... | collective-permute-start | bytes 196616 | tf_op jit(solution)/shard_map/ppermute | solution.py:173
  182.9 10.5 %collective-permute-start.12 = (f32[2,4,32,128]{3,2,1,0:T(8,128)S(1)}, f32[2,4,32,128]{3,2,1,0:T(8,128)S(1)}, u32[]{:S(2)}, u32[]{:S(2)}) collective-permute-start(f32[2,4,32,128]{3,2,1,0:T(8,128)S(1)} %get-tuple-element.29), channel_id=1, source_target_pairs={{0,28},{1,29},{2,30},{3,31},{4,0},{5,1},{6,2},{7,3},{8,4},{9,5},{1... | collective-permute-start | bytes 393224 | tf_op jit(solution)/shard_map/ppermute | solution.py:187
  193.5 23.7 %copy-start.13 = (f32[2,64,128]{2,1,0:T(8,128)S(1)}, f32[2,64,128]{2,1,0:T(8,128)}, u32[]{:S(2)}) copy-start(f32[2,64,128]{2,1,0:T(8,128)} %shard_map.64.first) | copy-start | bytes 196612

commit v7 on v6

--- a/solution.py
+++ b/solution.py
@@ -11,7 +11,7 @@
 ANY = pl.BlockSpec(memory_space=pl.ANY)
 VMEM = pl.BlockSpec(memory_space=pltpu.VMEM)
 SMEM = pl.BlockSpec(memory_space=pltpu.SMEM)
-PARAMS = pltpu.CompilerParams(vmem_limit_bytes=32 * 1024 * 1024)
+PARAMS = pltpu.CompilerParams(vmem_limit_bytes=16 * 1024 * 1024)
 CORES = 2
 STRIDE = 4
 
@@ -183,13 +183,13 @@
 
 
 def gather_near(mine, cols):
-    def shift(x, k):
-        return lax.ppermute(x, "col", [(i, (i + CORES * k) % cols) for i in range(cols)])
-
-    half = mine.shape[0] // 2
-    below, above = shift(mine, 1), shift(mine, -1)
-    low, high = shift(mine[:half], 2), shift(mine[half:], -2)
-    same = jnp.concatenate([mine, below, low, high, above])
+    def shift(x, even, odd):
+        step = (CORES * even, CORES * odd)
+        return lax.ppermute(x, "col", [(i, (i + step[i % CORES]) % cols) for i in range(cols)])
+
+    two = shift(mine, 2, -2)
+    below, above = shift(mine, 1, 1), shift(mine, -1, -1)
+    same = jnp.concatenate([mine, below, two, above])
     return same.reshape((-1,) + same.shape[2:])
 
 
@@ -240,15 +240,14 @@
             ]), cols)
             other = packed[packed.shape[0] - note.shape[0] :].astype(jnp.int32)
             infos = (info, other[: info.shape[0], :edges])
-        if last:
-            *blocks, mine = lax.optimization_barrier((*[h[slots:] for h in halves], mine))
-            theirs = swap(jnp.stack(blocks), cols)
         history.append(gather_near(mine, cols))
         terms = edge_terms(
             level, last, column, infos, couplings, history, rows, cols, slots
         )
         if last:
-            terms, theirs = lax.optimization_barrier((terms, theirs))
+            blocks = jnp.stack([h[slots:] for h in halves])
+            terms, blocks = lax.optimization_barrier((terms, blocks))
+            terms, theirs = lax.optimization_barrier((terms, swap(blocks, cols)))
             received = lax.all_to_all(
                 terms, ("row", "col"), 0, 0, tiled=True, axis_index_groups=chip_groups
             )

time: 220 us -> 228 us (1.036)
  waiting for transfers between devices: 27.6 us -> 47.9 us
  starting transfers between devices: 64.5 us -> 47.9 us
  blocking collectives: 104 us -> 107 us
    ppermute x12 -> x9, waiting for transfers between devices: 13.5 us -> 28.4 us  [shift(): lax.ppermute(x, 'col', [(i, (i + step[i % CORES]) % cols) for i in range(...]
    ppermute x12 -> x9, starting transfers between devices: 39.2 us -> 26.6 us  [shift(): lax.ppermute(x, 'col', [(i, (i + step[i % CORES]) % cols) for i in range(...]
    all_to_all x1, waiting for transfers between devices: 13.1 us -> 18.6 us  [on_device(): received = lax.all_to_all(terms, 'row', 0, 0, tiled=True)]
    ppermute x3, starting transfers between devices: 20.9 us -> 16.9 us  [swap(): return lax.ppermute(x, 'col', [(i, i ^ 1) for i in range(cols)])]
    unnamed x41 -> x31, local copies, waits for them, and re-layouts: 4.95 us -> 5.97 us
  transfers between devices with their start and end apart: 16 -> 13, of which waited for: 5 -> 9; matrix products, arithmetic and copies ran while one was open for 1% -> 2% of each run, Pallas kernels for 1% -> 0%
where the time goes in v7:
time: 228 us
  blocking collectives  107 us (47%)
  starting transfers between devices  47.9 us (21%)
  waiting for transfers between devices  47.9 us (21%)
  Pallas kernels  15.2 us (7%)
  local copies, waits for them, and re-layouts  8.61 us (4%)
    all_gather x3, blocking collectives, gather_far(): lax.all_gather(solved, 'col', axis=0, tiled=False, axis_index_groups=far)  53.6 us
    ppermute x9, waiting for transfers between devices, shift(): lax.ppermute(x, 'col', [(i, (i + step[i % CORES]) % cols) for i in range(...  28.4 us
    ppermute x9, starting transfers between devices, shift(): lax.ppermute(x, 'col', [(i, (i + step[i % CORES]) % cols) for i in range(...  26.6 us
    all_to_all x1, blocking collectives, on_device(): received = lax.all_to_all(terms, 'row', 0, 0, tiled=True)  24.8 us
    all_to_all x1, blocking collectives, on_device(): lax.all_to_all(terms, ('row', 'col'), 0, 0, tiled=True, axis_index_groups...  20.3 us
    all_to_all x1, waiting for transfers between devices, on_device(): received = lax.all_to_all(terms, 'row', 0, 0, tiled=True)  18.6 us
    ppermute x3, starting transfers between devices, swap(): return lax.ppermute(x, 'col', [(i, i ^ 1) for i in range(cols)])  16.9 us
    all_gather x1, blocking collectives, split_rows(): lax.all_gather(solved, 'col', axis=0, tiled=False, axis_index_groups=pairs)  8.64 us
  transfers between devices with their start and end apart: 13, of which 9 were waited for; matrix products, arithmetic and copies ran while one was open for 2% of the time, Pallas kernels for 0%

profile of v7, /device:TPU:1, one launch (start us, length us, event | category | flops | bytes accessed | tf_op | source)
XLA Modules:
  0.0 227.7 jit_solution(8222234162705461219)
XLA Ops:
  0.0 2.8 %shard_map.64.first = f32[2,64,128]{2,1,0:T(8,128)} custom-call(s32[1,1,4]{2,1,0:T(1,128)} %bitcast.38, f32[4,1,2,64,128]{4,3,2,1,0:T(8,128)} %right.5, f32[4,1,2,128,128]{4,3,2,1,0:T(8,128)} %inverse.5), custom_call_target="tpu_custom_call" | custom-call | tf_op jit(solution)/shard_map/pallas_call | solution.py:41
  2.8 8.6 %all-gather = f32[4,64,128]{2,1,0:T(8,128)S(1)} all-gather(f32[2,64,128]{2,1,0:T(8,128)} %shard_map.64.first), channel_id=2, replica_groups={{0,1},{2,3},{4,5},{6,7},{8,9},{10,11},{12,13},{14,15},{16,17},{18,19},{..., dimensions={0}, use_global_device_ids=true | all-gather | bytes 196608 | tf_op jit(solution)/shard_map/all_gather | solution.py:198
  11.4 19.1 %all_gather.23 = f32[4,4,32,128]{3,2,1,0:T(8,128)S(1)} all-gather(f32[1,4,32,128]{3,2,1,0:T(8,128)S(1)} %bitcast.37), channel_id=1, replica_groups={{0,8,16,24},{1,9,17,25},{2,10,18,26},{3,11,19,27},{4,12,20,28},{5,13,21..., dimensions={0}, use_global_device_ids=true | all-gather | bytes 327680 | tf_op jit(solution)/shard_map/all_gather | solution.py:182
  30.5 5.6 %collective-permute-start.1 = (f32[3,1,16,128,128]{4,3,2,1,0:T(8,128)}, f32[3,1,16,128,128]{4,3,2,1,0:T(8,128)S(1)}, u32[]{:S(2)}, u32[]{:S(2)}) collective-permute-start(f32[3,1,16,128,128]{4,3,2,1,0:T(8,128)} %refs_2_.5), channel_id=1, source_target_pairs={{0,1},{1,0},{2,3},{3,2},{4,5},{5,4},{6,7},{7,6},{8,9},{9,8},{10,11... | collective-permute-start | bytes 9437192 | tf_op jit(solution)/shard_map/ppermute | solution.py:173
  39.6 1.9 collective-permute-start
  41.5 2.9 %collective-permute-start.2 = (f32[4,4,32,128]{3,2,1,0:T(8,128)S(1)}, f32[4,4,32,128]{3,2,1,0:T(8,128)S(1)}, u32[]{:S(2)}, u32[]{:S(2)}) collective-permute-start(f32[4,4,32,128]{3,2,1,0:T(8,128)S(1)} %all_gather.23), channel_id=1, source_target_pairs={{0,2},{1,3},{2,4},{3,5},{4,6},{5,7},{6,8},{7,9},{8,10},{9,11},{10,... | collective-permute-start | bytes 786440 | tf_op jit(solution)/shard_map/ppermute | solution.py:188
  44.4 3.4 %collective-permute-start.3 = (f32[4,4,32,128]{3,2,1,0:T(8,128)S(1)}, f32[4,4,32,128]{3,2,1,0:T(8,128)S(1)}, u32[]{:S(2)}, u32[]{:S(2)}) collective-permute-start(f32[4,4,32,128]{3,2,1,0:T(8,128)S(1)} %all_gather.23), channel_id=1, source_target_pairs={{0,4},{1,29},{2,6},{3,31},{4,8},{5,1},{6,10},{7,3},{8,12},{9,5},{1... | collective-permute-start | bytes 786440 | tf_op jit(solution)/shard_map/ppermute | solution.py:188
  47.9 2.1 collective-permute-start.4
  50.0 2.0 collective-permute-done.2
  52.0 4.2 %collective-permute-done.3 = f32[4,4,32,128]{3,2,1,0:T(8,128)S(1)} collective-permute-done((f32[4,4,32,128]{3,2,1,0:T(8,128)S(1)}, f32[4,4,32,128]{3,2,1,0:T(8,128)S(1)}, u32[]{:S(2)}, u32[]{:S(2)}) %collective-permute-start.3) | collective-permute-done | bytes 262176 | tf_op jit(solution)/shard_map/ppermute | solution.py:188
  56.2 4.7 %collective-permute-done.4 = f32[4,4,32,128]{3,2,1,0:T(8,128)S(1)} collective-permute-done((f32[4,4,32,128]{3,2,1,0:T(8,128)S(1)}, f32[4,4,32,128]{3,2,1,0:T(8,128)S(1)}, u32[]{:S(2)}, u32[]{:S(2)}) %collective-permute-start.4) | collective-permute-done | bytes 262176 | tf_op jit(solution)/shard_map/ppermute | solution.py:188
  61.1 2.6 %shard_map.65 = f32[64,32,128]{2,1,0:T(8,128)S(1)} custom-call(s32[1]{0:T(128)} %bitcast.column, s32[10,16]{1,0:T(8,128)S(1)} %get-tuple-element.28.refs_0_.info, s32[10,16]{1,0:T(8,128)S(1)} %slice_convert_fusion.refs_1_.other_info, f32[3,1,16,128,128]{4,3,2,1,0:T(8,128)S(1)} %copy-done, f32[3,1,16,128,128]{4,3,2,1,0:T(8,128)S(1)} %collective-permute-done.1.refs_3_, ...), custom_call_target="tpu_custom_call" | custom-call | tf_op jit(solution)/shard_map/pallas_call | solution.py:162
  63.7 24.8 %all_to_all.15.received = f32[64,32,128]{2,1,0:T(8,128)S(1)} all-to-all(f32[64,32,128]{2,1,0:T(8,128)S(1)} %shard_map.65), channel_id=1, replica_groups=mesh['row'=16,'col'=32] {'row'}, dimensions={0} | all-to-all | bytes 2097152 | tf_op jit(solution)/shard_map/all_to_all | solution.py:257
  89.7 19.4 %all-gather.1 = f32[16,32,128]{2,1,0:T(8,128)S(1)} all-gather(f32[4,32,128]{2,1,0:T(8,128)S(1)} %shard_map.66.refs_0_), channel_id=3, replica_groups={{0,8,16,24},{1,9,17,25},{2,10,18,26},{3,11,19,27},{4,12,20,28},{5,13,21..., dimensions={0}, use_global_device_ids=true | all-gather | bytes 327680 | tf_op jit(solution)/shard_map/all_gather | solution.py:182
  109.1 1.9 collective-permute-start.5
  111.0 1.9 collective-permute-start.6
  112.9 4.6 %collective-permute-start.7 = (f32[4,4,32,128]{3,2,1,0:T(8,128)S(1)}, f32[4,4,32,128]{3,2,1,0:T(8,128)S(1)}, u32[]{:S(2)}, u32[]{:S(2)}) collective-permute-start(f32[4,4,32,128]{3,2,1,0:T(8,128)S(1)} %bitcast.33), channel_id=1, source_target_pairs={{0,30},{1,31},{2,0},{3,1},{4,2},{5,3},{6,4},{7,5},{8,6},{9,7},{10,... | collective-permute-start | bytes 786440 | tf_op jit(solution)/shard_map/ppermute | solution.py:188
  117.5 3.5 %collective-permute-done.5 = f32[4,4,32,128]{3,2,1,0:T(8,128)S(1)} collective-permute-done((f32[4,4,32,128]{3,2,1,0:T(8,128)S(1)}, f32[4,4,32,128]{3,2,1,0:T(8,128)S(1)}, u32[]{:S(2)}, u32[]{:S(2)}) %collective-permute-start.5) | collective-permute-done | bytes 262176 | tf_op jit(solution)/shard_map/ppermute | solution.py:188
  121.0 6.5 %collective-permute-done.7 = f32[4,4,32,128]{3,2,1,0:T(8,128)S(1)} collective-permute-done((f32[4,4,32,128]{3,2,1,0:T(8,128)S(1)}, f32[4,4,32,128]{3,2,1,0:T(8,128)S(1)}, u32[]{:S(2)}, u32[]{:S(2)}) %collective-permute-start.7) | collective-permute-done | bytes 262176 | tf_op jit(solution)/shard_map/ppermute | solution.py:188
  127.6 2.6 %shard_map.67 = f32[64,32,128]{2,1,0:T(8,128)S(1)} custom-call(s32[1]{0:T(128)} %bitcast.column, s32[10,16]{1,0:T(8,128)S(1)} %get-tuple-element.28.refs_0_.info, s32[10,16]{1,0:T(8,128)S(1)} %slice_convert_fusion.refs_1_.other_info, f32[3,1,16,128,128]{4,3,2,1,0:T(8,128)S(1)} %copy-done, f32[3,1,16,128,128]{4,3,2,1,0:T(8,128)S(1)} %collective-permute-done.1.refs_3_, ...), custom_call_target="tpu_custom_call" | custom-call | tf_op jit(solution)/shard_map/pallas_call | solution.py:162
  132.2 4.4 %all-to-all-start.1 = ((f32[64,32,128]{2,1,0:T(8,128)}), f32[64,32,128]{2,1,0:T(8,128)}, u32[]{:S(2)}, u32[]{:S(2)}) async-start(f32[64,32,128]{2,1,0:T(8,128)} %copy-done.11), calls=%async_computation.1 | async-start | bytes 2097152 | tf_op jit(solution)/shard_map/all_to_all | solution.py:257
  136.6 18.6 %all-to-all-done.1.received = f32[64,32,128]{2,1,0:T(8,128)} async-done(((f32[64,32,128]{2,1,0:T(8,128)}), f32[64,32,128]{2,1,0:T(8,128)}, u32[]{:S(2)}, u32[]{:S(2)}) %all-to-all-start.1) | async-done | bytes 1048608 | tf_op jit(solution)/shard_map/all_to_all | solution.py:257
  157.2 1.7 shard_map.68.refs_1_
  159.0 15.1 %all-gather.2 = f32[16,32,128]{2,1,0:T(8,128)S(1)} all-gather(f32[4,32,128]{2,1,0:T(8,128)S(1)} %shard_map.68.refs_1_), channel_id=4, replica_groups={{0,8,16,24},{1,9,17,25},{2,10,18,26},{3,11,19,27},{4,12,20,28},{5,13,21..., dimensions={0}, use_global_device_ids=true | all-gather | bytes 327680 | tf_op jit(solution)/shard_map/all_gather | solution.py:182
  174.1 1.9 collective-permute-start.10
  176.0 3.4 %collective-permute-start.8 = (f32[4,4,32,128]{3,2,1,0:T(8,128)S(1)}, f32[4,4,32,128]{3,2,1,0:T(8,128)S(1)}, u32[]{:S(2)}, u32[]{:S(2)}) collective-permute-start(f32[4,4,32,128]{3,2,1,0:T(8,128)S(1)} %bitcast.28), channel_id=1, source_target_pairs={{0,2},{1,3},{2,4},{3,5},{4,6},{5,7},{6,8},{7,9},{8,10},{9,11},{10,... | collective-permute-start | bytes 786440 | tf_op jit(solution)/shard_map/ppermute | solution.py:188
  179.4 4.6 %collective-permute-start.9 = (f32[4,4,32,128]{3,2,1,0:T(8,128)S(1)}, f32[4,4,32,128]{3,2,1,0:T(8,128)S(1)}, u32[]{:S(2)}, u32[]{:S(2)}) collective-permute-start(f32[4,4,32,128]{3,2,1,0:T(8,128)S(1)} %bitcast.29), channel_id=1, source_target_pairs={{0,4},{1,29},{2,6},{3,31},{4,8},{5,1},{6,10},{7,3},{8,12},{9,5},{1... | collective-permute-start | bytes 786440 | tf_op jit(solution)/shard_map/ppermute | solution.py:188
  184.6 6.9 %collective-permute-done.9 = f32[4,4,32,128]{3,2,1,0:T(8,128)S(1)} collective-permute-done((f32[4,4,32,128]{3,2,1,0:T(8,128)S(1)}, f32[4,4,32,128]{3,2,1,0:T(8,128)S(1)}, u32[]{:S(2)}, u32[]{:S(2)}) %collective-permute-start.9) | collective-permute-done | bytes 262176 | tf_op jit(solution)/shard_map/ppermute | solution.py:188
  192.8 2.6 %shard_map.69 = f32[64,32,128]{2,1,0:T(8,128)S(1)} custom-call(s32[1]{0:T(128)} %bitcast.column, s32[10,16]{1,0:T(8,128)S(1)} %get-tuple-element.28.refs_0_.info, s32[10,16]{1,0:T(8,128)S(1)} %slice_convert_fusion.refs_1_.other_info, f32[3,1,16,128,128]{4,3,2,1,0:T(8,128)S(1)} %copy-done, f32[3,1,16,128,128]{4,3,2,1,0:T(8,128)S(1)} %copy-done.2, ...), custom_call_target="tpu_custom_call" | custom-call | tf_op jit(solution)/shard_map/pallas_call | solution.py:162
  195.5 9.4 %collective-permute-start.11 = (f32[2,2,32,128]{3,2,1,0:T(8,128)S(1)}, f32[2,2,32,128]{3,2,1,0:T(8,128)S(1)}, u32[]{:S(2)}, u32[]{:S(2)}) collective-permute-start(f32[2,2,32,128]{3,2,1,0:T(8,128)S(1)} %pad_maximum_fusion.3), channel_id=1, source_target_pairs={{0,1},{1,0},{2,3},{3,2},{4,5},{5,4},{6,7},{7,6},{8,9},{9,8},{10,11... | collective-permute-start | bytes 196616 | tf_op jit(solution)/shard_map/ppermute | solution.py:173
  205.7 20.3 %all_to_all.16.received = f32[64,32,128]{2,1,0:T(8,128)S(1)} all-to-all(f32[64,32,128]{2,1,0:T(8,128)S(1)} %shard_map.69), channel_id=1, replica_groups={{0,1,32,33,64,65,96,97,128,129,160,161,192,193,224,225,256,257,288,289,..., dimensions={0} | all-to-all | bytes 2097152 | tf_op jit(solution)/shard_map/all_to_all | solution.py:251
  226.0 1.7 shard_map.70
  (53 shorter events, 11.6 us)
Async XLA Ops:
  0.0 61.1 %copy-start = (f32[3,1,16,128,128]{4,3,2,1,0:T(8,128)S(1)}, f32[3,1,16,128,128]{4,3,2,1,0:T(8,128)}, u32[]{:S(2)}) copy-start(f32[3,1,16,128,128]{4,3,2,1,0:T(8,128)} %refs_2_.5) | copy-start | bytes 9437188
  30.5 30.5 %collective-permute-start.1 = (f32[3,1,16,128,128]{4,3,2,1,0:T(8,128)}, f32[3,1,16,128,128]{4,3,2,1,0:T(8,128)S(1)}, u32[]{:S(2)}, u32[]{:S(2)}) collective-permute-start(f32[3,1,16,128,128]{4,3,2,1,0:T(8,128)} %refs_2_.5), channel_id=1, source_target_pairs={{0,1},{1,0},{2,3},{3,2},{4,5},{5,4},{6,7},{7,6},{8,9},{9,8},{10,11... | collective-permute-start | bytes 9437192 | tf_op jit(solution)/shard_map/ppermute | solution.py:173
  39.6 21.4 %collective-permute-start = (f32[784,128]{1,0:T(8,128)S(1)}, f32[784,128]{1,0:T(8,128)S(1)}, u32[]{:S(2)}, u32[]{:S(2)}) collective-permute-start(f32[784,128]{1,0:T(8,128)S(1)} %select_maximum_fusion), channel_id=1, source_target_pairs={{0,1},{1,0},{2,3},{3,2},{4,5},{5,4},{6,7},{7,6},{8,9},{9,8},{10,11... | collective-permute-start | bytes 1204232 | tf_op jit(solution)/shard_map/ppermute | solution.py:173
  41.5 10.5 %collective-permute-start.2 = (f32[4,4,32,128]{3,2,1,0:T(8,128)S(1)}, f32[4,4,32,128]{3,2,1,0:T(8,128)S(1)}, u32[]{:S(2)}, u32[]{:S(2)}) collective-permute-start(f32[4,4,32,128]{3,2,1,0:T(8,128)S(1)} %all_gather.23), channel_id=1, source_target_pairs={{0,2},{1,3},{2,4},{3,5},{4,6},{5,7},{6,8},{7,9},{8,10},{9,11},{10,... | collective-permute-start | bytes 786440 | tf_op jit(solution)/shard_map/ppermute | solution.py:188
  44.4 11.8 %collective-permute-start.3 = (f32[4,4,32,128]{3,2,1,0:T(8,128)S(1)}, f32[4,4,32,128]{3,2,1,0:T(8,128)S(1)}, u32[]{:S(2)}, u32[]{:S(2)}) collective-permute-start(f32[4,4,32,128]{3,2,1,0:T(8,128)S(1)} %all_gather.23), channel_id=1, source_target_pairs={{0,4},{1,29},{2,6},{3,31},{4,8},{5,1},{6,10},{7,3},{8,12},{9,5},{1... | collective-permute-start | bytes 786440 | tf_op jit(solution)/shard_map/ppermute | solution.py:188
  47.9 13.0 %collective-permute-start.4 = (f32[4,4,32,128]{3,2,1,0:T(8,128)S(1)}, f32[4,4,32,128]{3,2,1,0:T(8,128)S(1)}, u32[]{:S(2)}, u32[]{:S(2)}) collective-permute-start(f32[4,4,32,128]{3,2,1,0:T(8,128)S(1)} %all_gather.23), channel_id=1, source_target_pairs={{0,30},{1,31},{2,0},{3,1},{4,2},{5,3},{6,4},{7,5},{8,6},{9,7},{10,... | collective-permute-start | bytes 786440 | tf_op jit(solution)/shard_map/ppermute | solution.py:188
  61.0 66.6 %copy-start.3 = (f32[16,4,32,128]{3,2,1,0:T(8,128)}, f32[16,4,32,128]{3,2,1,0:T(8,128)S(1)}, u32[]{:S(2)}) copy-start(f32[16,4,32,128]{3,2,1,0:T(8,128)S(1)} %pad_maximum_fusion) | copy-start | bytes 3145732
  61.0 27.6 %copy-start.12 = (f32[784,128]{1,0:T(8,128)}, f32[784,128]{1,0:T(8,128)S(1)}, u32[]{:S(2)}) copy-start(f32[784,128]{1,0:T(8,128)S(1)} %collective-permute-done.packed) | copy-start | bytes 1204228
  61.1 66.5 %copy-start.1 = (f32[3,1,16,128,128]{4,3,2,1,0:T(8,128)}, f32[3,1,16,128,128]{4,3,2,1,0:T(8,128)S(1)}, u32[]{:S(2)}) copy-start(f32[3,1,16,128,128]{4,3,2,1,0:T(8,128)S(1)} %collective-permute-done.1.refs_3_) | copy-start | bytes 9437188
  61.1 27.5 %copy-start.5 = (f32[4,1,2,128,128]{4,3,2,1,0:T(8,128)S(1)}, f32[4,1,2,128,128]{4,3,2,1,0:T(8,128)}, u32[]{:S(2)}) copy-start(f32[4,1,2,128,128]{4,3,2,1,0:T(8,128)} %inverse.5) | copy-start | bytes 1572868
  61.1 27.5 %copy-start.10 = (f32[4,1,2,64,128]{4,3,2,1,0:T(8,128)S(1)}, f32[4,1,2,64,128]{4,3,2,1,0:T(8,128)}, u32[]{:S(2)}) copy-start(f32[4,1,2,64,128]{4,3,2,1,0:T(8,128)} %right.5) | copy-start | bytes 786436
  109.1 11.9 %collective-permute-start.5 = (f32[4,4,32,128]{3,2,1,0:T(8,128)S(1)}, f32[4,4,32,128]{3,2,1,0:T(8,128)S(1)}, u32[]{:S(2)}, u32[]{:S(2)}) collective-permute-start(f32[4,4,32,128]{3,2,1,0:T(8,128)S(1)} %bitcast.31), channel_id=1, source_target_pairs={{0,2},{1,3},{2,4},{3,5},{4,6},{5,7},{6,8},{7,9},{8,10},{9,11},{10,... | collective-permute-start | bytes 786440 | tf_op jit(solution)/shard_map/ppermute | solution.py:188
  111.0 10.0 %collective-permute-start.6 = (f32[4,4,32,128]{3,2,1,0:T(8,128)S(1)}, f32[4,4,32,128]{3,2,1,0:T(8,128)S(1)}, u32[]{:S(2)}, u32[]{:S(2)}) collective-permute-start(f32[4,4,32,128]{3,2,1,0:T(8,128)S(1)} %bitcast.32), channel_id=1, source_target_pairs={{0,4},{1,29},{2,6},{3,31},{4,8},{5,1},{6,10},{7,3},{8,12},{9,5},{1... | collective-permute-start | bytes 786440 | tf_op jit(solution)/shard_map/ppermute | solution.py:188
  112.9 14.5 %collective-permute-start.7 = (f32[4,4,32,128]{3,2,1,0:T(8,128)S(1)}, f32[4,4,32,128]{3,2,1,0:T(8,128)S(1)}, u32[]{:S(2)}, u32[]{:S(2)}) collective-permute-start(f32[4,4,32,128]{3,2,1,0:T(8,128)S(1)} %bitcast.33), channel_id=1, source_target_pairs={{0,30},{1,31},{2,0},{3,1},{4,2},{5,3},{6,4},{7,5},{8,6},{9,7},{10,... | collective-permute-start | bytes 786440 | tf_op jit(solution)/shard_map/ppermute | solution.py:188
  130.2 1.0 copy-start.8
  131.2 1.0 copy-start.11
  132.2 23.0 %all-to-all-start.1 = ((f32[64,32,128]{2,1,0:T(8,128)}), f32[64,32,128]{2,1,0:T(8,128)}, u32[]{:S(2)}, u32[]{:S(2)}) async-start(f32[64,32,128]{2,1,0:T(8,128)} %copy-done.11), calls=%async_computation.1 | async-start | bytes 2097152 | tf_op jit(solution)/shard_map/all_to_all | solution.py:257
  155.2 1.0 copy-start.6
  156.2 1.0 copy-start.13
  157.2 34.4 %copy-start.2 = (f32[3,1,16,128,128]{4,3,2,1,0:T(8,128)S(1)}, f32[3,1,16,128,128]{4,3,2,1,0:T(8,128)}, u32[]{:S(2)}) copy-start(f32[3,1,16,128,128]{4,3,2,1,0:T(8,128)} %copy-done.1) | copy-start | bytes 9437188
  157.2 34.4 %copy-start.4 = (f32[16,4,32,128]{3,2,1,0:T(8,128)S(1)}, f32[16,4,32,128]{3,2,1,0:T(8,128)}, u32[]{:S(2)}) copy-start(f32[16,4,32,128]{3,2,1,0:T(8,128)} %copy-done.3) | copy-start | bytes 3145732
  174.1 9.9 %collective-permute-start.10 = (f32[4,4,32,128]{3,2,1,0:T(8,128)S(1)}, f32[4,4,32,128]{3,2,1,0:T(8,128)S(1)}, u32[]{:S(2)}, u32[]{:S(2)}) collective-permute-start(f32[4,4,32,128]{3,2,1,0:T(8,128)S(1)} %bitcast.27), channel_id=1, source_target_pairs={{0,30},{1,31},{2,0},{3,1},{4,2},{5,3},{6,4},{7,5},{8,6},{9,7},{10,... | collective-permute-start | bytes 786440 | tf_op jit(solution)/shard_map/ppermute | solution.py:188
  176.0 8.6 %collective-permute-start.8 = (f32[4,4,32,128]{3,2,1,0:T(8,128)S(1)}, f32[4,4,32,128]{3,2,1,0:T(8,128)S(1)}, u32[]{:S(2)}, u32[]{:S(2)}) collective-permute-start(f32[4,4,32,128]{3,2,1,0:T(8,128)S(1)} %bitcast.28), channel_id=1, source_target_pairs={{0,2},{1,3},{2,4},{3,5},{4,6},{5,7},{6,8},{7,9},{8,10},{9,11},{10,... | collective-permute-start | bytes 786440 | tf_op jit(solution)/shard_map/ppermute | solution.py:188
  179.4 12.1 %collective-permute-start.9 = (f32[4,4,32,128]{3,2,1,0:T(8,128)S(1)}, f32[4,4,32,128]{3,2,1,0:T(8,128)S(1)}, u32[]{:S(2)}, u32[]{:S(2)}) collective-permute-start(f32[4,4,32,128]{3,2,1,0:T(8,128)S(1)} %bitcast.29), channel_id=1, source_target_pairs={{0,4},{1,29},{2,6},{3,31},{4,8},{5,1},{6,10},{7,3},{8,12},{9,5},{1... | collective-permute-start | bytes 786440 | tf_op jit(solution)/shard_map/ppermute | solution.py:188
  191.6 1.2 copy-start.9
  192.8 33.2 %copy-start.7 = (f32[4,1,2,128,128]{4,3,2,1,0:T(8,128)S(1)}, f32[4,1,2,128,128]{4,3,2,1,0:T(8,128)}, u32[]{:S(2)}) copy-start(f32[4,1,2,128,128]{4,3,2,1,0:T(8,128)} %inverse.5) | copy-start | bytes 1572868
  192.8 33.2 %copy-start.14 = (f32[2,64,128]{2,1,0:T(8,128)S(1)}, f32[2,64,128]{2,1,0:T(8,128)}, u32[]{:S(2)}) copy-start(f32[2,64,128]{2,1,0:T(8,128)} %shard_map.64.first) | copy-start | bytes 196612
  195.5 10.3 %collective-permute-start.11 = (f32[2,2,32,128]{3,2,1,0:T(8,128)S(1)}, f32[2,2,32,128]{3,2,1,0:T(8,128)S(1)}, u32[]{:S(2)}, u32[]{:S(2)}) collective-permute-start(f32[2,2,32,128]{3,2,1,0:T(8,128)S(1)} %pad_maximum_fusion.3), channel_id=1, source_target_pairs={{0,1},{1,0},{2,3},{3,2},{4,5},{5,4},{6,7},{7,6},{8,9},{9,8},{10,11... | collective-permute-start | bytes 196616 | tf_op jit(solution)/shard_map/ppermute | solution.py:173

commit v8 on v7

--- a/solution.py
+++ b/solution.py
@@ -22,71 +22,96 @@
     )
 
 
-def first_kernel(counts, right_all, inverse_all, out, right, inverse, sem):
+def first_kernel(counts, right_all, inverse_all, sources, targets, out, pack, right, inverse, sem):
+    levels = right_all.shape[0]
+    slots, rows = right.shape[:2]
+    order = inverse.shape[1]
     loads = [
         pltpu.make_async_copy(right_all.at[0, 0], right, sem.at[0]),
         pltpu.make_async_copy(inverse_all.at[0, 0], inverse, sem.at[1]),
     ]
+    for level in range(1, levels - 1):
+        for s in range(slots):
+            place = (level - 1) * slots + s
+            start = (levels - 2) * slots * rows + place * order
+            loads.append(pltpu.make_async_copy(
+                right_all.at[level, 0, s], pack.at[pl.ds(place * rows, rows)],
+                sem.at[2 * place + 2]))
+            loads.append(pltpu.make_async_copy(
+                inverse_all.at[level, 0, s], pack.at[pl.ds(start, order)],
+                sem.at[2 * place + 3]))
     for load in loads:
         load.start()
-    for load in loads:
-        load.wait()
-    for s in range(right.shape[0]):
+    notes = (levels - 2) * slots * (rows + order)
+    edges = sources.shape[2]
+    pack[notes:, :] = jnp.zeros((pack.shape[0] - notes, order), jnp.float32)
+    for level in range(levels - 1):
+        pack[pl.ds(notes + level, 1), pl.ds(0, edges)] = sources[level].astype(jnp.float32)
+        pack[pl.ds(notes + levels - 1 + level, 1), pl.ds(0, edges)] = (
+            targets[level].astype(jnp.float32))
+    for level in range(levels):
+        pack[pl.ds(notes + 2 * (levels - 1) + level, 1), :] = jnp.full(
+            (1, order), counts[0, 0, level].astype(jnp.float32))
+    loads[0].wait()
+    loads[1].wait()
+    for s in range(slots):
         value = dot(right[s], inverse[s])
         out[s] = jnp.where(s < counts[0, 0, 0], value, jnp.zeros_like(value))
-
-
-def first_solve(counts, right, inverse):
-    slots, rows, order = right.shape[2:]
+    for load in loads[2:]:
+        load.wait()
+
+
+def first_solve(counts, right, inverse, sources, targets):
+    levels, _, slots, rows, order = right.shape
+    notes = 3 * levels - 2
+    packed_rows = (levels - 2) * slots * (rows + order) + notes + -notes % 8
     return pl.pallas_call(
         first_kernel,
-        out_shape=jax.ShapeDtypeStruct((slots, rows, order), jnp.float32),
-        in_specs=[SMEM, ANY, ANY],
-        out_specs=VMEM,
+        out_shape=(
+            jax.ShapeDtypeStruct((slots, rows, order), jnp.float32),
+            jax.ShapeDtypeStruct((packed_rows, order), jnp.float32),
+        ),
+        in_specs=[SMEM, ANY, ANY, VMEM, VMEM],
+        out_specs=(VMEM, VMEM),
         scratch_shapes=[
             pltpu.VMEM((slots, rows, order), jnp.float32),
             pltpu.VMEM((slots, order, order), jnp.float32),
-            pltpu.SemaphoreType.DMA((2,)),
+            pltpu.SemaphoreType.DMA((2 + 2 * (levels - 2) * slots,)),
         ],
         compiler_params=pltpu.CompilerParams(vmem_limit_bytes=60 * 1024 * 1024),
-    )(counts, right, inverse)
-
-
-def half_kernel(level, received, column, info, other_info, right, inverse, packed, out):
-    levels, _, slots, rows = right.shape[:4]
-    half, order = rows // CORES, inverse.shape[3]
+    )(counts, right, inverse, sources, targets)
+
+
+def half_kernel(level, levels, slots, received, column, info, other_info, packed, other_packed, out):
+    half, order = received.shape[1:]
+    rows = half * CORES
     peers = received.shape[0] // (CORES * slots)
     first = pl.multiple_of((column[0] % CORES) * half, half)
     kept = levels - 2
-    for c in range(CORES):
+    for c, (notes, data) in enumerate(((info, packed), (other_info, other_packed))):
         for s in range(slots):
             index = c * slots + s
             update = received[index]
             for peer in range(1, peers):
                 update = update + received[peer * CORES * slots + index]
-            if c == 0:
-                value = right[level, 0, s, pl.ds(first, half), :]
-                weight = inverse[level, 0, s]
-                count = info[2 * (levels - 1) + level, 0]
-            else:
-                place = (level - 1) * slots + s
-                start = pl.multiple_of(place * rows + first, half)
-                value = packed[pl.ds(start, half), :]
-                weight = packed[pl.ds(kept * slots * rows + place * order, order), :]
-                count = other_info[2 * (levels - 1) + level, 0]
+            place = (level - 1) * slots + s
+            start = pl.multiple_of(place * rows + first, half)
+            value = data[pl.ds(start, half), :]
+            weight = data[pl.ds(kept * slots * rows + place * order, order), :]
             value = dot(value - update, weight)
-            out[index] = jnp.where(s < count, value, jnp.zeros_like(value))
-
-
-def half_solve(level, received, column, infos, right, inverse, packed):
-    slots, rows, order = right.shape[2:]
-    return pl.pallas_call(
-        functools.partial(half_kernel, level),
-        out_shape=jax.ShapeDtypeStruct((CORES * slots, rows // CORES, order), jnp.float32),
-        in_specs=[VMEM, SMEM, SMEM, SMEM, VMEM, VMEM, VMEM],
+            live = s < notes[2 * (levels - 1) + level, 0]
+            out[index] = jnp.where(live, value, jnp.zeros_like(value))
+
+
+def half_solve(level, levels, slots, received, column, infos, packs):
+    half, order = received.shape[1:]
+    return pl.pallas_call(
+        functools.partial(half_kernel, level, levels, slots),
+        out_shape=jax.ShapeDtypeStruct((CORES * slots, half, order), jnp.float32),
+        in_specs=[VMEM, SMEM, SMEM, SMEM, VMEM, VMEM],
         out_specs=VMEM,
         compiler_params=PARAMS,
-    )(received, column, *infos, right, inverse, packed)
+    )(received, column, *infos, *packs)
 
 
 def last_kernel(level, received, column, info, right, inverse, first, *refs):
@@ -214,7 +239,9 @@
         for chip in range(cols // CORES)
     ]
     edges = edge_sources.shape[2]
-    first = first_solve(counts, right_sides, inverse_blocks)
+    first, pack = first_solve(
+        counts, right_sides, inverse_blocks, edge_sources, edge_targets
+    )
     solved = split_rows(first, column % CORES, cols)
     column = column.reshape(1)
     history, halves = [], []
@@ -222,24 +249,14 @@
         last = level + 1 == level_total
         mine = gather_far(solved, cols)
         if level == 1:
-            coupling, right, inverse, sources, targets, live, mine = lax.optimization_barrier((
-                coupling_blocks, right_sides, inverse_blocks, edge_sources, edge_targets,
-                slot_counts, mine,
-            ))
+            coupling, pack, mine = lax.optimization_barrier((coupling_blocks, pack, mine))
             couplings = (coupling_blocks, swap(coupling, cols))
-            info = jnp.concatenate([
-                sources[:, 0], targets[:, 0],
-                jnp.broadcast_to(live[:, 0], (level_total, edges)),
-            ])
-            order = right.shape[-1]
-            note = jnp.pad(
-                info.astype(jnp.float32), ((0, -info.shape[0] % 8), (0, order - edges))
+            packs = (pack, swap(pack, cols))
+            notes = 3 * level_total - 2
+            start = pack.shape[0] - notes - -notes % 8
+            infos = tuple(
+                block[start : start + notes, :edges].astype(jnp.int32) for block in packs
             )
-            packed = swap(jnp.concatenate([
-                right[1:-1].reshape(-1, order), inverse[1:-1].reshape(-1, order), note,
-            ]), cols)
-            other = packed[packed.shape[0] - note.shape[0] :].astype(jnp.int32)
-            infos = (info, other[: info.shape[0], :edges])
         history.append(gather_near(mine, cols))
         terms = edge_terms(
             level, last, column, infos, couplings, history, rows, cols, slots
@@ -252,11 +269,11 @@
                 terms, ("row", "col"), 0, 0, tiled=True, axis_index_groups=chip_groups
             )
             return last_solve(
-                received, column, info, right_sides, inverse_blocks, first, halves, theirs
+                received, column, infos[0], right_sides, inverse_blocks, first, halves, theirs
             )
         received = lax.all_to_all(terms, "row", 0, 0, tiled=True)
         solved = half_solve(
-            level, received, column, infos, right_sides, inverse_blocks, packed
+            level, level_total, slots, received, column, infos, packs
         )
         halves.append(solved)
 

time: 228 us -> 225 us (0.987)
  waiting for transfers between devices: 47.9 us -> 45.3 us
    unnamed x31 -> x38, local copies, waits for them, and re-layouts: 5.97 us -> 4.96 us
  transfers between devices with their start and end apart: 13 -> 13, of which waited for: 9 -> 10; matrix products, arithmetic and copies ran while one was open for 2% -> 1% of each run, Pallas kernels for 0% -> 0%
where the time goes in v8:
time: 225 us; the launch traced here: 224 us
  blocking collectives  109 us (48%)
  starting transfers between devices  45.9 us (20%)
  waiting for transfers between devices  45.3 us (20%)
  Pallas kernels  15.5 us (7%)
  local copies, waits for them, and re-layouts  6.35 us (3%)
    all_gather x3, blocking collectives, gather_far(): lax.all_gather(solved, 'col', axis=0, tiled=False, axis_index_groups=far)  53.8 us
    ppermute x9, waiting for transfers between devices, shift(): lax.ppermute(x, 'col', [(i, (i + step[i % CORES]) % cols) for i in range(...  27.6 us
    ppermute x9, starting transfers between devices, shift(): lax.ppermute(x, 'col', [(i, (i + step[i % CORES]) % cols) for i in range(...  25.6 us
    all_to_all x1, blocking collectives, on_device(): received = lax.all_to_all(terms, 'row', 0, 0, tiled=True)  24.8 us
    all_to_all x1, blocking collectives, on_device(): lax.all_to_all(terms, ('row', 'col'), 0, 0, tiled=True, axis_index_groups...  22.1 us
    all_to_all x1, waiting for transfers between devices, on_device(): received = lax.all_to_all(terms, 'row', 0, 0, tiled=True)  16.8 us
    ppermute x3, starting transfers between devices, swap(): return lax.ppermute(x, 'col', [(i, i ^ 1) for i in range(cols)])  15.9 us
    all_gather x1, blocking collectives, split_rows(): lax.all_gather(solved, 'col', axis=0, tiled=False, axis_index_groups=pairs)  8.64 us
  transfers between devices with their start and end apart: 13, of which 10 were waited for; matrix products, arithmetic and copies ran while one was open for 1% of the time, Pallas kernels for 0%

profile of v8, /device:TPU:1, one launch (start us, length us, event | category | flops | bytes accessed | tf_op | source)
XLA Modules:
  0.0 224.4 jit_solution(12894499670448917281)
XLA Ops:
  0.0 3.0 %shard_map.64 = (f32[2,64,128]{2,1,0:T(8,128)}, f32[784,128]{1,0:T(8,128)}) custom-call(s32[1,1,4]{2,1,0:T(1,128)} %bitcast.29, f32[4,1,2,64,128]{4,3,2,1,0:T(8,128)} %right.1, f32[4,1,2,128,128]{4,3,2,1,0:T(8,128)} %inverse.1, s32[3,1,16]{2,1,0:T(1,128)} %sources.1, s32[3,1,16]{2,1,0:T(1,128)} %targets.1), custom_call_target="tpu_custom_call" | custom-call | tf_op jit(solution)/shard_map/pallas_call | solution.py:68
  3.0 8.6 %all-gather = f32[4,64,128]{2,1,0:T(8,128)S(1)} all-gather(f32[2,64,128]{2,1,0:T(8,128)} %get-tuple-element.15.first), channel_id=2, replica_groups={{0,1},{2,3},{4,5},{6,7},{8,9},{10,11},{12,13},{14,15},{16,17},{18,19},{..., dimensions={0}, use_global_device_ids=true | all-gather | bytes 196608 | tf_op jit(solution)/shard_map/all_gather | solution.py:223
  11.7 19.1 %all_gather.23 = f32[4,4,32,128]{3,2,1,0:T(8,128)S(1)} all-gather(f32[1,4,32,128]{3,2,1,0:T(8,128)S(1)} %bitcast.28), channel_id=1, replica_groups={{0,8,16,24},{1,9,17,25},{2,10,18,26},{3,11,19,27},{4,12,20,28},{5,13,21..., dimensions={0}, use_global_device_ids=true | all-gather | bytes 327680 | tf_op jit(solution)/shard_map/all_gather | solution.py:207
  30.8 5.6 %collective-permute-start.1 = (f32[3,1,16,128,128]{4,3,2,1,0:T(8,128)}, f32[3,1,16,128,128]{4,3,2,1,0:T(8,128)S(1)}, u32[]{:S(2)}, u32[]{:S(2)}) collective-permute-start(f32[3,1,16,128,128]{4,3,2,1,0:T(8,128)} %refs_2_.5), channel_id=1, source_target_pairs={{0,1},{1,0},{2,3},{3,2},{4,5},{5,4},{6,7},{7,6},{8,9},{9,8},{10,11... | collective-permute-start | bytes 9437192 | tf_op jit(solution)/shard_map/ppermute | solution.py:198
  36.4 1.9 collective-permute-start
  38.3 2.9 %collective-permute-start.2 = (f32[4,4,32,128]{3,2,1,0:T(8,128)S(1)}, f32[4,4,32,128]{3,2,1,0:T(8,128)S(1)}, u32[]{:S(2)}, u32[]{:S(2)}) collective-permute-start(f32[4,4,32,128]{3,2,1,0:T(8,128)S(1)} %all_gather.23), channel_id=1, source_target_pairs={{0,2},{1,3},{2,4},{3,5},{4,6},{5,7},{6,8},{7,9},{8,10},{9,11},{10,... | collective-permute-start | bytes 786440 | tf_op jit(solution)/shard_map/ppermute | solution.py:213
  41.2 3.4 %collective-permute-start.3 = (f32[4,4,32,128]{3,2,1,0:T(8,128)S(1)}, f32[4,4,32,128]{3,2,1,0:T(8,128)S(1)}, u32[]{:S(2)}, u32[]{:S(2)}) collective-permute-start(f32[4,4,32,128]{3,2,1,0:T(8,128)S(1)} %all_gather.23), channel_id=1, source_target_pairs={{0,4},{1,29},{2,6},{3,31},{4,8},{5,1},{6,10},{7,3},{8,12},{9,5},{1... | collective-permute-start | bytes 786440 | tf_op jit(solution)/shard_map/ppermute | solution.py:213
  44.7 2.1 collective-permute-start.4
  48.8 4.2 %collective-permute-done.3 = f32[4,4,32,128]{3,2,1,0:T(8,128)S(1)} collective-permute-done((f32[4,4,32,128]{3,2,1,0:T(8,128)S(1)}, f32[4,4,32,128]{3,2,1,0:T(8,128)S(1)}, u32[]{:S(2)}, u32[]{:S(2)}) %collective-permute-start.3) | collective-permute-done | bytes 262176 | tf_op jit(solution)/shard_map/ppermute | solution.py:213
  53.0 4.7 %collective-permute-done.4 = f32[4,4,32,128]{3,2,1,0:T(8,128)S(1)} collective-permute-done((f32[4,4,32,128]{3,2,1,0:T(8,128)S(1)}, f32[4,4,32,128]{3,2,1,0:T(8,128)S(1)}, u32[]{:S(2)}, u32[]{:S(2)}) %collective-permute-start.4) | collective-permute-done | bytes 262176 | tf_op jit(solution)/shard_map/ppermute | solution.py:213
  57.9 2.6 %shard_map.65 = f32[64,32,128]{2,1,0:T(8,128)S(1)} custom-call(s32[1]{0:T(128)} %bitcast.column, s32[10,16]{1,0:T(8,128)S(1)} %slice_convert_fusion.1.refs_0_.info, s32[10,16]{1,0:T(8,128)S(1)} %slice_convert_fusion.refs_1_.other_info, f32[3,1,16,128,128]{4,3,2,1,0:T(8,128)S(1)} %copy-done, f32[3,1,16,128,128]{4,3,2,1,0:T(8,128)S(1)} %collective-permute-done.1.refs_3_, ...), custom_call_target="tpu_custom_call" | custom-call | tf_op jit(solution)/shard_map/pallas_call | solution.py:187
  60.6 24.8 %all_to_all.15.received = f32[64,32,128]{2,1,0:T(8,128)S(1)} all-to-all(f32[64,32,128]{2,1,0:T(8,128)S(1)} %shard_map.65), channel_id=1, replica_groups=mesh['row'=16,'col'=32] {'row'}, dimensions={0} | all-to-all | bytes 2097152 | tf_op jit(solution)/shard_map/all_to_all | solution.py:274
  86.6 19.4 %all-gather.1 = f32[16,32,128]{2,1,0:T(8,128)S(1)} all-gather(f32[4,32,128]{2,1,0:T(8,128)S(1)} %shard_map.66.refs_0_), channel_id=3, replica_groups={{0,8,16,24},{1,9,17,25},{2,10,18,26},{3,11,19,27},{4,12,20,28},{5,13,21..., dimensions={0}, use_global_device_ids=true | all-gather | bytes 327680 | tf_op jit(solution)/shard_map/all_gather | solution.py:207
  106.0 1.9 collective-permute-start.5
  107.9 1.9 collective-permute-start.6
  109.8 4.6 %collective-permute-start.7 = (f32[4,4,32,128]{3,2,1,0:T(8,128)S(1)}, f32[4,4,32,128]{3,2,1,0:T(8,128)S(1)}, u32[]{:S(2)}, u32[]{:S(2)}) collective-permute-start(f32[4,4,32,128]{3,2,1,0:T(8,128)S(1)} %bitcast.25), channel_id=1, source_target_pairs={{0,30},{1,31},{2,0},{3,1},{4,2},{5,3},{6,4},{7,5},{8,6},{9,7},{10,... | collective-permute-start | bytes 786440 | tf_op jit(solution)/shard_map/ppermute | solution.py:213
  114.4 1.4 collective-permute-done.5
  116.7 7.7 %collective-permute-done.7 = f32[4,4,32,128]{3,2,1,0:T(8,128)S(1)} collective-permute-done((f32[4,4,32,128]{3,2,1,0:T(8,128)S(1)}, f32[4,4,32,128]{3,2,1,0:T(8,128)S(1)}, u32[]{:S(2)}, u32[]{:S(2)}) %collective-permute-start.7) | collective-permute-done | bytes 262176 | tf_op jit(solution)/shard_map/ppermute | solution.py:213
  124.5 2.6 %shard_map.67 = f32[64,32,128]{2,1,0:T(8,128)S(1)} custom-call(s32[1]{0:T(128)} %bitcast.column, s32[10,16]{1,0:T(8,128)S(1)} %slice_convert_fusion.1.refs_0_.info, s32[10,16]{1,0:T(8,128)S(1)} %slice_convert_fusion.refs_1_.other_info, f32[3,1,16,128,128]{4,3,2,1,0:T(8,128)S(1)} %copy-done, f32[3,1,16,128,128]{4,3,2,1,0:T(8,128)S(1)} %collective-permute-done.1.refs_3_, ...), custom_call_target="tpu_custom_call" | custom-call | tf_op jit(solution)/shard_map/pallas_call | solution.py:187
  129.1 4.3 %all-to-all-start.1 = ((f32[64,32,128]{2,1,0:T(8,128)}), f32[64,32,128]{2,1,0:T(8,128)}, u32[]{:S(2)}, u32[]{:S(2)}) async-start(f32[64,32,128]{2,1,0:T(8,128)} %copy-done.7), calls=%async_computation.1 | async-start | bytes 2097152 | tf_op jit(solution)/shard_map/all_to_all | solution.py:274
  133.5 1.4 slice_bitcast_fusion.1
  134.8 16.8 %all-to-all-done.1.received = f32[64,32,128]{2,1,0:T(8,128)} async-done(((f32[64,32,128]{2,1,0:T(8,128)}), f32[64,32,128]{2,1,0:T(8,128)}, u32[]{:S(2)}, u32[]{:S(2)}) %all-to-all-start.1) | async-done | bytes 1048608 | tf_op jit(solution)/shard_map/all_to_all | solution.py:274
  153.3 1.7 shard_map.68.refs_1_
  155.1 15.2 %all-gather.2 = f32[16,32,128]{2,1,0:T(8,128)S(1)} all-gather(f32[4,32,128]{2,1,0:T(8,128)S(1)} %shard_map.68.refs_1_), channel_id=4, replica_groups={{0,8,16,24},{1,9,17,25},{2,10,18,26},{3,11,19,27},{4,12,20,28},{5,13,21..., dimensions={0}, use_global_device_ids=true | all-gather | bytes 327680 | tf_op jit(solution)/shard_map/all_gather | solution.py:207
  170.3 1.9 collective-permute-start.10
  172.2 3.4 %collective-permute-start.8 = (f32[4,4,32,128]{3,2,1,0:T(8,128)S(1)}, f32[4,4,32,128]{3,2,1,0:T(8,128)S(1)}, u32[]{:S(2)}, u32[]{:S(2)}) collective-permute-start(f32[4,4,32,128]{3,2,1,0:T(8,128)S(1)} %bitcast.20), channel_id=1, source_target_pairs={{0,2},{1,3},{2,4},{3,5},{4,6},{5,7},{6,8},{7,9},{8,10},{9,11},{10,... | collective-permute-start | bytes 786440 | tf_op jit(solution)/shard_map/ppermute | solution.py:213
  175.6 3.6 %collective-permute-start.9 = (f32[4,4,32,128]{3,2,1,0:T(8,128)S(1)}, f32[4,4,32,128]{3,2,1,0:T(8,128)S(1)}, u32[]{:S(2)}, u32[]{:S(2)}) collective-permute-start(f32[4,4,32,128]{3,2,1,0:T(8,128)S(1)} %bitcast.21), channel_id=1, source_target_pairs={{0,4},{1,29},{2,6},{3,31},{4,8},{5,1},{6,10},{7,3},{8,12},{9,5},{1... | collective-permute-start | bytes 786440 | tf_op jit(solution)/shard_map/ppermute | solution.py:213
  180.5 6.8 %collective-permute-done.9 = f32[4,4,32,128]{3,2,1,0:T(8,128)S(1)} collective-permute-done((f32[4,4,32,128]{3,2,1,0:T(8,128)S(1)}, f32[4,4,32,128]{3,2,1,0:T(8,128)S(1)}, u32[]{:S(2)}, u32[]{:S(2)}) %collective-permute-start.9) | collective-permute-done | bytes 262176 | tf_op jit(solution)/shard_map/ppermute | solution.py:213
  188.7 2.6 %shard_map.69 = f32[64,32,128]{2,1,0:T(8,128)S(1)} custom-call(s32[1]{0:T(128)} %bitcast.column, s32[10,16]{1,0:T(8,128)S(1)} %slice_convert_fusion.1.refs_0_.info, s32[10,16]{1,0:T(8,128)S(1)} %copy-done.17, f32[3,1,16,128,128]{4,3,2,1,0:T(8,128)S(1)} %copy-done, f32[3,1,16,128,128]{4,3,2,1,0:T(8,128)S(1)} %copy-done.2, f32[64,32,128]{2,1,0:T(8,128)S(1)} %bitcast.15, ...), custom_call_target="tpu_custom_call" | custom-call | tf_op jit(solution)/shard_map/pallas_call | solution.py:187
  191.3 8.4 %collective-permute-start.11 = (f32[2,2,32,128]{3,2,1,0:T(8,128)S(1)}, f32[2,2,32,128]{3,2,1,0:T(8,128)S(1)}, u32[]{:S(2)}, u32[]{:S(2)}) collective-permute-start(f32[2,2,32,128]{3,2,1,0:T(8,128)S(1)} %pad_maximum_fusion.3), channel_id=1, source_target_pairs={{0,1},{1,0},{2,3},{3,2},{4,5},{5,4},{6,7},{7,6},{8,9},{9,8},{10,11... | collective-permute-start | bytes 196616 | tf_op jit(solution)/shard_map/ppermute | solution.py:198
  200.6 22.1 %all_to_all.16.received = f32[64,32,128]{2,1,0:T(8,128)S(1)} all-to-all(f32[64,32,128]{2,1,0:T(8,128)S(1)} %shard_map.69), channel_id=1, replica_groups={{0,1,32,33,64,65,96,97,128,129,160,161,192,193,224,225,256,257,288,289,..., dimensions={0} | all-to-all | bytes 2097152 | tf_op jit(solution)/shard_map/all_to_all | solution.py:268
  222.7 1.7 shard_map.70
  (55 shorter events, 11.5 us)
Async XLA Ops:
  0.0 57.9 %copy-start = (f32[3,1,16,128,128]{4,3,2,1,0:T(8,128)S(1)}, f32[3,1,16,128,128]{4,3,2,1,0:T(8,128)}, u32[]{:S(2)}) copy-start(f32[3,1,16,128,128]{4,3,2,1,0:T(8,128)} %refs_2_.5) | copy-start | bytes 9437188
  30.8 27.1 %collective-permute-start.1 = (f32[3,1,16,128,128]{4,3,2,1,0:T(8,128)}, f32[3,1,16,128,128]{4,3,2,1,0:T(8,128)S(1)}, u32[]{:S(2)}, u32[]{:S(2)}) collective-permute-start(f32[3,1,16,128,128]{4,3,2,1,0:T(8,128)} %refs_2_.5), channel_id=1, source_target_pairs={{0,1},{1,0},{2,3},{3,2},{4,5},{5,4},{6,7},{7,6},{8,9},{9,8},{10,11... | collective-permute-start | bytes 9437192 | tf_op jit(solution)/shard_map/ppermute | solution.py:198
  36.4 21.4 %collective-permute-start = (f32[784,128]{1,0:T(8,128)}, f32[784,128]{1,0:T(8,128)S(1)}, u32[]{:S(2)}, u32[]{:S(2)}) collective-permute-start(f32[784,128]{1,0:T(8,128)} %get-tuple-element.16.packed), channel_id=1, source_target_pairs={{0,1},{1,0},{2,3},{3,2},{4,5},{5,4},{6,7},{7,6},{8,9},{9,8},{10,11... | collective-permute-start | bytes 1204232 | tf_op jit(solution)/shard_map/ppermute | solution.py:198
  38.3 10.5 %collective-permute-start.2 = (f32[4,4,32,128]{3,2,1,0:T(8,128)S(1)}, f32[4,4,32,128]{3,2,1,0:T(8,128)S(1)}, u32[]{:S(2)}, u32[]{:S(2)}) collective-permute-start(f32[4,4,32,128]{3,2,1,0:T(8,128)S(1)} %all_gather.23), channel_id=1, source_target_pairs={{0,2},{1,3},{2,4},{3,5},{4,6},{5,7},{6,8},{7,9},{8,10},{9,11},{10,... | collective-permute-start | bytes 786440 | tf_op jit(solution)/shard_map/ppermute | solution.py:213
  41.2 11.8 %collective-permute-start.3 = (f32[4,4,32,128]{3,2,1,0:T(8,128)S(1)}, f32[4,4,32,128]{3,2,1,0:T(8,128)S(1)}, u32[]{:S(2)}, u32[]{:S(2)}) collective-permute-start(f32[4,4,32,128]{3,2,1,0:T(8,128)S(1)} %all_gather.23), channel_id=1, source_target_pairs={{0,4},{1,29},{2,6},{3,31},{4,8},{5,1},{6,10},{7,3},{8,12},{9,5},{1... | collective-permute-start | bytes 786440 | tf_op jit(solution)/shard_map/ppermute | solution.py:213
  44.7 13.1 %collective-permute-start.4 = (f32[4,4,32,128]{3,2,1,0:T(8,128)S(1)}, f32[4,4,32,128]{3,2,1,0:T(8,128)S(1)}, u32[]{:S(2)}, u32[]{:S(2)}) collective-permute-start(f32[4,4,32,128]{3,2,1,0:T(8,128)S(1)} %all_gather.23), channel_id=1, source_target_pairs={{0,30},{1,31},{2,0},{3,1},{4,2},{5,3},{6,4},{7,5},{8,6},{9,7},{10,... | collective-permute-start | bytes 786440 | tf_op jit(solution)/shard_map/ppermute | solution.py:213
  57.8 66.6 %copy-start.3 = (f32[16,4,32,128]{3,2,1,0:T(8,128)}, f32[16,4,32,128]{3,2,1,0:T(8,128)S(1)}, u32[]{:S(2)}) copy-start(f32[16,4,32,128]{3,2,1,0:T(8,128)S(1)} %pad_maximum_fusion) | copy-start | bytes 3145732
  57.9 27.5 %copy-start.10 = (f32[784,128]{1,0:T(8,128)}, f32[784,128]{1,0:T(8,128)S(1)}, u32[]{:S(2)}) copy-start(f32[784,128]{1,0:T(8,128)S(1)} %collective-permute-done.other_packed) | copy-start | bytes 1204228
  57.9 66.6 %copy-start.15 = (s32[10,16]{1,0:T(8,128)}, s32[10,16]{1,0:T(8,128)S(1)}, u32[]{:S(2)}) copy-start(s32[10,16]{1,0:T(8,128)S(1)} %slice_convert_fusion.refs_1_.other_info) | copy-start | bytes 1924
  57.9 66.6 %copy-start.1 = (f32[3,1,16,128,128]{4,3,2,1,0:T(8,128)}, f32[3,1,16,128,128]{4,3,2,1,0:T(8,128)S(1)}, u32[]{:S(2)}) copy-start(f32[3,1,16,128,128]{4,3,2,1,0:T(8,128)S(1)} %collective-permute-done.1.refs_3_) | copy-start | bytes 9437188
  57.9 27.5 %copy-start.9 = (f32[784,128]{1,0:T(8,128)S(1)}, f32[784,128]{1,0:T(8,128)}, u32[]{:S(2)}) copy-start(f32[784,128]{1,0:T(8,128)} %get-tuple-element.16.packed) | copy-start | bytes 1204228
  86.6 30.1 %copy-start.13 = (f32[4,32,128]{2,1,0:T(8,128)}, f32[4,32,128]{2,1,0:T(8,128)S(1)}, u32[]{:S(2)}) copy-start(f32[4,32,128]{2,1,0:T(8,128)S(1)} %shard_map.66.refs_0_) | copy-start | bytes 196612
  106.0 9.9 %collective-permute-start.5 = (f32[4,4,32,128]{3,2,1,0:T(8,128)S(1)}, f32[4,4,32,128]{3,2,1,0:T(8,128)S(1)}, u32[]{:S(2)}, u32[]{:S(2)}) collective-permute-start(f32[4,4,32,128]{3,2,1,0:T(8,128)S(1)} %bitcast.23), channel_id=1, source_target_pairs={{0,2},{1,3},{2,4},{3,5},{4,6},{5,7},{6,8},{7,9},{8,10},{9,11},{10,... | collective-permute-start | bytes 786440 | tf_op jit(solution)/shard_map/ppermute | solution.py:213
  107.9 8.7 %collective-permute-start.6 = (f32[4,4,32,128]{3,2,1,0:T(8,128)S(1)}, f32[4,4,32,128]{3,2,1,0:T(8,128)S(1)}, u32[]{:S(2)}, u32[]{:S(2)}) collective-permute-start(f32[4,4,32,128]{3,2,1,0:T(8,128)S(1)} %bitcast.24), channel_id=1, source_target_pairs={{0,4},{1,29},{2,6},{3,31},{4,8},{5,1},{6,10},{7,3},{8,12},{9,5},{1... | collective-permute-start | bytes 786440 | tf_op jit(solution)/shard_map/ppermute | solution.py:213
  109.8 14.5 %collective-permute-start.7 = (f32[4,4,32,128]{3,2,1,0:T(8,128)S(1)}, f32[4,4,32,128]{3,2,1,0:T(8,128)S(1)}, u32[]{:S(2)}, u32[]{:S(2)}) collective-permute-start(f32[4,4,32,128]{3,2,1,0:T(8,128)S(1)} %bitcast.25), channel_id=1, source_target_pairs={{0,30},{1,31},{2,0},{3,1},{4,2},{5,3},{6,4},{7,5},{8,6},{9,7},{10,... | collective-permute-start | bytes 786440 | tf_op jit(solution)/shard_map/ppermute | solution.py:213
  127.1 1.0 copy-start.5
  128.2 1.0 copy-start.7
  129.1 22.5 %all-to-all-start.1 = ((f32[64,32,128]{2,1,0:T(8,128)}), f32[64,32,128]{2,1,0:T(8,128)}, u32[]{:S(2)}, u32[]{:S(2)}) async-start(f32[64,32,128]{2,1,0:T(8,128)} %copy-done.7), calls=%async_computation.1 | async-start | bytes 2097152 | tf_op jit(solution)/shard_map/all_to_all | solution.py:274
  151.6 1.0 copy-start.11
  152.6 0.7 copy-start.16
  153.3 34.1 %copy-start.2 = (f32[3,1,16,128,128]{4,3,2,1,0:T(8,128)S(1)}, f32[3,1,16,128,128]{4,3,2,1,0:T(8,128)}, u32[]{:S(2)}) copy-start(f32[3,1,16,128,128]{4,3,2,1,0:T(8,128)} %copy-done.1) | copy-start | bytes 9437188
  153.3 34.1 %copy-start.4 = (f32[16,4,32,128]{3,2,1,0:T(8,128)S(1)}, f32[16,4,32,128]{3,2,1,0:T(8,128)}, u32[]{:S(2)}) copy-start(f32[16,4,32,128]{3,2,1,0:T(8,128)} %copy-done.3) | copy-start | bytes 3145732
  153.3 34.1 %copy-start.17 = (s32[10,16]{1,0:T(8,128)S(1)}, s32[10,16]{1,0:T(8,128)}, u32[]{:S(2)}) copy-start(s32[10,16]{1,0:T(8,128)} %copy-done.15) | copy-start | bytes 1924
  170.3 9.6 %collective-permute-start.10 = (f32[4,4,32,128]{3,2,1,0:T(8,128)S(1)}, f32[4,4,32,128]{3,2,1,0:T(8,128)S(1)}, u32[]{:S(2)}, u32[]{:S(2)}) collective-permute-start(f32[4,4,32,128]{3,2,1,0:T(8,128)S(1)} %bitcast.19), channel_id=1, source_target_pairs={{0,30},{1,31},{2,0},{3,1},{4,2},{5,3},{6,4},{7,5},{8,6},{9,7},{10,... | collective-permute-start | bytes 786440 | tf_op jit(solution)/shard_map/ppermute | solution.py:213
  172.2 8.3 %collective-permute-start.8 = (f32[4,4,32,128]{3,2,1,0:T(8,128)S(1)}, f32[4,4,32,128]{3,2,1,0:T(8,128)S(1)}, u32[]{:S(2)}, u32[]{:S(2)}) collective-permute-start(f32[4,4,32,128]{3,2,1,0:T(8,128)S(1)} %bitcast.20), channel_id=1, source_target_pairs={{0,2},{1,3},{2,4},{3,5},{4,6},{5,7},{6,8},{7,9},{8,10},{9,11},{10,... | collective-permute-start | bytes 786440 | tf_op jit(solution)/shard_map/ppermute | solution.py:213
  175.6 11.8 %collective-permute-start.9 = (f32[4,4,32,128]{3,2,1,0:T(8,128)S(1)}, f32[4,4,32,128]{3,2,1,0:T(8,128)S(1)}, u32[]{:S(2)}, u32[]{:S(2)}) collective-permute-start(f32[4,4,32,128]{3,2,1,0:T(8,128)S(1)} %bitcast.21), channel_id=1, source_target_pairs={{0,4},{1,29},{2,6},{3,31},{4,8},{5,1},{6,10},{7,3},{8,12},{9,5},{1... | collective-permute-start | bytes 786440 | tf_op jit(solution)/shard_map/ppermute | solution.py:213
  187.5 1.2 copy-start.6
  188.7 34.0 %copy-start.8 = (f32[4,1,2,128,128]{4,3,2,1,0:T(8,128)S(1)}, f32[4,1,2,128,128]{4,3,2,1,0:T(8,128)}, u32[]{:S(2)}) copy-start(f32[4,1,2,128,128]{4,3,2,1,0:T(8,128)} %inverse.1) | copy-start | bytes 1572868
  188.7 34.0 %copy-start.12 = (f32[4,1,2,64,128]{4,3,2,1,0:T(8,128)S(1)}, f32[4,1,2,64,128]{4,3,2,1,0:T(8,128)}, u32[]{:S(2)}) copy-start(f32[4,1,2,64,128]{4,3,2,1,0:T(8,128)} %right.1) | copy-start | bytes 786436
  188.7 34.0 %copy-start.14 = (f32[4,32,128]{2,1,0:T(8,128)S(1)}, f32[4,32,128]{2,1,0:T(8,128)}, u32[]{:S(2)}) copy-start(f32[4,32,128]{2,1,0:T(8,128)} %copy-done.13) | copy-start | bytes 196612
  188.7 34.0 %copy-start.18 = (f32[2,64,128]{2,1,0:T(8,128)S(1)}, f32[2,64,128]{2,1,0:T(8,128)}, u32[]{:S(2)}) copy-start(f32[2,64,128]{2,1,0:T(8,128)} %get-tuple-element.15.first) | copy-start | bytes 196612
  191.3 9.3 %collective-permute-start.11 = (f32[2,2,32,128]{3,2,1,0:T(8,128)S(1)}, f32[2,2,32,128]{3,2,1,0:T(8,128)S(1)}, u32[]{:S(2)}, u32[]{:S(2)}) collective-permute-start(f32[2,2,32,128]{3,2,1,0:T(8,128)S(1)} %pad_maximum_fusion.3), channel_id=1, source_target_pairs={{0,1},{1,0},{2,3},{3,2},{4,5},{5,4},{6,7},{7,6},{8,9},{9,8},{10,11... | collective-permute-start | bytes 196616 | tf_op jit(solution)/shard_map/ppermute | solution.py:198

commit v9 on v8

--- a/solution.py
+++ b/solution.py
@@ -208,13 +208,13 @@
 
 
 def gather_near(mine, cols):
-    def shift(x, even, odd):
-        step = (CORES * even, CORES * odd)
-        return lax.ppermute(x, "col", [(i, (i + step[i % CORES]) % cols) for i in range(cols)])
-
-    two = shift(mine, 2, -2)
-    below, above = shift(mine, 1, 1), shift(mine, -1, -1)
-    same = jnp.concatenate([mine, below, two, above])
+    def shift(x, k):
+        return lax.ppermute(x, "col", [(i, (i + CORES * k) % cols) for i in range(cols)])
+
+    half = mine.shape[0] // 2
+    below, above = shift(mine, 1), shift(mine, -1)
+    low, high = shift(mine[:half], 2), shift(mine[half:], -2)
+    same = jnp.concatenate([mine, below, low, high, above])
     return same.reshape((-1,) + same.shape[2:])
 
 

time: 225 us -> 222 us (0.987)
  starting transfers between devices: 45.9 us -> 66.5 us
  waiting for transfers between devices: 45.3 us -> 26.1 us
  blocking collectives: 109 us -> 105 us
    ppermute x9 -> x12, starting transfers between devices: 25.6 us -> 40.5 us  [shift(): lax.ppermute(x, 'col', [(i, (i + CORES * k) % cols) for i in range(cols)])]
    ppermute x9 -> x12, waiting for transfers between devices: 27.6 us -> 14.3 us  [shift(): lax.ppermute(x, 'col', [(i, (i + CORES * k) % cols) for i in range(cols)])]
    all_to_all x1, waiting for transfers between devices: 16.8 us -> 10.9 us  [on_device(): received = lax.all_to_all(terms, 'row', 0, 0, tiled=True)]
    ppermute x3, starting transfers between devices: 15.9 us -> 21.7 us  [swap(): return lax.ppermute(x, 'col', [(i, i ^ 1) for i in range(cols)])]
    unnamed x38 -> x50, local copies, waits for them, and re-layouts: 4.96 us -> 5.13 us
  transfers between devices with their start and end apart: 13 -> 16, of which waited for: 10 -> 5; matrix products, arithmetic and copies ran while one was open for 1% -> 1% of each run, Pallas kernels for 0% -> 0%
where the time goes in v9:
time: 222 us; the launch traced here: 221 us
  blocking collectives  105 us (47%)
  starting transfers between devices  66.5 us (30%)
  waiting for transfers between devices  26.1 us (12%)
  Pallas kernels  15.5 us (7%)
  local copies, waits for them, and re-layouts  6.63 us (3%)
    all_gather x3, blocking collectives, gather_far(): lax.all_gather(solved, 'col', axis=0, tiled=False, axis_index_groups=far)  52.8 us
    ppermute x12, starting transfers between devices, shift(): lax.ppermute(x, 'col', [(i, (i + CORES * k) % cols) for i in range(cols)])  40.5 us
    all_to_all x1, blocking collectives, on_device(): received = lax.all_to_all(terms, 'row', 0, 0, tiled=True)  22.8 us
    ppermute x3, starting transfers between devices, swap(): return lax.ppermute(x, 'col', [(i, i ^ 1) for i in range(cols)])  21.7 us
    all_to_all x1, blocking collectives, on_device(): lax.all_to_all(terms, ('row', 'col'), 0, 0, tiled=True, axis_index_groups...  20.5 us
    ppermute x12, waiting for transfers between devices, shift(): lax.ppermute(x, 'col', [(i, (i + CORES * k) % cols) for i in range(cols)])  14.3 us
    all_to_all x1, waiting for transfers between devices, on_device(): received = lax.all_to_all(terms, 'row', 0, 0, tiled=True)  10.9 us
    all_gather x1, blocking collectives, split_rows(): lax.all_gather(solved, 'col', axis=0, tiled=False, axis_index_groups=pairs)  8.64 us
  transfers between devices with their start and end apart: 16, of which 5 were waited for; matrix products, arithmetic and copies ran while one was open for 1% of the time, Pallas kernels for 0%

profile of v9, /device:TPU:1, one launch (start us, length us, event | category | flops | bytes accessed | tf_op | source)
XLA Modules:
  0.0 221.4 jit_solution(1553944414376243557)
XLA Ops:
  0.0 3.0 %shard_map.64 = (f32[2,64,128]{2,1,0:T(8,128)}, f32[784,128]{1,0:T(8,128)}) custom-call(s32[1,1,4]{2,1,0:T(1,128)} %bitcast.35, f32[4,1,2,64,128]{4,3,2,1,0:T(8,128)} %right.1, f32[4,1,2,128,128]{4,3,2,1,0:T(8,128)} %inverse.1, s32[3,1,16]{2,1,0:T(1,128)} %sources.1, s32[3,1,16]{2,1,0:T(1,128)} %targets.1), custom_call_target="tpu_custom_call" | custom-call | tf_op jit(solution)/shard_map/pallas_call | solution.py:68
  3.1 8.6 %all-gather = f32[4,64,128]{2,1,0:T(8,128)S(1)} all-gather(f32[2,64,128]{2,1,0:T(8,128)} %get-tuple-element.15.first), channel_id=2, replica_groups={{0,1},{2,3},{4,5},{6,7},{8,9},{10,11},{12,13},{14,15},{16,17},{18,19},{..., dimensions={0}, use_global_device_ids=true | all-gather | bytes 196608 | tf_op jit(solution)/shard_map/all_gather | solution.py:223
  11.7 19.1 %all_gather.23 = f32[4,4,32,128]{3,2,1,0:T(8,128)S(1)} all-gather(f32[1,4,32,128]{3,2,1,0:T(8,128)S(1)} %bitcast.30), channel_id=1, replica_groups={{0,8,16,24},{1,9,17,25},{2,10,18,26},{3,11,19,27},{4,12,20,28},{5,13,21..., dimensions={0}, use_global_device_ids=true | all-gather | bytes 327680 | tf_op jit(solution)/shard_map/all_gather | solution.py:207
  30.8 5.6 %collective-permute-start.1 = (f32[3,1,16,128,128]{4,3,2,1,0:T(8,128)}, f32[3,1,16,128,128]{4,3,2,1,0:T(8,128)S(1)}, u32[]{:S(2)}, u32[]{:S(2)}) collective-permute-start(f32[3,1,16,128,128]{4,3,2,1,0:T(8,128)} %refs_2_.5), channel_id=1, source_target_pairs={{0,1},{1,0},{2,3},{3,2},{4,5},{5,4},{6,7},{7,6},{8,9},{9,8},{10,11... | collective-permute-start | bytes 9437192 | tf_op jit(solution)/shard_map/ppermute | solution.py:198
  36.4 2.9 %collective-permute-start.2 = (f32[4,4,32,128]{3,2,1,0:T(8,128)S(1)}, f32[4,4,32,128]{3,2,1,0:T(8,128)S(1)}, u32[]{:S(2)}, u32[]{:S(2)}) collective-permute-start(f32[4,4,32,128]{3,2,1,0:T(8,128)S(1)} %all_gather.23), channel_id=1, source_target_pairs={{0,2},{1,3},{2,4},{3,5},{4,6},{5,7},{6,8},{7,9},{8,10},{9,11},{10,... | collective-permute-start | bytes 786440 | tf_op jit(solution)/shard_map/ppermute | solution.py:212
  39.3 3.6 %collective-permute-start.5 = (f32[4,4,32,128]{3,2,1,0:T(8,128)S(1)}, f32[4,4,32,128]{3,2,1,0:T(8,128)S(1)}, u32[]{:S(2)}, u32[]{:S(2)}) collective-permute-start(f32[4,4,32,128]{3,2,1,0:T(8,128)S(1)} %all_gather.23), channel_id=1, source_target_pairs={{0,30},{1,31},{2,0},{3,1},{4,2},{5,3},{6,4},{7,5},{8,6},{9,7},{10,... | collective-permute-start | bytes 786440 | tf_op jit(solution)/shard_map/ppermute | solution.py:212
  43.0 2.1 collective-permute-start.3
  45.1 2.8 %collective-permute-start = (f32[784,128]{1,0:T(8,128)}, f32[784,128]{1,0:T(8,128)S(1)}, u32[]{:S(2)}, u32[]{:S(2)}) collective-permute-start(f32[784,128]{1,0:T(8,128)} %get-tuple-element.16.packed), channel_id=1, source_target_pairs={{0,1},{1,0},{2,3},{3,2},{4,5},{5,4},{6,7},{7,6},{8,9},{9,8},{10,11... | collective-permute-start | bytes 1204232 | tf_op jit(solution)/shard_map/ppermute | solution.py:198
  48.6 5.3 %collective-permute-start.4 = (f32[2,4,32,128]{3,2,1,0:T(8,128)S(1)}, f32[2,4,32,128]{3,2,1,0:T(8,128)S(1)}, u32[]{:S(2)}, u32[]{:S(2)}) collective-permute-start(f32[2,4,32,128]{3,2,1,0:T(8,128)S(1)} %get-tuple-element.27), channel_id=1, source_target_pairs={{0,28},{1,29},{2,30},{3,31},{4,0},{5,1},{6,2},{7,3},{8,4},{9,5},{1... | collective-permute-start | bytes 393224 | tf_op jit(solution)/shard_map/ppermute | solution.py:212
  53.9 5.9 %collective-permute-done.4 = f32[2,4,32,128]{3,2,1,0:T(8,128)S(1)} collective-permute-done((f32[2,4,32,128]{3,2,1,0:T(8,128)S(1)}, f32[2,4,32,128]{3,2,1,0:T(8,128)S(1)}, u32[]{:S(2)}, u32[]{:S(2)}) %collective-permute-start.4) | collective-permute-done | bytes 131104 | tf_op jit(solution)/shard_map/ppermute | solution.py:212
  60.0 2.6 %shard_map.65 = f32[64,32,128]{2,1,0:T(8,128)S(1)} custom-call(s32[1]{0:T(128)} %bitcast.column, s32[10,16]{1,0:T(8,128)S(1)} %slice_convert_fusion.1.refs_0_.info, s32[10,16]{1,0:T(8,128)S(1)} %slice_convert_fusion.refs_1_.other_info, f32[3,1,16,128,128]{4,3,2,1,0:T(8,128)S(1)} %copy-done, f32[3,1,16,128,128]{4,3,2,1,0:T(8,128)S(1)} %collective-permute-done.1.refs_3_, ...), custom_call_target="tpu_custom_call" | custom-call | tf_op jit(solution)/shard_map/pallas_call | solution.py:187
  62.6 22.8 %all_to_all.15.received = f32[64,32,128]{2,1,0:T(8,128)S(1)} all-to-all(f32[64,32,128]{2,1,0:T(8,128)S(1)} %shard_map.65), channel_id=1, replica_groups=mesh['row'=16,'col'=32] {'row'}, dimensions={0} | all-to-all | bytes 2097152 | tf_op jit(solution)/shard_map/all_to_all | solution.py:274
  86.6 16.8 %all-gather.1 = f32[16,32,128]{2,1,0:T(8,128)S(1)} all-gather(f32[4,32,128]{2,1,0:T(8,128)S(1)} %shard_map.66.refs_0_), channel_id=3, replica_groups={{0,8,16,24},{1,9,17,25},{2,10,18,26},{3,11,19,27},{4,12,20,28},{5,13,21..., dimensions={0}, use_global_device_ids=true | all-gather | bytes 327680 | tf_op jit(solution)/shard_map/all_gather | solution.py:207
  103.4 1.9 collective-permute-start.6
  105.3 3.9 %collective-permute-start.7 = (f32[2,4,32,128]{3,2,1,0:T(8,128)S(1)}, f32[2,4,32,128]{3,2,1,0:T(8,128)S(1)}, u32[]{:S(2)}, u32[]{:S(2)}) collective-permute-start(f32[2,4,32,128]{3,2,1,0:T(8,128)S(1)} %bitcast.34), channel_id=1, source_target_pairs={{0,4},{1,5},{2,6},{3,7},{4,8},{5,9},{6,10},{7,11},{8,12},{9,13},{1... | collective-permute-start | bytes 393224 | tf_op jit(solution)/shard_map/ppermute | solution.py:212
  109.3 4.6 %collective-permute-start.9 = (f32[4,4,32,128]{3,2,1,0:T(8,128)S(1)}, f32[4,4,32,128]{3,2,1,0:T(8,128)S(1)}, u32[]{:S(2)}, u32[]{:S(2)}) collective-permute-start(f32[4,4,32,128]{3,2,1,0:T(8,128)S(1)} %bitcast.28), channel_id=1, source_target_pairs={{0,30},{1,31},{2,0},{3,1},{4,2},{5,3},{6,4},{7,5},{8,6},{9,7},{10,... | collective-permute-start | bytes 786440 | tf_op jit(solution)/shard_map/ppermute | solution.py:212
  113.8 2.3 %collective-permute-start.8 = (f32[2,4,32,128]{3,2,1,0:T(8,128)S(1)}, f32[2,4,32,128]{3,2,1,0:T(8,128)S(1)}, u32[]{:S(2)}, u32[]{:S(2)}) collective-permute-start(f32[2,4,32,128]{3,2,1,0:T(8,128)S(1)} %bitcast.33), channel_id=1, source_target_pairs={{0,28},{1,29},{2,30},{3,31},{4,0},{5,1},{6,2},{7,3},{8,4},{9,5},{1... | collective-permute-start | bytes 393224 | tf_op jit(solution)/shard_map/ppermute | solution.py:212
  116.3 6.6 %collective-permute-done.8 = f32[2,4,32,128]{3,2,1,0:T(8,128)S(1)} collective-permute-done((f32[2,4,32,128]{3,2,1,0:T(8,128)S(1)}, f32[2,4,32,128]{3,2,1,0:T(8,128)S(1)}, u32[]{:S(2)}, u32[]{:S(2)}) %collective-permute-start.8) | collective-permute-done | bytes 131104 | tf_op jit(solution)/shard_map/ppermute | solution.py:212
  123.0 2.6 %shard_map.67 = f32[64,32,128]{2,1,0:T(8,128)S(1)} custom-call(s32[1]{0:T(128)} %bitcast.column, s32[10,16]{1,0:T(8,128)S(1)} %slice_convert_fusion.1.refs_0_.info, s32[10,16]{1,0:T(8,128)S(1)} %slice_convert_fusion.refs_1_.other_info, f32[3,1,16,128,128]{4,3,2,1,0:T(8,128)S(1)} %copy-done, f32[3,1,16,128,128]{4,3,2,1,0:T(8,128)S(1)} %collective-permute-done.1.refs_3_, ...), custom_call_target="tpu_custom_call" | custom-call | tf_op jit(solution)/shard_map/pallas_call | solution.py:187
  127.6 4.3 %all-to-all-start.1 = ((f32[64,32,128]{2,1,0:T(8,128)}), f32[64,32,128]{2,1,0:T(8,128)}, u32[]{:S(2)}, u32[]{:S(2)}) async-start(f32[64,32,128]{2,1,0:T(8,128)} %copy-done.7), calls=%async_computation.1 | async-start | bytes 2097152 | tf_op jit(solution)/shard_map/all_to_all | solution.py:274
  133.3 10.9 %all-to-all-done.1.received = f32[64,32,128]{2,1,0:T(8,128)} async-done(((f32[64,32,128]{2,1,0:T(8,128)}), f32[64,32,128]{2,1,0:T(8,128)}, u32[]{:S(2)}, u32[]{:S(2)}) %all-to-all-start.1) | async-done | bytes 1048608 | tf_op jit(solution)/shard_map/all_to_all | solution.py:274
  146.0 1.7 shard_map.68.refs_1_
  147.7 16.8 %all-gather.2 = f32[16,32,128]{2,1,0:T(8,128)S(1)} all-gather(f32[4,32,128]{2,1,0:T(8,128)S(1)} %shard_map.68.refs_1_), channel_id=4, replica_groups={{0,8,16,24},{1,9,17,25},{2,10,18,26},{3,11,19,27},{4,12,20,28},{5,13,21..., dimensions={0}, use_global_device_ids=true | all-gather | bytes 327680 | tf_op jit(solution)/shard_map/all_gather | solution.py:207
  164.6 1.9 collective-permute-start.10
  166.5 4.6 %collective-permute-start.13 = (f32[4,4,32,128]{3,2,1,0:T(8,128)S(1)}, f32[4,4,32,128]{3,2,1,0:T(8,128)S(1)}, u32[]{:S(2)}, u32[]{:S(2)}) collective-permute-start(f32[4,4,32,128]{3,2,1,0:T(8,128)S(1)} %bitcast.24), channel_id=1, source_target_pairs={{0,30},{1,31},{2,0},{3,1},{4,2},{5,3},{6,4},{7,5},{8,6},{9,7},{10,... | collective-permute-start | bytes 786440 | tf_op jit(solution)/shard_map/ppermute | solution.py:212
  171.1 1.9 collective-permute-start.11
  173.0 5.5 %collective-permute-start.12 = (f32[2,4,32,128]{3,2,1,0:T(8,128)S(1)}, f32[2,4,32,128]{3,2,1,0:T(8,128)S(1)}, u32[]{:S(2)}, u32[]{:S(2)}) collective-permute-start(f32[2,4,32,128]{3,2,1,0:T(8,128)S(1)} %bitcast.31), channel_id=1, source_target_pairs={{0,28},{1,29},{2,30},{3,31},{4,0},{5,1},{6,2},{7,3},{8,4},{9,5},{1... | collective-permute-start | bytes 393224 | tf_op jit(solution)/shard_map/ppermute | solution.py:212
  179.3 1.7 collective-permute-done.11
  182.4 2.6 %shard_map.69 = f32[64,32,128]{2,1,0:T(8,128)S(1)} custom-call(s32[1]{0:T(128)} %bitcast.column, s32[10,16]{1,0:T(8,128)S(1)} %slice_convert_fusion.1.refs_0_.info, s32[10,16]{1,0:T(8,128)S(1)} %copy-done.17, f32[3,1,16,128,128]{4,3,2,1,0:T(8,128)S(1)} %copy-done, f32[3,1,16,128,128]{4,3,2,1,0:T(8,128)S(1)} %copy-done.2, f32[64,32,128]{2,1,0:T(8,128)S(1)} %bitcast.19, ...), custom_call_target="tpu_custom_call" | custom-call | tf_op jit(solution)/shard_map/pallas_call | solution.py:187
  185.0 13.3 %collective-permute-start.14 = (f32[2,2,32,128]{3,2,1,0:T(8,128)S(1)}, f32[2,2,32,128]{3,2,1,0:T(8,128)S(1)}, u32[]{:S(2)}, u32[]{:S(2)}) collective-permute-start(f32[2,2,32,128]{3,2,1,0:T(8,128)S(1)} %pad_maximum_fusion), channel_id=1, source_target_pairs={{0,1},{1,0},{2,3},{3,2},{4,5},{5,4},{6,7},{7,6},{8,9},{9,8},{10,11... | collective-permute-start | bytes 196616 | tf_op jit(solution)/shard_map/ppermute | solution.py:198
  199.2 20.5 %all_to_all.16.received = f32[64,32,128]{2,1,0:T(8,128)S(1)} all-to-all(f32[64,32,128]{2,1,0:T(8,128)S(1)} %shard_map.69), channel_id=1, replica_groups={{0,1,32,33,64,65,96,97,128,129,160,161,192,193,224,225,256,257,288,289,..., dimensions={0} | all-to-all | bytes 2097152 | tf_op jit(solution)/shard_map/all_to_all | solution.py:268
  219.8 1.7 shard_map.70
  (76 shorter events, 10.2 us)
Async XLA Ops:
  0.0 60.0 %copy-start = (f32[3,1,16,128,128]{4,3,2,1,0:T(8,128)S(1)}, f32[3,1,16,128,128]{4,3,2,1,0:T(8,128)}, u32[]{:S(2)}) copy-start(f32[3,1,16,128,128]{4,3,2,1,0:T(8,128)} %refs_2_.5) | copy-start | bytes 9437188
  30.8 29.1 %collective-permute-start.1 = (f32[3,1,16,128,128]{4,3,2,1,0:T(8,128)}, f32[3,1,16,128,128]{4,3,2,1,0:T(8,128)S(1)}, u32[]{:S(2)}, u32[]{:S(2)}) collective-permute-start(f32[3,1,16,128,128]{4,3,2,1,0:T(8,128)} %refs_2_.5), channel_id=1, source_target_pairs={{0,1},{1,0},{2,3},{3,2},{4,5},{5,4},{6,7},{7,6},{8,9},{9,8},{10,11... | collective-permute-start | bytes 9437192 | tf_op jit(solution)/shard_map/ppermute | solution.py:198
  36.4 12.1 %collective-permute-start.2 = (f32[4,4,32,128]{3,2,1,0:T(8,128)S(1)}, f32[4,4,32,128]{3,2,1,0:T(8,128)S(1)}, u32[]{:S(2)}, u32[]{:S(2)}) collective-permute-start(f32[4,4,32,128]{3,2,1,0:T(8,128)S(1)} %all_gather.23), channel_id=1, source_target_pairs={{0,2},{1,3},{2,4},{3,5},{4,6},{5,7},{6,8},{7,9},{8,10},{9,11},{10,... | collective-permute-start | bytes 786440 | tf_op jit(solution)/shard_map/ppermute | solution.py:212
  39.3 20.5 %collective-permute-start.5 = (f32[4,4,32,128]{3,2,1,0:T(8,128)S(1)}, f32[4,4,32,128]{3,2,1,0:T(8,128)S(1)}, u32[]{:S(2)}, u32[]{:S(2)}) collective-permute-start(f32[4,4,32,128]{3,2,1,0:T(8,128)S(1)} %all_gather.23), channel_id=1, source_target_pairs={{0,30},{1,31},{2,0},{3,1},{4,2},{5,3},{6,4},{7,5},{8,6},{9,7},{10,... | collective-permute-start | bytes 786440 | tf_op jit(solution)/shard_map/ppermute | solution.py:212
  43.0 11.0 %collective-permute-start.3 = (f32[2,4,32,128]{3,2,1,0:T(8,128)S(1)}, f32[2,4,32,128]{3,2,1,0:T(8,128)S(1)}, u32[]{:S(2)}, u32[]{:S(2)}) collective-permute-start(f32[2,4,32,128]{3,2,1,0:T(8,128)S(1)} %get-tuple-element.28), channel_id=1, source_target_pairs={{0,4},{1,5},{2,6},{3,7},{4,8},{5,9},{6,10},{7,11},{8,12},{9,13},{1... | collective-permute-start | bytes 393224 | tf_op jit(solution)/shard_map/ppermute | solution.py:212
  45.1 14.8 %collective-permute-start = (f32[784,128]{1,0:T(8,128)}, f32[784,128]{1,0:T(8,128)S(1)}, u32[]{:S(2)}, u32[]{:S(2)}) collective-permute-start(f32[784,128]{1,0:T(8,128)} %get-tuple-element.16.packed), channel_id=1, source_target_pairs={{0,1},{1,0},{2,3},{3,2},{4,5},{5,4},{6,7},{7,6},{8,9},{9,8},{10,11... | collective-permute-start | bytes 1204232 | tf_op jit(solution)/shard_map/ppermute | solution.py:198
  48.6 11.2 %collective-permute-start.4 = (f32[2,4,32,128]{3,2,1,0:T(8,128)S(1)}, f32[2,4,32,128]{3,2,1,0:T(8,128)S(1)}, u32[]{:S(2)}, u32[]{:S(2)}) collective-permute-start(f32[2,4,32,128]{3,2,1,0:T(8,128)S(1)} %get-tuple-element.27), channel_id=1, source_target_pairs={{0,28},{1,29},{2,30},{3,31},{4,0},{5,1},{6,2},{7,3},{8,4},{9,5},{1... | collective-permute-start | bytes 393224 | tf_op jit(solution)/shard_map/ppermute | solution.py:212
  59.9 63.1 %copy-start.3 = (f32[16,4,32,128]{3,2,1,0:T(8,128)}, f32[16,4,32,128]{3,2,1,0:T(8,128)S(1)}, u32[]{:S(2)}) copy-start(f32[16,4,32,128]{3,2,1,0:T(8,128)S(1)} %constant_dynamic-update-slice_fusion) | copy-start | bytes 3145732
  59.9 25.5 %copy-start.10 = (f32[784,128]{1,0:T(8,128)}, f32[784,128]{1,0:T(8,128)S(1)}, u32[]{:S(2)}) copy-start(f32[784,128]{1,0:T(8,128)S(1)} %collective-permute-done.other_packed) | copy-start | bytes 1204228
  59.9 63.0 %copy-start.15 = (s32[10,16]{1,0:T(8,128)}, s32[10,16]{1,0:T(8,128)S(1)}, u32[]{:S(2)}) copy-start(s32[10,16]{1,0:T(8,128)S(1)} %slice_convert_fusion.refs_1_.other_info) | copy-start | bytes 1924
  60.0 63.0 %copy-start.1 = (f32[3,1,16,128,128]{4,3,2,1,0:T(8,128)}, f32[3,1,16,128,128]{4,3,2,1,0:T(8,128)S(1)}, u32[]{:S(2)}) copy-start(f32[3,1,16,128,128]{4,3,2,1,0:T(8,128)S(1)} %collective-permute-done.1.refs_3_) | copy-start | bytes 9437188
  60.0 25.4 %copy-start.9 = (f32[784,128]{1,0:T(8,128)S(1)}, f32[784,128]{1,0:T(8,128)}, u32[]{:S(2)}) copy-start(f32[784,128]{1,0:T(8,128)} %get-tuple-element.16.packed) | copy-start | bytes 1204228
  86.6 18.8 %copy-start.13 = (f32[4,32,128]{2,1,0:T(8,128)}, f32[4,32,128]{2,1,0:T(8,128)S(1)}, u32[]{:S(2)}) copy-start(f32[4,32,128]{2,1,0:T(8,128)S(1)} %shard_map.66.refs_0_) | copy-start | bytes 196612
  103.4 12.8 %collective-permute-start.6 = (f32[4,4,32,128]{3,2,1,0:T(8,128)S(1)}, f32[4,4,32,128]{3,2,1,0:T(8,128)S(1)}, u32[]{:S(2)}, u32[]{:S(2)}) collective-permute-start(f32[4,4,32,128]{3,2,1,0:T(8,128)S(1)} %bitcast.26), channel_id=1, source_target_pairs={{0,2},{1,3},{2,4},{3,5},{4,6},{5,7},{6,8},{7,9},{8,10},{9,11},{10,... | collective-permute-start | bytes 786440 | tf_op jit(solution)/shard_map/ppermute | solution.py:212
  105.3 10.9 %collective-permute-start.7 = (f32[2,4,32,128]{3,2,1,0:T(8,128)S(1)}, f32[2,4,32,128]{3,2,1,0:T(8,128)S(1)}, u32[]{:S(2)}, u32[]{:S(2)}) collective-permute-start(f32[2,4,32,128]{3,2,1,0:T(8,128)S(1)} %bitcast.34), channel_id=1, source_target_pairs={{0,4},{1,5},{2,6},{3,7},{4,8},{5,9},{6,10},{7,11},{8,12},{9,13},{1... | collective-permute-start | bytes 393224 | tf_op jit(solution)/shard_map/ppermute | solution.py:212
  109.3 13.7 %collective-permute-start.9 = (f32[4,4,32,128]{3,2,1,0:T(8,128)S(1)}, f32[4,4,32,128]{3,2,1,0:T(8,128)S(1)}, u32[]{:S(2)}, u32[]{:S(2)}) collective-permute-start(f32[4,4,32,128]{3,2,1,0:T(8,128)S(1)} %bitcast.28), channel_id=1, source_target_pairs={{0,30},{1,31},{2,0},{3,1},{4,2},{5,3},{6,4},{7,5},{8,6},{9,7},{10,... | collective-permute-start | bytes 786440 | tf_op jit(solution)/shard_map/ppermute | solution.py:212
  113.8 9.1 %collective-permute-start.8 = (f32[2,4,32,128]{3,2,1,0:T(8,128)S(1)}, f32[2,4,32,128]{3,2,1,0:T(8,128)S(1)}, u32[]{:S(2)}, u32[]{:S(2)}) collective-permute-start(f32[2,4,32,128]{3,2,1,0:T(8,128)S(1)} %bitcast.33), channel_id=1, source_target_pairs={{0,28},{1,29},{2,30},{3,31},{4,0},{5,1},{6,2},{7,3},{8,4},{9,5},{1... | collective-permute-start | bytes 393224 | tf_op jit(solution)/shard_map/ppermute | solution.py:212
  125.6 1.0 copy-start.5
  127.6 16.6 %all-to-all-start.1 = ((f32[64,32,128]{2,1,0:T(8,128)}), f32[64,32,128]{2,1,0:T(8,128)}, u32[]{:S(2)}, u32[]{:S(2)}) async-start(f32[64,32,128]{2,1,0:T(8,128)} %copy-done.7), calls=%async_computation.1 | async-start | bytes 2097152 | tf_op jit(solution)/shard_map/all_to_all | solution.py:274
  145.9 35.2 %copy-start.2 = (f32[3,1,16,128,128]{4,3,2,1,0:T(8,128)S(1)}, f32[3,1,16,128,128]{4,3,2,1,0:T(8,128)}, u32[]{:S(2)}) copy-start(f32[3,1,16,128,128]{4,3,2,1,0:T(8,128)} %copy-done.1) | copy-start | bytes 9437188
  146.0 35.2 %copy-start.4 = (f32[16,4,32,128]{3,2,1,0:T(8,128)S(1)}, f32[16,4,32,128]{3,2,1,0:T(8,128)}, u32[]{:S(2)}) copy-start(f32[16,4,32,128]{3,2,1,0:T(8,128)} %copy-done.3) | copy-start | bytes 3145732
  146.0 35.2 %copy-start.17 = (s32[10,16]{1,0:T(8,128)S(1)}, s32[10,16]{1,0:T(8,128)}, u32[]{:S(2)}) copy-start(s32[10,16]{1,0:T(8,128)} %copy-done.15) | copy-start | bytes 1924
  164.6 14.7 %collective-permute-start.10 = (f32[4,4,32,128]{3,2,1,0:T(8,128)S(1)}, f32[4,4,32,128]{3,2,1,0:T(8,128)S(1)}, u32[]{:S(2)}, u32[]{:S(2)}) collective-permute-start(f32[4,4,32,128]{3,2,1,0:T(8,128)S(1)} %bitcast.23), channel_id=1, source_target_pairs={{0,2},{1,3},{2,4},{3,5},{4,6},{5,7},{6,8},{7,9},{8,10},{9,11},{10,... | collective-permute-start | bytes 786440 | tf_op jit(solution)/shard_map/ppermute | solution.py:212
  166.5 14.6 %collective-permute-start.13 = (f32[4,4,32,128]{3,2,1,0:T(8,128)S(1)}, f32[4,4,32,128]{3,2,1,0:T(8,128)S(1)}, u32[]{:S(2)}, u32[]{:S(2)}) collective-permute-start(f32[4,4,32,128]{3,2,1,0:T(8,128)S(1)} %bitcast.24), channel_id=1, source_target_pairs={{0,30},{1,31},{2,0},{3,1},{4,2},{5,3},{6,4},{7,5},{8,6},{9,7},{10,... | collective-permute-start | bytes 786440 | tf_op jit(solution)/shard_map/ppermute | solution.py:212
  171.1 10.0 %collective-permute-start.11 = (f32[2,4,32,128]{3,2,1,0:T(8,128)S(1)}, f32[2,4,32,128]{3,2,1,0:T(8,128)S(1)}, u32[]{:S(2)}, u32[]{:S(2)}) collective-permute-start(f32[2,4,32,128]{3,2,1,0:T(8,128)S(1)} %bitcast.32), channel_id=1, source_target_pairs={{0,4},{1,5},{2,6},{3,7},{4,8},{5,9},{6,10},{7,11},{8,12},{9,13},{1... | collective-permute-start | bytes 393224 | tf_op jit(solution)/shard_map/ppermute | solution.py:212
  173.0 8.1 %collective-permute-start.12 = (f32[2,4,32,128]{3,2,1,0:T(8,128)S(1)}, f32[2,4,32,128]{3,2,1,0:T(8,128)S(1)}, u32[]{:S(2)}, u32[]{:S(2)}) collective-permute-start(f32[2,4,32,128]{3,2,1,0:T(8,128)S(1)} %bitcast.31), channel_id=1, source_target_pairs={{0,28},{1,29},{2,30},{3,31},{4,0},{5,1},{6,2},{7,3},{8,4},{9,5},{1... | collective-permute-start | bytes 393224 | tf_op jit(solution)/shard_map/ppermute | solution.py:212
  181.2 1.2 copy-start.6
  182.4 37.4 %copy-start.8 = (f32[4,1,2,128,128]{4,3,2,1,0:T(8,128)S(1)}, f32[4,1,2,128,128]{4,3,2,1,0:T(8,128)}, u32[]{:S(2)}) copy-start(f32[4,1,2,128,128]{4,3,2,1,0:T(8,128)} %inverse.1) | copy-start | bytes 1572868
  182.4 37.4 %copy-start.12 = (f32[4,1,2,64,128]{4,3,2,1,0:T(8,128)S(1)}, f32[4,1,2,64,128]{4,3,2,1,0:T(8,128)}, u32[]{:S(2)}) copy-start(f32[4,1,2,64,128]{4,3,2,1,0:T(8,128)} %right.1) | copy-start | bytes 786436
  182.4 37.4 %copy-start.14 = (f32[4,32,128]{2,1,0:T(8,128)S(1)}, f32[4,32,128]{2,1,0:T(8,128)}, u32[]{:S(2)}) copy-start(f32[4,32,128]{2,1,0:T(8,128)} %copy-done.13) | copy-start | bytes 196612
  182.4 37.4 %copy-start.18 = (f32[2,64,128]{2,1,0:T(8,128)S(1)}, f32[2,64,128]{2,1,0:T(8,128)}, u32[]{:S(2)}) copy-start(f32[2,64,128]{2,1,0:T(8,128)} %get-tuple-element.15.first) | copy-start | bytes 196612
  185.0 14.2 %collective-permute-start.14 = (f32[2,2,32,128]{3,2,1,0:T(8,128)S(1)}, f32[2,2,32,128]{3,2,1,0:T(8,128)S(1)}, u32[]{:S(2)}, u32[]{:S(2)}) collective-permute-start(f32[2,2,32,128]{3,2,1,0:T(8,128)S(1)} %pad_maximum_fusion), channel_id=1, source_target_pairs={{0,1},{1,0},{2,3},{3,2},{4,5},{5,4},{6,7},{7,6},{8,9},{9,8},{10,11... | collective-permute-start | bytes 196616 | tf_op jit(solution)/shard_map/ppermute | solution.py:198
  (3 other events, 2.7 us)

commit v10 on v9

--- a/solution.py
+++ b/solution.py
@@ -247,9 +247,8 @@
     history, halves = [], []
     for level in range(1, level_total):
         last = level + 1 == level_total
-        mine = gather_far(solved, cols)
         if level == 1:
-            coupling, pack, mine = lax.optimization_barrier((coupling_blocks, pack, mine))
+            coupling, pack, solved = lax.optimization_barrier((coupling_blocks, pack, solved))
             couplings = (coupling_blocks, swap(coupling, cols))
             packs = (pack, swap(pack, cols))
             notes = 3 * level_total - 2
@@ -257,6 +256,7 @@
             infos = tuple(
                 block[start : start + notes, :edges].astype(jnp.int32) for block in packs
             )
+        mine = gather_far(solved, cols)
         history.append(gather_near(mine, cols))
         terms = edge_terms(
             level, last, column, infos, couplings, history, rows, cols, slots

time: 222 us -> 223 us (level)
  transfers between devices with their start and end apart: 16 -> 16, of which waited for: 5 -> 6; matrix products, arithmetic and copies ran while one was open for 1% -> 1% of each run, Pallas kernels for 0% -> 0%
where the time goes in v10:
time: 223 us; the launch traced here: 222 us
  blocking collectives  103 us (46%)
  starting transfers between devices  66.9 us (30%)
  waiting for transfers between devices  27.6 us (12%)
  Pallas kernels  15.5 us (7%)
  local copies, waits for them, and re-layouts  6.63 us (3%)
    all_gather x3, blocking collectives, gather_far(): lax.all_gather(solved, 'col', axis=0, tiled=False, axis_index_groups=far)  51.1 us
    ppermute x12, starting transfers between devices, shift(): lax.ppermute(x, 'col', [(i, (i + CORES * k) % cols) for i in range(cols)])  41.1 us
    all_to_all x1, blocking collectives, on_device(): received = lax.all_to_all(terms, 'row', 0, 0, tiled=True)  22.8 us
    ppermute x3, starting transfers between devices, swap(): return lax.ppermute(x, 'col', [(i, i ^ 1) for i in range(cols)])  21.5 us
    all_to_all x1, blocking collectives, on_device(): lax.all_to_all(terms, ('row', 'col'), 0, 0, tiled=True, axis_index_groups...  20.5 us
    ppermute x12, waiting for transfers between devices, shift(): lax.ppermute(x, 'col', [(i, (i + CORES * k) % cols) for i in range(cols)])  15.5 us
    all_to_all x1, waiting for transfers between devices, on_device(): received = lax.all_to_all(terms, 'row', 0, 0, tiled=True)  11.2 us
    all_gather x1, blocking collectives, split_rows(): lax.all_gather(solved, 'col', axis=0, tiled=False, axis_index_groups=pairs)  8.64 us
  transfers between devices with their start and end apart: 16, of which 6 were waited for; matrix products, arithmetic and copies ran while one was open for 1% of the time, Pallas kernels for 0%

profile of v10, /device:TPU:1, one launch (start us, length us, event | category | flops | bytes accessed | tf_op | source)
XLA Modules:
  0.0 221.7 jit_solution(16840989109913821590)
XLA Ops:
  0.0 3.0 %shard_map.64 = (f32[2,64,128]{2,1,0:T(8,128)}, f32[784,128]{1,0:T(8,128)}) custom-call(s32[1,1,4]{2,1,0:T(1,128)} %bitcast.43, f32[4,1,2,64,128]{4,3,2,1,0:T(8,128)} %right.1, f32[4,1,2,128,128]{4,3,2,1,0:T(8,128)} %inverse.1, s32[3,1,16]{2,1,0:T(1,128)} %sources.1, s32[3,1,16]{2,1,0:T(1,128)} %targets.1), custom_call_target="tpu_custom_call" | custom-call | tf_op jit(solution)/shard_map/pallas_call | solution.py:68
  3.1 8.6 %all-gather = f32[4,64,128]{2,1,0:T(8,128)S(1)} all-gather(f32[2,64,128]{2,1,0:T(8,128)} %get-tuple-element.15.first), channel_id=2, replica_groups={{0,1},{2,3},{4,5},{6,7},{8,9},{10,11},{12,13},{14,15},{16,17},{18,19},{..., dimensions={0}, use_global_device_ids=true | all-gather | bytes 196608 | tf_op jit(solution)/shard_map/all_gather | solution.py:223
  11.7 2.3 %collective-permute-start.1 = (f32[3,1,16,128,128]{4,3,2,1,0:T(8,128)}, f32[3,1,16,128,128]{4,3,2,1,0:T(8,128)S(1)}, u32[]{:S(2)}, u32[]{:S(2)}) collective-permute-start(f32[3,1,16,128,128]{4,3,2,1,0:T(8,128)} %refs_2_.5), channel_id=1, source_target_pairs={{0,1},{1,0},{2,3},{3,2},{4,5},{5,4},{6,7},{7,6},{8,9},{9,8},{10,11... | collective-permute-start | bytes 9437192 | tf_op jit(solution)/shard_map/ppermute | solution.py:198
  14.0 19.1 %all-gather.1 = f32[16,32,128]{2,1,0:T(8,128)S(1)} all-gather(f32[4,32,128]{2,1,0:T(8,128)S(1)} %bitcast.36), channel_id=3, replica_groups={{0,8,16,24},{1,9,17,25},{2,10,18,26},{3,11,19,27},{4,12,20,28},{5,13,21..., dimensions={0}, use_global_device_ids=true | all-gather | bytes 327680 | tf_op jit(solution)/shard_map/all_gather | solution.py:207
  33.1 2.7 %collective-permute-start.2 = (f32[4,4,32,128]{3,2,1,0:T(8,128)S(1)}, f32[4,4,32,128]{3,2,1,0:T(8,128)S(1)}, u32[]{:S(2)}, u32[]{:S(2)}) collective-permute-start(f32[4,4,32,128]{3,2,1,0:T(8,128)S(1)} %bitcast.26), channel_id=1, source_target_pairs={{0,2},{1,3},{2,4},{3,5},{4,6},{5,7},{6,8},{7,9},{8,10},{9,11},{10,... | collective-permute-start | bytes 786440 | tf_op jit(solution)/shard_map/ppermute | solution.py:212
  35.8 3.8 %collective-permute-start.5 = (f32[4,4,32,128]{3,2,1,0:T(8,128)S(1)}, f32[4,4,32,128]{3,2,1,0:T(8,128)S(1)}, u32[]{:S(2)}, u32[]{:S(2)}) collective-permute-start(f32[4,4,32,128]{3,2,1,0:T(8,128)S(1)} %bitcast.27), channel_id=1, source_target_pairs={{0,30},{1,31},{2,0},{3,1},{4,2},{5,3},{6,4},{7,5},{8,6},{9,7},{10,... | collective-permute-start | bytes 786440 | tf_op jit(solution)/shard_map/ppermute | solution.py:212
  39.6 1.9 collective-permute-start.3
  41.6 5.9 %collective-permute-start = (f32[784,128]{1,0:T(8,128)}, f32[784,128]{1,0:T(8,128)S(1)}, u32[]{:S(2)}, u32[]{:S(2)}) collective-permute-start(f32[784,128]{1,0:T(8,128)} %get-tuple-element.16.packed), channel_id=1, source_target_pairs={{0,1},{1,0},{2,3},{3,2},{4,5},{5,4},{6,7},{7,6},{8,9},{9,8},{10,11... | collective-permute-start | bytes 1204232 | tf_op jit(solution)/shard_map/ppermute | solution.py:198
  48.2 5.5 %collective-permute-start.4 = (f32[2,4,32,128]{3,2,1,0:T(8,128)S(1)}, f32[2,4,32,128]{3,2,1,0:T(8,128)S(1)}, u32[]{:S(2)}, u32[]{:S(2)}) collective-permute-start(f32[2,4,32,128]{3,2,1,0:T(8,128)S(1)} %bitcast.39), channel_id=1, source_target_pairs={{0,28},{1,29},{2,30},{3,31},{4,0},{5,1},{6,2},{7,3},{8,4},{9,5},{1... | collective-permute-start | bytes 393224 | tf_op jit(solution)/shard_map/ppermute | solution.py:212
  53.8 6.2 %collective-permute-done.4 = f32[2,4,32,128]{3,2,1,0:T(8,128)S(1)} collective-permute-done((f32[2,4,32,128]{3,2,1,0:T(8,128)S(1)}, f32[2,4,32,128]{3,2,1,0:T(8,128)S(1)}, u32[]{:S(2)}, u32[]{:S(2)}) %collective-permute-start.4) | collective-permute-done | bytes 131104 | tf_op jit(solution)/shard_map/ppermute | solution.py:212
  60.1 2.6 %shard_map.65 = f32[64,32,128]{2,1,0:T(8,128)S(1)} custom-call(s32[1]{0:T(128)} %bitcast.column, s32[10,16]{1,0:T(8,128)S(1)} %slice_convert_fusion.1.refs_0_.info, s32[10,16]{1,0:T(8,128)S(1)} %slice_convert_fusion.refs_1_.other_info, f32[3,1,16,128,128]{4,3,2,1,0:T(8,128)S(1)} %copy-done, f32[3,1,16,128,128]{4,3,2,1,0:T(8,128)S(1)} %collective-permute-done.1.refs_3_, ...), custom_call_target="tpu_custom_call" | custom-call | tf_op jit(solution)/shard_map/pallas_call | solution.py:187
  62.8 22.8 %all_to_all.15.received = f32[64,32,128]{2,1,0:T(8,128)S(1)} all-to-all(f32[64,32,128]{2,1,0:T(8,128)S(1)} %shard_map.65), channel_id=1, replica_groups=mesh['row'=16,'col'=32] {'row'}, dimensions={0} | all-to-all | bytes 2097152 | tf_op jit(solution)/shard_map/all_to_all | solution.py:274
  86.8 15.9 %all-gather.2 = f32[16,32,128]{2,1,0:T(8,128)S(1)} all-gather(f32[4,32,128]{2,1,0:T(8,128)S(1)} %shard_map.66.refs_0_), channel_id=4, replica_groups={{0,8,16,24},{1,9,17,25},{2,10,18,26},{3,11,19,27},{4,12,20,28},{5,13,21..., dimensions={0}, use_global_device_ids=true | all-gather | bytes 327680 | tf_op jit(solution)/shard_map/all_gather | solution.py:207
  102.7 1.9 collective-permute-start.6
  104.6 4.8 %collective-permute-start.7 = (f32[2,4,32,128]{3,2,1,0:T(8,128)S(1)}, f32[2,4,32,128]{3,2,1,0:T(8,128)S(1)}, u32[]{:S(2)}, u32[]{:S(2)}) collective-permute-start(f32[2,4,32,128]{3,2,1,0:T(8,128)S(1)} %bitcast.42), channel_id=1, source_target_pairs={{0,4},{1,5},{2,6},{3,7},{4,8},{5,9},{6,10},{7,11},{8,12},{9,13},{1... | collective-permute-start | bytes 393224 | tf_op jit(solution)/shard_map/ppermute | solution.py:212
  109.5 4.6 %collective-permute-start.9 = (f32[4,4,32,128]{3,2,1,0:T(8,128)S(1)}, f32[4,4,32,128]{3,2,1,0:T(8,128)S(1)}, u32[]{:S(2)}, u32[]{:S(2)}) collective-permute-start(f32[4,4,32,128]{3,2,1,0:T(8,128)S(1)} %bitcast.34), channel_id=1, source_target_pairs={{0,30},{1,31},{2,0},{3,1},{4,2},{5,3},{6,4},{7,5},{8,6},{9,7},{10,... | collective-permute-start | bytes 786440 | tf_op jit(solution)/shard_map/ppermute | solution.py:212
  114.1 1.9 collective-permute-start.8
  116.1 6.4 %collective-permute-done.8 = f32[2,4,32,128]{3,2,1,0:T(8,128)S(1)} collective-permute-done((f32[2,4,32,128]{3,2,1,0:T(8,128)S(1)}, f32[2,4,32,128]{3,2,1,0:T(8,128)S(1)}, u32[]{:S(2)}, u32[]{:S(2)}) %collective-permute-start.8) | collective-permute-done | bytes 131104 | tf_op jit(solution)/shard_map/ppermute | solution.py:212
  122.5 2.6 %shard_map.67 = f32[64,32,128]{2,1,0:T(8,128)S(1)} custom-call(s32[1]{0:T(128)} %bitcast.column, s32[10,16]{1,0:T(8,128)S(1)} %slice_convert_fusion.1.refs_0_.info, s32[10,16]{1,0:T(8,128)S(1)} %slice_convert_fusion.refs_1_.other_info, f32[3,1,16,128,128]{4,3,2,1,0:T(8,128)S(1)} %copy-done, f32[3,1,16,128,128]{4,3,2,1,0:T(8,128)S(1)} %collective-permute-done.1.refs_3_, ...), custom_call_target="tpu_custom_call" | custom-call | tf_op jit(solution)/shard_map/pallas_call | solution.py:187
  127.1 4.3 %all-to-all-start.1 = ((f32[64,32,128]{2,1,0:T(8,128)}), f32[64,32,128]{2,1,0:T(8,128)}, u32[]{:S(2)}, u32[]{:S(2)}) async-start(f32[64,32,128]{2,1,0:T(8,128)} %copy-done.7), calls=%async_computation.1 | async-start | bytes 2097152 | tf_op jit(solution)/shard_map/all_to_all | solution.py:274
  132.9 11.2 %all-to-all-done.1.received = f32[64,32,128]{2,1,0:T(8,128)} async-done(((f32[64,32,128]{2,1,0:T(8,128)}), f32[64,32,128]{2,1,0:T(8,128)}, u32[]{:S(2)}, u32[]{:S(2)}) %all-to-all-start.1) | async-done | bytes 1048608 | tf_op jit(solution)/shard_map/all_to_all | solution.py:274
  145.8 1.7 shard_map.68.refs_1_
  147.5 16.0 %all-gather.3 = f32[16,32,128]{2,1,0:T(8,128)S(1)} all-gather(f32[4,32,128]{2,1,0:T(8,128)S(1)} %shard_map.68.refs_1_), channel_id=5, replica_groups={{0,8,16,24},{1,9,17,25},{2,10,18,26},{3,11,19,27},{4,12,20,28},{5,13,21..., dimensions={0}, use_global_device_ids=true | all-gather | bytes 327680 | tf_op jit(solution)/shard_map/all_gather | solution.py:207
  163.5 1.9 collective-permute-start.10
  165.5 4.6 %collective-permute-start.13 = (f32[4,4,32,128]{3,2,1,0:T(8,128)S(1)}, f32[4,4,32,128]{3,2,1,0:T(8,128)S(1)}, u32[]{:S(2)}, u32[]{:S(2)}) collective-permute-start(f32[4,4,32,128]{3,2,1,0:T(8,128)S(1)} %bitcast.30), channel_id=1, source_target_pairs={{0,30},{1,31},{2,0},{3,1},{4,2},{5,3},{6,4},{7,5},{8,6},{9,7},{10,... | collective-permute-start | bytes 786440 | tf_op jit(solution)/shard_map/ppermute | solution.py:212
  170.1 3.1 %collective-permute-start.11 = (f32[2,4,32,128]{3,2,1,0:T(8,128)S(1)}, f32[2,4,32,128]{3,2,1,0:T(8,128)S(1)}, u32[]{:S(2)}, u32[]{:S(2)}) collective-permute-start(f32[2,4,32,128]{3,2,1,0:T(8,128)S(1)} %bitcast.38), channel_id=1, source_target_pairs={{0,4},{1,5},{2,6},{3,7},{4,8},{5,9},{6,10},{7,11},{8,12},{9,13},{1... | collective-permute-start | bytes 393224 | tf_op jit(solution)/shard_map/ppermute | solution.py:212
  173.2 4.3 %collective-permute-start.12 = (f32[2,4,32,128]{3,2,1,0:T(8,128)S(1)}, f32[2,4,32,128]{3,2,1,0:T(8,128)S(1)}, u32[]{:S(2)}, u32[]{:S(2)}) collective-permute-start(f32[2,4,32,128]{3,2,1,0:T(8,128)S(1)} %bitcast.37), channel_id=1, source_target_pairs={{0,28},{1,29},{2,30},{3,31},{4,0},{5,1},{6,2},{7,3},{8,4},{9,5},{1... | collective-permute-start | bytes 393224 | tf_op jit(solution)/shard_map/ppermute | solution.py:212
  178.9 2.3 %collective-permute-done.12 = f32[2,4,32,128]{3,2,1,0:T(8,128)S(1)} collective-permute-done((f32[2,4,32,128]{3,2,1,0:T(8,128)S(1)}, f32[2,4,32,128]{3,2,1,0:T(8,128)S(1)}, u32[]{:S(2)}, u32[]{:S(2)}) %collective-permute-start.12) | collective-permute-done | bytes 131104 | tf_op jit(solution)/shard_map/ppermute | solution.py:212
  182.6 2.6 %shard_map.69 = f32[64,32,128]{2,1,0:T(8,128)S(1)} custom-call(s32[1]{0:T(128)} %bitcast.column, s32[10,16]{1,0:T(8,128)S(1)} %slice_convert_fusion.1.refs_0_.info, s32[10,16]{1,0:T(8,128)S(1)} %copy-done.17, f32[3,1,16,128,128]{4,3,2,1,0:T(8,128)S(1)} %copy-done, f32[3,1,16,128,128]{4,3,2,1,0:T(8,128)S(1)} %copy-done.2, f32[64,32,128]{2,1,0:T(8,128)S(1)} %bitcast.22, ...), custom_call_target="tpu_custom_call" | custom-call | tf_op jit(solution)/shard_map/pallas_call | solution.py:187
  185.2 13.4 %collective-permute-start.14 = (f32[2,2,32,128]{3,2,1,0:T(8,128)S(1)}, f32[2,2,32,128]{3,2,1,0:T(8,128)S(1)}, u32[]{:S(2)}, u32[]{:S(2)}) collective-permute-start(f32[2,2,32,128]{3,2,1,0:T(8,128)S(1)} %pad_maximum_fusion), channel_id=1, source_target_pairs={{0,1},{1,0},{2,3},{3,2},{4,5},{5,4},{6,7},{7,6},{8,9},{9,8},{10,11... | collective-permute-start | bytes 196616 | tf_op jit(solution)/shard_map/ppermute | solution.py:198
  199.5 20.5 %all_to_all.16.received = f32[64,32,128]{2,1,0:T(8,128)S(1)} all-to-all(f32[64,32,128]{2,1,0:T(8,128)S(1)} %shard_map.69), channel_id=1, replica_groups={{0,1,32,33,64,65,96,97,128,129,160,161,192,193,224,225,256,257,288,289,..., dimensions={0} | all-to-all | bytes 2097152 | tf_op jit(solution)/shard_map/all_to_all | solution.py:268
  220.0 1.7 shard_map.70
  (76 shorter events, 10.8 us)
Async XLA Ops:
  0.0 60.1 %copy-start = (f32[3,1,16,128,128]{4,3,2,1,0:T(8,128)S(1)}, f32[3,1,16,128,128]{4,3,2,1,0:T(8,128)}, u32[]{:S(2)}) copy-start(f32[3,1,16,128,128]{4,3,2,1,0:T(8,128)} %refs_2_.5) | copy-start | bytes 9437188
  11.7 48.4 %collective-permute-start.1 = (f32[3,1,16,128,128]{4,3,2,1,0:T(8,128)}, f32[3,1,16,128,128]{4,3,2,1,0:T(8,128)S(1)}, u32[]{:S(2)}, u32[]{:S(2)}) collective-permute-start(f32[3,1,16,128,128]{4,3,2,1,0:T(8,128)} %refs_2_.5), channel_id=1, source_target_pairs={{0,1},{1,0},{2,3},{3,2},{4,5},{5,4},{6,7},{7,6},{8,9},{9,8},{10,11... | collective-permute-start | bytes 9437192 | tf_op jit(solution)/shard_map/ppermute | solution.py:198
  33.1 15.1 %collective-permute-start.2 = (f32[4,4,32,128]{3,2,1,0:T(8,128)S(1)}, f32[4,4,32,128]{3,2,1,0:T(8,128)S(1)}, u32[]{:S(2)}, u32[]{:S(2)}) collective-permute-start(f32[4,4,32,128]{3,2,1,0:T(8,128)S(1)} %bitcast.26), channel_id=1, source_target_pairs={{0,2},{1,3},{2,4},{3,5},{4,6},{5,7},{6,8},{7,9},{8,10},{9,11},{10,... | collective-permute-start | bytes 786440 | tf_op jit(solution)/shard_map/ppermute | solution.py:212
  35.8 24.2 %collective-permute-start.5 = (f32[4,4,32,128]{3,2,1,0:T(8,128)S(1)}, f32[4,4,32,128]{3,2,1,0:T(8,128)S(1)}, u32[]{:S(2)}, u32[]{:S(2)}) collective-permute-start(f32[4,4,32,128]{3,2,1,0:T(8,128)S(1)} %bitcast.27), channel_id=1, source_target_pairs={{0,30},{1,31},{2,0},{3,1},{4,2},{5,3},{6,4},{7,5},{8,6},{9,7},{10,... | collective-permute-start | bytes 786440 | tf_op jit(solution)/shard_map/ppermute | solution.py:212
  39.6 14.1 %collective-permute-start.3 = (f32[2,4,32,128]{3,2,1,0:T(8,128)S(1)}, f32[2,4,32,128]{3,2,1,0:T(8,128)S(1)}, u32[]{:S(2)}, u32[]{:S(2)}) collective-permute-start(f32[2,4,32,128]{3,2,1,0:T(8,128)S(1)} %bitcast.41), channel_id=1, source_target_pairs={{0,4},{1,5},{2,6},{3,7},{4,8},{5,9},{6,10},{7,11},{8,12},{9,13},{1... | collective-permute-start | bytes 393224 | tf_op jit(solution)/shard_map/ppermute | solution.py:212
  41.6 18.5 %collective-permute-start = (f32[784,128]{1,0:T(8,128)}, f32[784,128]{1,0:T(8,128)S(1)}, u32[]{:S(2)}, u32[]{:S(2)}) collective-permute-start(f32[784,128]{1,0:T(8,128)} %get-tuple-element.16.packed), channel_id=1, source_target_pairs={{0,1},{1,0},{2,3},{3,2},{4,5},{5,4},{6,7},{7,6},{8,9},{9,8},{10,11... | collective-permute-start | bytes 1204232 | tf_op jit(solution)/shard_map/ppermute | solution.py:198
  48.2 11.8 %collective-permute-start.4 = (f32[2,4,32,128]{3,2,1,0:T(8,128)S(1)}, f32[2,4,32,128]{3,2,1,0:T(8,128)S(1)}, u32[]{:S(2)}, u32[]{:S(2)}) collective-permute-start(f32[2,4,32,128]{3,2,1,0:T(8,128)S(1)} %bitcast.39), channel_id=1, source_target_pairs={{0,28},{1,29},{2,30},{3,31},{4,0},{5,1},{6,2},{7,3},{8,4},{9,5},{1... | collective-permute-start | bytes 393224 | tf_op jit(solution)/shard_map/ppermute | solution.py:212
  60.0 62.5 %copy-start.3 = (f32[16,4,32,128]{3,2,1,0:T(8,128)}, f32[16,4,32,128]{3,2,1,0:T(8,128)S(1)}, u32[]{:S(2)}) copy-start(f32[16,4,32,128]{3,2,1,0:T(8,128)S(1)} %constant_dynamic-update-slice_fusion) | copy-start | bytes 3145732
  60.1 25.6 %copy-start.10 = (f32[784,128]{1,0:T(8,128)}, f32[784,128]{1,0:T(8,128)S(1)}, u32[]{:S(2)}) copy-start(f32[784,128]{1,0:T(8,128)S(1)} %collective-permute-done.other_packed) | copy-start | bytes 1204228
  60.1 62.4 %copy-start.15 = (s32[10,16]{1,0:T(8,128)}, s32[10,16]{1,0:T(8,128)S(1)}, u32[]{:S(2)}) copy-start(s32[10,16]{1,0:T(8,128)S(1)} %slice_convert_fusion.refs_1_.other_info) | copy-start | bytes 1924
  60.1 62.4 %copy-start.1 = (f32[3,1,16,128,128]{4,3,2,1,0:T(8,128)}, f32[3,1,16,128,128]{4,3,2,1,0:T(8,128)S(1)}, u32[]{:S(2)}) copy-start(f32[3,1,16,128,128]{4,3,2,1,0:T(8,128)S(1)} %collective-permute-done.1.refs_3_) | copy-start | bytes 9437188
  60.1 25.5 %copy-start.9 = (f32[784,128]{1,0:T(8,128)S(1)}, f32[784,128]{1,0:T(8,128)}, u32[]{:S(2)}) copy-start(f32[784,128]{1,0:T(8,128)} %get-tuple-element.16.packed) | copy-start | bytes 1204228
  86.8 17.9 %copy-start.13 = (f32[4,32,128]{2,1,0:T(8,128)}, f32[4,32,128]{2,1,0:T(8,128)S(1)}, u32[]{:S(2)}) copy-start(f32[4,32,128]{2,1,0:T(8,128)S(1)} %shard_map.66.refs_0_) | copy-start | bytes 196612
  102.7 13.3 %collective-permute-start.6 = (f32[4,4,32,128]{3,2,1,0:T(8,128)S(1)}, f32[4,4,32,128]{3,2,1,0:T(8,128)S(1)}, u32[]{:S(2)}, u32[]{:S(2)}) collective-permute-start(f32[4,4,32,128]{3,2,1,0:T(8,128)S(1)} %bitcast.32), channel_id=1, source_target_pairs={{0,2},{1,3},{2,4},{3,5},{4,6},{5,7},{6,8},{7,9},{8,10},{9,11},{10,... | collective-permute-start | bytes 786440 | tf_op jit(solution)/shard_map/ppermute | solution.py:212
  104.6 11.4 %collective-permute-start.7 = (f32[2,4,32,128]{3,2,1,0:T(8,128)S(1)}, f32[2,4,32,128]{3,2,1,0:T(8,128)S(1)}, u32[]{:S(2)}, u32[]{:S(2)}) collective-permute-start(f32[2,4,32,128]{3,2,1,0:T(8,128)S(1)} %bitcast.42), channel_id=1, source_target_pairs={{0,4},{1,5},{2,6},{3,7},{4,8},{5,9},{6,10},{7,11},{8,12},{9,13},{1... | collective-permute-start | bytes 393224 | tf_op jit(solution)/shard_map/ppermute | solution.py:212
  109.5 13.0 %collective-permute-start.9 = (f32[4,4,32,128]{3,2,1,0:T(8,128)S(1)}, f32[4,4,32,128]{3,2,1,0:T(8,128)S(1)}, u32[]{:S(2)}, u32[]{:S(2)}) collective-permute-start(f32[4,4,32,128]{3,2,1,0:T(8,128)S(1)} %bitcast.34), channel_id=1, source_target_pairs={{0,30},{1,31},{2,0},{3,1},{4,2},{5,3},{6,4},{7,5},{8,6},{9,7},{10,... | collective-permute-start | bytes 786440 | tf_op jit(solution)/shard_map/ppermute | solution.py:212
  114.1 8.4 %collective-permute-start.8 = (f32[2,4,32,128]{3,2,1,0:T(8,128)S(1)}, f32[2,4,32,128]{3,2,1,0:T(8,128)S(1)}, u32[]{:S(2)}, u32[]{:S(2)}) collective-permute-start(f32[2,4,32,128]{3,2,1,0:T(8,128)S(1)} %bitcast.40), channel_id=1, source_target_pairs={{0,28},{1,29},{2,30},{3,31},{4,0},{5,1},{6,2},{7,3},{8,4},{9,5},{1... | collective-permute-start | bytes 393224 | tf_op jit(solution)/shard_map/ppermute | solution.py:212
  125.2 1.0 copy-start.5
  127.1 16.9 %all-to-all-start.1 = ((f32[64,32,128]{2,1,0:T(8,128)}), f32[64,32,128]{2,1,0:T(8,128)}, u32[]{:S(2)}, u32[]{:S(2)}) async-start(f32[64,32,128]{2,1,0:T(8,128)} %copy-done.7), calls=%async_computation.1 | async-start | bytes 2097152 | tf_op jit(solution)/shard_map/all_to_all | solution.py:274
  145.7 35.5 %copy-start.2 = (f32[3,1,16,128,128]{4,3,2,1,0:T(8,128)S(1)}, f32[3,1,16,128,128]{4,3,2,1,0:T(8,128)}, u32[]{:S(2)}) copy-start(f32[3,1,16,128,128]{4,3,2,1,0:T(8,128)} %copy-done.1) | copy-start | bytes 9437188
  145.7 35.6 %copy-start.4 = (f32[16,4,32,128]{3,2,1,0:T(8,128)S(1)}, f32[16,4,32,128]{3,2,1,0:T(8,128)}, u32[]{:S(2)}) copy-start(f32[16,4,32,128]{3,2,1,0:T(8,128)} %copy-done.3) | copy-start | bytes 3145732
  145.8 35.6 %copy-start.17 = (s32[10,16]{1,0:T(8,128)S(1)}, s32[10,16]{1,0:T(8,128)}, u32[]{:S(2)}) copy-start(s32[10,16]{1,0:T(8,128)} %copy-done.15) | copy-start | bytes 1924
  163.5 14.7 %collective-permute-start.10 = (f32[4,4,32,128]{3,2,1,0:T(8,128)S(1)}, f32[4,4,32,128]{3,2,1,0:T(8,128)S(1)}, u32[]{:S(2)}, u32[]{:S(2)}) collective-permute-start(f32[4,4,32,128]{3,2,1,0:T(8,128)S(1)} %bitcast.29), channel_id=1, source_target_pairs={{0,2},{1,3},{2,4},{3,5},{4,6},{5,7},{6,8},{7,9},{8,10},{9,11},{10,... | collective-permute-start | bytes 786440 | tf_op jit(solution)/shard_map/ppermute | solution.py:212
  165.5 15.8 %collective-permute-start.13 = (f32[4,4,32,128]{3,2,1,0:T(8,128)S(1)}, f32[4,4,32,128]{3,2,1,0:T(8,128)S(1)}, u32[]{:S(2)}, u32[]{:S(2)}) collective-permute-start(f32[4,4,32,128]{3,2,1,0:T(8,128)S(1)} %bitcast.30), channel_id=1, source_target_pairs={{0,30},{1,31},{2,0},{3,1},{4,2},{5,3},{6,4},{7,5},{8,6},{9,7},{10,... | collective-permute-start | bytes 786440 | tf_op jit(solution)/shard_map/ppermute | solution.py:212
  170.1 8.8 %collective-permute-start.11 = (f32[2,4,32,128]{3,2,1,0:T(8,128)S(1)}, f32[2,4,32,128]{3,2,1,0:T(8,128)S(1)}, u32[]{:S(2)}, u32[]{:S(2)}) collective-permute-start(f32[2,4,32,128]{3,2,1,0:T(8,128)S(1)} %bitcast.38), channel_id=1, source_target_pairs={{0,4},{1,5},{2,6},{3,7},{4,8},{5,9},{6,10},{7,11},{8,12},{9,13},{1... | collective-permute-start | bytes 393224 | tf_op jit(solution)/shard_map/ppermute | solution.py:212
  173.2 8.1 %collective-permute-start.12 = (f32[2,4,32,128]{3,2,1,0:T(8,128)S(1)}, f32[2,4,32,128]{3,2,1,0:T(8,128)S(1)}, u32[]{:S(2)}, u32[]{:S(2)}) collective-permute-start(f32[2,4,32,128]{3,2,1,0:T(8,128)S(1)} %bitcast.37), channel_id=1, source_target_pairs={{0,28},{1,29},{2,30},{3,31},{4,0},{5,1},{6,2},{7,3},{8,4},{9,5},{1... | collective-permute-start | bytes 393224 | tf_op jit(solution)/shard_map/ppermute | solution.py:212
  181.3 1.2 copy-start.6
  182.5 37.5 %copy-start.8 = (f32[4,1,2,128,128]{4,3,2,1,0:T(8,128)S(1)}, f32[4,1,2,128,128]{4,3,2,1,0:T(8,128)}, u32[]{:S(2)}) copy-start(f32[4,1,2,128,128]{4,3,2,1,0:T(8,128)} %inverse.1) | copy-start | bytes 1572868
  182.5 37.5 %copy-start.12 = (f32[4,1,2,64,128]{4,3,2,1,0:T(8,128)S(1)}, f32[4,1,2,64,128]{4,3,2,1,0:T(8,128)}, u32[]{:S(2)}) copy-start(f32[4,1,2,64,128]{4,3,2,1,0:T(8,128)} %right.1) | copy-start | bytes 786436
  182.6 37.5 %copy-start.14 = (f32[4,32,128]{2,1,0:T(8,128)S(1)}, f32[4,32,128]{2,1,0:T(8,128)}, u32[]{:S(2)}) copy-start(f32[4,32,128]{2,1,0:T(8,128)} %copy-done.13) | copy-start | bytes 196612
  182.6 37.5 %copy-start.18 = (f32[2,64,128]{2,1,0:T(8,128)S(1)}, f32[2,64,128]{2,1,0:T(8,128)}, u32[]{:S(2)}) copy-start(f32[2,64,128]{2,1,0:T(8,128)} %get-tuple-element.15.first) | copy-start | bytes 196612
  185.2 14.3 %collective-permute-start.14 = (f32[2,2,32,128]{3,2,1,0:T(8,128)S(1)}, f32[2,2,32,128]{3,2,1,0:T(8,128)S(1)}, u32[]{:S(2)}, u32[]{:S(2)}) collective-permute-start(f32[2,2,32,128]{3,2,1,0:T(8,128)S(1)} %pad_maximum_fusion), channel_id=1, source_target_pairs={{0,1},{1,0},{2,3},{3,2},{4,5},{5,4},{6,7},{7,6},{8,9},{9,8},{10,11... | collective-permute-start | bytes 196616 | tf_op jit(solution)/shard_map/ppermute | solution.py:198
  (3 other events, 2.7 us)

commit v11 on v6

--- a/solution.py
+++ b/solution.py
@@ -121,7 +121,7 @@
         out_shape=jax.ShapeDtypeStruct(right.shape, jnp.float32),
         in_specs=[VMEM, SMEM, SMEM] + [VMEM] * (4 + len(mine)),
         out_specs=VMEM,
-        compiler_params=PARAMS,
+        compiler_params=pltpu.CompilerParams(vmem_limit_bytes=60 * 1024 * 1024),
     )(received, column, info, right, inverse, first, *mine, theirs)
 
 

time: 220 us -> 221 us (level)
    unnamed x41 -> x47, local copies, waits for them, and re-layouts: 4.95 us -> 4.97 us
where the time goes in v11:
time: 221 us; the launch traced here: 220 us
  blocking collectives  105 us (48%)
  starting transfers between devices  63.9 us (29%)
  waiting for transfers between devices  27.7 us (13%)
  Pallas kernels  16.1 us (7%)
  local copies, waits for them, and re-layouts  6.76 us (3%)
    all_gather x3, blocking collectives, gather_far(): lax.all_gather(solved, 'col', axis=0, tiled=False, axis_index_groups=far)  52.4 us
    ppermute x12, starting transfers between devices, shift(): lax.ppermute(x, 'col', [(i, (i + CORES * k) % cols) for i in range(cols)])  38.8 us
    all_to_all x1, blocking collectives, on_device(): received = lax.all_to_all(terms, 'row', 0, 0, tiled=True)  22.9 us
    all_to_all x1, blocking collectives, on_device(): lax.all_to_all(terms, ('row', 'col'), 0, 0, tiled=True, axis_index_groups...  21.1 us
    ppermute x3, starting transfers between devices, swap(): return lax.ppermute(x, 'col', [(i, i ^ 1) for i in range(cols)])  20.7 us
    ppermute x12, waiting for transfers between devices, shift(): lax.ppermute(x, 'col', [(i, (i + CORES * k) % cols) for i in range(cols)])  13.8 us
    all_to_all x1, waiting for transfers between devices, on_device(): received = lax.all_to_all(terms, 'row', 0, 0, tiled=True)  13 us
    all_gather x1, blocking collectives, split_rows(): lax.all_gather(solved, 'col', axis=0, tiled=False, axis_index_groups=pairs)  8.64 us
  transfers between devices with their start and end apart: 16, of which 5 were waited for; matrix products, arithmetic and copies ran while one was open for 1% of the time, Pallas kernels for 1%

profile of v11, /device:TPU:1, one launch (start us, length us, event | category | flops | bytes accessed | tf_op | source)
XLA Modules:
  0.0 220.2 jit_solution(8154526931504342500)
XLA Ops:
  0.0 2.8 %shard_map.64.first = f32[2,64,128]{2,1,0:T(8,128)} custom-call(s32[1,1,4]{2,1,0:T(1,128)} %bitcast.41, f32[4,1,2,64,128]{4,3,2,1,0:T(8,128)} %right.5, f32[4,1,2,128,128]{4,3,2,1,0:T(8,128)} %inverse.5), custom_call_target="tpu_custom_call" | custom-call | tf_op jit(solution)/shard_map/pallas_call | solution.py:41
  2.9 8.6 %all-gather = f32[4,64,128]{2,1,0:T(8,128)S(1)} all-gather(f32[2,64,128]{2,1,0:T(8,128)} %shard_map.64.first), channel_id=2, replica_groups={{0,1},{2,3},{4,5},{6,7},{8,9},{10,11},{12,13},{14,15},{16,17},{18,19},{..., dimensions={0}, use_global_device_ids=true | all-gather | bytes 196608 | tf_op jit(solution)/shard_map/all_gather | solution.py:198
  11.5 19.1 %all_gather.23 = f32[4,4,32,128]{3,2,1,0:T(8,128)S(1)} all-gather(f32[1,4,32,128]{3,2,1,0:T(8,128)S(1)} %bitcast.36), channel_id=1, replica_groups={{0,8,16,24},{1,9,17,25},{2,10,18,26},{3,11,19,27},{4,12,20,28},{5,13,21..., dimensions={0}, use_global_device_ids=true | all-gather | bytes 327680 | tf_op jit(solution)/shard_map/all_gather | solution.py:182
  30.6 5.6 %collective-permute-start.1 = (f32[3,1,16,128,128]{4,3,2,1,0:T(8,128)}, f32[3,1,16,128,128]{4,3,2,1,0:T(8,128)S(1)}, u32[]{:S(2)}, u32[]{:S(2)}) collective-permute-start(f32[3,1,16,128,128]{4,3,2,1,0:T(8,128)} %refs_2_.5), channel_id=1, source_target_pairs={{0,1},{1,0},{2,3},{3,2},{4,5},{5,4},{6,7},{7,6},{8,9},{9,8},{10,11... | collective-permute-start | bytes 9437192 | tf_op jit(solution)/shard_map/ppermute | solution.py:173
  36.2 2.9 %collective-permute-start.2 = (f32[4,4,32,128]{3,2,1,0:T(8,128)S(1)}, f32[4,4,32,128]{3,2,1,0:T(8,128)S(1)}, u32[]{:S(2)}, u32[]{:S(2)}) collective-permute-start(f32[4,4,32,128]{3,2,1,0:T(8,128)S(1)} %all_gather.23), channel_id=1, source_target_pairs={{0,2},{1,3},{2,4},{3,5},{4,6},{5,7},{6,8},{7,9},{8,10},{9,11},{10,... | collective-permute-start | bytes 786440 | tf_op jit(solution)/shard_map/ppermute | solution.py:187
  39.1 3.6 %collective-permute-start.5 = (f32[4,4,32,128]{3,2,1,0:T(8,128)S(1)}, f32[4,4,32,128]{3,2,1,0:T(8,128)S(1)}, u32[]{:S(2)}, u32[]{:S(2)}) collective-permute-start(f32[4,4,32,128]{3,2,1,0:T(8,128)S(1)} %all_gather.23), channel_id=1, source_target_pairs={{0,30},{1,31},{2,0},{3,1},{4,2},{5,3},{6,4},{7,5},{8,6},{9,7},{10,... | collective-permute-start | bytes 786440 | tf_op jit(solution)/shard_map/ppermute | solution.py:187
  42.8 2.1 collective-permute-start.3
  44.9 5.3 %collective-permute-start.4 = (f32[2,4,32,128]{3,2,1,0:T(8,128)S(1)}, f32[2,4,32,128]{3,2,1,0:T(8,128)S(1)}, u32[]{:S(2)}, u32[]{:S(2)}) collective-permute-start(f32[2,4,32,128]{3,2,1,0:T(8,128)S(1)} %get-tuple-element.33), channel_id=1, source_target_pairs={{0,28},{1,29},{2,30},{3,31},{4,0},{5,1},{6,2},{7,3},{8,4},{9,5},{1... | collective-permute-start | bytes 393224 | tf_op jit(solution)/shard_map/ppermute | solution.py:187
  52.7 3.0 %collective-permute-start = (f32[784,128]{1,0:T(8,128)S(1)}, f32[784,128]{1,0:T(8,128)S(1)}, u32[]{:S(2)}, u32[]{:S(2)}) collective-permute-start(f32[784,128]{1,0:T(8,128)S(1)} %select_maximum_fusion), channel_id=1, source_target_pairs={{0,1},{1,0},{2,3},{3,2},{4,5},{5,4},{6,7},{7,6},{8,9},{9,8},{10,11... | collective-permute-start | bytes 1204232 | tf_op jit(solution)/shard_map/ppermute | solution.py:173
  57.2 2.6 %shard_map.65 = f32[64,32,128]{2,1,0:T(8,128)S(1)} custom-call(s32[1]{0:T(128)} %bitcast.column, s32[10,16]{1,0:T(8,128)S(1)} %get-tuple-element.36.refs_0_.info, s32[10,16]{1,0:T(8,128)S(1)} %slice_convert_fusion.refs_1_.other_info, f32[3,1,16,128,128]{4,3,2,1,0:T(8,128)S(1)} %copy-done, f32[3,1,16,128,128]{4,3,2,1,0:T(8,128)S(1)} %collective-permute-done.1.refs_3_, ...), custom_call_target="tpu_custom_call" | custom-call | tf_op jit(solution)/shard_map/pallas_call | solution.py:162
  59.8 22.9 %all_to_all.15.received = f32[64,32,128]{2,1,0:T(8,128)S(1)} all-to-all(f32[64,32,128]{2,1,0:T(8,128)S(1)} %shard_map.65), channel_id=1, replica_groups=mesh['row'=16,'col'=32] {'row'}, dimensions={0} | all-to-all | bytes 2097152 | tf_op jit(solution)/shard_map/all_to_all | solution.py:258
  82.7 1.2 shard_map.66.refs_0_
  83.8 16.0 %all-gather.1 = f32[16,32,128]{2,1,0:T(8,128)S(1)} all-gather(f32[4,32,128]{2,1,0:T(8,128)S(1)} %shard_map.66.refs_0_), channel_id=3, replica_groups={{0,8,16,24},{1,9,17,25},{2,10,18,26},{3,11,19,27},{4,12,20,28},{5,13,21..., dimensions={0}, use_global_device_ids=true | all-gather | bytes 327680 | tf_op jit(solution)/shard_map/all_gather | solution.py:182
  99.8 1.9 collective-permute-start.6
  101.8 4.5 %collective-permute-start.7 = (f32[2,4,32,128]{3,2,1,0:T(8,128)S(1)}, f32[2,4,32,128]{3,2,1,0:T(8,128)S(1)}, u32[]{:S(2)}, u32[]{:S(2)}) collective-permute-start(f32[2,4,32,128]{3,2,1,0:T(8,128)S(1)} %bitcast.40), channel_id=1, source_target_pairs={{0,4},{1,5},{2,6},{3,7},{4,8},{5,9},{6,10},{7,11},{8,12},{9,13},{1... | collective-permute-start | bytes 393224 | tf_op jit(solution)/shard_map/ppermute | solution.py:187
  106.3 4.6 %collective-permute-start.9 = (f32[4,4,32,128]{3,2,1,0:T(8,128)S(1)}, f32[4,4,32,128]{3,2,1,0:T(8,128)S(1)}, u32[]{:S(2)}, u32[]{:S(2)}) collective-permute-start(f32[4,4,32,128]{3,2,1,0:T(8,128)S(1)} %bitcast.33), channel_id=1, source_target_pairs={{0,30},{1,31},{2,0},{3,1},{4,2},{5,3},{6,4},{7,5},{8,6},{9,7},{10,... | collective-permute-start | bytes 786440 | tf_op jit(solution)/shard_map/ppermute | solution.py:187
  110.9 1.9 collective-permute-start.8
  112.9 6.5 %collective-permute-done.8 = f32[2,4,32,128]{3,2,1,0:T(8,128)S(1)} collective-permute-done((f32[2,4,32,128]{3,2,1,0:T(8,128)S(1)}, f32[2,4,32,128]{3,2,1,0:T(8,128)S(1)}, u32[]{:S(2)}, u32[]{:S(2)}) %collective-permute-start.8) | collective-permute-done | bytes 131104 | tf_op jit(solution)/shard_map/ppermute | solution.py:187
  119.5 2.6 %shard_map.67 = f32[64,32,128]{2,1,0:T(8,128)S(1)} custom-call(s32[1]{0:T(128)} %bitcast.column, s32[10,16]{1,0:T(8,128)S(1)} %get-tuple-element.36.refs_0_.info, s32[10,16]{1,0:T(8,128)S(1)} %slice_convert_fusion.refs_1_.other_info, f32[3,1,16,128,128]{4,3,2,1,0:T(8,128)S(1)} %copy-done, f32[3,1,16,128,128]{4,3,2,1,0:T(8,128)S(1)} %collective-permute-done.1.refs_3_, ...), custom_call_target="tpu_custom_call" | custom-call | tf_op jit(solution)/shard_map/pallas_call | solution.py:162
  124.1 4.3 %all-to-all-start.1 = ((f32[64,32,128]{2,1,0:T(8,128)}), f32[64,32,128]{2,1,0:T(8,128)}, u32[]{:S(2)}, u32[]{:S(2)}) async-start(f32[64,32,128]{2,1,0:T(8,128)} %copy-done.10), calls=%async_computation.1 | async-start | bytes 2097152 | tf_op jit(solution)/shard_map/all_to_all | solution.py:258
  128.5 13.0 %all-to-all-done.1.received = f32[64,32,128]{2,1,0:T(8,128)} async-done(((f32[64,32,128]{2,1,0:T(8,128)}), f32[64,32,128]{2,1,0:T(8,128)}, u32[]{:S(2)}, u32[]{:S(2)}) %all-to-all-start.1) | async-done | bytes 1048608 | tf_op jit(solution)/shard_map/all_to_all | solution.py:258
  143.6 1.7 shard_map.68.refs_1_
  145.3 17.3 %all-gather.2 = f32[16,32,128]{2,1,0:T(8,128)S(1)} all-gather(f32[4,32,128]{2,1,0:T(8,128)S(1)} %shard_map.68.refs_1_), channel_id=4, replica_groups={{0,8,16,24},{1,9,17,25},{2,10,18,26},{3,11,19,27},{4,12,20,28},{5,13,21..., dimensions={0}, use_global_device_ids=true | all-gather | bytes 327680 | tf_op jit(solution)/shard_map/all_gather | solution.py:182
  162.7 1.9 collective-permute-start.10
  164.6 4.6 %collective-permute-start.13 = (f32[4,4,32,128]{3,2,1,0:T(8,128)S(1)}, f32[4,4,32,128]{3,2,1,0:T(8,128)S(1)}, u32[]{:S(2)}, u32[]{:S(2)}) collective-permute-start(f32[4,4,32,128]{3,2,1,0:T(8,128)S(1)} %bitcast.29), channel_id=1, source_target_pairs={{0,30},{1,31},{2,0},{3,1},{4,2},{5,3},{6,4},{7,5},{8,6},{9,7},{10,... | collective-permute-start | bytes 786440 | tf_op jit(solution)/shard_map/ppermute | solution.py:187
  169.2 1.9 collective-permute-start.11
  171.2 12.1 %collective-permute-start.14 = (f32[2,2,32,128]{3,2,1,0:T(8,128)S(1)}, f32[2,2,32,128]{3,2,1,0:T(8,128)S(1)}, u32[]{:S(2)}, u32[]{:S(2)}) collective-permute-start(f32[2,2,32,128]{3,2,1,0:T(8,128)S(1)} %pad_maximum_fusion), channel_id=1, source_target_pairs={{0,1},{1,0},{2,3},{3,2},{4,5},{5,4},{6,7},{7,6},{8,9},{9,8},{10,11... | collective-permute-start | bytes 196616 | tf_op jit(solution)/shard_map/ppermute | solution.py:173
  183.2 3.6 %collective-permute-start.12 = (f32[2,4,32,128]{3,2,1,0:T(8,128)S(1)}, f32[2,4,32,128]{3,2,1,0:T(8,128)S(1)}, u32[]{:S(2)}, u32[]{:S(2)}) collective-permute-start(f32[2,4,32,128]{3,2,1,0:T(8,128)S(1)} %get-tuple-element.29), channel_id=1, source_target_pairs={{0,28},{1,29},{2,30},{3,31},{4,0},{5,1},{6,2},{7,3},{8,4},{9,5},{1... | collective-permute-start | bytes 393224 | tf_op jit(solution)/shard_map/ppermute | solution.py:187
  186.9 6.9 %collective-permute-done.12 = f32[2,4,32,128]{3,2,1,0:T(8,128)S(1)} collective-permute-done((f32[2,4,32,128]{3,2,1,0:T(8,128)S(1)}, f32[2,4,32,128]{3,2,1,0:T(8,128)S(1)}, u32[]{:S(2)}, u32[]{:S(2)}) %collective-permute-start.12) | collective-permute-done | bytes 131104 | tf_op jit(solution)/shard_map/ppermute | solution.py:187
  193.9 2.6 %shard_map.69 = f32[64,32,128]{2,1,0:T(8,128)S(1)} custom-call(s32[1]{0:T(128)} %bitcast.column, s32[10,16]{1,0:T(8,128)S(1)} %get-tuple-element.36.refs_0_.info, s32[10,16]{1,0:T(8,128)S(1)} %slice_convert_fusion.refs_1_.other_info, f32[3,1,16,128,128]{4,3,2,1,0:T(8,128)S(1)} %copy-done, f32[3,1,16,128,128]{4,3,2,1,0:T(8,128)S(1)} %copy-done.2, ...), custom_call_target="tpu_custom_call" | custom-call | tf_op jit(solution)/shard_map/pallas_call | solution.py:162
  196.6 21.1 %all_to_all.16.received = f32[64,32,128]{2,1,0:T(8,128)} all-to-all(f32[64,32,128]{2,1,0:T(8,128)S(1)} %shard_map.69), channel_id=1, replica_groups={{0,1,32,33,64,65,96,97,128,129,160,161,192,193,224,225,256,257,288,289,..., dimensions={0} | all-to-all | bytes 2097152 | tf_op jit(solution)/shard_map/all_to_all | solution.py:252
  217.7 2.5 %shard_map.70 = f32[4,1,2,64,128]{4,3,2,1,0:T(8,128)} custom-call(f32[64,32,128]{2,1,0:T(8,128)} %all_to_all.16.received, s32[1]{0:T(128)} %bitcast.column, s32[10,16]{1,0:T(8,128)} %copy-done.15, f32[4,1,2,64,128]{4,3,2,1,0:T(8,128)} %right.5, f32[4,1,2,128,128]{4,3,2,1,0:T(8,128)} %inverse.5, f32[2,64,128]{2,1,0:T(8,128)} %shard_map.64.first, ...), custom_call_target="tpu_custom_call" | custom-call | tf_op jit(solution)/shard_map/pallas_call | solution.py:119
  (79 shorter events, 8.1 us)
Async XLA Ops:
  0.0 52.6 %slice-start = ((f32[4,1,2,128,128]{4,3,2,1,0:T(8,128)}), f32[2,1,2,128,128]{4,3,2,1,0:T(8,128)S(1)}, s32[]{:S(2)}) async-start(f32[4,1,2,128,128]{4,3,2,1,0:T(8,128)} %inverse.5), calls=%async_computation.3 | async-start | bytes 524288 | tf_op jit(solution)/shard_map/slice | solution.py:239
  0.0 57.1 %copy-start = (f32[3,1,16,128,128]{4,3,2,1,0:T(8,128)S(1)}, f32[3,1,16,128,128]{4,3,2,1,0:T(8,128)}, u32[]{:S(2)}) copy-start(f32[3,1,16,128,128]{4,3,2,1,0:T(8,128)} %refs_2_.5) | copy-start | bytes 9437188
  30.6 26.5 %collective-permute-start.1 = (f32[3,1,16,128,128]{4,3,2,1,0:T(8,128)}, f32[3,1,16,128,128]{4,3,2,1,0:T(8,128)S(1)}, u32[]{:S(2)}, u32[]{:S(2)}) collective-permute-start(f32[3,1,16,128,128]{4,3,2,1,0:T(8,128)} %refs_2_.5), channel_id=1, source_target_pairs={{0,1},{1,0},{2,3},{3,2},{4,5},{5,4},{6,7},{7,6},{8,9},{9,8},{10,11... | collective-permute-start | bytes 9437192 | tf_op jit(solution)/shard_map/ppermute | solution.py:173
  36.2 16.5 %collective-permute-start.2 = (f32[4,4,32,128]{3,2,1,0:T(8,128)S(1)}, f32[4,4,32,128]{3,2,1,0:T(8,128)S(1)}, u32[]{:S(2)}, u32[]{:S(2)}) collective-permute-start(f32[4,4,32,128]{3,2,1,0:T(8,128)S(1)} %all_gather.23), channel_id=1, source_target_pairs={{0,2},{1,3},{2,4},{3,5},{4,6},{5,7},{6,8},{7,9},{8,10},{9,11},{10,... | collective-permute-start | bytes 786440 | tf_op jit(solution)/shard_map/ppermute | solution.py:187
  39.1 17.0 %collective-permute-start.5 = (f32[4,4,32,128]{3,2,1,0:T(8,128)S(1)}, f32[4,4,32,128]{3,2,1,0:T(8,128)S(1)}, u32[]{:S(2)}, u32[]{:S(2)}) collective-permute-start(f32[4,4,32,128]{3,2,1,0:T(8,128)S(1)} %all_gather.23), channel_id=1, source_target_pairs={{0,30},{1,31},{2,0},{3,1},{4,2},{5,3},{6,4},{7,5},{8,6},{9,7},{10,... | collective-permute-start | bytes 786440 | tf_op jit(solution)/shard_map/ppermute | solution.py:187
  42.8 13.0 %collective-permute-start.3 = (f32[2,4,32,128]{3,2,1,0:T(8,128)S(1)}, f32[2,4,32,128]{3,2,1,0:T(8,128)S(1)}, u32[]{:S(2)}, u32[]{:S(2)}) collective-permute-start(f32[2,4,32,128]{3,2,1,0:T(8,128)S(1)} %get-tuple-element.34), channel_id=1, source_target_pairs={{0,4},{1,5},{2,6},{3,7},{4,8},{5,9},{6,10},{7,11},{8,12},{9,13},{1... | collective-permute-start | bytes 393224 | tf_op jit(solution)/shard_map/ppermute | solution.py:187
  44.9 11.3 %collective-permute-start.4 = (f32[2,4,32,128]{3,2,1,0:T(8,128)S(1)}, f32[2,4,32,128]{3,2,1,0:T(8,128)S(1)}, u32[]{:S(2)}, u32[]{:S(2)}) collective-permute-start(f32[2,4,32,128]{3,2,1,0:T(8,128)S(1)} %get-tuple-element.33), channel_id=1, source_target_pairs={{0,28},{1,29},{2,30},{3,31},{4,0},{5,1},{6,2},{7,3},{8,4},{9,5},{1... | collective-permute-start | bytes 393224 | tf_op jit(solution)/shard_map/ppermute | solution.py:187
  51.7 142.2 %copy-start.15 = (s32[10,16]{1,0:T(8,128)}, s32[10,16]{1,0:T(8,128)S(1)}, u32[]{:S(2)}) copy-start(s32[10,16]{1,0:T(8,128)S(1)} %get-tuple-element.36.refs_0_.info) | copy-start | bytes 1924
  52.7 4.4 %collective-permute-start = (f32[784,128]{1,0:T(8,128)S(1)}, f32[784,128]{1,0:T(8,128)S(1)}, u32[]{:S(2)}, u32[]{:S(2)}) collective-permute-start(f32[784,128]{1,0:T(8,128)S(1)} %select_maximum_fusion), channel_id=1, source_target_pairs={{0,1},{1,0},{2,3},{3,2},{4,5},{5,4},{6,7},{7,6},{8,9},{9,8},{10,11... | collective-permute-start | bytes 1204232 | tf_op jit(solution)/shard_map/ppermute | solution.py:173
  56.2 63.3 %copy-start.3 = (f32[16,4,32,128]{3,2,1,0:T(8,128)}, f32[16,4,32,128]{3,2,1,0:T(8,128)S(1)}, u32[]{:S(2)}) copy-start(f32[16,4,32,128]{3,2,1,0:T(8,128)S(1)} %constant_dynamic-update-slice_fusion) | copy-start | bytes 3145732
  57.1 25.6 %copy-start.11 = (f32[784,128]{1,0:T(8,128)}, f32[784,128]{1,0:T(8,128)S(1)}, u32[]{:S(2)}) copy-start(f32[784,128]{1,0:T(8,128)S(1)} %collective-permute-done.packed) | copy-start | bytes 1204228
  57.1 62.4 %copy-start.1 = (f32[3,1,16,128,128]{4,3,2,1,0:T(8,128)}, f32[3,1,16,128,128]{4,3,2,1,0:T(8,128)S(1)}, u32[]{:S(2)}) copy-start(f32[3,1,16,128,128]{4,3,2,1,0:T(8,128)S(1)} %collective-permute-done.1.refs_3_) | copy-start | bytes 9437188
  57.1 25.5 %copy-start.5 = (f32[4,1,2,128,128]{4,3,2,1,0:T(8,128)S(1)}, f32[4,1,2,128,128]{4,3,2,1,0:T(8,128)}, u32[]{:S(2)}) copy-start(f32[4,1,2,128,128]{4,3,2,1,0:T(8,128)} %inverse.5) | copy-start | bytes 1572868
  57.1 25.5 %copy-start.7 = (f32[4,1,2,64,128]{4,3,2,1,0:T(8,128)S(1)}, f32[4,1,2,64,128]{4,3,2,1,0:T(8,128)}, u32[]{:S(2)}) copy-start(f32[4,1,2,64,128]{4,3,2,1,0:T(8,128)} %right.5) | copy-start | bytes 786436
  83.8 44.6 %copy-start.13 = (f32[4,32,128]{2,1,0:T(8,128)}, f32[4,32,128]{2,1,0:T(8,128)S(1)}, u32[]{:S(2)}) copy-start(f32[4,32,128]{2,1,0:T(8,128)S(1)} %shard_map.66.refs_0_) | copy-start | bytes 196612
  99.8 13.0 %collective-permute-start.6 = (f32[4,4,32,128]{3,2,1,0:T(8,128)S(1)}, f32[4,4,32,128]{3,2,1,0:T(8,128)S(1)}, u32[]{:S(2)}, u32[]{:S(2)}) collective-permute-start(f32[4,4,32,128]{3,2,1,0:T(8,128)S(1)} %bitcast.31), channel_id=1, source_target_pairs={{0,2},{1,3},{2,4},{3,5},{4,6},{5,7},{6,8},{7,9},{8,10},{9,11},{10,... | collective-permute-start | bytes 786440 | tf_op jit(solution)/shard_map/ppermute | solution.py:187
  101.8 11.1 %collective-permute-start.7 = (f32[2,4,32,128]{3,2,1,0:T(8,128)S(1)}, f32[2,4,32,128]{3,2,1,0:T(8,128)S(1)}, u32[]{:S(2)}, u32[]{:S(2)}) collective-permute-start(f32[2,4,32,128]{3,2,1,0:T(8,128)S(1)} %bitcast.40), channel_id=1, source_target_pairs={{0,4},{1,5},{2,6},{3,7},{4,8},{5,9},{6,10},{7,11},{8,12},{9,13},{1... | collective-permute-start | bytes 393224 | tf_op jit(solution)/shard_map/ppermute | solution.py:187
  106.3 13.1 %collective-permute-start.9 = (f32[4,4,32,128]{3,2,1,0:T(8,128)S(1)}, f32[4,4,32,128]{3,2,1,0:T(8,128)S(1)}, u32[]{:S(2)}, u32[]{:S(2)}) collective-permute-start(f32[4,4,32,128]{3,2,1,0:T(8,128)S(1)} %bitcast.33), channel_id=1, source_target_pairs={{0,30},{1,31},{2,0},{3,1},{4,2},{5,3},{6,4},{7,5},{8,6},{9,7},{10,... | collective-permute-start | bytes 786440 | tf_op jit(solution)/shard_map/ppermute | solution.py:187
  110.9 8.5 %collective-permute-start.8 = (f32[2,4,32,128]{3,2,1,0:T(8,128)S(1)}, f32[2,4,32,128]{3,2,1,0:T(8,128)S(1)}, u32[]{:S(2)}, u32[]{:S(2)}) collective-permute-start(f32[2,4,32,128]{3,2,1,0:T(8,128)S(1)} %bitcast.39), channel_id=1, source_target_pairs={{0,28},{1,29},{2,30},{3,31},{4,0},{5,1},{6,2},{7,3},{8,4},{9,5},{1... | collective-permute-start | bytes 393224 | tf_op jit(solution)/shard_map/ppermute | solution.py:187
  122.1 1.0 copy-start.8
  124.1 17.4 %all-to-all-start.1 = ((f32[64,32,128]{2,1,0:T(8,128)}), f32[64,32,128]{2,1,0:T(8,128)}, u32[]{:S(2)}, u32[]{:S(2)}) async-start(f32[64,32,128]{2,1,0:T(8,128)} %copy-done.10), calls=%async_computation.1 | async-start | bytes 2097152 | tf_op jit(solution)/shard_map/all_to_all | solution.py:258
  141.5 1.0 copy-start.6
  143.6 50.3 %copy-start.2 = (f32[3,1,16,128,128]{4,3,2,1,0:T(8,128)S(1)}, f32[3,1,16,128,128]{4,3,2,1,0:T(8,128)}, u32[]{:S(2)}) copy-start(f32[3,1,16,128,128]{4,3,2,1,0:T(8,128)} %copy-done.1) | copy-start | bytes 9437188
  143.6 50.3 %copy-start.4 = (f32[16,4,32,128]{3,2,1,0:T(8,128)S(1)}, f32[16,4,32,128]{3,2,1,0:T(8,128)}, u32[]{:S(2)}) copy-start(f32[16,4,32,128]{3,2,1,0:T(8,128)} %copy-done.3) | copy-start | bytes 3145732
  143.6 50.3 %copy-start.9 = (f32[16,4,32,128]{3,2,1,0:T(8,128)S(1)}, f32[16,4,32,128]{3,2,1,0:T(8,128)}, u32[]{:S(2)}) copy-start(f32[16,4,32,128]{3,2,1,0:T(8,128)} %copy-done.8) | copy-start | bytes 3145732
  145.3 51.2 %copy-start.14 = (f32[4,32,128]{2,1,0:T(8,128)}, f32[4,32,128]{2,1,0:T(8,128)S(1)}, u32[]{:S(2)}) copy-start(f32[4,32,128]{2,1,0:T(8,128)S(1)} %shard_map.68.refs_1_) | copy-start | bytes 196612
  162.7 24.2 %collective-permute-start.10 = (f32[4,4,32,128]{3,2,1,0:T(8,128)S(1)}, f32[4,4,32,128]{3,2,1,0:T(8,128)S(1)}, u32[]{:S(2)}, u32[]{:S(2)}) collective-permute-start(f32[4,4,32,128]{3,2,1,0:T(8,128)S(1)} %bitcast.27), channel_id=1, source_target_pairs={{0,2},{1,3},{2,4},{3,5},{4,6},{5,7},{6,8},{7,9},{8,10},{9,11},{10,... | collective-permute-start | bytes 786440 | tf_op jit(solution)/shard_map/ppermute | solution.py:187
  164.6 29.2 %collective-permute-start.13 = (f32[4,4,32,128]{3,2,1,0:T(8,128)S(1)}, f32[4,4,32,128]{3,2,1,0:T(8,128)S(1)}, u32[]{:S(2)}, u32[]{:S(2)}) collective-permute-start(f32[4,4,32,128]{3,2,1,0:T(8,128)S(1)} %bitcast.29), channel_id=1, source_target_pairs={{0,30},{1,31},{2,0},{3,1},{4,2},{5,3},{6,4},{7,5},{8,6},{9,7},{10,... | collective-permute-start | bytes 786440 | tf_op jit(solution)/shard_map/ppermute | solution.py:187
  169.2 17.7 %collective-permute-start.11 = (f32[2,4,32,128]{3,2,1,0:T(8,128)S(1)}, f32[2,4,32,128]{3,2,1,0:T(8,128)S(1)}, u32[]{:S(2)}, u32[]{:S(2)}) collective-permute-start(f32[2,4,32,128]{3,2,1,0:T(8,128)S(1)} %get-tuple-element.30), channel_id=1, source_target_pairs={{0,4},{1,5},{2,6},{3,7},{4,8},{5,9},{6,10},{7,11},{8,12},{9,13},{1... | collective-permute-start | bytes 393224 | tf_op jit(solution)/shard_map/ppermute | solution.py:187
  171.2 25.4 %collective-permute-start.14 = (f32[2,2,32,128]{3,2,1,0:T(8,128)S(1)}, f32[2,2,32,128]{3,2,1,0:T(8,128)S(1)}, u32[]{:S(2)}, u32[]{:S(2)}) collective-permute-start(f32[2,2,32,128]{3,2,1,0:T(8,128)S(1)} %pad_maximum_fusion), channel_id=1, source_target_pairs={{0,1},{1,0},{2,3},{3,2},{4,5},{5,4},{6,7},{7,6},{8,9},{9,8},{10,11... | collective-permute-start | bytes 196616 | tf_op jit(solution)/shard_map/ppermute | solution.py:173
  183.2 10.6 %collective-permute-start.12 = (f32[2,4,32,128]{3,2,1,0:T(8,128)S(1)}, f32[2,4,32,128]{3,2,1,0:T(8,128)S(1)}, u32[]{:S(2)}, u32[]{:S(2)}) collective-permute-start(f32[2,4,32,128]{3,2,1,0:T(8,128)S(1)} %get-tuple-element.29), channel_id=1, source_target_pairs={{0,28},{1,29},{2,30},{3,31},{4,0},{5,1},{6,2},{7,3},{8,4},{9,5},{1... | collective-permute-start | bytes 393224 | tf_op jit(solution)/shard_map/ppermute | solution.py:187
  196.6 21.1 %copy-start.16 = (f32[2,2,32,128]{3,2,1,0:T(8,128)}, f32[2,2,32,128]{3,2,1,0:T(8,128)S(1)}, u32[]{:S(2)}) copy-start(f32[2,2,32,128]{3,2,1,0:T(8,128)S(1)} %collective-permute-done.14.refs_2_) | copy-start | bytes 196612
  (2 other events, 2.0 us)
